TPU v7x, 32 devices: a whole 2x2x4 slice. The times are simulated.
32 devices in a mesh: groups: 2 (over y), expert: 16 (over z, x, core), node: 1.
Axes of the slice: x: 2, y: 2, z: 4, core: 2. Of those that a mesh axis runs over, the one named last changes fastest.
Arguments:
- tokens: bfloat16 [768, 2048], P(('groups', 'expert')), parts along dimension 0, may hold values from -6 to 6
- norm_gain: float32 [2048], replicated, may hold values from 0.5 to 1.5
- probe_signs: int32 [768, 2048], P(('groups', 'expert')), parts along dimension 0, may hold values from 0 to 1
- cotangent: bfloat16 [768, 2048], P(('groups', 'expert')), parts along dimension 0, may hold values from -6 to 6
- routes: int32 [2, 768, 4], P('node', ('groups', 'expert')), parts along dimension 1, may hold values from 0 to 7, all different within a row; in each aligned block of 24 rows (0 to 23, 24 to 47, ..., all dimensions but the last counted through in order) at most 16 rows name the same one
- gates: float32 [2, 768, 4], P('node', ('groups', 'expert')), parts along dimension 1, may hold values from 0.05 to 0.5
- expert_weights: bfloat16 [3, 2048, 6144], P(None, None, ('expert', 'node')), may hold values from -0.125 to 0.125
Outputs:
- hvp: float32 [768, 2048], P(('groups', 'expert'), 'node'), parts along dimension 0
- quad: float32 [768], P(('groups', 'expert')), parts along dimension 0
There are 2 independent parts, one for each index of `groups`. A program takes and returns all parts, laid end to end along the dimension named above; an argument that names none is the same for every part. Nothing has to cross between parts.
Inputs may be any that keep to these rules, and one draw needn't show every extreme that they name: Each row of routes names 4 different experts. In every aligned block of 24 rows of one node group no expert is named more than 16 times, a bound that some block reaches.
All inputs are finite; a program needn't handle non-finite values.
Results may differ from a plain program's by a relative error of at most 0.0048.
Values may be sent and summed in bfloat16 or wider, within the bound.
No kernel may reach another device: no remote copies, remote signals or barrier semaphores. Data moves between devices by JAX's collectives and lax.ppermute only.
A program may use at most 64 MiB of HBM per device.

v0:
```python
import jax
import jax.numpy as jnp
from jax import lax
from jax.sharding import PartitionSpec as P

EPS = 1e-06


def expert_terms(weights, rows, rows_t, cotan):
    count = rows.shape[0]
    both = jnp.concatenate([rows, rows_t], 0)
    pre_gate = jnp.dot(both, weights[0], preferred_element_type=jnp.float32)
    pre_up = jnp.dot(both, weights[1], preferred_element_type=jnp.float32)
    gate, gate_t = (pre_gate[:count], pre_gate[count:])
    up, up_t = (pre_up[:count], pre_up[count:])
    back = jnp.dot(cotan, weights[2], preferred_element_type=jnp.float32)
    sig = jax.nn.sigmoid(gate)
    act = gate * sig
    slope = sig * (1.0 + gate * (1.0 - sig))
    bend = sig * (1.0 - sig) * (2.0 + gate * (1.0 - 2.0 * sig))
    d_gate = (back * slope * up).astype(jnp.bfloat16)
    d_up = (back * act).astype(jnp.bfloat16)
    t_gate = (back * (bend * gate_t * up + slope * up_t)).astype(jnp.bfloat16)
    t_up = (back * slope * gate_t).astype(jnp.bfloat16)
    contract = (((1,), (1,)), ((), ()))
    lhs_gate = jnp.concatenate([d_gate, t_gate], 0)
    lhs_up = jnp.concatenate([d_up, t_up], 0)
    total = lax.dot_general(lhs_gate, weights[0], contract, preferred_element_type=jnp.float32)
    total = total + lax.dot_general(
        lhs_up, weights[1], contract, preferred_element_type=jnp.float32
    )
    return (total[:count], total[count:])


def slot_targets(route_ids, expert_count, capacity):
    flat = route_ids.reshape(-1)
    count = flat.shape[0]
    onehot = (flat[:, None] == jnp.arange(expert_count, dtype=jnp.int32)[None, :]).astype(
        jnp.float32
    )
    lower = (jnp.arange(count)[:, None] > jnp.arange(count)[None, :]).astype(jnp.float32)
    before = jnp.dot(lower, onehot, precision=lax.Precision.HIGHEST)
    rank = jnp.sum(before * onehot, axis=1).astype(jnp.int32)
    return flat * capacity + rank


def local(tokens, norm_gain, probe_signs, cotangent, routes, gates, expert_weights):
    xf = tokens.astype(jnp.float32)
    probe = (2 * probe_signs - 1).astype(jnp.float32)
    tok_dev, width = xf.shape
    groups_here = routes.shape[0]
    half = routes.shape[2]
    n_exp = lax.axis_size("expert")
    expert_count = n_exp // 2
    cap = min(2 * ((2 * tok_dev * half + 3 * expert_count - 1) // (3 * expert_count)), tok_dev)
    buffer_rows = expert_count * cap
    scale = lax.rsqrt(jnp.mean(xf * xf, axis=1, keepdims=True) + EPS)
    along = jnp.mean(xf * probe, axis=1, keepdims=True)
    normed = (xf * scale * norm_gain).astype(jnp.bfloat16)
    normed_t = (norm_gain * (scale * probe - scale**3 * xf * along)).astype(jnp.bfloat16)
    stack_z, stack_t, stack_c, stack_w = ([], [], [], [])
    for group in range(groups_here):
        target = slot_targets(routes[group], expert_count, cap)
        place = (jnp.arange(buffer_rows, dtype=jnp.int32)[:, None] == target[None, :]).reshape(
            buffer_rows, tok_dev, half
        )
        place_tok = jnp.sum(place.astype(jnp.float32), axis=2).astype(jnp.bfloat16)
        stack_w.append(jnp.sum(place.astype(jnp.float32) * gates[group][None, :, :], axis=2))
        stack_z.append(
            jnp.dot(place_tok, normed, preferred_element_type=jnp.float32).astype(jnp.bfloat16)
        )
        stack_t.append(
            jnp.dot(place_tok, normed_t, preferred_element_type=jnp.float32).astype(jnp.bfloat16)
        )
        stack_c.append(
            jnp.dot(place_tok, cotangent, preferred_element_type=jnp.float32).astype(jnp.bfloat16)
        )
    rows_z = jnp.stack(stack_z, 0)
    rows_t = jnp.stack(stack_t, 0)
    rows_c = jnp.stack(stack_c, 0)
    weighted = jnp.stack(stack_w, 0)
    own_half = lax.all_gather(expert_weights, "node", axis=2, tiled=True)

    def arrange(rows):
        shaped = rows.reshape(groups_here, expert_count, 1, cap, width)
        shaped = jnp.broadcast_to(shaped, (groups_here, expert_count, 2, cap, width))
        return jnp.transpose(shaped, (1, 2, 0, 3, 4)).reshape(n_exp, groups_here * cap, width)

    send_z, send_t, send_c = (arrange(rows_z), arrange(rows_t), arrange(rows_c))
    got_z = lax.all_to_all(send_z, "expert", split_axis=0, concat_axis=0, tiled=True)
    got_t = lax.all_to_all(send_t, "expert", split_axis=0, concat_axis=0, tiled=True)
    got_c = lax.all_to_all(send_c, "expert", split_axis=0, concat_axis=0, tiled=True)
    sources, items, cols = got_z.shape
    g_rows, t_rows = expert_terms(
        own_half, got_z.reshape(-1, cols), got_t.reshape(-1, cols), got_c.reshape(-1, cols)
    )
    g_rows = g_rows.reshape(sources, items, cols)
    t_rows = t_rows.reshape(sources, items, cols)
    back_g = lax.all_to_all(g_rows, "expert", split_axis=0, concat_axis=0, tiled=True)
    back_t = lax.all_to_all(t_rows, "expert", split_axis=0, concat_axis=0, tiled=True)

    def restore(rows):
        shaped = jnp.sum(rows.reshape(expert_count, 2, groups_here, cap, width), axis=1)
        return jnp.transpose(shaped, (1, 0, 2, 3)).reshape(groups_here, buffer_rows, width)

    back_g = restore(back_g)
    back_t = restore(back_t)
    contract = (((0, 1), (0, 1)), ((), ()))
    grad_z = lax.dot_general(weighted, back_g, contract, precision=lax.Precision.HIGHEST)
    tan_z = lax.dot_general(weighted, back_t, contract, precision=lax.Precision.HIGHEST)
    share = width // lax.axis_size("node")
    start = lax.axis_index("node") * share
    slope_r = -(scale**3) * along
    grad_z, tan_z = lax.psum((grad_z, tan_z), "node")
    lifted = norm_gain * grad_z
    lifted_t = norm_gain * tan_z
    first = jnp.mean(xf * lifted, axis=1, keepdims=True)
    second = jnp.mean(xf * lifted_t, axis=1, keepdims=True)
    third = jnp.mean(probe * lifted, axis=1, keepdims=True)
    whole_hvp = (
        scale * lifted_t
        + slope_r * lifted
        - 3.0 * scale**2 * slope_r * first * xf
        - scale**3 * first * probe
        - scale**3 * (second + third) * xf
    )
    quad = jnp.mean(probe * whole_hvp, axis=1)
    hvp = lax.dynamic_slice_in_dim(whole_hvp, start, share, 1)
    return (hvp, quad)


def solution(mesh):
    placed = (
        P(("groups", "expert"), None),
        P(),
        P(("groups", "expert"), None),
        P(("groups", "expert"), None),
        P("node", ("groups", "expert"), None),
        P("node", ("groups", "expert"), None),
        P(None, None, ("expert", "node")),
    )
    return jax.shard_map(
        local,
        mesh=mesh,
        in_specs=placed,
        out_specs=(P(("groups", "expert"), "node"), P(("groups", "expert"))),
        check_vma=False,
    )
```

profile of v0, /device:TPU:11, one launch (start us, length us, event | category | flops | bytes accessed | tf_op | source)
XLA Modules:
  0.0 390.3 jit_solution(11563090511799865117)
XLA Ops:
  0.6 0.0 copy-start
  0.6 0.7 slice_bitcast_fusion.1
  1.4 0.7 fusion.67
  2.1 0.1 copy.53
  2.2 0.1 eq.59
  2.3 0.1 fusion.16
  2.4 0.1 convert_element_type.82
  2.5 0.1 copy.54
  2.6 0.1 copy.55
  2.7 0.1 eq.66
  2.8 0.1 fusion.17
  3.0 0.1 convert_element_type.84
  3.1 0.1 copy.56
  3.2 1.1 fusion.32
  4.3 0.0 copy-start.16
  4.3 0.5 copy-done.14
  4.8 0.1 copy-done.16
  4.9 0.7 bitcast_add_fusion.1
  5.6 0.7 select_reduce_fusion
  6.3 1.2 convolution_convert_fusion.2
  7.6 1.2 convolution_convert_fusion.3
  8.9 0.1 maximum_bitcast_fusion.1
  9.0 0.1 copy.58
  9.0 1.6 broadcast_in_dim.15
  10.7 6.7 %all-to-all-start.1 = ((bf16[16,32,2048]{2,1,0:T(8,128)(2,1)}), bf16[16,32,2048]{2,1,0:T(8,128)(2,1)S(1)}, u32[]{:S(2)}, u32[]{:S(2)}) async-start(bf16[16,32,2048]{2,1,0:T(8,128)(2,1)} %bitcast.17), calls=%async_computation.1 | async-start | bytes 4194304 | tf_op jit(solution)/shard_map/all_to_all | solution.py:90
  17.4 0.4 convolution_convert_fusion
  17.8 0.0 copy-done.10
  17.8 0.0 copy-done.12
  17.8 0.4 convolution_convert_fusion.1
  18.1 0.1 maximum_bitcast_fusion.2
  18.2 0.1 copy.59
  18.3 46.4 %all-to-all-done.1 = bf16[16,32,2048]{2,1,0:T(8,128)(2,1)S(1)} async-done(((bf16[16,32,2048]{2,1,0:T(8,128)(2,1)}), bf16[16,32,2048]{2,1,0:T(8,128)(2,1)S(1)}, u32[]{:S(2)}, u32[]{:S(2)}) %all-to-all-start.1) | async-done | bytes 2097184 | tf_op jit(solution)/shard_map/all_to_all | solution.py:90
  64.8 1.6 broadcast_in_dim.17
  66.4 5.0 %all-to-all-start.2 = ((bf16[16,32,2048]{2,1,0:T(8,128)(2,1)}), bf16[16,32,2048]{2,1,0:T(8,128)(2,1)}, u32[]{:S(2)}, u32[]{:S(2)}) async-start(bf16[16,32,2048]{2,1,0:T(8,128)(2,1)} %bitcast.23), calls=%async_computation.2 | async-start | bytes 4194304 | tf_op jit(solution)/shard_map/all_to_all | solution.py:91
  71.4 0.3 convolution_convert_fusion.4
  71.8 0.3 convolution_convert_fusion.5
  72.1 0.1 maximum_bitcast_fusion
  72.2 0.1 copy.57
  72.3 46.6 %all-to-all-done.2 = bf16[16,32,2048]{2,1,0:T(8,128)(2,1)} async-done(((bf16[16,32,2048]{2,1,0:T(8,128)(2,1)}), bf16[16,32,2048]{2,1,0:T(8,128)(2,1)}, u32[]{:S(2)}, u32[]{:S(2)}) %all-to-all-start.2) | async-done | bytes 2097184 | tf_op jit(solution)/shard_map/all_to_all | solution.py:91
  119.0 1.6 broadcast_in_dim.13
  120.5 4.9 %all-to-all-start = ((bf16[16,32,2048]{2,1,0:T(8,128)(2,1)}), bf16[16,32,2048]{2,1,0:T(8,128)(2,1)}, u32[]{:S(2)}, u32[]{:S(2)}) async-start(bf16[16,32,2048]{2,1,0:T(8,128)(2,1)} %bitcast.10), calls=%async_computation | async-start | bytes 4194304 | tf_op jit(solution)/shard_map/all_to_all | solution.py:92
  125.4 5.6 %fusion = f32[1024,384]{1,0:T(8,128)} fusion(bf16[512,2048]{1,0:T(8,128)(2,1)} %bitcast.24, bf16[512,2048]{1,0:T(8,128)(2,1)S(1)} %bitcast.83, bf16[3,2048,384]{2,1,0:T(8,128)(2,1)} %param.13), kind=kOutput, calls=%fused_computation.2 | convolution fusion | flops 1619001344 | bytes 7340032 | tf_op jit(solution)/shard_map/dot_general | solution.py:13
  131.0 5.5 %fusion.1 = f32[1024,384]{1,0:T(8,128)} fusion(bf16[512,2048]{1,0:T(8,128)(2,1)} %bitcast.24, bf16[512,2048]{1,0:T(8,128)(2,1)S(1)} %bitcast.84, bf16[3,2048,384]{2,1,0:T(8,128)(2,1)} %param.13), kind=kOutput, calls=%fused_computation.3 | convolution fusion | flops 1619001344 | bytes 7340032 | tf_op jit(solution)/shard_map/dot_general | solution.py:12
  136.6 36.4 %all-to-all-done = bf16[16,32,2048]{2,1,0:T(8,128)(2,1)} async-done(((bf16[16,32,2048]{2,1,0:T(8,128)(2,1)}), bf16[16,32,2048]{2,1,0:T(8,128)(2,1)}, u32[]{:S(2)}, u32[]{:S(2)}) %all-to-all-start) | async-done | bytes 2097184 | tf_op jit(solution)/shard_map/all_to_all | solution.py:92
  173.0 4.7 %multiply_convert_fusion.1 = (bf16[512,384]{1,0:T(8,128)(2,1)S(1)}, bf16[512,384]{1,0:T(8,128)(2,1)S(1)}, bf16[512,384]{1,0:T(8,128)(2,1)S(1)}, bf16[512,384]{1,0:T(8,128)(2,1)S(1)}) fusion(f32[1024,384]{1,0:T(8,128)} %fusion.1, f32[1024,384]{1,0:T(8,128)} %fusion, bf16[512,2048]{1,0:T(8,128)(2,1)} %bitcast.11, bf16[3,2048,384]{2,1,0:T(8,128)(2,1)} %param.13), kind=kOutput, calls=%fused_computation.51 | convolution fusion | flops 810614784 | bytes 8388608 | tf_op jit(solution)/shard_map/dot_general | solution.py:16
  177.7 3.8 fusion.6
  181.5 3.8 convolution_add_fusion
  185.2 2.8 fusion.66
  188.0 97.0 %all_to_all.25 = f32[16,32,2048]{2,1,0:T(8,128)} all-to-all(f32[16,32,2048]{2,1,0:T(8,128)S(1)} %bitcast.78), channel_id=1, replica_groups=mesh['groups'=2,'expert'=16,'node'=1] {'expert'}, dimensions={0} | all-to-all | bytes 8388608 | tf_op jit(solution)/shard_map/all_to_all | solution.py:99
  285.1 5.3 %all-to-all-start.3 = ((f32[16,32,2048]{2,1,0:T(8,128)}), f32[16,32,2048]{2,1,0:T(8,128)}, u32[]{:S(2)}, u32[]{:S(2)}) async-start(f32[16,32,2048]{2,1,0:T(8,128)} %bitcast.77), calls=%async_computation.3 | async-start | bytes 8388608 | tf_op jit(solution)/shard_map/all_to_all | solution.py:100
  290.4 2.8 reduce_sum.135
  293.2 1.5 copy.61
  294.7 88.1 %all-to-all-done.3 = f32[16,32,2048]{2,1,0:T(8,128)} async-done(((f32[16,32,2048]{2,1,0:T(8,128)}), f32[16,32,2048]{2,1,0:T(8,128)}, u32[]{:S(2)}, u32[]{:S(2)}) %all-to-all-start.3) | async-done | bytes 4194336 | tf_op jit(solution)/shard_map/all_to_all | solution.py:100
  382.8 2.8 reduce_sum.134
  385.6 0.0 copy-start.6
  385.7 0.1 copy.60
  385.8 0.5 copy-done.6
  386.4 0.0 copy-done.7
  386.4 0.0 copy-start.1
  386.4 1.1 fusion.3
  387.5 0.0 copy-done.2
  387.5 1.3 fusion.40
  388.8 1.0 multiply_reduce_fusion
  389.8 0.5 broadcast_multiply_fusion
  (29 shorter events, 0.1 us)
Async XLA Ops:
  0.6 70.8 %copy-start = (bf16[24,2048]{1,0:T(8,128)(2,1)S(1)}, bf16[24,2048]{1,0:T(8,128)(2,1)}, u32[]{:S(2)}) copy-start(bf16[24,2048]{1,0:T(8,128)(2,1)} %param.10) | copy-start | bytes 294916
  4.3 0.5 copy-start.14
  4.3 0.6 copy-start.16
  4.9 12.8 %copy-start.10 = (f32[24]{0:T(128)}, f32[24]{0:T(128)S(1)}, u32[]{:S(2)}) copy-start(f32[24]{0:T(128)S(1)} %get-tuple-element.31) | copy-start | bytes 292
  4.9 12.9 %copy-start.12 = (f32[24]{0:T(128)}, f32[24]{0:T(128)S(1)}, u32[]{:S(2)}) copy-start(f32[24]{0:T(128)S(1)} %get-tuple-element.32) | copy-start | bytes 292
  6.3 11.0 %copy-start.8 = (bf16[128,24]{0,1:T(8,128)(2,1)}, bf16[128,24]{0,1:T(8,128)(2,1)S(1)}, u32[]{:S(2)}) copy-start(bf16[128,24]{0,1:T(8,128)(2,1)S(1)} %get-tuple-element.10) | copy-start | bytes 18436
  10.6 6.7 %copy-start.3 = (s32[24,2048]{1,0:T(8,128)S(1)}, s32[24,2048]{1,0:T(8,128)}, u32[]{:S(2)}) copy-start(s32[24,2048]{1,0:T(8,128)} %param.9) | copy-start | bytes 589828
  10.6 6.7 %copy-start.4 = (bf16[24,2048]{1,0:T(8,128)(2,1)S(1)}, bf16[24,2048]{1,0:T(8,128)(2,1)}, u32[]{:S(2)}) copy-start(bf16[24,2048]{1,0:T(8,128)(2,1)} %param.7) | copy-start | bytes 294916
  10.6 6.7 %copy-start.5 = (f32[2048]{0:T(1024)S(1)}, f32[2048]{0:T(1024)}, u32[]{:S(2)}) copy-start(f32[2048]{0:T(1024)} %param.8) | copy-start | bytes 24580
  10.7 54.1 %all-to-all-start.1 = ((bf16[16,32,2048]{2,1,0:T(8,128)(2,1)}), bf16[16,32,2048]{2,1,0:T(8,128)(2,1)S(1)}, u32[]{:S(2)}, u32[]{:S(2)}) async-start(bf16[16,32,2048]{2,1,0:T(8,128)(2,1)} %bitcast.17), calls=%async_computation.1 | async-start | bytes 4194304 | tf_op jit(solution)/shard_map/all_to_all | solution.py:90
  66.4 5.1 %copy-start.9 = (bf16[128,24]{0,1:T(8,128)(2,1)S(1)}, bf16[128,24]{0,1:T(8,128)(2,1)}, u32[]{:S(2)}) copy-start(bf16[128,24]{0,1:T(8,128)(2,1)} %copy-done.8) | copy-start | bytes 18436
  66.4 52.6 %all-to-all-start.2 = ((bf16[16,32,2048]{2,1,0:T(8,128)(2,1)}), bf16[16,32,2048]{2,1,0:T(8,128)(2,1)}, u32[]{:S(2)}, u32[]{:S(2)}) async-start(bf16[16,32,2048]{2,1,0:T(8,128)(2,1)} %bitcast.23), calls=%async_computation.2 | async-start | bytes 4194304 | tf_op jit(solution)/shard_map/all_to_all | solution.py:91
  120.5 52.4 %all-to-all-start = ((bf16[16,32,2048]{2,1,0:T(8,128)(2,1)}), bf16[16,32,2048]{2,1,0:T(8,128)(2,1)}, u32[]{:S(2)}, u32[]{:S(2)}) async-start(bf16[16,32,2048]{2,1,0:T(8,128)(2,1)} %bitcast.10), calls=%async_computation | async-start | bytes 4194304 | tf_op jit(solution)/shard_map/all_to_all | solution.py:92
  285.1 97.8 %all-to-all-start.3 = ((f32[16,32,2048]{2,1,0:T(8,128)}), f32[16,32,2048]{2,1,0:T(8,128)}, u32[]{:S(2)}, u32[]{:S(2)}) async-start(f32[16,32,2048]{2,1,0:T(8,128)} %bitcast.77), calls=%async_computation.3 | async-start | bytes 8388608 | tf_op jit(solution)/shard_map/all_to_all | solution.py:100
  385.6 0.7 copy-start.6
  385.7 0.7 copy-start.7
  385.8 1.7 copy-start.2
  386.4 2.4 copy-start.13
  386.4 2.4 copy-start.15
  386.4 2.4 copy-start.17
  386.4 2.4 copy-start.11
  386.4 3.9 %copy-start.1 = (bf16[24,2048]{1,0:T(8,128)(2,1)S(1)}, bf16[24,2048]{1,0:T(8,128)(2,1)}, u32[]{:S(2)}) copy-start(bf16[24,2048]{1,0:T(8,128)(2,1)} %param.10) | copy-start | bytes 294916
where the time goes:
time: 391 us; the launch traced here: 390 us
  waiting for transfers between devices  218 us (56%)
  blocking collectives  97 us (25%)
  matrix products  29.9 us (8%)
  starting transfers between devices  22 us (6%)
  local copies, waits for them, and re-layouts  12.8 us (3%)
  other arithmetic  9.99 us (3%)
    all_to_all x1, blocking collectives, local(): lax.all_to_all(g_rows, 'expert', split_axis=0, concat_axis=0, tiled=True)  97 us
    all_to_all x1, waiting for transfers between devices, local(): lax.all_to_all(t_rows, 'expert', split_axis=0, concat_axis=0, tiled=True)  88.1 us
    all_to_all x1, waiting for transfers between devices, local(): lax.all_to_all(send_t, 'expert', split_axis=0, concat_axis=0, tiled=True)  46.6 us
    all_to_all x1, waiting for transfers between devices, local(): lax.all_to_all(send_z, 'expert', split_axis=0, concat_axis=0, tiled=True)  46.4 us
    all_to_all x1, waiting for transfers between devices, local(): lax.all_to_all(send_c, 'expert', split_axis=0, concat_axis=0, tiled=True)  36.4 us
  transfers between devices with their start and end apart: 4, of which 4 were waited for; matrix products, arithmetic and copies ran while one was open for 4% of the time, Pallas kernels for 0%

commit v1 on v0

--- a/solution.py
+++ b/solution.py
@@ -44,20 +44,48 @@
     return flat * capacity + rank
 
 
-def local(tokens, norm_gain, probe_signs, cotangent, routes, gates, expert_weights):
-    xf = tokens.astype(jnp.float32)
-    probe = (2 * probe_signs - 1).astype(jnp.float32)
-    tok_dev, width = xf.shape
+def capacity(tok_dev, half, expert_count):
+    return min(2 * ((2 * tok_dev * half + 3 * expert_count - 1) // (3 * expert_count)), tok_dev)
+
+
+def summed_gates(routes, gates, expert_count):
+    named = routes[..., None] == jnp.arange(expert_count, dtype=jnp.int32)
+    return jnp.sum(jnp.where(named, gates[..., None], 0.0), axis=(0, 2))
+
+
+def dense_rows(normed, normed_t, cotangent, routes, gates, weights):
+    width = normed.shape[1]
+    expert_count = lax.axis_size("expert") // 2
+    gate = summed_gates(routes, gates, expert_count)
+    high = lax.reduce_precision(gate, 8, 7)
+    low = gate - high
+    pad = jnp.zeros((gate.shape[0], -2 * expert_count % 128), jnp.bfloat16)
+    pack = jnp.concatenate(
+        [normed, normed_t, cotangent, high.astype(jnp.bfloat16), low.astype(jnp.bfloat16), pad], 1
+    )
+    got = lax.all_gather(pack, "expert", axis=0, tiled=True)
+    mine = lax.axis_index("expert") // 2
+    pick = (jnp.arange(expert_count) == mine).astype(jnp.float32)
+    tail = got[:, 3 * width :].astype(jnp.float32)
+    weight = jnp.sum(
+        (tail[:, :expert_count] + tail[:, expert_count : 2 * expert_count]) * pick, 1, keepdims=True
+    )
+    g_rows, t_rows = expert_terms(
+        weights, got[:, :width], got[:, width : 2 * width], got[:, 2 * width : 3 * width]
+    )
+    both = jnp.concatenate([weight * g_rows, weight * t_rows], 1).astype(jnp.bfloat16)
+    total = lax.psum_scatter(both, "expert", scatter_dimension=0, tiled=True).astype(jnp.float32)
+    return (total[:, :width], total[:, width:])
+
+
+def routed_rows(normed, normed_t, cotangent, routes, gates, weights):
+    tok_dev, width = normed.shape
     groups_here = routes.shape[0]
     half = routes.shape[2]
     n_exp = lax.axis_size("expert")
     expert_count = n_exp // 2
-    cap = min(2 * ((2 * tok_dev * half + 3 * expert_count - 1) // (3 * expert_count)), tok_dev)
+    cap = capacity(tok_dev, half, expert_count)
     buffer_rows = expert_count * cap
-    scale = lax.rsqrt(jnp.mean(xf * xf, axis=1, keepdims=True) + EPS)
-    along = jnp.mean(xf * probe, axis=1, keepdims=True)
-    normed = (xf * scale * norm_gain).astype(jnp.bfloat16)
-    normed_t = (norm_gain * (scale * probe - scale**3 * xf * along)).astype(jnp.bfloat16)
     stack_z, stack_t, stack_c, stack_w = ([], [], [], [])
     for group in range(groups_here):
         target = slot_targets(routes[group], expert_count, cap)
@@ -79,7 +107,6 @@
     rows_t = jnp.stack(stack_t, 0)
     rows_c = jnp.stack(stack_c, 0)
     weighted = jnp.stack(stack_w, 0)
-    own_half = lax.all_gather(expert_weights, "node", axis=2, tiled=True)
 
     def arrange(rows):
         shaped = rows.reshape(groups_here, expert_count, 1, cap, width)
@@ -92,7 +119,7 @@
     got_c = lax.all_to_all(send_c, "expert", split_axis=0, concat_axis=0, tiled=True)
     sources, items, cols = got_z.shape
     g_rows, t_rows = expert_terms(
-        own_half, got_z.reshape(-1, cols), got_t.reshape(-1, cols), got_c.reshape(-1, cols)
+        weights, got_z.reshape(-1, cols), got_t.reshape(-1, cols), got_c.reshape(-1, cols)
     )
     g_rows = g_rows.reshape(sources, items, cols)
     t_rows = t_rows.reshape(sources, items, cols)
@@ -108,6 +135,21 @@
     contract = (((0, 1), (0, 1)), ((), ()))
     grad_z = lax.dot_general(weighted, back_g, contract, precision=lax.Precision.HIGHEST)
     tan_z = lax.dot_general(weighted, back_t, contract, precision=lax.Precision.HIGHEST)
+    return (grad_z, tan_z)
+
+
+def local(tokens, norm_gain, probe_signs, cotangent, routes, gates, expert_weights):
+    xf = tokens.astype(jnp.float32)
+    probe = (2 * probe_signs - 1).astype(jnp.float32)
+    tok_dev, width = xf.shape
+    cap = capacity(tok_dev, routes.shape[2], lax.axis_size("expert") // 2)
+    scale = lax.rsqrt(jnp.mean(xf * xf, axis=1, keepdims=True) + EPS)
+    along = jnp.mean(xf * probe, axis=1, keepdims=True)
+    normed = (xf * scale * norm_gain).astype(jnp.bfloat16)
+    normed_t = (norm_gain * (scale * probe - scale**3 * xf * along)).astype(jnp.bfloat16)
+    own_half = lax.all_gather(expert_weights, "node", axis=2, tiled=True)
+    rows = dense_rows if routes.shape[0] * cap >= tok_dev else routed_rows
+    grad_z, tan_z = rows(normed, normed_t, cotangent, routes, gates, own_half)
     share = width // lax.axis_size("node")
     start = lax.axis_index("node") * share
     slope_r = -(scale**3) * along

time: 391 us -> 161 us (0.41)
  the two profiles are of different devices: /device:TPU:11 before, /device:TPU:0 now
where the time goes in v1:
time: 161 us
  waiting for transfers between devices  122 us (76%)
  between operations  14.2 us (9%)
  matrix products  10 us (6%)
  other arithmetic  9.81 us (6%)
  local copies, waits for them, and re-layouts  5.18 us (3%)
    reduce_scatter x1, waiting for transfers between devices, dense_rows(): lax.psum_scatter(both, 'expert', scatter_dimension=0, tiled=True)  64.9 us
    all_gather x1, waiting for transfers between devices, dense_rows(): got = lax.all_gather(pack, 'expert', axis=0, tiled=True)  56.7 us
  transfers between devices with their start and end apart: 2, of which 2 were waited for; matrix products, arithmetic and copies ran while one was open for 0% of the time, Pallas kernels for 0%

profile of v1, /device:TPU:0, one launch (start us, length us, event | category | flops | bytes accessed | tf_op | source)
XLA Modules:
  0.0 160.9 jit_solution(367197248918496932)
XLA Ops:
  7.2 0.0 all-gather.2.cloned.1.call-start
  7.2 0.7 select_reduce_fusion
  7.9 0.1 copy.14
  8.0 0.1 copy.13
  8.1 1.1 fusion.38
  9.3 1.2 fusion.37
  10.4 1.7 %concatenate.16 = bf16[24,6272]{1,0:T(8,128)(2,1)} concatenate(bf16[24,2048]{1,0:T(8,128)(2,1)S(1)} %get-tuple-element.22, bf16[24,2048]{1,0:T(8,128)(2,1)S(1)} %get-tuple-element.21, bf16[24,2048]{1,0:T(8,128)(2,1)} %param.10, bf16[24,8]{1,0:T(8,128)(2,1)S(1)} %copy.13, bf16[24,8]{1,0:T(8,128)(2,1)S(1)} %copy.14, bf16[24,112]{1,0:T(8,128)(2,1)S(1)} %broadcast_in_dim.16), dimensions={1} | concatenate | bytes 602112 | tf_op jit(solution)/shard_map/concatenate | solution.py:63
  12.2 0.0 all-gather.2.cloned.1.call-update
  12.2 0.0 reduce-scatter.2.cloned.1.call-start
  12.3 56.7 %all-gather.2.cloned.1.call-done = bf16[384,6272]{1,0:T(8,128)(2,1)} async-done(((bf16[24,6272]{1,0:T(8,128)(2,1)}), bf16[384,6272]{1,0:T(8,128)(2,1)}) %all-gather.2.cloned.1.call-update) | async-done | bytes 4816912 | tf_op jit(solution)/shard_map/all_gather | solution.py:66
  69.0 0.0 copy-start.1
  69.0 2.4 %fusion.54 = (bf16[384,2048]{1,0:T(8,128)(2,1)S(1)}, bf16[384,2048]{1,0:T(8,128)(2,1)S(1)}) fusion(bf16[384,6272]{1,0:T(8,128)(2,1)} %all-gather.2.cloned.1.call-done), kind=kLoop, calls=%fused_computation.93 | loop fusion | bytes 6291456 | tf_op jit(solution)/shard_map/slice | solution.py:74
  71.4 0.9 copy-done.1
  72.3 1.8 %fusion.2 = f32[768,384]{1,0:T(8,128)S(1)} fusion(bf16[384,2048]{1,0:T(8,128)(2,1)S(1)} %get-tuple-element.14, bf16[384,2048]{1,0:T(8,128)(2,1)S(1)} %get-tuple-element.13, bf16[3,2048,384]{2,1,0:T(8,128)(2,1)S(1)} %copy-done.1), kind=kOutput, calls=%fused_computation.7 | convolution fusion | flops 1214251008 | bytes 5898240 | tf_op jit(solution)/shard_map/dot_general | solution.py:13
  74.1 1.8 %fusion.3 = f32[768,384]{1,0:T(8,128)S(1)} fusion(bf16[384,2048]{1,0:T(8,128)(2,1)S(1)} %get-tuple-element.14, bf16[384,2048]{1,0:T(8,128)(2,1)S(1)} %get-tuple-element.13, bf16[3,2048,384]{2,1,0:T(8,128)(2,1)S(1)} %copy-done.1), kind=kOutput, calls=%fused_computation.8 | convolution fusion | flops 1214251008 | bytes 5898240 | tf_op jit(solution)/shard_map/dot_general | solution.py:12
  75.9 0.9 slice_convert_fusion
  76.8 0.2 fusion.45
  77.0 2.8 %multiply_convert_fusion.1 = (bf16[384,384]{1,0:T(8,128)(2,1)S(1)}, bf16[384,384]{1,0:T(8,128)(2,1)S(1)}, bf16[384,384]{1,0:T(8,128)(2,1)S(1)}, bf16[384,384]{1,0:T(8,128)(2,1)S(1)}) fusion(f32[768,384]{1,0:T(8,128)S(1)} %fusion.3, f32[768,384]{1,0:T(8,128)S(1)} %fusion.2, bf16[3,2048,384]{2,1,0:T(8,128)(2,1)S(1)} %copy-done.1, ...), kind=kOutput, calls=%fused_computation.40 | convolution fusion | flops 607961088 | bytes 6684672 | tf_op jit(solution)/shard_map/dot_general | solution.py:16
  79.8 1.8 %fusion.8 = f32[768,2048]{1,0:T(8,128)S(1)} fusion(bf16[3,2048,384]{2,1,0:T(8,128)(2,1)S(1)} %copy-done.1, bf16[384,384]{1,0:T(8,128)(2,1)S(1)} %get-tuple-element.19, bf16[384,384]{1,0:T(8,128)(2,1)S(1)} %get-tuple-element.20), kind=kOutput, calls=%fused_computation.13 | convolution fusion | flops 1209139200 | bytes 8454144 | tf_op jit(solution)/shard_map/dot_general | solution.py:28
  81.6 1.8 %convolution_add_fusion = f32[768,2048]{1,0:T(8,128)S(1)} fusion(f32[768,2048]{1,0:T(8,128)S(1)} %fusion.8, bf16[3,2048,384]{2,1,0:T(8,128)(2,1)S(1)} %copy-done.1, bf16[384,384]{1,0:T(8,128)(2,1)S(1)} %get-tuple-element.18, bf16[384,384]{1,0:T(8,128)(2,1)S(1)} %get-tuple-element.17), kind=kOutput, calls=%fused_computation | convolution fusion | flops 1210712064 | bytes 14745600 | tf_op jit(solution)/shard_map/dot_general | solution.py:29
  83.4 0.9 fusion.1
  84.4 2.0 %pad_maximum_fusion.1 = bf16[384,4096]{1,0:T(8,128)(2,1)} fusion(bf16[384,2048]{1,0:T(8,128)(2,1)S(1)} %get-tuple-element.12, bf16[384,2048]{1,0:T(8,128)(2,1)S(1)} %get-tuple-element.11), kind=kLoop, calls=%fused_computation.6 | loop fusion | flops 6291456 | bytes 6291456 | tf_op jit(solution)/shard_map/concatenate | solution.py:76
  86.4 0.0 copy-start
  86.4 0.0 copy-start.2
  86.4 0.0 copy-start.3
  86.4 0.0 reduce-scatter.2.cloned.1.call-update
  86.4 64.9 %reduce-scatter.2.cloned.1.call-done = bf16[24,4096]{1,0:T(8,128)(2,1)} async-done(((bf16[384,4096]{1,0:T(8,128)(2,1)}), bf16[24,4096]{1,0:T(8,128)(2,1)}) %reduce-scatter.2.cloned.1.call-update) | async-done | bytes 196624 | tf_op jit(solution)/shard_map/reduce_scatter | solution.py:77
  151.4 1.0 convert_element_type.56
  152.3 0.0 copy-done
  152.3 0.0 copy-done.2
  152.3 0.0 copy-done.3
  152.3 0.2 fusion.39
  152.6 1.0 multiply_reduce_fusion
  153.5 0.5 broadcast_multiply_fusion
  (5 shorter events, 0.0 us)
Async XLA Ops:
  7.2 61.8 %all-gather.2.cloned.1.call-start = ((), (), s32[]{:S(2)}) async-start(), calls=%async_computation.1 | async-start | bytes 5117952 | tf_op jit(solution)/shard_map/all_gather | solution.py:66
  12.2 139.2 %reduce-scatter.2.cloned.1.call-start = ((), (), s32[]{:S(2)}) async-start(), calls=%async_computation.2 | async-start | bytes 3342336 | tf_op jit(solution)/shard_map/reduce_scatter | solution.py:77
  69.0 3.3 %copy-start.1 = (bf16[3,2048,384]{2,1,0:T(8,128)(2,1)S(1)}, bf16[3,2048,384]{2,1,0:T(8,128)(2,1)}, u32[]{:S(2)}) copy-start(bf16[3,2048,384]{2,1,0:T(8,128)(2,1)} %param.13) | copy-start | bytes 14155780
  86.4 65.9 %copy-start = (s32[24,2048]{1,0:T(8,128)S(1)}, s32[24,2048]{1,0:T(8,128)}, u32[]{:S(2)}) copy-start(s32[24,2048]{1,0:T(8,128)} %param.9) | copy-start | bytes 589828
  86.4 65.9 %copy-start.2 = (bf16[24,2048]{1,0:T(8,128)(2,1)S(1)}, bf16[24,2048]{1,0:T(8,128)(2,1)}, u32[]{:S(2)}) copy-start(bf16[24,2048]{1,0:T(8,128)(2,1)} %param.7) | copy-start | bytes 294916
  86.4 65.9 %copy-start.3 = (f32[2048]{0:T(1024)S(1)}, f32[2048]{0:T(1024)}, u32[]{:S(2)}) copy-start(f32[2048]{0:T(1024)} %param.8) | copy-start | bytes 24580
Sparse Core Ops, SparseCore 0:
  12.3 56.6 all-gather.1
  86.6 64.7 reduce-scatter.1

commit v2 on v1

--- a/solution.py
+++ b/solution.py
@@ -53,9 +53,20 @@
     return jnp.sum(jnp.where(named, gates[..., None], 0.0), axis=(0, 2))
 
 
+def moved(rows, turns, flip_x=False, flip_core=False):
+    count = lax.axis_size("expert")
+    pairs = [
+        (i, (i + 4 * turns) % count ^ (2 * flip_x) ^ (1 * flip_core)) for i in range(count)
+    ]
+    return lax.ppermute(rows, "expert", pairs)
+
+
 def dense_rows(normed, normed_t, cotangent, routes, gates, weights):
-    width = normed.shape[1]
-    expert_count = lax.axis_size("expert") // 2
+    tok_dev, width = normed.shape
+    n_exp = lax.axis_size("expert")
+    expert_count = n_exp // 2
+    turns = n_exp // 4
+    weights_other = moved(weights, 0, flip_core=True)
     gate = summed_gates(routes, gates, expert_count)
     high = lax.reduce_precision(gate, 8, 7)
     low = gate - high
@@ -63,18 +74,40 @@
     pack = jnp.concatenate(
         [normed, normed_t, cotangent, high.astype(jnp.bfloat16), low.astype(jnp.bfloat16), pad], 1
     )
-    got = lax.all_gather(pack, "expert", axis=0, tiled=True)
+    same = {0: pack}
+    ahead, behind = turns // 2, (turns - 1) // 2
+    for k in range(1, ahead + 1):
+        same[k] = moved(same[k - 1], 1)
+    for k in range(1, behind + 1):
+        same[turns - k] = moved(same[(turns - k + 1) % turns], -1)
+    across = {k: moved(same[k], 0, flip_x=True) for k in same}
+    got = jnp.concatenate([same[k] for k in range(turns)] + [across[k] for k in range(turns)], 0)
     mine = lax.axis_index("expert") // 2
     pick = (jnp.arange(expert_count) == mine).astype(jnp.float32)
     tail = got[:, 3 * width :].astype(jnp.float32)
     weight = jnp.sum(
         (tail[:, :expert_count] + tail[:, expert_count : 2 * expert_count]) * pick, 1, keepdims=True
     )
-    g_rows, t_rows = expert_terms(
-        weights, got[:, :width], got[:, width : 2 * width], got[:, 2 * width : 3 * width]
-    )
-    both = jnp.concatenate([weight * g_rows, weight * t_rows], 1).astype(jnp.bfloat16)
-    total = lax.psum_scatter(both, "expert", scatter_dimension=0, tiled=True).astype(jnp.float32)
+    rows = (got[:, :width], got[:, width : 2 * width], got[:, 2 * width : 3 * width])
+    g_own, t_own = expert_terms(weights, *rows)
+    g_other, t_other = expert_terms(weights_other, *rows)
+    both = jnp.concatenate([weight * (g_own + g_other), weight * (t_own + t_other)], 1)
+    both = both.reshape(2, turns, tok_dev, 2 * width)
+
+    def summed(k):
+        return both[0, k] + moved(both[1, k].astype(jnp.bfloat16), 0, flip_x=True).astype(jnp.float32)
+
+    def passed(rows, step):
+        return moved(rows.astype(jnp.bfloat16), step).astype(jnp.float32)
+
+    forward, backward = None, None
+    for k in range(ahead, 0, -1):
+        part = summed(k)
+        forward = passed(part if forward is None else part + forward, -1)
+    for k in range(behind, 0, -1):
+        part = summed(turns - k)
+        backward = passed(part if backward is None else part + backward, 1)
+    total = summed(0) + forward + backward
     return (total[:, :width], total[:, width:])
 
 

time: 161 us -> 88.7 us (0.55)
  waiting for transfers between devices: 122 us -> 36.7 us
  starting transfers between devices: 0.08 us -> 24.9 us
  between operations: 14.2 us -> 0.93 us
  matrix products: 10 us -> 16.5 us
  other arithmetic: 9.81 us -> 6.58 us
  local copies, waits for them, and re-layouts: 5.18 us -> 2.62 us
    reduce_scatter x1 -> x0, waiting for transfers between devices: 64.9 us -> none  [dense_rows(): lax.psum_scatter(both, 'expert', scatter_dimension=0, tiled=True)]
    all_gather x1 -> x0, waiting for transfers between devices: 56.7 us -> none  [dense_rows(): got = lax.all_gather(pack, 'expert', axis=0, tiled=True)]
    ppermute x0 -> x15, waiting for transfers between devices: none -> 36.7 us  [moved(): return lax.ppermute(rows, 'expert', pairs)]
    ppermute x0 -> x15, starting transfers between devices: none -> 24.9 us  [moved(): return lax.ppermute(rows, 'expert', pairs)]
    slice x1, local copies, waits for them, and re-layouts: 2.42 us -> 0.19 us  [dense_rows(): got[:, :width]]
    concatenate x1, other arithmetic: 2.02 us -> 0.3 us  [dense_rows(): jnp.concatenate([weight * (g_own + g_other), weight * (t_own + t_other)], 1)]
    dot_general x1 -> x2, matrix products: 1.83 us -> 3.45 us  [expert_terms(): lax.dot_general(lhs_gate, weights[0], contract, preferred_element_type=jn...]
    dot_general x1 -> x2, matrix products: 1.82 us -> 3.44 us  [expert_terms(): lax.dot_general(lhs_up, weights[1], contract, preferred_element_type=jnp....]
  transfers between devices with their start and end apart: 2 -> 15, of which waited for: 2 -> 9; matrix products, arithmetic and copies ran while one was open for 0% -> 7% of each run, Pallas kernels for 0% -> 0%
where the time goes in v2:
time: 88.7 us; the launch traced here: 88.3 us
  waiting for transfers between devices  36.7 us (41%)
  starting transfers between devices  24.9 us (28%)
  matrix products  16.5 us (19%)
  other arithmetic  6.58 us (7%)
  local copies, waits for them, and re-layouts  2.62 us (3%)
  between operations  0.93 us (1%)
    ppermute x15, waiting for transfers between devices, moved(): return lax.ppermute(rows, 'expert', pairs)  36.7 us
    ppermute x15, starting transfers between devices, moved(): return lax.ppermute(rows, 'expert', pairs)  24.9 us
    dot_general x2, matrix products, expert_terms(): lax.dot_general(lhs_gate, weights[0], contract, preferred_element_type=jn...  3.45 us
    dot_general x2, matrix products, expert_terms(): lax.dot_general(lhs_up, weights[1], contract, preferred_element_type=jnp....  3.44 us
    dot_general x2, matrix products, expert_terms(): pre_up = jnp.dot(both, weights[1], preferred_element_type=jnp.float32)  3.39 us
    dot_general x2, matrix products, expert_terms(): pre_gate = jnp.dot(both, weights[0], preferred_element_type=jnp.float32)  3.38 us
    dot_general x2, matrix products, expert_terms(): back = jnp.dot(cotan, weights[2], preferred_element_type=jnp.float32)  2.87 us
  transfers between devices with their start and end apart: 15, of which 9 were waited for; matrix products, arithmetic and copies ran while one was open for 7% of the time, Pallas kernels for 0%

profile of v2, /device:TPU:0, one launch (start us, length us, event | category | flops | bytes accessed | tf_op | source)
XLA Modules:
  0.0 88.3 jit_solution(4287143711946528043)
XLA Ops:
  0.6 0.7 select_reduce_fusion
  1.4 0.1 copy.11
  1.4 0.1 copy.12
  1.5 1.1 %fusion.67 = (f32[24]{0:T(128)S(1)}, f32[24]{0:T(128)S(1)}) fusion(bf16[24,2048]{1,0:T(8,128)(2,1)} %param.7, s32[24,2048]{1,0:T(8,128)} %param.9), kind=kLoop, calls=%fused_computation.102 | loop fusion | flops 393168 | bytes 295104 | tf_op jit(solution)/shard_map/reduce_sum | solution.py:180
  2.7 1.2 %fusion.66 = (bf16[24,2048]{1,0:T(8,128)(2,1)S(1)}, bf16[24,2048]{1,0:T(8,128)(2,1)S(1)}) fusion(bf16[24,2048]{1,0:T(8,128)(2,1)} %param.7, s32[24,2048]{1,0:T(8,128)} %param.9, f32[24]{0:T(128)S(1)} %get-tuple-element.39, f32[24]{0:T(128)S(1)} %get-tuple-element.38, f32[2048]{0:T(1024)} %param.8, f32[24]{0:T(128)S(1)} %get-tuple-element.37), kind=kLoop, calls=%fused_computation.101 | loop fusion | flops 638976 | bytes 500000 | tf_op jit(solution)/shard_map/convert_element_type | solution.py:182
  3.9 1.0 %concatenate.25 = bf16[24,6272]{1,0:T(8,128)(2,1)S(1)} concatenate(bf16[24,2048]{1,0:T(8,128)(2,1)S(1)} %get-tuple-element.32, bf16[24,2048]{1,0:T(8,128)(2,1)S(1)} %get-tuple-element.31, bf16[24,2048]{1,0:T(8,128)(2,1)} %param.10, bf16[24,8]{1,0:T(8,128)(2,1)S(1)} %copy.11, bf16[24,8]{1,0:T(8,128)(2,1)S(1)} %copy.12, bf16[24,112]{1,0:T(8,128)(2,1)S(1)} %broadcast_in_dim.16), dimensions={1} | concatenate | bytes 602112 | tf_op jit(solution)/shard_map/concatenate | solution.py:74
  4.9 3.1 %collective-permute-start = (bf16[24,6272]{1,0:T(8,128)(2,1)S(1)}, bf16[24,6272]{1,0:T(8,128)(2,1)S(1)}, u32[]{:S(2)}, u32[]{:S(2)}) collective-permute-start(bf16[24,6272]{1,0:T(8,128)(2,1)S(1)} %concatenate.25), channel_id=1, source_target_pairs={{0,4},{1,5},{2,6},{3,7},{4,8},{5,9},{6,10},{7,11},{8,12},{9,13},{1... | collective-permute-start | bytes 903176 | tf_op jit(solution)/shard_map/ppermute | solution.py:61
  7.9 2.1 %collective-permute-start.2 = (bf16[24,6272]{1,0:T(8,128)(2,1)S(1)}, bf16[24,6272]{1,0:T(8,128)(2,1)S(1)}, u32[]{:S(2)}, u32[]{:S(2)}) collective-permute-start(bf16[24,6272]{1,0:T(8,128)(2,1)S(1)} %concatenate.25), channel_id=1, source_target_pairs={{0,12},{1,13},{2,14},{3,15},{4,0},{5,1},{6,2},{7,3},{8,4},{9,5},{1... | collective-permute-start | bytes 903176 | tf_op jit(solution)/shard_map/ppermute | solution.py:61
  10.0 1.6 %collective-permute-start.3 = (bf16[24,6272]{1,0:T(8,128)(2,1)S(1)}, bf16[24,6272]{1,0:T(8,128)(2,1)}, u32[]{:S(2)}, u32[]{:S(2)}) collective-permute-start(bf16[24,6272]{1,0:T(8,128)(2,1)S(1)} %concatenate.25), channel_id=1, source_target_pairs={{0,2},{1,3},{2,0},{3,1},{4,6},{5,7},{6,4},{7,5},{8,10},{9,11},{10,... | collective-permute-start | bytes 903176 | tf_op jit(solution)/shard_map/ppermute | solution.py:61
  11.7 0.0 collective-permute-start.7
  11.7 6.2 %collective-permute-done = bf16[24,6272]{1,0:T(8,128)(2,1)S(1)} collective-permute-done((bf16[24,6272]{1,0:T(8,128)(2,1)S(1)}, bf16[24,6272]{1,0:T(8,128)(2,1)S(1)}, u32[]{:S(2)}, u32[]{:S(2)}) %collective-permute-start) | collective-permute-done | bytes 301088 | tf_op jit(solution)/shard_map/ppermute | solution.py:61
  18.0 0.0 collective-permute-start.1
  18.0 1.7 %collective-permute-start.4 = (bf16[24,6272]{1,0:T(8,128)(2,1)S(1)}, bf16[24,6272]{1,0:T(8,128)(2,1)S(1)}, u32[]{:S(2)}, u32[]{:S(2)}) collective-permute-start(bf16[24,6272]{1,0:T(8,128)(2,1)S(1)} %collective-permute-done), channel_id=1, source_target_pairs={{0,2},{1,3},{2,0},{3,1},{4,6},{5,7},{6,4},{7,5},{8,10},{9,11},{10,... | collective-permute-start | bytes 903176 | tf_op jit(solution)/shard_map/ppermute | solution.py:61
  19.7 3.5 %collective-permute-done.2 = bf16[24,6272]{1,0:T(8,128)(2,1)S(1)} collective-permute-done((bf16[24,6272]{1,0:T(8,128)(2,1)S(1)}, bf16[24,6272]{1,0:T(8,128)(2,1)S(1)}, u32[]{:S(2)}, u32[]{:S(2)}) %collective-permute-start.2) | collective-permute-done | bytes 301088 | tf_op jit(solution)/shard_map/ppermute | solution.py:61
  23.2 1.7 %collective-permute-start.6 = (bf16[24,6272]{1,0:T(8,128)(2,1)S(1)}, bf16[24,6272]{1,0:T(8,128)(2,1)S(1)}, u32[]{:S(2)}, u32[]{:S(2)}) collective-permute-start(bf16[24,6272]{1,0:T(8,128)(2,1)S(1)} %collective-permute-done.2), channel_id=1, source_target_pairs={{0,2},{1,3},{2,0},{3,1},{4,6},{5,7},{6,4},{7,5},{8,10},{9,11},{10,... | collective-permute-start | bytes 903176 | tf_op jit(solution)/shard_map/ppermute | solution.py:61
  24.9 5.1 %collective-permute-done.1 = bf16[24,6272]{1,0:T(8,128)(2,1)S(1)} collective-permute-done((bf16[24,6272]{1,0:T(8,128)(2,1)S(1)}, bf16[24,6272]{1,0:T(8,128)(2,1)S(1)}, u32[]{:S(2)}, u32[]{:S(2)}) %collective-permute-start.1) | collective-permute-done | bytes 301088 | tf_op jit(solution)/shard_map/ppermute | solution.py:61
  30.0 1.5 %collective-permute-start.5 = (bf16[24,6272]{1,0:T(8,128)(2,1)S(1)}, bf16[24,6272]{1,0:T(8,128)(2,1)S(1)}, u32[]{:S(2)}, u32[]{:S(2)}) collective-permute-start(bf16[24,6272]{1,0:T(8,128)(2,1)S(1)} %collective-permute-done.1), channel_id=1, source_target_pairs={{0,2},{1,3},{2,0},{3,1},{4,6},{5,7},{6,4},{7,5},{8,10},{9,11},{10,... | collective-permute-start | bytes 903176 | tf_op jit(solution)/shard_map/ppermute | solution.py:61
  31.6 0.0 collective-permute-done.3
  31.6 1.0 %constant_dynamic-update-slice_fusion.3 = bf16[192,6272]{1,0:T(8,128)(2,1)S(1)} fusion(bf16[192,6272]{1,0:T(8,128)(2,1)S(1)} %constant_dynamic-update-slice_fusion.4, bf16[24,6272]{1,0:T(8,128)(2,1)} %collective-permute-done.3), kind=kLoop, calls=%fused_computation.126 | loop fusion | bytes 602112
  32.6 0.0 collective-permute-done.4
  32.6 0.0 copy-start.1
  32.6 5.7 %collective-permute-done.5 = bf16[24,6272]{1,0:T(8,128)(2,1)S(1)} collective-permute-done((bf16[24,6272]{1,0:T(8,128)(2,1)S(1)}, bf16[24,6272]{1,0:T(8,128)(2,1)S(1)}, u32[]{:S(2)}, u32[]{:S(2)}) %collective-permute-start.5) | collective-permute-done | bytes 301088 | tf_op jit(solution)/shard_map/ppermute | solution.py:61
  38.4 0.0 collective-permute-done.6
  38.4 0.2 fusion.74
  38.6 0.2 fusion.83
  38.8 0.0 copy-done.1
  38.8 1.0 %fusion.8 = f32[384,384]{1,0:T(8,128)S(1)} fusion(bf16[3,2048,384]{2,1,0:T(8,128)(2,1)S(1)} %copy-done.1, bf16[192,2048]{1,0:T(8,128)(2,1)S(1)} %get-tuple-element.16, bf16[192,2048]{1,0:T(8,128)(2,1)S(1)} %get-tuple-element.15), kind=kOutput, calls=%fused_computation.17 | convolution fusion | flops 607125504 | bytes 3735552 | tf_op jit(solution)/shard_map/dot_general | solution.py:12
  39.8 1.0 %fusion.4 = f32[384,384]{1,0:T(8,128)S(1)} fusion(bf16[3,2048,384]{2,1,0:T(8,128)(2,1)S(1)} %copy-done.1, bf16[192,2048]{1,0:T(8,128)(2,1)S(1)} %get-tuple-element.16, bf16[192,2048]{1,0:T(8,128)(2,1)S(1)} %get-tuple-element.15), kind=kOutput, calls=%fused_computation.13 | convolution fusion | flops 607125504 | bytes 3735552 | tf_op jit(solution)/shard_map/dot_general | solution.py:13
  40.8 0.7 multiply_convert_fusion.4
  41.6 1.0 %fusion.6 = f32[384,2048]{1,0:T(8,128)S(1)} fusion(bf16[3,2048,384]{2,1,0:T(8,128)(2,1)S(1)} %copy-done.1, bf16[192,384]{1,0:T(8,128)(2,1)S(1)} %get-tuple-element.27, bf16[192,384]{1,0:T(8,128)(2,1)S(1)} %get-tuple-element.28), kind=kOutput, calls=%fused_computation.15 | convolution fusion | flops 604569600 | bytes 5013504 | tf_op jit(solution)/shard_map/dot_general | solution.py:28
  42.6 1.0 %convolution_add_fusion.1 = f32[384,2048]{1,0:T(8,128)S(1)} fusion(f32[384,2048]{1,0:T(8,128)S(1)} %fusion.6, bf16[3,2048,384]{2,1,0:T(8,128)(2,1)S(1)} %copy-done.1, bf16[192,384]{1,0:T(8,128)(2,1)S(1)} %get-tuple-element.26, bf16[192,384]{1,0:T(8,128)(2,1)S(1)} %get-tuple-element.25), kind=kOutput, calls=%fused_computation.2 | convolution fusion | flops 605356032 | bytes 8159232 | tf_op jit(solution)/shard_map/dot_general | solution.py:29
  43.6 0.0 collective-permute-done.7
  43.6 2.4 %fusion.15 = f32[384,384]{1,0:T(8,128)S(1)} fusion(bf16[3,2048,384]{2,1,0:T(8,128)(2,1)} %collective-permute-done.7, bf16[192,2048]{1,0:T(8,128)(2,1)S(1)} %get-tuple-element.16, bf16[192,2048]{1,0:T(8,128)(2,1)S(1)} %get-tuple-element.15), kind=kOutput, calls=%fused_computation.24 | convolution fusion | flops 607125504 | bytes 3735552 | tf_op jit(solution)/shard_map/dot_general | solution.py:13
  46.0 2.4 %fusion.13 = f32[384,384]{1,0:T(8,128)S(1)} fusion(bf16[3,2048,384]{2,1,0:T(8,128)(2,1)} %collective-permute-done.7, bf16[192,2048]{1,0:T(8,128)(2,1)S(1)} %get-tuple-element.16, bf16[192,2048]{1,0:T(8,128)(2,1)S(1)} %get-tuple-element.15), kind=kOutput, calls=%fused_computation.22 | convolution fusion | flops 607125504 | bytes 3735552 | tf_op jit(solution)/shard_map/dot_general | solution.py:12
  48.4 2.1 %multiply_convert_fusion.2 = (bf16[192,384]{1,0:T(8,128)(2,1)S(1)}, bf16[192,384]{1,0:T(8,128)(2,1)S(1)}, bf16[192,384]{1,0:T(8,128)(2,1)S(1)}, bf16[192,384]{1,0:T(8,128)(2,1)S(1)}) fusion(f32[384,384]{1,0:T(8,128)S(1)} %fusion.15, f32[384,384]{1,0:T(8,128)S(1)} %fusion.13, bf16[3,2048,384]{2,1,0:T(8,128)(2,1)} %collective-permute-done.7, ...), kind=kOutput, calls=%fused_computation.89 | convolution fusion | flops 303980544 | bytes 4128768 | tf_op jit(solution)/shard_map/dot_general | solution.py:16
  50.6 2.4 %fusion.14 = f32[384,2048]{1,0:T(8,128)S(1)} fusion(bf16[3,2048,384]{2,1,0:T(8,128)(2,1)} %collective-permute-done.7, bf16[192,384]{1,0:T(8,128)(2,1)S(1)} %get-tuple-element.29, bf16[192,384]{1,0:T(8,128)(2,1)S(1)} %get-tuple-element.30), kind=kOutput, calls=%fused_computation.23 | convolution fusion | flops 604569600 | bytes 5013504 | tf_op jit(solution)/shard_map/dot_general | solution.py:29
  53.0 2.4 %convolution_add_fusion = f32[384,2048]{1,0:T(8,128)S(1)} fusion(f32[384,2048]{1,0:T(8,128)S(1)} %fusion.14, bf16[3,2048,384]{2,1,0:T(8,128)(2,1)} %collective-permute-done.7, bf16[192,384]{1,0:T(8,128)(2,1)S(1)} %get-tuple-element.24, bf16[192,384]{1,0:T(8,128)(2,1)S(1)} %get-tuple-element.23), kind=kOutput, calls=%fused_computation.1 | convolution fusion | flops 605356032 | bytes 8159232 | tf_op jit(solution)/shard_map/dot_general | solution.py:28
  55.5 0.9 %fusion.1 = (f32[192,2048]{1,0:T(8,128)S(1)}, f32[192,2048]{1,0:T(8,128)S(1)}) fusion(f32[384,2048]{1,0:T(8,128)S(1)} %convolution_add_fusion, f32[384,2048]{1,0:T(8,128)S(1)} %convolution_add_fusion.1, f32[192]{0:T(256)S(1)} %fusion.74), kind=kLoop, calls=%fused_computation.6 | loop fusion | flops 1572864 | bytes 9437952 | tf_op jit(solution)/shard_map/mul | solution.py:94
  56.4 0.3 pad_maximum_fusion
  56.7 0.2 convert.6
  56.9 0.0 copy-start
  56.9 0.0 copy-start.2
  56.9 0.0 copy-start.3
  56.9 0.1 slice_bitcast_fusion.15
  57.0 1.3 %collective-permute-start.10 = (bf16[24,4096]{1,0:T(8,128)(2,1)S(1)}, bf16[24,4096]{1,0:T(8,128)(2,1)S(1)}, u32[]{:S(2)}, u32[]{:S(2)}) collective-permute-start(bf16[24,4096]{1,0:T(8,128)(2,1)S(1)} %get-tuple-element.19), channel_id=1, source_target_pairs={{0,2},{1,3},{2,0},{3,1},{4,6},{5,7},{6,4},{7,5},{8,10},{9,11},{10,... | collective-permute-start | bytes 589832 | tf_op jit(solution)/shard_map/ppermute | solution.py:61
  58.3 0.8 collective-permute-start.9
  59.1 1.2 %collective-permute-start.13 = (bf16[24,4096]{1,0:T(8,128)(2,1)S(1)}, bf16[24,4096]{1,0:T(8,128)(2,1)S(1)}, u32[]{:S(2)}, u32[]{:S(2)}) collective-permute-start(bf16[24,4096]{1,0:T(8,128)(2,1)S(1)} %get-tuple-element.18), channel_id=1, source_target_pairs={{0,2},{1,3},{2,0},{3,1},{4,6},{5,7},{6,4},{7,5},{8,10},{9,11},{10,... | collective-permute-start | bytes 589832 | tf_op jit(solution)/shard_map/ppermute | solution.py:61
  60.3 4.6 %collective-permute-done.10 = bf16[24,4096]{1,0:T(8,128)(2,1)S(1)} collective-permute-done((bf16[24,4096]{1,0:T(8,128)(2,1)S(1)}, bf16[24,4096]{1,0:T(8,128)(2,1)S(1)}, u32[]{:S(2)}, u32[]{:S(2)}) %collective-permute-start.10) | collective-permute-done | bytes 196640 | tf_op jit(solution)/shard_map/ppermute | solution.py:61
  64.9 4.5 %collective-permute-start.11 = (bf16[24,4096]{1,0:T(8,128)(2,1)S(1)}, bf16[24,4096]{1,0:T(8,128)(2,1)S(1)}, u32[]{:S(2)}, u32[]{:S(2)}) collective-permute-start(bf16[24,4096]{1,0:T(8,128)(2,1)S(1)} %fusion.25), channel_id=1, source_target_pairs={{0,12},{1,13},{2,14},{3,15},{4,0},{5,1},{6,2},{7,3},{8,4},{9,5},{1... | collective-permute-start | bytes 589832 | tf_op jit(solution)/shard_map/ppermute | solution.py:61
  69.4 1.5 %collective-permute-start.8 = (bf16[24,4096]{1,0:T(8,128)(2,1)S(1)}, bf16[24,4096]{1,0:T(8,128)(2,1)S(1)}, u32[]{:S(2)}, u32[]{:S(2)}) collective-permute-start(bf16[24,4096]{1,0:T(8,128)(2,1)S(1)} %get-tuple-element.17), channel_id=1, source_target_pairs={{0,2},{1,3},{2,0},{3,1},{4,6},{5,7},{6,4},{7,5},{8,10},{9,11},{10,... | collective-permute-start | bytes 589832 | tf_op jit(solution)/shard_map/ppermute | solution.py:61
  70.9 0.0 collective-permute-done.9
  70.9 1.9 %collective-permute-done.13 = bf16[24,4096]{1,0:T(8,128)(2,1)S(1)} collective-permute-done((bf16[24,4096]{1,0:T(8,128)(2,1)S(1)}, bf16[24,4096]{1,0:T(8,128)(2,1)S(1)}, u32[]{:S(2)}, u32[]{:S(2)}) %collective-permute-start.13) | collective-permute-done | bytes 196640 | tf_op jit(solution)/shard_map/ppermute | solution.py:61
  72.7 3.9 %collective-permute-done.11 = bf16[24,4096]{1,0:T(8,128)(2,1)S(1)} collective-permute-done((bf16[24,4096]{1,0:T(8,128)(2,1)S(1)}, bf16[24,4096]{1,0:T(8,128)(2,1)S(1)}, u32[]{:S(2)}, u32[]{:S(2)}) %collective-permute-start.11) | collective-permute-done | bytes 196640 | tf_op jit(solution)/shard_map/ppermute | solution.py:61
  76.6 0.1 fusion.28
  76.8 3.0 %collective-permute-start.14 = (bf16[24,4096]{1,0:T(8,128)(2,1)S(1)}, bf16[24,4096]{1,0:T(8,128)(2,1)S(1)}, u32[]{:S(2)}, u32[]{:S(2)}) collective-permute-start(bf16[24,4096]{1,0:T(8,128)(2,1)S(1)} %get-tuple-element.14), channel_id=1, source_target_pairs={{0,4},{1,5},{2,6},{3,7},{4,8},{5,9},{6,10},{7,11},{8,12},{9,13},{1... | collective-permute-start | bytes 589832 | tf_op jit(solution)/shard_map/ppermute | solution.py:61
  79.7 0.9 %collective-permute-start.12 = (bf16[24,4096]{1,0:T(8,128)(2,1)S(1)}, bf16[24,4096]{1,0:T(8,128)(2,1)S(1)}, u32[]{:S(2)}, u32[]{:S(2)}) collective-permute-start(bf16[24,4096]{1,0:T(8,128)(2,1)S(1)} %get-tuple-element.13), channel_id=1, source_target_pairs={{0,12},{1,13},{2,14},{3,15},{4,0},{5,1},{6,2},{7,3},{8,4},{9,5},{1... | collective-permute-start | bytes 589832 | tf_op jit(solution)/shard_map/ppermute | solution.py:61
  80.6 0.0 collective-permute-done.8
  80.6 3.8 %collective-permute-done.14 = bf16[24,4096]{1,0:T(8,128)(2,1)S(1)} collective-permute-done((bf16[24,4096]{1,0:T(8,128)(2,1)S(1)}, bf16[24,4096]{1,0:T(8,128)(2,1)S(1)}, u32[]{:S(2)}, u32[]{:S(2)}) %collective-permute-start.14) | collective-permute-done | bytes 196640 | tf_op jit(solution)/shard_map/ppermute | solution.py:61
  84.4 2.0 %collective-permute-done.12 = bf16[24,4096]{1,0:T(8,128)(2,1)S(1)} collective-permute-done((bf16[24,4096]{1,0:T(8,128)(2,1)S(1)}, bf16[24,4096]{1,0:T(8,128)(2,1)S(1)}, u32[]{:S(2)}, u32[]{:S(2)}) %collective-permute-start.12) | collective-permute-done | bytes 196640 | tf_op jit(solution)/shard_map/ppermute | solution.py:61
  86.4 0.1 fusion.31
  86.5 0.0 copy-done
  86.5 0.2 fusion.68
  86.8 1.0 %multiply_reduce_fusion = (f32[24]{0:T(128)S(1)}, f32[24,2048]{1,0:T(8,128)}) fusion(s32[24,2048]{1,0:T(8,128)S(1)} %copy-done, f32[24]{0:T(128)S(1)} %get-tuple-element.36, f32[24]{0:T(128)S(1)} %get-tuple-element.35, bf16[24,2048]{1,0:T(8,128)(2,1)S(1)} %copy-done.2, f32[24]{0:T(128)S(1)} %get-tuple-element.9, f32[24,4096]{1,0:T(8,128)S(1)} %fusion.31, ...), kind=kLoop, calls=%fused_computation.114 | loop fusion | flops 835560 | bytes 893504 | tf_op jit(solution)/shard_map/reduce_sum | solution.py:202
  87.7 0.5 broadcast_multiply_fusion
  (16 shorter events, 0.3 us)
Async XLA Ops:
  4.9 13.1 %collective-permute-start = (bf16[24,6272]{1,0:T(8,128)(2,1)S(1)}, bf16[24,6272]{1,0:T(8,128)(2,1)S(1)}, u32[]{:S(2)}, u32[]{:S(2)}) collective-permute-start(bf16[24,6272]{1,0:T(8,128)(2,1)S(1)} %concatenate.25), channel_id=1, source_target_pairs={{0,4},{1,5},{2,6},{3,7},{4,8},{5,9},{6,10},{7,11},{8,12},{9,13},{1... | collective-permute-start | bytes 903176 | tf_op jit(solution)/shard_map/ppermute | solution.py:61
  7.9 15.3 %collective-permute-start.2 = (bf16[24,6272]{1,0:T(8,128)(2,1)S(1)}, bf16[24,6272]{1,0:T(8,128)(2,1)S(1)}, u32[]{:S(2)}, u32[]{:S(2)}) collective-permute-start(bf16[24,6272]{1,0:T(8,128)(2,1)S(1)} %concatenate.25), channel_id=1, source_target_pairs={{0,12},{1,13},{2,14},{3,15},{4,0},{5,1},{6,2},{7,3},{8,4},{9,5},{1... | collective-permute-start | bytes 903176 | tf_op jit(solution)/shard_map/ppermute | solution.py:61
  10.0 21.6 %collective-permute-start.3 = (bf16[24,6272]{1,0:T(8,128)(2,1)S(1)}, bf16[24,6272]{1,0:T(8,128)(2,1)}, u32[]{:S(2)}, u32[]{:S(2)}) collective-permute-start(bf16[24,6272]{1,0:T(8,128)(2,1)S(1)} %concatenate.25), channel_id=1, source_target_pairs={{0,2},{1,3},{2,0},{3,1},{4,6},{5,7},{6,4},{7,5},{8,10},{9,11},{10,... | collective-permute-start | bytes 903176 | tf_op jit(solution)/shard_map/ppermute | solution.py:61
  11.7 32.0 %collective-permute-start.7 = (bf16[3,2048,384]{2,1,0:T(8,128)(2,1)}, bf16[3,2048,384]{2,1,0:T(8,128)(2,1)}, u32[]{:S(2)}, u32[]{:S(2)}) collective-permute-start(bf16[3,2048,384]{2,1,0:T(8,128)(2,1)} %param.13), channel_id=1, source_target_pairs={{0,1},{1,0},{2,3},{3,2},{4,5},{5,4},{6,7},{7,6},{8,9},{9,8},{10,11... | collective-permute-start | bytes 14155784 | tf_op jit(solution)/shard_map/ppermute | solution.py:61
  18.0 12.1 %collective-permute-start.1 = (bf16[24,6272]{1,0:T(8,128)(2,1)S(1)}, bf16[24,6272]{1,0:T(8,128)(2,1)S(1)}, u32[]{:S(2)}, u32[]{:S(2)}) collective-permute-start(bf16[24,6272]{1,0:T(8,128)(2,1)S(1)} %collective-permute-done), channel_id=1, source_target_pairs={{0,4},{1,5},{2,6},{3,7},{4,8},{5,9},{6,10},{7,11},{8,12},{9,13},{1... | collective-permute-start | bytes 903176 | tf_op jit(solution)/shard_map/ppermute | solution.py:61
  18.0 14.6 %collective-permute-start.4 = (bf16[24,6272]{1,0:T(8,128)(2,1)S(1)}, bf16[24,6272]{1,0:T(8,128)(2,1)S(1)}, u32[]{:S(2)}, u32[]{:S(2)}) collective-permute-start(bf16[24,6272]{1,0:T(8,128)(2,1)S(1)} %collective-permute-done), channel_id=1, source_target_pairs={{0,2},{1,3},{2,0},{3,1},{4,6},{5,7},{6,4},{7,5},{8,10},{9,11},{10,... | collective-permute-start | bytes 903176 | tf_op jit(solution)/shard_map/ppermute | solution.py:61
  23.2 15.2 %collective-permute-start.6 = (bf16[24,6272]{1,0:T(8,128)(2,1)S(1)}, bf16[24,6272]{1,0:T(8,128)(2,1)S(1)}, u32[]{:S(2)}, u32[]{:S(2)}) collective-permute-start(bf16[24,6272]{1,0:T(8,128)(2,1)S(1)} %collective-permute-done.2), channel_id=1, source_target_pairs={{0,2},{1,3},{2,0},{3,1},{4,6},{5,7},{6,4},{7,5},{8,10},{9,11},{10,... | collective-permute-start | bytes 903176 | tf_op jit(solution)/shard_map/ppermute | solution.py:61
  30.0 8.3 %collective-permute-start.5 = (bf16[24,6272]{1,0:T(8,128)(2,1)S(1)}, bf16[24,6272]{1,0:T(8,128)(2,1)S(1)}, u32[]{:S(2)}, u32[]{:S(2)}) collective-permute-start(bf16[24,6272]{1,0:T(8,128)(2,1)S(1)} %collective-permute-done.1), channel_id=1, source_target_pairs={{0,2},{1,3},{2,0},{3,1},{4,6},{5,7},{6,4},{7,5},{8,10},{9,11},{10,... | collective-permute-start | bytes 903176 | tf_op jit(solution)/shard_map/ppermute | solution.py:61
  32.6 6.2 %copy-start.1 = (bf16[3,2048,384]{2,1,0:T(8,128)(2,1)S(1)}, bf16[3,2048,384]{2,1,0:T(8,128)(2,1)}, u32[]{:S(2)}) copy-start(bf16[3,2048,384]{2,1,0:T(8,128)(2,1)} %param.13) | copy-start | bytes 14155780
  56.9 29.7 %copy-start = (s32[24,2048]{1,0:T(8,128)S(1)}, s32[24,2048]{1,0:T(8,128)}, u32[]{:S(2)}) copy-start(s32[24,2048]{1,0:T(8,128)} %param.9) | copy-start | bytes 589828
  56.9 29.7 %copy-start.2 = (bf16[24,2048]{1,0:T(8,128)(2,1)S(1)}, bf16[24,2048]{1,0:T(8,128)(2,1)}, u32[]{:S(2)}) copy-start(bf16[24,2048]{1,0:T(8,128)(2,1)} %param.7) | copy-start | bytes 294916
  56.9 29.7 %copy-start.3 = (f32[2048]{0:T(1024)S(1)}, f32[2048]{0:T(1024)}, u32[]{:S(2)}) copy-start(f32[2048]{0:T(1024)} %param.8) | copy-start | bytes 24580
  57.0 7.9 %collective-permute-start.10 = (bf16[24,4096]{1,0:T(8,128)(2,1)S(1)}, bf16[24,4096]{1,0:T(8,128)(2,1)S(1)}, u32[]{:S(2)}, u32[]{:S(2)}) collective-permute-start(bf16[24,4096]{1,0:T(8,128)(2,1)S(1)} %get-tuple-element.19), channel_id=1, source_target_pairs={{0,2},{1,3},{2,0},{3,1},{4,6},{5,7},{6,4},{7,5},{8,10},{9,11},{10,... | collective-permute-start | bytes 589832 | tf_op jit(solution)/shard_map/ppermute | solution.py:61
  58.3 12.6 %collective-permute-start.9 = (bf16[24,4096]{1,0:T(8,128)(2,1)S(1)}, bf16[24,4096]{1,0:T(8,128)(2,1)S(1)}, u32[]{:S(2)}, u32[]{:S(2)}) collective-permute-start(bf16[24,4096]{1,0:T(8,128)(2,1)S(1)} %get-tuple-element.20), channel_id=1, source_target_pairs={{0,2},{1,3},{2,0},{3,1},{4,6},{5,7},{6,4},{7,5},{8,10},{9,11},{10,... | collective-permute-start | bytes 589832 | tf_op jit(solution)/shard_map/ppermute | solution.py:61
  59.1 13.7 %collective-permute-start.13 = (bf16[24,4096]{1,0:T(8,128)(2,1)S(1)}, bf16[24,4096]{1,0:T(8,128)(2,1)S(1)}, u32[]{:S(2)}, u32[]{:S(2)}) collective-permute-start(bf16[24,4096]{1,0:T(8,128)(2,1)S(1)} %get-tuple-element.18), channel_id=1, source_target_pairs={{0,2},{1,3},{2,0},{3,1},{4,6},{5,7},{6,4},{7,5},{8,10},{9,11},{10,... | collective-permute-start | bytes 589832 | tf_op jit(solution)/shard_map/ppermute | solution.py:61
  64.9 11.7 %collective-permute-start.11 = (bf16[24,4096]{1,0:T(8,128)(2,1)S(1)}, bf16[24,4096]{1,0:T(8,128)(2,1)S(1)}, u32[]{:S(2)}, u32[]{:S(2)}) collective-permute-start(bf16[24,4096]{1,0:T(8,128)(2,1)S(1)} %fusion.25), channel_id=1, source_target_pairs={{0,12},{1,13},{2,14},{3,15},{4,0},{5,1},{6,2},{7,3},{8,4},{9,5},{1... | collective-permute-start | bytes 589832 | tf_op jit(solution)/shard_map/ppermute | solution.py:61
  69.4 11.3 %collective-permute-start.8 = (bf16[24,4096]{1,0:T(8,128)(2,1)S(1)}, bf16[24,4096]{1,0:T(8,128)(2,1)S(1)}, u32[]{:S(2)}, u32[]{:S(2)}) collective-permute-start(bf16[24,4096]{1,0:T(8,128)(2,1)S(1)} %get-tuple-element.17), channel_id=1, source_target_pairs={{0,2},{1,3},{2,0},{3,1},{4,6},{5,7},{6,4},{7,5},{8,10},{9,11},{10,... | collective-permute-start | bytes 589832 | tf_op jit(solution)/shard_map/ppermute | solution.py:61
  76.8 7.7 %collective-permute-start.14 = (bf16[24,4096]{1,0:T(8,128)(2,1)S(1)}, bf16[24,4096]{1,0:T(8,128)(2,1)S(1)}, u32[]{:S(2)}, u32[]{:S(2)}) collective-permute-start(bf16[24,4096]{1,0:T(8,128)(2,1)S(1)} %get-tuple-element.14), channel_id=1, source_target_pairs={{0,4},{1,5},{2,6},{3,7},{4,8},{5,9},{6,10},{7,11},{8,12},{9,13},{1... | collective-permute-start | bytes 589832 | tf_op jit(solution)/shard_map/ppermute | solution.py:61
  79.7 6.7 %collective-permute-start.12 = (bf16[24,4096]{1,0:T(8,128)(2,1)S(1)}, bf16[24,4096]{1,0:T(8,128)(2,1)S(1)}, u32[]{:S(2)}, u32[]{:S(2)}) collective-permute-start(bf16[24,4096]{1,0:T(8,128)(2,1)S(1)} %get-tuple-element.13), channel_id=1, source_target_pairs={{0,12},{1,13},{2,14},{3,15},{4,0},{5,1},{6,2},{7,3},{8,4},{9,5},{1... | collective-permute-start | bytes 589832 | tf_op jit(solution)/shard_map/ppermute | solution.py:61

commit v3 on v1

--- a/solution.py
+++ b/solution.py
@@ -1,9 +1,14 @@
+import functools
+
 import jax
 import jax.numpy as jnp
 from jax import lax
+from jax.experimental import pallas as pl
+from jax.experimental.pallas import tpu as pltpu
 from jax.sharding import PartitionSpec as P
 
 EPS = 1e-06
+VMEM = 32 * 1024 * 1024
 
 
 def expert_terms(weights, rows, rows_t, cotan):
@@ -48,34 +53,231 @@
     return min(2 * ((2 * tok_dev * half + 3 * expert_count - 1) // (3 * expert_count)), tok_dev)
 
 
-def summed_gates(routes, gates, expert_count):
-    named = routes[..., None] == jnp.arange(expert_count, dtype=jnp.int32)
-    return jnp.sum(jnp.where(named, gates[..., None], 0.0), axis=(0, 2))
-
-
-def dense_rows(normed, normed_t, cotangent, routes, gates, weights):
-    width = normed.shape[1]
-    expert_count = lax.axis_size("expert") // 2
-    gate = summed_gates(routes, gates, expert_count)
-    high = lax.reduce_precision(gate, 8, 7)
-    low = gate - high
-    pad = jnp.zeros((gate.shape[0], -2 * expert_count % 128), jnp.bfloat16)
-    pack = jnp.concatenate(
-        [normed, normed_t, cotangent, high.astype(jnp.bfloat16), low.astype(jnp.bfloat16), pad], 1
-    )
-    got = lax.all_gather(pack, "expert", axis=0, tiled=True)
+def rms_terms(xf, probe):
+    scale = lax.rsqrt(jnp.mean(xf * xf, axis=1, keepdims=True) + EPS)
+    along = jnp.mean(xf * probe, axis=1, keepdims=True)
+    return scale, along
+
+
+def pack_kernel(expert_count, tokens, gain, signs, cotangent, routes, gates, pack):
+    width = tokens.shape[1]
+    xf = tokens[...].astype(jnp.float32)
+    probe = (2 * signs[...] - 1).astype(jnp.float32)
+    scale, along = rms_terms(xf, probe)
+    pack[:, :width] = (xf * scale * gain[...]).astype(jnp.bfloat16)
+    tangent = gain[...] * (scale * probe - scale**3 * xf * along)
+    pack[:, width : 2 * width] = tangent.astype(jnp.bfloat16)
+    pack[:, 2 * width : 3 * width] = cotangent[...]
+    lane = lax.broadcasted_iota(jnp.int32, (tokens.shape[0], pack.shape[1] - 3 * width), 1)
+    expert = lax.rem(lane, expert_count)
+    gate = jnp.zeros(lane.shape, jnp.float32)
+    for group in range(routes.shape[0]):
+        for slot in range(routes.shape[2]):
+            named = routes[group, :, slot : slot + 1] == expert
+            gate = gate + jnp.where(named, gates[group, :, slot : slot + 1], 0.0)
+    high = gate.astype(jnp.bfloat16).astype(jnp.float32)
+    tail = jnp.where(lane < expert_count, high, gate - high)
+    tail = jnp.where(lane < 2 * expert_count, tail, 0.0)
+    pack[:, 3 * width :] = tail.astype(jnp.bfloat16)
+
+
+def packed(tokens, norm_gain, probe_signs, cotangent, routes, gates, expert_count):
+    tok_dev, width = tokens.shape
+    tail = -(-2 * expert_count // 128) * 128
+    return pl.pallas_call(
+        functools.partial(pack_kernel, expert_count),
+        out_shape=jax.ShapeDtypeStruct((tok_dev, 3 * width + tail), jnp.bfloat16),
+        compiler_params=pltpu.CompilerParams(vmem_limit_bytes=VMEM),
+        cost_estimate=pl.CostEstimate(
+            flops=20 * tok_dev * width, bytes_accessed=14 * tok_dev * width, transcendentals=0
+        ),
+    )(tokens, norm_gain.reshape(1, width), probe_signs, cotangent, routes, gates)
+
+
+def expert_kernel(count, expert_count, *refs):
+    packs, halves, outs = (refs[:count], refs[count : count + 2], refs[count + 2 : 2 * count + 2])
+    held, both, cotan, acc, sems = refs[2 * count + 2 :]
+    tok_dev = packs[0].shape[0]
+    _, width, hidden = held.shape
+    half = hidden // 2
+    rows = count * tok_dev
+    copies = [
+        [
+            pltpu.make_async_copy(
+                halves[h].at[part], held.at[part, :, pl.ds(h * half, half)], sems.at[h, part]
+            )
+            for part in range(3)
+        ]
+        for h in range(2)
+    ]
+    for h in range(2):
+        for part in range(3):
+            copies[h][part].start()
+
+    def stacked(start, size):
+        return jnp.concatenate([p[:, start : start + size].astype(jnp.float32) for p in packs], 0)
+
+    both[:rows, :] = stacked(0, width).astype(jnp.bfloat16)
+    both[rows:, :] = stacked(width, width).astype(jnp.bfloat16)
+    cotan[...] = stacked(2 * width, width).astype(jnp.bfloat16)
+    tail = stacked(3 * width, packs[0].shape[1] - 3 * width)
     mine = lax.axis_index("expert") // 2
-    pick = (jnp.arange(expert_count) == mine).astype(jnp.float32)
-    tail = got[:, 3 * width :].astype(jnp.float32)
-    weight = jnp.sum(
-        (tail[:, :expert_count] + tail[:, expert_count : 2 * expert_count]) * pick, 1, keepdims=True
-    )
-    g_rows, t_rows = expert_terms(
-        weights, got[:, :width], got[:, width : 2 * width], got[:, 2 * width : 3 * width]
-    )
-    both = jnp.concatenate([weight * g_rows, weight * t_rows], 1).astype(jnp.bfloat16)
-    total = lax.psum_scatter(both, "expert", scatter_dimension=0, tiled=True).astype(jnp.float32)
-    return (total[:, :width], total[:, width:])
+    lane = lax.broadcasted_iota(jnp.int32, tail.shape, 1)
+    picked = (lane == mine) | (lane == mine + expert_count)
+    gate_row = jnp.sum(jnp.where(picked, tail, 0.0), axis=1, keepdims=True)
+    waited = set()
+
+    def weights(part, start, size):
+        for h in range(2):
+            if start < (h + 1) * half and start + size > h * half and (h, part) not in waited:
+                copies[h][part].wait()
+                waited.add((h, part))
+        return held[part, :, start : start + size]
+
+    block = 256 if hidden % 256 == 0 else half
+    contract = (((1,), (1,)), ((), ()))
+    for start in range(0, hidden, block):
+        pre_gate = jnp.dot(
+            both[...], weights(0, start, block), preferred_element_type=jnp.float32
+        )
+        pre_up = jnp.dot(both[...], weights(1, start, block), preferred_element_type=jnp.float32)
+        back = jnp.dot(cotan[...], weights(2, start, block), preferred_element_type=jnp.float32)
+        gate, gate_t = (pre_gate[:rows], pre_gate[rows:])
+        up, up_t = (pre_up[:rows], pre_up[rows:])
+        sig = jax.nn.sigmoid(gate)
+        act = gate * sig
+        slope = sig * (1.0 + gate * (1.0 - sig))
+        bend = sig * (1.0 - sig) * (2.0 + gate * (1.0 - 2.0 * sig))
+        d_gate = (back * slope * up).astype(jnp.bfloat16)
+        d_up = (back * act).astype(jnp.bfloat16)
+        t_gate = (back * (bend * gate_t * up + slope * up_t)).astype(jnp.bfloat16)
+        t_up = (back * slope * gate_t).astype(jnp.bfloat16)
+        total = lax.dot_general(
+            jnp.concatenate([d_gate, t_gate], 0),
+            weights(0, start, block),
+            contract,
+            preferred_element_type=jnp.float32,
+        )
+        total = total + lax.dot_general(
+            jnp.concatenate([d_up, t_up], 0),
+            weights(1, start, block),
+            contract,
+            preferred_element_type=jnp.float32,
+        )
+        acc[...] = total if start == 0 else acc[...] + total
+    for n in range(count):
+        part = slice(n * tok_dev, (n + 1) * tok_dev)
+        later = slice(rows + n * tok_dev, rows + (n + 1) * tok_dev)
+        outs[n][:, :width] = (acc[part] * gate_row[part]).astype(outs[n].dtype)
+        outs[n][:, width:] = (acc[later] * gate_row[part]).astype(outs[n].dtype)
+
+
+def experts(packs, kinds, own, other, expert_count):
+    count = len(packs)
+    tok_dev = packs[0].shape[0]
+    _, width, half = own.shape
+    rows = count * tok_dev
+    whole = pl.BlockSpec(memory_space=pltpu.VMEM)
+    flops = 2 * 9 * rows * width * 2 * half
+    return pl.pallas_call(
+        functools.partial(expert_kernel, count, expert_count),
+        out_shape=[jax.ShapeDtypeStruct((tok_dev, 2 * width), kind) for kind in kinds],
+        in_specs=[whole] * count + [pl.BlockSpec(memory_space=pl.ANY)] * 2,
+        out_specs=[whole] * count,
+        scratch_shapes=[
+            pltpu.VMEM((3, width, 2 * half), jnp.bfloat16),
+            pltpu.VMEM((2 * rows, width), jnp.bfloat16),
+            pltpu.VMEM((rows, width), jnp.bfloat16),
+            pltpu.VMEM((2 * rows, width), jnp.float32),
+            pltpu.SemaphoreType.DMA((2, 3)),
+        ],
+        compiler_params=pltpu.CompilerParams(vmem_limit_bytes=VMEM),
+        cost_estimate=pl.CostEstimate(
+            flops=flops, bytes_accessed=12 * width * half, transcendentals=2 * rows * half
+        ),
+    )(*packs, own, other)
+
+
+def finish_kernel(tokens, gain, signs, kept, forward, backward, hvp, quad):
+    width = tokens.shape[1]
+    xf = tokens[...].astype(jnp.float32)
+    probe = (2 * signs[...] - 1).astype(jnp.float32)
+    scale, along = rms_terms(xf, probe)
+    slope_r = -(scale**3) * along
+    rows = kept[...] + forward[...].astype(jnp.float32) + backward[...].astype(jnp.float32)
+    lifted = gain[...] * rows[:, :width]
+    lifted_t = gain[...] * rows[:, width:]
+    first = jnp.mean(xf * lifted, axis=1, keepdims=True)
+    second = jnp.mean(xf * lifted_t, axis=1, keepdims=True)
+    third = jnp.mean(probe * lifted, axis=1, keepdims=True)
+    whole = (
+        scale * lifted_t
+        + slope_r * lifted
+        - 3.0 * scale**2 * slope_r * first * xf
+        - scale**3 * first * probe
+        - scale**3 * (second + third) * xf
+    )
+    hvp[...] = whole
+    quad[...] = jnp.mean(probe * whole, axis=1, keepdims=True)
+
+
+def moved(rows, turns, flip_x=False, flip_core=False):
+    count = lax.axis_size("expert")
+    pairs = [
+        (i, (i + 4 * turns) % count ^ (2 * flip_x) ^ (1 * flip_core)) for i in range(count)
+    ]
+    return lax.ppermute(rows, "expert", pairs)
+
+
+def dense_local(tokens, norm_gain, probe_signs, cotangent, routes, gates, weights):
+    tok_dev, width = tokens.shape
+    n_exp = lax.axis_size("expert")
+    expert_count = n_exp // 2
+    turns = n_exp // 4
+    ahead, behind = turns // 2, (turns - 1) // 2
+    pack = packed(tokens, norm_gain, probe_signs, cotangent, routes, gates, expert_count)
+    same, across = {0: pack}, {}
+    across[0] = moved(pack, 0, flip_x=True)
+    weights_other = moved(weights, 0, flip_core=True)
+    for k in range(1, ahead + 1):
+        same[k] = moved(same[k - 1], 1)
+        across[k] = moved(same[k], 0, flip_x=True) if k == 1 else moved(across[k - 1], 1)
+    for k in range(turns - 1, turns - 1 - behind, -1):
+        same[k] = moved(same[(k + 1) % turns], -1)
+        across[k] = moved(same[k], 0, flip_x=True)
+    here, there = {}, {}
+    distance = [(0,)] + [
+        tuple(sorted({d, turns - d})) for d in range(1, ahead + 1)
+    ]
+    for batch in distance:
+        packs = [same[k] for k in batch] + [across[k] for k in batch]
+        kinds = [jnp.float32] * len(batch) + [jnp.bfloat16] * len(batch)
+        results = experts(packs, kinds, weights, weights_other, expert_count)
+        for n, k in enumerate(batch):
+            here[k], there[k] = (results[n], results[n + len(batch)])
+    summed = {k: here[k] + moved(there[k], 0, flip_x=True).astype(jnp.float32) for k in here}
+
+    def passed(ks, step):
+        rows = None
+        for k in ks:
+            part = summed[k] if rows is None else summed[k] + rows.astype(jnp.float32)
+            rows = moved(part.astype(jnp.bfloat16), step)
+        return rows
+
+    forward = passed(range(ahead, 0, -1), -1)
+    backward = passed(range(turns - behind, turns), 1)
+    hvp, quad = pl.pallas_call(
+        finish_kernel,
+        out_shape=[
+            jax.ShapeDtypeStruct((tok_dev, width), jnp.float32),
+            jax.ShapeDtypeStruct((tok_dev, 1), jnp.float32),
+        ],
+        compiler_params=pltpu.CompilerParams(vmem_limit_bytes=VMEM),
+        cost_estimate=pl.CostEstimate(
+            flops=40 * tok_dev * width, bytes_accessed=26 * tok_dev * width, transcendentals=0
+        ),
+    )(tokens, norm_gain.reshape(1, width), probe_signs, summed[0], forward, backward)
+    return (hvp, quad.reshape(tok_dev))
 
 
 def routed_rows(normed, normed_t, cotangent, routes, gates, weights):
@@ -139,17 +341,20 @@
 
 
 def local(tokens, norm_gain, probe_signs, cotangent, routes, gates, expert_weights):
+    cap = capacity(tokens.shape[0], routes.shape[2], lax.axis_size("expert") // 2)
+    if lax.axis_size("node") == 1 and routes.shape[0] * cap >= tokens.shape[0]:
+        return dense_local(
+            tokens, norm_gain, probe_signs, cotangent, routes, gates, expert_weights
+        )
     xf = tokens.astype(jnp.float32)
     probe = (2 * probe_signs - 1).astype(jnp.float32)
     tok_dev, width = xf.shape
-    cap = capacity(tok_dev, routes.shape[2], lax.axis_size("expert") // 2)
     scale = lax.rsqrt(jnp.mean(xf * xf, axis=1, keepdims=True) + EPS)
     along = jnp.mean(xf * probe, axis=1, keepdims=True)
     normed = (xf * scale * norm_gain).astype(jnp.bfloat16)
     normed_t = (norm_gain * (scale * probe - scale**3 * xf * along)).astype(jnp.bfloat16)
     own_half = lax.all_gather(expert_weights, "node", axis=2, tiled=True)
-    rows = dense_rows if routes.shape[0] * cap >= tok_dev else routed_rows
-    grad_z, tan_z = rows(normed, normed_t, cotangent, routes, gates, own_half)
+    grad_z, tan_z = routed_rows(normed, normed_t, cotangent, routes, gates, own_half)
     share = width // lax.axis_size("node")
     start = lax.axis_index("node") * share
     slope_r = -(scale**3) * along

time: 161 us -> 85.1 us (0.53)
  waiting for transfers between devices: 122 us -> 40.9 us
  Pallas kernels: 0 us -> 19.7 us
  starting transfers between devices: 0.08 us -> 15.2 us
  between operations: 14.2 us -> 0.74 us
  matrix products: 10 us -> 0 us
  other arithmetic: 9.81 us -> 0.84 us
  local copies, waits for them, and re-layouts: 5.18 us -> 7.31 us
    reduce_scatter x1 -> x0, waiting for transfers between devices: 64.9 us -> none  [dense_rows(): lax.psum_scatter(both, 'expert', scatter_dimension=0, tiled=True)]
    all_gather x1 -> x0, waiting for transfers between devices: 56.7 us -> none  [dense_rows(): got = lax.all_gather(pack, 'expert', axis=0, tiled=True)]
    ppermute x0 -> x15, waiting for transfers between devices: none -> 40.9 us  [moved(): return lax.ppermute(rows, 'expert', pairs)]
    pallas_call x0 -> x5, Pallas kernels: none -> 19.7 us  [the longest x3 18.6 us: experts(): pl.pallas_call(functools.partial(expert_kernel, count, expert_count), out...]
    ppermute x0 -> x15, starting transfers between devices: none -> 15.2 us  [moved(): return lax.ppermute(rows, 'expert', pairs)]
    dot_general x5 -> x0, matrix products: 10 us -> none  [the longest x1 2.76 us: expert_terms(): back = jnp.dot(cotan, weights[2], preferred_element_type=jnp.float32)]
    unnamed x8 -> x22, local copies, waits for them, and re-layouts: 0.87 us -> 7.31 us
    reduce_sum x5 -> x0, other arithmetic: 3.25 us -> none  [the longest x1 1.14 us: local(): along = jnp.mean(xf * probe, axis=1, keepdims=True)]
  transfers between devices with their start and end apart: 2 -> 15, of which waited for: 2 -> 8; matrix products, arithmetic and copies ran while one was open for 0% -> 2% of each run, Pallas kernels for 0% -> 22%
where the time goes in v3:
time: 85.1 us; the launch traced here: 84.7 us
  waiting for transfers between devices  40.9 us (48%)
  Pallas kernels  19.7 us (23%)
  starting transfers between devices  15.2 us (18%)
  local copies, waits for them, and re-layouts  7.31 us (9%)
    ppermute x15, waiting for transfers between devices, moved(): return lax.ppermute(rows, 'expert', pairs)  40.9 us
    pallas_call x3, Pallas kernels, experts(): pl.pallas_call(functools.partial(expert_kernel, count, expert_count), out...  18.6 us
    ppermute x15, starting transfers between devices, moved(): return lax.ppermute(rows, 'expert', pairs)  15.2 us
    unnamed x22, local copies, waits for them, and re-layouts  7.31 us
  transfers between devices with their start and end apart: 15, of which 8 were waited for; matrix products, arithmetic and copies ran while one was open for 2% of the time, Pallas kernels for 22%

profile of v3, /device:TPU:0, one launch (start us, length us, event | category | flops | bytes accessed | tf_op | source)
XLA Modules:
  0.0 84.7 jit_solution(14415699718540412118)
XLA Ops:
  0.6 0.5 collective-permute-start.1
  1.1 0.8 copy.11.routes
  1.9 0.8 copy.12.gates
  2.7 0.0 copy-start.1
  2.7 0.9 %copy-done.1 = s32[24,2048]{1,0:T(8,128)S(1)} copy-done((s32[24,2048]{1,0:T(8,128)S(1)}, s32[24,2048]{1,0:T(8,128)}, u32[]{:S(2)}) %copy-start.1) | copy-done | bytes 196632
  3.6 0.0 copy-start.3
  3.6 0.9 %copy-done.3 = bf16[24,2048]{1,0:T(8,128)(2,1)S(1)} copy-done((bf16[24,2048]{1,0:T(8,128)(2,1)S(1)}, bf16[24,2048]{1,0:T(8,128)(2,1)}, u32[]{:S(2)}) %copy-start.3) | copy-done | bytes 98328
  4.5 0.0 copy-start.5
  4.5 0.9 %copy-done.5 = bf16[24,2048]{1,0:T(8,128)(2,1)S(1)} copy-done((bf16[24,2048]{1,0:T(8,128)(2,1)S(1)}, bf16[24,2048]{1,0:T(8,128)(2,1)}, u32[]{:S(2)}) %copy-start.5) | copy-done | bytes 98328
  5.4 0.0 copy-start.6
  5.4 0.7 copy-done.6
  6.1 0.2 shard_map.86.refs_0_
  6.3 2.6 %collective-permute-start.3 = (bf16[24,6272]{1,0:T(8,128)(2,1)S(1)}, bf16[24,6272]{1,0:T(8,128)(2,1)S(1)}, u32[]{:S(2)}, u32[]{:S(2)}) collective-permute-start(bf16[24,6272]{1,0:T(8,128)(2,1)S(1)} %shard_map.86.refs_0_), channel_id=1, source_target_pairs={{0,4},{1,5},{2,6},{3,7},{4,8},{5,9},{6,10},{7,11},{8,12},{9,13},{1... | collective-permute-start | bytes 903176 | tf_op jit(solution)/shard_map/ppermute | solution.py:229
  9.0 9.8 %collective-permute-done.3.refs_0_ = bf16[24,6272]{1,0:T(8,128)(2,1)S(1)} collective-permute-done((bf16[24,6272]{1,0:T(8,128)(2,1)S(1)}, bf16[24,6272]{1,0:T(8,128)(2,1)S(1)}, u32[]{:S(2)}, u32[]{:S(2)}) %collective-permute-start.3) | collective-permute-done | bytes 301088 | tf_op jit(solution)/shard_map/ppermute | solution.py:229
  18.8 1.5 %collective-permute-start.5 = (bf16[24,6272]{1,0:T(8,128)(2,1)S(1)}, bf16[24,6272]{1,0:T(8,128)(2,1)S(1)}, u32[]{:S(2)}, u32[]{:S(2)}) collective-permute-start(bf16[24,6272]{1,0:T(8,128)(2,1)S(1)} %collective-permute-done.3.refs_0_), channel_id=1, source_target_pairs={{0,2},{1,3},{2,0},{3,1},{4,6},{5,7},{6,4},{7,5},{8,10},{9,11},{10,... | collective-permute-start | bytes 903176 | tf_op jit(solution)/shard_map/ppermute | solution.py:229
  20.3 1.7 %collective-permute-start.4 = (bf16[24,6272]{1,0:T(8,128)(2,1)S(1)}, bf16[24,6272]{1,0:T(8,128)(2,1)S(1)}, u32[]{:S(2)}, u32[]{:S(2)}) collective-permute-start(bf16[24,6272]{1,0:T(8,128)(2,1)S(1)} %shard_map.86.refs_0_), channel_id=1, source_target_pairs={{0,12},{1,13},{2,14},{3,15},{4,0},{5,1},{6,2},{7,3},{8,4},{9,5},{1... | collective-permute-start | bytes 903176 | tf_op jit(solution)/shard_map/ppermute | solution.py:229
  22.0 0.3 collective-permute-start.8
  22.3 5.4 %collective-permute-done.5.refs_2_ = bf16[24,6272]{1,0:T(8,128)(2,1)S(1)} collective-permute-done((bf16[24,6272]{1,0:T(8,128)(2,1)S(1)}, bf16[24,6272]{1,0:T(8,128)(2,1)S(1)}, u32[]{:S(2)}, u32[]{:S(2)}) %collective-permute-start.5) | collective-permute-done | bytes 301088 | tf_op jit(solution)/shard_map/ppermute | solution.py:229
  27.7 0.0 collective-permute-start.9
  27.7 2.6 %collective-permute-done.4.refs_1_ = bf16[24,6272]{1,0:T(8,128)(2,1)S(1)} collective-permute-done((bf16[24,6272]{1,0:T(8,128)(2,1)S(1)}, bf16[24,6272]{1,0:T(8,128)(2,1)S(1)}, u32[]{:S(2)}, u32[]{:S(2)}) %collective-permute-start.4) | collective-permute-done | bytes 301088 | tf_op jit(solution)/shard_map/ppermute | solution.py:229
  30.3 1.1 %collective-permute-start.6 = (bf16[24,6272]{1,0:T(8,128)(2,1)S(1)}, bf16[24,6272]{1,0:T(8,128)(2,1)S(1)}, u32[]{:S(2)}, u32[]{:S(2)}) collective-permute-start(bf16[24,6272]{1,0:T(8,128)(2,1)S(1)} %collective-permute-done.4.refs_1_), channel_id=1, source_target_pairs={{0,2},{1,3},{2,0},{3,1},{4,6},{5,7},{6,4},{7,5},{8,10},{9,11},{10,... | collective-permute-start | bytes 903176 | tf_op jit(solution)/shard_map/ppermute | solution.py:229
  31.4 0.9 %collective-permute-start = (bf16[24,6272]{1,0:T(8,128)(2,1)S(1)}, bf16[24,6272]{1,0:T(8,128)(2,1)S(1)}, u32[]{:S(2)}, u32[]{:S(2)}) collective-permute-start(bf16[24,6272]{1,0:T(8,128)(2,1)S(1)} %shard_map.86.refs_0_), channel_id=1, source_target_pairs={{0,2},{1,3},{2,0},{3,1},{4,6},{5,7},{6,4},{7,5},{8,10},{9,11},{10,... | collective-permute-start | bytes 903176 | tf_op jit(solution)/shard_map/ppermute | solution.py:229
  32.4 4.6 %collective-permute-done.8.refs_0_ = bf16[24,6272]{1,0:T(8,128)(2,1)S(1)} collective-permute-done((bf16[24,6272]{1,0:T(8,128)(2,1)S(1)}, bf16[24,6272]{1,0:T(8,128)(2,1)S(1)}, u32[]{:S(2)}, u32[]{:S(2)}) %collective-permute-start.8) | collective-permute-done | bytes 301088 | tf_op jit(solution)/shard_map/ppermute | solution.py:229
  37.0 4.8 %collective-permute-done.9.refs_1_ = bf16[24,6272]{1,0:T(8,128)(2,1)S(1)} collective-permute-done((bf16[24,6272]{1,0:T(8,128)(2,1)S(1)}, bf16[24,6272]{1,0:T(8,128)(2,1)S(1)}, u32[]{:S(2)}, u32[]{:S(2)}) %collective-permute-start.9) | collective-permute-done | bytes 301088 | tf_op jit(solution)/shard_map/ppermute | solution.py:229
  41.8 0.0 collective-permute-done.1.refs_3_.refs_5_
  41.8 0.0 copy-start
  41.8 2.3 %copy-done = bf16[3,2048,384]{2,1,0:T(8,128)(2,1)S(1)} copy-done((bf16[3,2048,384]{2,1,0:T(8,128)(2,1)S(1)}, bf16[3,2048,384]{2,1,0:T(8,128)(2,1)}, u32[]{:S(2)}) %copy-start) | copy-done | bytes 4718616
  44.2 5.9 %shard_map.89 = (f32[24,4096]{1,0:T(8,128)S(1)}, bf16[24,4096]{1,0:T(8,128)(2,1)S(1)}) custom-call(bf16[24,6272]{1,0:T(8,128)(2,1)S(1)} %collective-permute-done.8.refs_0_, bf16[24,6272]{1,0:T(8,128)(2,1)S(1)} %collective-permute-done.9.refs_1_, bf16[3,2048,384]{2,1,0:T(8,128)(2,1)S(1)} %copy-done, bf16[3,2048,384]{2,1,0:T(8,128)(2,1)} %collective-permute-done.1.refs_3_.refs_5_), custom_call_target="tpu_custom_call" | custom-call | flops 1358954496 | bytes 9437184 | tf_op jit(solution)/shard_map/pallas_call | solution.py:182
  50.1 0.0 slice-start
  50.1 0.0 slice-start.1
  50.1 0.6 collective-permute-start.10
  50.8 0.0 collective-permute-done.6.refs_3_
  50.8 6.7 %shard_map.88 = (f32[24,4096]{1,0:T(8,128)S(1)}, f32[24,4096]{1,0:T(8,128)S(1)}, bf16[24,4096]{1,0:T(8,128)(2,1)S(1)}, bf16[24,4096]{1,0:T(8,128)(2,1)S(1)}) custom-call(bf16[24,6272]{1,0:T(8,128)(2,1)S(1)} %collective-permute-done.3.refs_0_, bf16[24,6272]{1,0:T(8,128)(2,1)S(1)} %collective-permute-done.4.refs_1_, ...), custom_call_target="tpu_custom_call" | custom-call | flops 2717908992 | bytes 9437184 | tf_op jit(solution)/shard_map/pallas_call | solution.py:182
  57.5 1.5 %collective-permute-start.7 = (bf16[24,4096]{1,0:T(8,128)(2,1)S(1)}, bf16[24,4096]{1,0:T(8,128)(2,1)S(1)}, u32[]{:S(2)}, u32[]{:S(2)}) collective-permute-start(bf16[24,4096]{1,0:T(8,128)(2,1)S(1)} %get-tuple-element.15), channel_id=1, source_target_pairs={{0,2},{1,3},{2,0},{3,1},{4,6},{5,7},{6,4},{7,5},{8,10},{9,11},{10,... | collective-permute-start | bytes 589832 | tf_op jit(solution)/shard_map/ppermute | solution.py:229
  59.0 0.0 copy-start.2
  59.0 0.0 copy-start.4
  59.0 0.0 copy-start.7
  59.0 0.6 collective-permute-start.13
  59.6 0.0 collective-permute-done.refs_1_
  59.6 0.0 slice-done
  59.6 0.0 slice-done.1
  59.6 5.9 %shard_map.87 = (f32[24,4096]{1,0:T(8,128)S(1)}, bf16[24,4096]{1,0:T(8,128)(2,1)S(1)}) custom-call(bf16[24,6272]{1,0:T(8,128)(2,1)S(1)} %shard_map.86.refs_0_, bf16[24,6272]{1,0:T(8,128)(2,1)S(1)} %collective-permute-done.refs_1_, bf16[3,2048,384]{2,1,0:T(8,128)(2,1)S(1)} %bitcast.2, bf16[3,2048,384]{2,1,0:T(8,128)(2,1)} %collective-permute-done.1.refs_3_.refs_5_), custom_call_target="tpu_custom_call" | custom-call | flops 1358954496 | bytes 9437184 | tf_op jit(solution)/shard_map/pallas_call | solution.py:182
  65.5 1.5 %collective-permute-start.2 = (bf16[24,4096]{1,0:T(8,128)(2,1)S(1)}, bf16[24,4096]{1,0:T(8,128)(2,1)S(1)}, u32[]{:S(2)}, u32[]{:S(2)}) collective-permute-start(bf16[24,4096]{1,0:T(8,128)(2,1)S(1)} %get-tuple-element.13), channel_id=1, source_target_pairs={{0,2},{1,3},{2,0},{3,1},{4,6},{5,7},{6,4},{7,5},{8,10},{9,11},{10,... | collective-permute-start | bytes 589832 | tf_op jit(solution)/shard_map/ppermute | solution.py:229
  67.1 0.0 collective-permute-done.10
  67.1 1.8 %collective-permute-start.11 = (bf16[24,4096]{1,0:T(8,128)(2,1)S(1)}, bf16[24,4096]{1,0:T(8,128)(2,1)S(1)}, u32[]{:S(2)}, u32[]{:S(2)}) collective-permute-start(bf16[24,4096]{1,0:T(8,128)(2,1)S(1)} %add_convert_fusion.2), channel_id=1, source_target_pairs={{0,12},{1,13},{2,14},{3,15},{4,0},{5,1},{6,2},{7,3},{8,4},{9,5},{1... | collective-permute-start | bytes 589832 | tf_op jit(solution)/shard_map/ppermute | solution.py:229
  68.9 0.0 collective-permute-done.13
  68.9 0.1 add_convert_fusion
  69.0 0.4 collective-permute-start.14
  69.4 0.0 collective-permute-done.7
  69.4 8.0 %collective-permute-done.11 = bf16[24,4096]{1,0:T(8,128)(2,1)S(1)} collective-permute-done((bf16[24,4096]{1,0:T(8,128)(2,1)S(1)}, bf16[24,4096]{1,0:T(8,128)(2,1)S(1)}, u32[]{:S(2)}, u32[]{:S(2)}) %collective-permute-start.11) | collective-permute-done | bytes 196640 | tf_op jit(solution)/shard_map/ppermute | solution.py:229
  77.4 0.1 add_convert_fusion.1
  77.4 0.1 collective-permute-start.12
  77.5 0.0 collective-permute-done.2
  77.5 0.1 convert_add_fusion.kept
  77.6 1.4 %collective-permute-done.14.backward = bf16[24,4096]{1,0:T(8,128)(2,1)S(1)} collective-permute-done((bf16[24,4096]{1,0:T(8,128)(2,1)S(1)}, bf16[24,4096]{1,0:T(8,128)(2,1)S(1)}, u32[]{:S(2)}, u32[]{:S(2)}) %collective-permute-start.14) | collective-permute-done | bytes 196640 | tf_op jit(solution)/shard_map/ppermute | solution.py:229
  78.9 4.2 %collective-permute-done.12.forward = bf16[24,4096]{1,0:T(8,128)(2,1)S(1)} collective-permute-done((bf16[24,4096]{1,0:T(8,128)(2,1)S(1)}, bf16[24,4096]{1,0:T(8,128)(2,1)S(1)}, u32[]{:S(2)}, u32[]{:S(2)}) %collective-permute-start.12) | collective-permute-done | bytes 196640 | tf_op jit(solution)/shard_map/ppermute | solution.py:229
  83.2 0.0 copy-done.2
  83.2 0.0 copy-done.4
  83.2 0.0 copy-done.7
  83.2 0.9 %shard_map.90 = (f32[24,2048]{1,0:T(8,128)}, f32[24,1]{1,0:T(8,128)S(1)}) custom-call(bf16[24,2048]{1,0:T(8,128)(2,1)S(1)} %copy-done.4, f32[1,2048]{1,0:T(1,128)S(1)} %bitcast.4, s32[24,2048]{1,0:T(8,128)S(1)} %copy-done.2, f32[24,4096]{1,0:T(8,128)S(1)} %convert_add_fusion.kept, bf16[24,4096]{1,0:T(8,128)(2,1)S(1)} %collective-permute-done.12.forward, ...), custom_call_target="tpu_custom_call" | custom-call | flops 1966080 | bytes 1277952 | tf_op jit(solution)/shard_map/pallas_call | solution.py:269
  84.1 0.6 reduce
  (2 shorter events, 0.0 us)
Async XLA Ops:
  0.6 41.2 %collective-permute-start.1 = (bf16[3,2048,384]{2,1,0:T(8,128)(2,1)}, bf16[3,2048,384]{2,1,0:T(8,128)(2,1)}, u32[]{:S(2)}, u32[]{:S(2)}) collective-permute-start(bf16[3,2048,384]{2,1,0:T(8,128)(2,1)} %refs_2_.3), channel_id=1, source_target_pairs={{0,1},{1,0},{2,3},{3,2},{4,5},{5,4},{6,7},{7,6},{8,9},{9,8},{10,11... | collective-permute-start | bytes 14155784 | tf_op jit(solution)/shard_map/ppermute | solution.py:229
  2.7 0.9 %copy-start.1 = (s32[24,2048]{1,0:T(8,128)S(1)}, s32[24,2048]{1,0:T(8,128)}, u32[]{:S(2)}) copy-start(s32[24,2048]{1,0:T(8,128)} %signs.3) | copy-start | bytes 589828
  3.6 0.9 %copy-start.3 = (bf16[24,2048]{1,0:T(8,128)(2,1)S(1)}, bf16[24,2048]{1,0:T(8,128)(2,1)}, u32[]{:S(2)}) copy-start(bf16[24,2048]{1,0:T(8,128)(2,1)} %tokens.3) | copy-start | bytes 294916
  4.5 0.9 %copy-start.5 = (bf16[24,2048]{1,0:T(8,128)(2,1)S(1)}, bf16[24,2048]{1,0:T(8,128)(2,1)}, u32[]{:S(2)}) copy-start(bf16[24,2048]{1,0:T(8,128)(2,1)} %cotangent.1) | copy-start | bytes 294916
  5.4 0.7 copy-start.6
  6.3 12.5 %collective-permute-start.3 = (bf16[24,6272]{1,0:T(8,128)(2,1)S(1)}, bf16[24,6272]{1,0:T(8,128)(2,1)S(1)}, u32[]{:S(2)}, u32[]{:S(2)}) collective-permute-start(bf16[24,6272]{1,0:T(8,128)(2,1)S(1)} %shard_map.86.refs_0_), channel_id=1, source_target_pairs={{0,4},{1,5},{2,6},{3,7},{4,8},{5,9},{6,10},{7,11},{8,12},{9,13},{1... | collective-permute-start | bytes 903176 | tf_op jit(solution)/shard_map/ppermute | solution.py:229
  18.8 9.0 %collective-permute-start.5 = (bf16[24,6272]{1,0:T(8,128)(2,1)S(1)}, bf16[24,6272]{1,0:T(8,128)(2,1)S(1)}, u32[]{:S(2)}, u32[]{:S(2)}) collective-permute-start(bf16[24,6272]{1,0:T(8,128)(2,1)S(1)} %collective-permute-done.3.refs_0_), channel_id=1, source_target_pairs={{0,2},{1,3},{2,0},{3,1},{4,6},{5,7},{6,4},{7,5},{8,10},{9,11},{10,... | collective-permute-start | bytes 903176 | tf_op jit(solution)/shard_map/ppermute | solution.py:229
  20.3 10.1 %collective-permute-start.4 = (bf16[24,6272]{1,0:T(8,128)(2,1)S(1)}, bf16[24,6272]{1,0:T(8,128)(2,1)S(1)}, u32[]{:S(2)}, u32[]{:S(2)}) collective-permute-start(bf16[24,6272]{1,0:T(8,128)(2,1)S(1)} %shard_map.86.refs_0_), channel_id=1, source_target_pairs={{0,12},{1,13},{2,14},{3,15},{4,0},{5,1},{6,2},{7,3},{8,4},{9,5},{1... | collective-permute-start | bytes 903176 | tf_op jit(solution)/shard_map/ppermute | solution.py:229
  22.0 15.0 %collective-permute-start.8 = (bf16[24,6272]{1,0:T(8,128)(2,1)S(1)}, bf16[24,6272]{1,0:T(8,128)(2,1)S(1)}, u32[]{:S(2)}, u32[]{:S(2)}) collective-permute-start(bf16[24,6272]{1,0:T(8,128)(2,1)S(1)} %collective-permute-done.3.refs_0_), channel_id=1, source_target_pairs={{0,4},{1,5},{2,6},{3,7},{4,8},{5,9},{6,10},{7,11},{8,12},{9,13},{1... | collective-permute-start | bytes 903176 | tf_op jit(solution)/shard_map/ppermute | solution.py:229
  27.7 14.1 %collective-permute-start.9 = (bf16[24,6272]{1,0:T(8,128)(2,1)S(1)}, bf16[24,6272]{1,0:T(8,128)(2,1)S(1)}, u32[]{:S(2)}, u32[]{:S(2)}) collective-permute-start(bf16[24,6272]{1,0:T(8,128)(2,1)S(1)} %collective-permute-done.5.refs_2_), channel_id=1, source_target_pairs={{0,4},{1,5},{2,6},{3,7},{4,8},{5,9},{6,10},{7,11},{8,12},{9,13},{1... | collective-permute-start | bytes 903176 | tf_op jit(solution)/shard_map/ppermute | solution.py:229
  30.3 20.5 %collective-permute-start.6 = (bf16[24,6272]{1,0:T(8,128)(2,1)S(1)}, bf16[24,6272]{1,0:T(8,128)(2,1)S(1)}, u32[]{:S(2)}, u32[]{:S(2)}) collective-permute-start(bf16[24,6272]{1,0:T(8,128)(2,1)S(1)} %collective-permute-done.4.refs_1_), channel_id=1, source_target_pairs={{0,2},{1,3},{2,0},{3,1},{4,6},{5,7},{6,4},{7,5},{8,10},{9,11},{10,... | collective-permute-start | bytes 903176 | tf_op jit(solution)/shard_map/ppermute | solution.py:229
  31.4 28.1 %collective-permute-start = (bf16[24,6272]{1,0:T(8,128)(2,1)S(1)}, bf16[24,6272]{1,0:T(8,128)(2,1)S(1)}, u32[]{:S(2)}, u32[]{:S(2)}) collective-permute-start(bf16[24,6272]{1,0:T(8,128)(2,1)S(1)} %shard_map.86.refs_0_), channel_id=1, source_target_pairs={{0,2},{1,3},{2,0},{3,1},{4,6},{5,7},{6,4},{7,5},{8,10},{9,11},{10,... | collective-permute-start | bytes 903176 | tf_op jit(solution)/shard_map/ppermute | solution.py:229
  41.8 2.3 %copy-start = (bf16[3,2048,384]{2,1,0:T(8,128)(2,1)S(1)}, bf16[3,2048,384]{2,1,0:T(8,128)(2,1)}, u32[]{:S(2)}) copy-start(bf16[3,2048,384]{2,1,0:T(8,128)(2,1)} %refs_2_.3) | copy-start | bytes 14155780
  50.1 9.5 %slice-start = ((s8[4718592]{0:T(1024)(128)(4,1)}), s8[4194304]{0:T(1024)(128)(4,1)S(1)}, s32[]{:S(2)}) async-start(s8[4718592]{0:T(1024)(128)(4,1)} %bitcast.1), calls=%async_computation | async-start | bytes 8388608
  50.1 9.5 %slice-start.1 = ((s8[4718592]{0:T(1024)(128)(4,1)}), s8[524288]{0:T(1024)(128)(4,1)S(1)}, s32[]{:S(2)}) async-start(s8[4718592]{0:T(1024)(128)(4,1)} %bitcast.1), calls=%async_computation.1 | async-start | bytes 1048576
  50.1 16.9 %collective-permute-start.10 = (bf16[24,4096]{1,0:T(8,128)(2,1)S(1)}, bf16[24,4096]{1,0:T(8,128)(2,1)S(1)}, u32[]{:S(2)}, u32[]{:S(2)}) collective-permute-start(bf16[24,4096]{1,0:T(8,128)(2,1)S(1)} %get-tuple-element.17), channel_id=1, source_target_pairs={{0,2},{1,3},{2,0},{3,1},{4,6},{5,7},{6,4},{7,5},{8,10},{9,11},{10,... | collective-permute-start | bytes 589832 | tf_op jit(solution)/shard_map/ppermute | solution.py:229
  57.5 11.9 %collective-permute-start.7 = (bf16[24,4096]{1,0:T(8,128)(2,1)S(1)}, bf16[24,4096]{1,0:T(8,128)(2,1)S(1)}, u32[]{:S(2)}, u32[]{:S(2)}) collective-permute-start(bf16[24,4096]{1,0:T(8,128)(2,1)S(1)} %get-tuple-element.15), channel_id=1, source_target_pairs={{0,2},{1,3},{2,0},{3,1},{4,6},{5,7},{6,4},{7,5},{8,10},{9,11},{10,... | collective-permute-start | bytes 589832 | tf_op jit(solution)/shard_map/ppermute | solution.py:229
  59.0 24.2 %copy-start.2 = (s32[24,2048]{1,0:T(8,128)S(1)}, s32[24,2048]{1,0:T(8,128)}, u32[]{:S(2)}) copy-start(s32[24,2048]{1,0:T(8,128)} %signs.3) | copy-start | bytes 589828
  59.0 24.2 %copy-start.4 = (bf16[24,2048]{1,0:T(8,128)(2,1)S(1)}, bf16[24,2048]{1,0:T(8,128)(2,1)}, u32[]{:S(2)}) copy-start(bf16[24,2048]{1,0:T(8,128)(2,1)} %tokens.3) | copy-start | bytes 294916
  59.0 24.2 %copy-start.7 = (f32[2048]{0:T(1024)S(1)}, f32[2048]{0:T(1024)}, u32[]{:S(2)}) copy-start(f32[2048]{0:T(1024)} %param.8) | copy-start | bytes 24580
  59.0 9.9 %collective-permute-start.13 = (bf16[24,4096]{1,0:T(8,128)(2,1)S(1)}, bf16[24,4096]{1,0:T(8,128)(2,1)S(1)}, u32[]{:S(2)}, u32[]{:S(2)}) collective-permute-start(bf16[24,4096]{1,0:T(8,128)(2,1)S(1)} %get-tuple-element.19), channel_id=1, source_target_pairs={{0,2},{1,3},{2,0},{3,1},{4,6},{5,7},{6,4},{7,5},{8,10},{9,11},{10,... | collective-permute-start | bytes 589832 | tf_op jit(solution)/shard_map/ppermute | solution.py:229
  65.5 12.0 %collective-permute-start.2 = (bf16[24,4096]{1,0:T(8,128)(2,1)S(1)}, bf16[24,4096]{1,0:T(8,128)(2,1)S(1)}, u32[]{:S(2)}, u32[]{:S(2)}) collective-permute-start(bf16[24,4096]{1,0:T(8,128)(2,1)S(1)} %get-tuple-element.13), channel_id=1, source_target_pairs={{0,2},{1,3},{2,0},{3,1},{4,6},{5,7},{6,4},{7,5},{8,10},{9,11},{10,... | collective-permute-start | bytes 589832 | tf_op jit(solution)/shard_map/ppermute | solution.py:229
  67.1 10.2 %collective-permute-start.11 = (bf16[24,4096]{1,0:T(8,128)(2,1)S(1)}, bf16[24,4096]{1,0:T(8,128)(2,1)S(1)}, u32[]{:S(2)}, u32[]{:S(2)}) collective-permute-start(bf16[24,4096]{1,0:T(8,128)(2,1)S(1)} %add_convert_fusion.2), channel_id=1, source_target_pairs={{0,12},{1,13},{2,14},{3,15},{4,0},{5,1},{6,2},{7,3},{8,4},{9,5},{1... | collective-permute-start | bytes 589832 | tf_op jit(solution)/shard_map/ppermute | solution.py:229
  69.0 10.0 %collective-permute-start.14 = (bf16[24,4096]{1,0:T(8,128)(2,1)S(1)}, bf16[24,4096]{1,0:T(8,128)(2,1)S(1)}, u32[]{:S(2)}, u32[]{:S(2)}) collective-permute-start(bf16[24,4096]{1,0:T(8,128)(2,1)S(1)} %add_convert_fusion), channel_id=1, source_target_pairs={{0,4},{1,5},{2,6},{3,7},{4,8},{5,9},{6,10},{7,11},{8,12},{9,13},{1... | collective-permute-start | bytes 589832 | tf_op jit(solution)/shard_map/ppermute | solution.py:229
  77.4 5.7 %collective-permute-start.12 = (bf16[24,4096]{1,0:T(8,128)(2,1)S(1)}, bf16[24,4096]{1,0:T(8,128)(2,1)S(1)}, u32[]{:S(2)}, u32[]{:S(2)}) collective-permute-start(bf16[24,4096]{1,0:T(8,128)(2,1)S(1)} %add_convert_fusion.1), channel_id=1, source_target_pairs={{0,12},{1,13},{2,14},{3,15},{4,0},{5,1},{6,2},{7,3},{8,4},{9,5},{1... | collective-permute-start | bytes 589832 | tf_op jit(solution)/shard_map/ppermute | solution.py:229

commit v4 on v3

--- a/solution.py
+++ b/solution.py
@@ -8,7 +8,8 @@
 from jax.sharding import PartitionSpec as P
 
 EPS = 1e-06
-VMEM = 32 * 1024 * 1024
+VMEM = 24 * 1024 * 1024
+VMEM_ALONE = 60 * 1024 * 1024
 
 
 def expert_terms(weights, rows, rows_t, cotan):
@@ -59,7 +60,17 @@
     return scale, along
 
 
-def pack_kernel(expert_count, tokens, gain, signs, cotangent, routes, gates, pack):
+def pack_kernel(expert_count, *refs):
+    sources, pack, held, sems = (refs[:6], refs[6], refs[7:13], refs[13])
+    copies = [
+        pltpu.make_async_copy(source, target, sems.at[n])
+        for n, (source, target) in enumerate(zip(sources, held))
+    ]
+    for copy in copies:
+        copy.start()
+    for copy in copies:
+        copy.wait()
+    tokens, gain, signs, cotangent, routes, gates = held
     width = tokens.shape[1]
     xf = tokens[...].astype(jnp.float32)
     probe = (2 * signs[...] - 1).astype(jnp.float32)
@@ -84,35 +95,57 @@
 def packed(tokens, norm_gain, probe_signs, cotangent, routes, gates, expert_count):
     tok_dev, width = tokens.shape
     tail = -(-2 * expert_count // 128) * 128
+    operands = (tokens, norm_gain.reshape(1, width), probe_signs, cotangent, routes, gates)
     return pl.pallas_call(
         functools.partial(pack_kernel, expert_count),
         out_shape=jax.ShapeDtypeStruct((tok_dev, 3 * width + tail), jnp.bfloat16),
-        compiler_params=pltpu.CompilerParams(vmem_limit_bytes=VMEM),
+        in_specs=[pl.BlockSpec(memory_space=pl.ANY)] * 6,
+        out_specs=pl.BlockSpec(memory_space=pltpu.VMEM),
+        scratch_shapes=[pltpu.VMEM(array.shape, array.dtype) for array in operands]
+        + [pltpu.SemaphoreType.DMA((6,))],
+        compiler_params=pltpu.CompilerParams(vmem_limit_bytes=VMEM_ALONE),
         cost_estimate=pl.CostEstimate(
             flops=20 * tok_dev * width, bytes_accessed=14 * tok_dev * width, transcendentals=0
         ),
-    )(tokens, norm_gain.reshape(1, width), probe_signs, cotangent, routes, gates)
+    )(*operands)
+
+
+def join_kernel(own, other, held, sems):
+    half = own.shape[2]
+    copies = [
+        pltpu.make_async_copy(
+            source.at[part], held.at[part, :, pl.ds(h * half, half)], sems.at[h, part]
+        )
+        for h, source in enumerate((own, other))
+        for part in range(3)
+    ]
+    for copy in copies:
+        copy.start()
+    for copy in copies:
+        copy.wait()
+
+
+def joined(own, other):
+    parts, width, half = own.shape
+    return pl.pallas_call(
+        join_kernel,
+        out_shape=jax.ShapeDtypeStruct((parts, width, 2 * half), own.dtype),
+        in_specs=[pl.BlockSpec(memory_space=pl.ANY)] * 2,
+        out_specs=pl.BlockSpec(memory_space=pltpu.VMEM),
+        scratch_shapes=[pltpu.SemaphoreType.DMA((2, parts))],
+        compiler_params=pltpu.CompilerParams(vmem_limit_bytes=VMEM),
+        cost_estimate=pl.CostEstimate(
+            flops=0, bytes_accessed=8 * parts * width * half, transcendentals=0
+        ),
+    )(own, other)
 
 
 def expert_kernel(count, expert_count, *refs):
-    packs, halves, outs = (refs[:count], refs[count : count + 2], refs[count + 2 : 2 * count + 2])
-    held, both, cotan, acc, sems = refs[2 * count + 2 :]
+    packs, held, outs = (refs[:count], refs[count], refs[count + 1 : 2 * count + 1])
+    both, cotan, acc = refs[2 * count + 1 :]
     tok_dev = packs[0].shape[0]
     _, width, hidden = held.shape
-    half = hidden // 2
     rows = count * tok_dev
-    copies = [
-        [
-            pltpu.make_async_copy(
-                halves[h].at[part], held.at[part, :, pl.ds(h * half, half)], sems.at[h, part]
-            )
-            for part in range(3)
-        ]
-        for h in range(2)
-    ]
-    for h in range(2):
-        for part in range(3):
-            copies[h][part].start()
 
     def stacked(start, size):
         return jnp.concatenate([p[:, start : start + size].astype(jnp.float32) for p in packs], 0)
@@ -125,16 +158,11 @@
     lane = lax.broadcasted_iota(jnp.int32, tail.shape, 1)
     picked = (lane == mine) | (lane == mine + expert_count)
     gate_row = jnp.sum(jnp.where(picked, tail, 0.0), axis=1, keepdims=True)
-    waited = set()
 
     def weights(part, start, size):
-        for h in range(2):
-            if start < (h + 1) * half and start + size > h * half and (h, part) not in waited:
-                copies[h][part].wait()
-                waited.add((h, part))
         return held[part, :, start : start + size]
 
-    block = 256 if hidden % 256 == 0 else half
+    block = 256 if hidden % 256 == 0 else 128
     contract = (((1,), (1,)), ((), ()))
     for start in range(0, hidden, block):
         pre_gate = jnp.dot(
@@ -172,39 +200,40 @@
         outs[n][:, width:] = (acc[later] * gate_row[part]).astype(outs[n].dtype)
 
 
-def experts(packs, kinds, own, other, expert_count):
+def experts(packs, kind, weights, expert_count):
     count = len(packs)
     tok_dev = packs[0].shape[0]
-    _, width, half = own.shape
+    _, width, hidden = weights.shape
     rows = count * tok_dev
     whole = pl.BlockSpec(memory_space=pltpu.VMEM)
-    flops = 2 * 9 * rows * width * 2 * half
     return pl.pallas_call(
         functools.partial(expert_kernel, count, expert_count),
-        out_shape=[jax.ShapeDtypeStruct((tok_dev, 2 * width), kind) for kind in kinds],
-        in_specs=[whole] * count + [pl.BlockSpec(memory_space=pl.ANY)] * 2,
+        out_shape=[jax.ShapeDtypeStruct((tok_dev, 2 * width), kind)] * count,
+        in_specs=[whole] * (count + 1),
         out_specs=[whole] * count,
         scratch_shapes=[
-            pltpu.VMEM((3, width, 2 * half), jnp.bfloat16),
             pltpu.VMEM((2 * rows, width), jnp.bfloat16),
             pltpu.VMEM((rows, width), jnp.bfloat16),
             pltpu.VMEM((2 * rows, width), jnp.float32),
-            pltpu.SemaphoreType.DMA((2, 3)),
         ],
         compiler_params=pltpu.CompilerParams(vmem_limit_bytes=VMEM),
         cost_estimate=pl.CostEstimate(
-            flops=flops, bytes_accessed=12 * width * half, transcendentals=2 * rows * half
+            flops=2 * 9 * rows * width * hidden,
+            bytes_accessed=6 * width * hidden,
+            transcendentals=rows * hidden,
         ),
-    )(*packs, own, other)
-
-
-def finish_kernel(tokens, gain, signs, kept, forward, backward, hvp, quad):
+    )(*packs, weights)
+
+
+def finish_kernel(tokens, gain, signs, here, there, forward, backward, hvp, quad):
     width = tokens.shape[1]
     xf = tokens[...].astype(jnp.float32)
     probe = (2 * signs[...] - 1).astype(jnp.float32)
     scale, along = rms_terms(xf, probe)
     slope_r = -(scale**3) * along
-    rows = kept[...] + forward[...].astype(jnp.float32) + backward[...].astype(jnp.float32)
+    rows = here[...]
+    for part in (there, forward, backward):
+        rows = rows + part[...].astype(jnp.float32)
     lifted = gain[...] * rows[:, :width]
     lifted_t = gain[...] * rows[:, width:]
     first = jnp.mean(xf * lifted, axis=1, keepdims=True)
@@ -218,7 +247,12 @@
         - scale**3 * (second + third) * xf
     )
     hvp[...] = whole
-    quad[...] = jnp.mean(probe * whole, axis=1, keepdims=True)
+    column = jnp.mean(probe * whole, axis=1, keepdims=True)
+    tok_dev = column.shape[0]
+    own = lax.broadcasted_iota(jnp.int32, (tok_dev, tok_dev), 0) == lax.broadcasted_iota(
+        jnp.int32, (tok_dev, tok_dev), 1
+    )
+    quad[...] = jnp.sum(jnp.where(own, column, 0.0), axis=0, keepdims=True)
 
 
 def moved(rows, turns, flip_x=False, flip_core=False):
@@ -241,26 +275,24 @@
     weights_other = moved(weights, 0, flip_core=True)
     for k in range(1, ahead + 1):
         same[k] = moved(same[k - 1], 1)
-        across[k] = moved(same[k], 0, flip_x=True) if k == 1 else moved(across[k - 1], 1)
+        across[k] = moved(same[k], 0, flip_x=True)
     for k in range(turns - 1, turns - 1 - behind, -1):
         same[k] = moved(same[(k + 1) % turns], -1)
         across[k] = moved(same[k], 0, flip_x=True)
-    here, there = {}, {}
-    distance = [(0,)] + [
-        tuple(sorted({d, turns - d})) for d in range(1, ahead + 1)
-    ]
-    for batch in distance:
-        packs = [same[k] for k in batch] + [across[k] for k in batch]
-        kinds = [jnp.float32] * len(batch) + [jnp.bfloat16] * len(batch)
-        results = experts(packs, kinds, weights, weights_other, expert_count)
-        for n, k in enumerate(batch):
-            here[k], there[k] = (results[n], results[n + len(batch)])
-    summed = {k: here[k] + moved(there[k], 0, flip_x=True).astype(jnp.float32) for k in here}
+    order = range(turns)
+    held = joined(weights, weights_other)
+    results = experts([same[k] for k in order], jnp.float32, held, expert_count)
+    here = dict(zip(order, results))
+    packs = [across[k] for k in order]
+    packs[0], here[0] = lax.optimization_barrier((packs[0], here[0]))
+    results = experts(packs, jnp.bfloat16, held, expert_count)
+    there = {k: moved(rows, 0, flip_x=True) for k, rows in zip(order, results)}
 
     def passed(ks, step):
         rows = None
         for k in ks:
-            part = summed[k] if rows is None else summed[k] + rows.astype(jnp.float32)
+            part = here[k] + there[k].astype(jnp.float32)
+            part = part if rows is None else part + rows.astype(jnp.float32)
             rows = moved(part.astype(jnp.bfloat16), step)
         return rows
 
@@ -270,13 +302,13 @@
         finish_kernel,
         out_shape=[
             jax.ShapeDtypeStruct((tok_dev, width), jnp.float32),
-            jax.ShapeDtypeStruct((tok_dev, 1), jnp.float32),
+            jax.ShapeDtypeStruct((1, tok_dev), jnp.float32),
         ],
         compiler_params=pltpu.CompilerParams(vmem_limit_bytes=VMEM),
         cost_estimate=pl.CostEstimate(
             flops=40 * tok_dev * width, bytes_accessed=26 * tok_dev * width, transcendentals=0
         ),
-    )(tokens, norm_gain.reshape(1, width), probe_signs, summed[0], forward, backward)
+    )(tokens, norm_gain.reshape(1, width), probe_signs, here[0], there[0], forward, backward)
     return (hvp, quad.reshape(tok_dev))
 
 

time: 85.1 us -> 77.4 us (0.910)
  starting transfers between devices: 15.2 us -> 22.4 us
  waiting for transfers between devices: 40.9 us -> 33.8 us
  Pallas kernels: 19.7 us -> 14.9 us
  local copies, waits for them, and re-layouts: 7.31 us -> 5.1 us
    pallas_call x3 -> x2, Pallas kernels: 18.6 us -> 9.08 us  [experts(): pl.pallas_call(functools.partial(expert_kernel, count, expert_count), out...]
    ppermute x15, starting transfers between devices: 15.2 us -> 22.4 us  [moved(): return lax.ppermute(rows, 'expert', pairs)]
    ppermute x15, waiting for transfers between devices: 40.9 us -> 33.8 us  [moved(): return lax.ppermute(rows, 'expert', pairs)]
    pallas_call x0 -> x1, Pallas kernels: none -> 2.88 us  [joined(): pl.pallas_call(join_kernel, out_shape=jax.ShapeDtypeStruct((parts, width,...]
    unnamed x22 -> x12, local copies, waits for them, and re-layouts: 7.31 us -> 5.1 us
    pallas_call x1, Pallas kernels: 0.22 us -> 2.03 us  [packed(): pl.pallas_call(functools.partial(pack_kernel, expert_count), out_shape=ja...]
  transfers between devices with their start and end apart: 15 -> 15, of which waited for: 8 -> 9; matrix products, arithmetic and copies ran while one was open for 2% -> 4% of each run, Pallas kernels for 22% -> 12%
where the time goes in v4:
time: 77.4 us; the launch traced here: 77.1 us
  waiting for transfers between devices  33.8 us (44%)
  starting transfers between devices  22.4 us (29%)
  Pallas kernels  14.9 us (19%)
  local copies, waits for them, and re-layouts  5.1 us (7%)
    ppermute x15, waiting for transfers between devices, moved(): return lax.ppermute(rows, 'expert', pairs)  33.8 us
    ppermute x15, starting transfers between devices, moved(): return lax.ppermute(rows, 'expert', pairs)  22.4 us
    pallas_call x2, Pallas kernels, experts(): pl.pallas_call(functools.partial(expert_kernel, count, expert_count), out...  9.08 us
    unnamed x12, local copies, waits for them, and re-layouts  5.1 us
    pallas_call x1, Pallas kernels, joined(): pl.pallas_call(join_kernel, out_shape=jax.ShapeDtypeStruct((parts, width,...  2.88 us
    pallas_call x1, Pallas kernels, packed(): pl.pallas_call(functools.partial(pack_kernel, expert_count), out_shape=ja...  2.03 us
  transfers between devices with their start and end apart: 15, of which 9 were waited for; matrix products, arithmetic and copies ran while one was open for 4% of the time, Pallas kernels for 12%

profile of v4, /device:TPU:0, one launch (start us, length us, event | category | flops | bytes accessed | tf_op | source)
XLA Modules:
  0.0 77.1 jit_solution(13509015091008663345)
XLA Ops:
  0.6 0.5 collective-permute-start.4
  1.1 1.4 %copy.10.refs_5_ = f32[2,24,4]{2,1,0:T(8,128)} copy(f32[2,24,4]{1,2,0:T(4,128)} %param.12) | data formatting | bytes 1536 | tf_op args[5]
  2.5 1.4 %copy.9.refs_4_ = s32[2,24,4]{2,1,0:T(8,128)} copy(s32[2,24,4]{1,2,0:T(4,128)} %param.11) | data formatting | bytes 1536 | tf_op args[4]
  3.9 2.0 %shard_map.86.refs_0_ = bf16[24,6272]{1,0:T(8,128)(2,1)} custom-call(bf16[24,2048]{1,0:T(8,128)(2,1)} %tokens.1, f32[1,2048]{1,0:T(1,128)} %bitcast.2, s32[24,2048]{1,0:T(8,128)} %signs.1, bf16[24,2048]{1,0:T(8,128)(2,1)} %refs_3_.1, s32[2,24,4]{2,1,0:T(8,128)} %copy.9.refs_4_, f32[2,24,4]{2,1,0:T(8,128)} %copy.10.refs_5_), custom_call_target="tpu_custom_call" | custom-call | flops 983040 | bytes 688128 | tf_op jit(solution)/shard_map/pallas_call | solution.py:99
  5.9 2.6 %collective-permute-start.1 = (bf16[24,6272]{1,0:T(8,128)(2,1)}, bf16[24,6272]{1,0:T(8,128)(2,1)S(1)}, u32[]{:S(2)}, u32[]{:S(2)}) collective-permute-start(bf16[24,6272]{1,0:T(8,128)(2,1)} %shard_map.86.refs_0_), channel_id=1, source_target_pairs={{0,4},{1,5},{2,6},{3,7},{4,8},{5,9},{6,10},{7,11},{8,12},{9,13},{1... | collective-permute-start | bytes 903176 | tf_op jit(solution)/shard_map/ppermute | solution.py:263
  8.6 2.1 %collective-permute-start.3 = (bf16[24,6272]{1,0:T(8,128)(2,1)}, bf16[24,6272]{1,0:T(8,128)(2,1)S(1)}, u32[]{:S(2)}, u32[]{:S(2)}) collective-permute-start(bf16[24,6272]{1,0:T(8,128)(2,1)} %shard_map.86.refs_0_), channel_id=1, source_target_pairs={{0,12},{1,13},{2,14},{3,15},{4,0},{5,1},{6,2},{7,3},{8,4},{9,5},{1... | collective-permute-start | bytes 903176 | tf_op jit(solution)/shard_map/ppermute | solution.py:263
  10.7 8.2 %collective-permute-done.1.refs_1_ = bf16[24,6272]{1,0:T(8,128)(2,1)S(1)} collective-permute-done((bf16[24,6272]{1,0:T(8,128)(2,1)}, bf16[24,6272]{1,0:T(8,128)(2,1)S(1)}, u32[]{:S(2)}, u32[]{:S(2)}) %collective-permute-start.1) | collective-permute-done | bytes 301088 | tf_op jit(solution)/shard_map/ppermute | solution.py:263
  18.8 0.0 collective-permute-start.2
  18.9 1.6 %collective-permute-start = (bf16[24,6272]{1,0:T(8,128)(2,1)}, bf16[24,6272]{1,0:T(8,128)(2,1)S(1)}, u32[]{:S(2)}, u32[]{:S(2)}) collective-permute-start(bf16[24,6272]{1,0:T(8,128)(2,1)} %shard_map.86.refs_0_), channel_id=1, source_target_pairs={{0,2},{1,3},{2,0},{3,1},{4,6},{5,7},{6,4},{7,5},{8,10},{9,11},{10,... | collective-permute-start | bytes 903176 | tf_op jit(solution)/shard_map/ppermute | solution.py:263
  20.5 0.4 collective-permute-start.5
  20.9 3.6 %collective-permute-done.3.refs_3_ = bf16[24,6272]{1,0:T(8,128)(2,1)S(1)} collective-permute-done((bf16[24,6272]{1,0:T(8,128)(2,1)}, bf16[24,6272]{1,0:T(8,128)(2,1)S(1)}, u32[]{:S(2)}, u32[]{:S(2)}) %collective-permute-start.3) | collective-permute-done | bytes 301088 | tf_op jit(solution)/shard_map/ppermute | solution.py:263
  24.5 1.5 %collective-permute-start.7 = (bf16[24,6272]{1,0:T(8,128)(2,1)S(1)}, bf16[24,6272]{1,0:T(8,128)(2,1)S(1)}, u32[]{:S(2)}, u32[]{:S(2)}) collective-permute-start(bf16[24,6272]{1,0:T(8,128)(2,1)S(1)} %collective-permute-done.3.refs_3_), channel_id=1, source_target_pairs={{0,2},{1,3},{2,0},{3,1},{4,6},{5,7},{6,4},{7,5},{8,10},{9,11},{10,... | collective-permute-start | bytes 903176 | tf_op jit(solution)/shard_map/ppermute | solution.py:263
  26.0 5.6 %collective-permute-done.2.refs_2_ = bf16[24,6272]{1,0:T(8,128)(2,1)S(1)} collective-permute-done((bf16[24,6272]{1,0:T(8,128)(2,1)S(1)}, bf16[24,6272]{1,0:T(8,128)(2,1)S(1)}, u32[]{:S(2)}, u32[]{:S(2)}) %collective-permute-start.2) | collective-permute-done | bytes 301088 | tf_op jit(solution)/shard_map/ppermute | solution.py:263
  31.6 1.5 %collective-permute-start.6 = (bf16[24,6272]{1,0:T(8,128)(2,1)S(1)}, bf16[24,6272]{1,0:T(8,128)(2,1)S(1)}, u32[]{:S(2)}, u32[]{:S(2)}) collective-permute-start(bf16[24,6272]{1,0:T(8,128)(2,1)S(1)} %collective-permute-done.2.refs_2_), channel_id=1, source_target_pairs={{0,2},{1,3},{2,0},{3,1},{4,6},{5,7},{6,4},{7,5},{8,10},{9,11},{10,... | collective-permute-start | bytes 903176 | tf_op jit(solution)/shard_map/ppermute | solution.py:263
  33.0 0.0 collective-permute-done.4.other
  33.0 0.0 copy-start
  33.0 2.3 %copy-done = bf16[3,2048,384]{2,1,0:T(8,128)(2,1)S(1)} copy-done((bf16[3,2048,384]{2,1,0:T(8,128)(2,1)S(1)}, bf16[3,2048,384]{2,1,0:T(8,128)(2,1)}, u32[]{:S(2)}) %copy-start) | copy-done | bytes 4718616
  35.4 0.0 copy-start.1
  35.4 2.9 %shard_map.87.refs_4_ = bf16[3,2048,768]{2,1,0:T(8,128)(2,1)S(1)} custom-call(bf16[3,2048,384]{2,1,0:T(8,128)(2,1)S(1)} %copy-done, bf16[3,2048,384]{2,1,0:T(8,128)(2,1)} %collective-permute-done.4.other), custom_call_target="tpu_custom_call" | custom-call | bytes 18874368 | tf_op jit(solution)/shard_map/pallas_call | solution.py:130
  38.3 0.0 copy-done.1
  38.3 4.5 %shard_map.88 = (f32[24,4096]{1,0:T(8,128)S(1)}, f32[24,4096]{1,0:T(8,128)S(1)}, f32[24,4096]{1,0:T(8,128)S(1)}, f32[24,4096]{1,0:T(8,128)S(1)}) custom-call(bf16[24,6272]{1,0:T(8,128)(2,1)S(1)} %copy-done.1, bf16[24,6272]{1,0:T(8,128)(2,1)S(1)} %collective-permute-done.1.refs_1_, bf16[24,6272]{1,0:T(8,128)(2,1)S(1)} %collective-permute-done.2.refs_2_, ...), custom_call_target="tpu_custom_call" | custom-call | flops 2717908992 | bytes 9437184 | tf_op jit(solution)/shard_map/pallas_call | solution.py:209
  42.8 0.0 collective-permute-done.refs_0_
  42.8 0.0 copy-start.2
  42.8 0.0 copy-start.3
  42.9 0.0 copy-start.4
  42.9 0.0 collective-permute-done.5.refs_1_
  42.9 0.0 collective-permute-done.7.refs_3_
  42.9 4.3 %collective-permute-done.6.refs_2_ = bf16[24,6272]{1,0:T(8,128)(2,1)S(1)} collective-permute-done((bf16[24,6272]{1,0:T(8,128)(2,1)S(1)}, bf16[24,6272]{1,0:T(8,128)(2,1)S(1)}, u32[]{:S(2)}, u32[]{:S(2)}) %collective-permute-start.6) | collective-permute-done | bytes 301088 | tf_op jit(solution)/shard_map/ppermute | solution.py:263
  47.2 4.5 %shard_map.89 = (bf16[24,4096]{1,0:T(8,128)(2,1)S(1)}, bf16[24,4096]{1,0:T(8,128)(2,1)S(1)}, bf16[24,4096]{1,0:T(8,128)(2,1)S(1)}, bf16[24,4096]{1,0:T(8,128)(2,1)S(1)}) custom-call(bf16[24,6272]{1,0:T(8,128)(2,1)S(1)} %collective-permute-done.refs_0_, bf16[24,6272]{1,0:T(8,128)(2,1)S(1)} %collective-permute-done.5.refs_1_, ...), custom_call_target="tpu_custom_call" | custom-call | flops 2717908992 | bytes 9437184 | tf_op jit(solution)/shard_map/pallas_call | solution.py:209
  51.7 1.4 %collective-permute-start.10 = (bf16[24,4096]{1,0:T(8,128)(2,1)S(1)}, bf16[24,4096]{1,0:T(8,128)(2,1)S(1)}, u32[]{:S(2)}, u32[]{:S(2)}) collective-permute-start(bf16[24,4096]{1,0:T(8,128)(2,1)S(1)} %get-tuple-element.21), channel_id=1, source_target_pairs={{0,2},{1,3},{2,0},{3,1},{4,6},{5,7},{6,4},{7,5},{8,10},{9,11},{10,... | collective-permute-start | bytes 589832 | tf_op jit(solution)/shard_map/ppermute | solution.py:263
  53.2 0.7 collective-permute-start.13
  53.8 1.4 %collective-permute-start.9 = (bf16[24,4096]{1,0:T(8,128)(2,1)S(1)}, bf16[24,4096]{1,0:T(8,128)(2,1)S(1)}, u32[]{:S(2)}, u32[]{:S(2)}) collective-permute-start(bf16[24,4096]{1,0:T(8,128)(2,1)S(1)} %get-tuple-element.19), channel_id=1, source_target_pairs={{0,2},{1,3},{2,0},{3,1},{4,6},{5,7},{6,4},{7,5},{8,10},{9,11},{10,... | collective-permute-start | bytes 589832 | tf_op jit(solution)/shard_map/ppermute | solution.py:263
  55.2 0.7 collective-permute-start.8
  55.8 3.8 %collective-permute-done.10 = bf16[24,4096]{1,0:T(8,128)(2,1)S(1)} collective-permute-done((bf16[24,4096]{1,0:T(8,128)(2,1)S(1)}, bf16[24,4096]{1,0:T(8,128)(2,1)S(1)}, u32[]{:S(2)}, u32[]{:S(2)}) %collective-permute-start.10) | collective-permute-done | bytes 196640 | tf_op jit(solution)/shard_map/ppermute | solution.py:263
  59.6 0.1 add_convert_fusion.2
  59.7 3.5 %collective-permute-start.11 = (bf16[24,4096]{1,0:T(8,128)(2,1)S(1)}, bf16[24,4096]{1,0:T(8,128)(2,1)S(1)}, u32[]{:S(2)}, u32[]{:S(2)}) collective-permute-start(bf16[24,4096]{1,0:T(8,128)(2,1)S(1)} %add_convert_fusion.2), channel_id=1, source_target_pairs={{0,12},{1,13},{2,14},{3,15},{4,0},{5,1},{6,2},{7,3},{8,4},{9,5},{1... | collective-permute-start | bytes 589832 | tf_op jit(solution)/shard_map/ppermute | solution.py:263
  63.2 0.7 collective-permute-done.13
  63.8 0.1 add_convert_fusion
  63.9 0.1 collective-permute-start.14
  64.0 4.0 %collective-permute-done.9 = bf16[24,4096]{1,0:T(8,128)(2,1)S(1)} collective-permute-done((bf16[24,4096]{1,0:T(8,128)(2,1)S(1)}, bf16[24,4096]{1,0:T(8,128)(2,1)S(1)}, u32[]{:S(2)}, u32[]{:S(2)}) %collective-permute-start.9) | collective-permute-done | bytes 196640 | tf_op jit(solution)/shard_map/ppermute | solution.py:263
  68.0 0.5 collective-permute-done.11
  68.5 0.1 add_convert_fusion.1
  68.5 4.4 %collective-permute-start.12 = (bf16[24,4096]{1,0:T(8,128)(2,1)S(1)}, bf16[24,4096]{1,0:T(8,128)(2,1)S(1)}, u32[]{:S(2)}, u32[]{:S(2)}) collective-permute-start(bf16[24,4096]{1,0:T(8,128)(2,1)S(1)} %add_convert_fusion.1), channel_id=1, source_target_pairs={{0,12},{1,13},{2,14},{3,15},{4,0},{5,1},{6,2},{7,3},{8,4},{9,5},{1... | collective-permute-start | bytes 589832 | tf_op jit(solution)/shard_map/ppermute | solution.py:263
  73.0 0.0 collective-permute-done.8.there
  73.0 0.0 collective-permute-done.14.backward
  73.0 3.2 %collective-permute-done.12.forward = bf16[24,4096]{1,0:T(8,128)(2,1)S(1)} collective-permute-done((bf16[24,4096]{1,0:T(8,128)(2,1)S(1)}, bf16[24,4096]{1,0:T(8,128)(2,1)S(1)}, u32[]{:S(2)}, u32[]{:S(2)}) %collective-permute-start.12) | collective-permute-done | bytes 196640 | tf_op jit(solution)/shard_map/ppermute | solution.py:263
  76.1 0.0 copy-done.2
  76.1 0.0 copy-done.3
  76.2 0.0 copy-done.4
  76.2 1.0 %shard_map.90 = (f32[24,2048]{1,0:T(8,128)}, f32[1,24]{1,0:T(1,128)}) custom-call(bf16[24,2048]{1,0:T(8,128)(2,1)S(1)} %copy-done.3, f32[1,2048]{1,0:T(1,128)S(1)} %bitcast.3, s32[24,2048]{1,0:T(8,128)S(1)} %copy-done.2, f32[24,4096]{1,0:T(8,128)S(1)} %get-tuple-element.15.here, bf16[24,4096]{1,0:T(8,128)(2,1)S(1)} %collective-permute-done.8.there, ...), custom_call_target="tpu_custom_call" | custom-call | flops 1966080 | bytes 1277952 | tf_op jit(solution)/shard_map/pallas_call | solution.py:301
Async XLA Ops:
  0.6 32.4 %collective-permute-start.4 = (bf16[3,2048,384]{2,1,0:T(8,128)(2,1)}, bf16[3,2048,384]{2,1,0:T(8,128)(2,1)}, u32[]{:S(2)}, u32[]{:S(2)}) collective-permute-start(bf16[3,2048,384]{2,1,0:T(8,128)(2,1)} %own.1), channel_id=1, source_target_pairs={{0,1},{1,0},{2,3},{3,2},{4,5},{5,4},{6,7},{7,6},{8,9},{9,8},{10,11... | collective-permute-start | bytes 14155784 | tf_op jit(solution)/shard_map/ppermute | solution.py:263
  5.9 12.9 %collective-permute-start.1 = (bf16[24,6272]{1,0:T(8,128)(2,1)}, bf16[24,6272]{1,0:T(8,128)(2,1)S(1)}, u32[]{:S(2)}, u32[]{:S(2)}) collective-permute-start(bf16[24,6272]{1,0:T(8,128)(2,1)} %shard_map.86.refs_0_), channel_id=1, source_target_pairs={{0,4},{1,5},{2,6},{3,7},{4,8},{5,9},{6,10},{7,11},{8,12},{9,13},{1... | collective-permute-start | bytes 903176 | tf_op jit(solution)/shard_map/ppermute | solution.py:263
  8.6 15.9 %collective-permute-start.3 = (bf16[24,6272]{1,0:T(8,128)(2,1)}, bf16[24,6272]{1,0:T(8,128)(2,1)S(1)}, u32[]{:S(2)}, u32[]{:S(2)}) collective-permute-start(bf16[24,6272]{1,0:T(8,128)(2,1)} %shard_map.86.refs_0_), channel_id=1, source_target_pairs={{0,12},{1,13},{2,14},{3,15},{4,0},{5,1},{6,2},{7,3},{8,4},{9,5},{1... | collective-permute-start | bytes 903176 | tf_op jit(solution)/shard_map/ppermute | solution.py:263
  18.8 12.7 %collective-permute-start.2 = (bf16[24,6272]{1,0:T(8,128)(2,1)S(1)}, bf16[24,6272]{1,0:T(8,128)(2,1)S(1)}, u32[]{:S(2)}, u32[]{:S(2)}) collective-permute-start(bf16[24,6272]{1,0:T(8,128)(2,1)S(1)} %collective-permute-done.1.refs_1_), channel_id=1, source_target_pairs={{0,4},{1,5},{2,6},{3,7},{4,8},{5,9},{6,10},{7,11},{8,12},{9,13},{1... | collective-permute-start | bytes 903176 | tf_op jit(solution)/shard_map/ppermute | solution.py:263
  18.9 24.0 %collective-permute-start = (bf16[24,6272]{1,0:T(8,128)(2,1)}, bf16[24,6272]{1,0:T(8,128)(2,1)S(1)}, u32[]{:S(2)}, u32[]{:S(2)}) collective-permute-start(bf16[24,6272]{1,0:T(8,128)(2,1)} %shard_map.86.refs_0_), channel_id=1, source_target_pairs={{0,2},{1,3},{2,0},{3,1},{4,6},{5,7},{6,4},{7,5},{8,10},{9,11},{10,... | collective-permute-start | bytes 903176 | tf_op jit(solution)/shard_map/ppermute | solution.py:263
  20.5 22.4 %collective-permute-start.5 = (bf16[24,6272]{1,0:T(8,128)(2,1)S(1)}, bf16[24,6272]{1,0:T(8,128)(2,1)S(1)}, u32[]{:S(2)}, u32[]{:S(2)}) collective-permute-start(bf16[24,6272]{1,0:T(8,128)(2,1)S(1)} %collective-permute-done.1.refs_1_), channel_id=1, source_target_pairs={{0,2},{1,3},{2,0},{3,1},{4,6},{5,7},{6,4},{7,5},{8,10},{9,11},{10,... | collective-permute-start | bytes 903176 | tf_op jit(solution)/shard_map/ppermute | solution.py:263
  24.5 18.4 %collective-permute-start.7 = (bf16[24,6272]{1,0:T(8,128)(2,1)S(1)}, bf16[24,6272]{1,0:T(8,128)(2,1)S(1)}, u32[]{:S(2)}, u32[]{:S(2)}) collective-permute-start(bf16[24,6272]{1,0:T(8,128)(2,1)S(1)} %collective-permute-done.3.refs_3_), channel_id=1, source_target_pairs={{0,2},{1,3},{2,0},{3,1},{4,6},{5,7},{6,4},{7,5},{8,10},{9,11},{10,... | collective-permute-start | bytes 903176 | tf_op jit(solution)/shard_map/ppermute | solution.py:263
  31.6 15.6 %collective-permute-start.6 = (bf16[24,6272]{1,0:T(8,128)(2,1)S(1)}, bf16[24,6272]{1,0:T(8,128)(2,1)S(1)}, u32[]{:S(2)}, u32[]{:S(2)}) collective-permute-start(bf16[24,6272]{1,0:T(8,128)(2,1)S(1)} %collective-permute-done.2.refs_2_), channel_id=1, source_target_pairs={{0,2},{1,3},{2,0},{3,1},{4,6},{5,7},{6,4},{7,5},{8,10},{9,11},{10,... | collective-permute-start | bytes 903176 | tf_op jit(solution)/shard_map/ppermute | solution.py:263
  33.0 2.3 %copy-start = (bf16[3,2048,384]{2,1,0:T(8,128)(2,1)S(1)}, bf16[3,2048,384]{2,1,0:T(8,128)(2,1)}, u32[]{:S(2)}) copy-start(bf16[3,2048,384]{2,1,0:T(8,128)(2,1)} %own.1) | copy-start | bytes 14155780
  35.4 2.9 %copy-start.1 = (bf16[24,6272]{1,0:T(8,128)(2,1)S(1)}, bf16[24,6272]{1,0:T(8,128)(2,1)}, u32[]{:S(2)}) copy-start(bf16[24,6272]{1,0:T(8,128)(2,1)} %shard_map.86.refs_0_) | copy-start | bytes 903172
  42.8 33.3 %copy-start.2 = (s32[24,2048]{1,0:T(8,128)S(1)}, s32[24,2048]{1,0:T(8,128)}, u32[]{:S(2)}) copy-start(s32[24,2048]{1,0:T(8,128)} %signs.1) | copy-start | bytes 589828
  42.8 33.3 %copy-start.3 = (bf16[24,2048]{1,0:T(8,128)(2,1)S(1)}, bf16[24,2048]{1,0:T(8,128)(2,1)}, u32[]{:S(2)}) copy-start(bf16[24,2048]{1,0:T(8,128)(2,1)} %tokens.1) | copy-start | bytes 294916
  42.9 33.3 %copy-start.4 = (f32[2048]{0:T(1024)S(1)}, f32[2048]{0:T(1024)}, u32[]{:S(2)}) copy-start(f32[2048]{0:T(1024)} %param.8) | copy-start | bytes 24580
  51.7 7.9 %collective-permute-start.10 = (bf16[24,4096]{1,0:T(8,128)(2,1)S(1)}, bf16[24,4096]{1,0:T(8,128)(2,1)S(1)}, u32[]{:S(2)}, u32[]{:S(2)}) collective-permute-start(bf16[24,4096]{1,0:T(8,128)(2,1)S(1)} %get-tuple-element.21), channel_id=1, source_target_pairs={{0,2},{1,3},{2,0},{3,1},{4,6},{5,7},{6,4},{7,5},{8,10},{9,11},{10,... | collective-permute-start | bytes 589832 | tf_op jit(solution)/shard_map/ppermute | solution.py:263
  53.2 10.7 %collective-permute-start.13 = (bf16[24,4096]{1,0:T(8,128)(2,1)S(1)}, bf16[24,4096]{1,0:T(8,128)(2,1)S(1)}, u32[]{:S(2)}, u32[]{:S(2)}) collective-permute-start(bf16[24,4096]{1,0:T(8,128)(2,1)S(1)} %get-tuple-element.23), channel_id=1, source_target_pairs={{0,2},{1,3},{2,0},{3,1},{4,6},{5,7},{6,4},{7,5},{8,10},{9,11},{10,... | collective-permute-start | bytes 589832 | tf_op jit(solution)/shard_map/ppermute | solution.py:263
  53.8 14.1 %collective-permute-start.9 = (bf16[24,4096]{1,0:T(8,128)(2,1)S(1)}, bf16[24,4096]{1,0:T(8,128)(2,1)S(1)}, u32[]{:S(2)}, u32[]{:S(2)}) collective-permute-start(bf16[24,4096]{1,0:T(8,128)(2,1)S(1)} %get-tuple-element.19), channel_id=1, source_target_pairs={{0,2},{1,3},{2,0},{3,1},{4,6},{5,7},{6,4},{7,5},{8,10},{9,11},{10,... | collective-permute-start | bytes 589832 | tf_op jit(solution)/shard_map/ppermute | solution.py:263
  55.2 17.8 %collective-permute-start.8 = (bf16[24,4096]{1,0:T(8,128)(2,1)S(1)}, bf16[24,4096]{1,0:T(8,128)(2,1)S(1)}, u32[]{:S(2)}, u32[]{:S(2)}) collective-permute-start(bf16[24,4096]{1,0:T(8,128)(2,1)S(1)} %get-tuple-element.17), channel_id=1, source_target_pairs={{0,2},{1,3},{2,0},{3,1},{4,6},{5,7},{6,4},{7,5},{8,10},{9,11},{10,... | collective-permute-start | bytes 589832 | tf_op jit(solution)/shard_map/ppermute | solution.py:263
  59.7 8.8 %collective-permute-start.11 = (bf16[24,4096]{1,0:T(8,128)(2,1)S(1)}, bf16[24,4096]{1,0:T(8,128)(2,1)S(1)}, u32[]{:S(2)}, u32[]{:S(2)}) collective-permute-start(bf16[24,4096]{1,0:T(8,128)(2,1)S(1)} %add_convert_fusion.2), channel_id=1, source_target_pairs={{0,12},{1,13},{2,14},{3,15},{4,0},{5,1},{6,2},{7,3},{8,4},{9,5},{1... | collective-permute-start | bytes 589832 | tf_op jit(solution)/shard_map/ppermute | solution.py:263
  63.9 9.1 %collective-permute-start.14 = (bf16[24,4096]{1,0:T(8,128)(2,1)S(1)}, bf16[24,4096]{1,0:T(8,128)(2,1)S(1)}, u32[]{:S(2)}, u32[]{:S(2)}) collective-permute-start(bf16[24,4096]{1,0:T(8,128)(2,1)S(1)} %add_convert_fusion), channel_id=1, source_target_pairs={{0,4},{1,5},{2,6},{3,7},{4,8},{5,9},{6,10},{7,11},{8,12},{9,13},{1... | collective-permute-start | bytes 589832 | tf_op jit(solution)/shard_map/ppermute | solution.py:263
  68.5 7.6 %collective-permute-start.12 = (bf16[24,4096]{1,0:T(8,128)(2,1)S(1)}, bf16[24,4096]{1,0:T(8,128)(2,1)S(1)}, u32[]{:S(2)}, u32[]{:S(2)}) collective-permute-start(bf16[24,4096]{1,0:T(8,128)(2,1)S(1)} %add_convert_fusion.1), channel_id=1, source_target_pairs={{0,12},{1,13},{2,14},{3,15},{4,0},{5,1},{6,2},{7,3},{8,4},{9,5},{1... | collective-permute-start | bytes 589832 | tf_op jit(solution)/shard_map/ppermute | solution.py:263

commit v5 on v4

--- a/solution.py
+++ b/solution.py
@@ -9,7 +9,6 @@
 
 EPS = 1e-06
 VMEM = 24 * 1024 * 1024
-VMEM_ALONE = 60 * 1024 * 1024
 
 
 def expert_terms(weights, rows, rows_t, cotan):
@@ -79,23 +78,43 @@
     tangent = gain[...] * (scale * probe - scale**3 * xf * along)
     pack[:, width : 2 * width] = tangent.astype(jnp.bfloat16)
     pack[:, 2 * width : 3 * width] = cotangent[...]
-    lane = lax.broadcasted_iota(jnp.int32, (tokens.shape[0], pack.shape[1] - 3 * width), 1)
+    tok_dev, lanes = (tokens.shape[0], pack.shape[1] - 3 * width)
+    lane = lax.broadcasted_iota(jnp.int32, (lanes, tok_dev), 0)
     expert = lax.rem(lane, expert_count)
     gate = jnp.zeros(lane.shape, jnp.float32)
     for group in range(routes.shape[0]):
-        for slot in range(routes.shape[2]):
-            named = routes[group, :, slot : slot + 1] == expert
-            gate = gate + jnp.where(named, gates[group, :, slot : slot + 1], 0.0)
+        for slot in range(routes.shape[1]):
+            named = routes[group, slot : slot + 1, :] == expert
+            gate = gate + jnp.where(named, gates[group, slot : slot + 1, :], 0.0)
     high = gate.astype(jnp.bfloat16).astype(jnp.float32)
     tail = jnp.where(lane < expert_count, high, gate - high)
-    tail = jnp.where(lane < 2 * expert_count, tail, 0.0)
-    pack[:, 3 * width :] = tail.astype(jnp.bfloat16)
+    tail = jnp.where(lane < 2 * expert_count, tail, 0.0).astype(jnp.bfloat16)
+    turned = lax.dot_general(
+        identity(tok_dev).astype(jnp.bfloat16),
+        tail,
+        (((1,), (1,)), ((), ())),
+        preferred_element_type=jnp.float32,
+    )
+    pack[:, 3 * width :] = turned.astype(jnp.bfloat16)
+
+
+def identity(size):
+    rows = lax.broadcasted_iota(jnp.int32, (size, size), 0)
+    return (rows == lax.broadcasted_iota(jnp.int32, (size, size), 1)).astype(jnp.float32)
 
 
 def packed(tokens, norm_gain, probe_signs, cotangent, routes, gates, expert_count):
     tok_dev, width = tokens.shape
     tail = -(-2 * expert_count // 128) * 128
-    operands = (tokens, norm_gain.reshape(1, width), probe_signs, cotangent, routes, gates)
+    token_minor = (0, 2, 1)
+    operands = (
+        tokens,
+        norm_gain.reshape(1, width),
+        probe_signs,
+        cotangent,
+        jnp.transpose(routes, token_minor),
+        jnp.transpose(gates, token_minor),
+    )
     return pl.pallas_call(
         functools.partial(pack_kernel, expert_count),
         out_shape=jax.ShapeDtypeStruct((tok_dev, 3 * width + tail), jnp.bfloat16),
@@ -103,11 +122,11 @@
         out_specs=pl.BlockSpec(memory_space=pltpu.VMEM),
         scratch_shapes=[pltpu.VMEM(array.shape, array.dtype) for array in operands]
         + [pltpu.SemaphoreType.DMA((6,))],
-        compiler_params=pltpu.CompilerParams(vmem_limit_bytes=VMEM_ALONE),
+        compiler_params=pltpu.CompilerParams(vmem_limit_bytes=VMEM),
         cost_estimate=pl.CostEstimate(
             flops=20 * tok_dev * width, bytes_accessed=14 * tok_dev * width, transcendentals=0
         ),
-    )(*operands)
+    )(*(pltpu.with_memory_space_constraint(array, pltpu.HBM) for array in operands))
 
 
 def join_kernel(own, other, held, sems):
@@ -129,7 +148,7 @@
     parts, width, half = own.shape
     return pl.pallas_call(
         join_kernel,
-        out_shape=jax.ShapeDtypeStruct((parts, width, 2 * half), own.dtype),
+        out_shape=pltpu.VMEM((parts, width, 2 * half), own.dtype),
         in_specs=[pl.BlockSpec(memory_space=pl.ANY)] * 2,
         out_specs=pl.BlockSpec(memory_space=pltpu.VMEM),
         scratch_shapes=[pltpu.SemaphoreType.DMA((2, parts))],
@@ -137,7 +156,7 @@
         cost_estimate=pl.CostEstimate(
             flops=0, bytes_accessed=8 * parts * width * half, transcendentals=0
         ),
-    )(own, other)
+    )(pltpu.with_memory_space_constraint(own, pltpu.HBM), other)
 
 
 def expert_kernel(count, expert_count, *refs):
@@ -200,15 +219,15 @@
         outs[n][:, width:] = (acc[later] * gate_row[part]).astype(outs[n].dtype)
 
 
-def experts(packs, kind, weights, expert_count):
+def experts(packs, kinds, held, expert_count):
     count = len(packs)
     tok_dev = packs[0].shape[0]
-    _, width, hidden = weights.shape
+    _, width, hidden = held.shape
     rows = count * tok_dev
     whole = pl.BlockSpec(memory_space=pltpu.VMEM)
     return pl.pallas_call(
         functools.partial(expert_kernel, count, expert_count),
-        out_shape=[jax.ShapeDtypeStruct((tok_dev, 2 * width), kind)] * count,
+        out_shape=[jax.ShapeDtypeStruct((tok_dev, 2 * width), kind) for kind in kinds],
         in_specs=[whole] * (count + 1),
         out_specs=[whole] * count,
         scratch_shapes=[
@@ -222,7 +241,7 @@
             bytes_accessed=6 * width * hidden,
             transcendentals=rows * hidden,
         ),
-    )(*packs, weights)
+    )(*packs, pltpu.with_memory_space_constraint(held, pltpu.VMEM))
 
 
 def finish_kernel(tokens, gain, signs, here, there, forward, backward, hvp, quad):
@@ -249,10 +268,7 @@
     hvp[...] = whole
     column = jnp.mean(probe * whole, axis=1, keepdims=True)
     tok_dev = column.shape[0]
-    own = lax.broadcasted_iota(jnp.int32, (tok_dev, tok_dev), 0) == lax.broadcasted_iota(
-        jnp.int32, (tok_dev, tok_dev), 1
-    )
-    quad[...] = jnp.sum(jnp.where(own, column, 0.0), axis=0, keepdims=True)
+    quad[...] = jnp.sum(identity(tok_dev) * column, axis=0, keepdims=True)
 
 
 def moved(rows, turns, flip_x=False, flip_core=False):
@@ -267,37 +283,35 @@
     tok_dev, width = tokens.shape
     n_exp = lax.axis_size("expert")
     expert_count = n_exp // 2
-    turns = n_exp // 4
-    ahead, behind = turns // 2, (turns - 1) // 2
     pack = packed(tokens, norm_gain, probe_signs, cotangent, routes, gates, expert_count)
+    held = joined(weights, moved(weights, 0, flip_core=True))
     same, across = {0: pack}, {}
+    same[1] = moved(pack, 1)
     across[0] = moved(pack, 0, flip_x=True)
-    weights_other = moved(weights, 0, flip_core=True)
-    for k in range(1, ahead + 1):
-        same[k] = moved(same[k - 1], 1)
-        across[k] = moved(same[k], 0, flip_x=True)
-    for k in range(turns - 1, turns - 1 - behind, -1):
-        same[k] = moved(same[(k + 1) % turns], -1)
-        across[k] = moved(same[k], 0, flip_x=True)
-    order = range(turns)
-    held = joined(weights, weights_other)
-    results = experts([same[k] for k in order], jnp.float32, held, expert_count)
-    here = dict(zip(order, results))
-    packs = [across[k] for k in order]
-    packs[0], here[0] = lax.optimization_barrier((packs[0], here[0]))
-    results = experts(packs, jnp.bfloat16, held, expert_count)
-    there = {k: moved(rows, 0, flip_x=True) for k, rows in zip(order, results)}
-
-    def passed(ks, step):
-        rows = None
-        for k in ks:
-            part = here[k] + there[k].astype(jnp.float32)
-            part = part if rows is None else part + rows.astype(jnp.float32)
-            rows = moved(part.astype(jnp.bfloat16), step)
-        return rows
-
-    forward = passed(range(ahead, 0, -1), -1)
-    backward = passed(range(turns - behind, turns), 1)
+    same[1] = lax.optimization_barrier((same[1], across[0], held))[0]
+    same[2] = moved(same[1], 1)
+    across[1] = moved(same[1], 0, flip_x=True)
+    same[3] = moved(lax.optimization_barrier((pack, same[1]))[0], -1)
+    across[2] = moved(same[2], 0, flip_x=True)
+    across[3] = moved(same[3], 0, flip_x=True)
+    wide, sent = (jnp.float32, jnp.bfloat16)
+    here, there = {}, {}
+    here[0], here[1], here[2], here[3], there[0], there[1], there[2] = experts(
+        [same[0], same[1], same[2], same[3], across[0], across[1], across[2]],
+        [wide, wide, wide, sent, wide, sent, sent],
+        held,
+        expert_count,
+    )
+    last = lax.optimization_barrier((across[3], here[1]))[0]
+    (there[3],) = experts([last], [sent], held, expert_count)
+
+    def total(*parts):
+        return sum(part.astype(jnp.float32) for part in parts).astype(jnp.bfloat16)
+
+    backward = moved(here[3], 1)
+    forward = moved(total(here[2], moved(there[2], 0, flip_x=True)), -1)
+    forward = moved(total(here[1], moved(there[1], 0, flip_x=True), forward), -1)
+    beside = moved(total(there[0], moved(there[3], 1)), 0, flip_x=True)
     hvp, quad = pl.pallas_call(
         finish_kernel,
         out_shape=[
@@ -308,7 +322,7 @@
         cost_estimate=pl.CostEstimate(
             flops=40 * tok_dev * width, bytes_accessed=26 * tok_dev * width, transcendentals=0
         ),
-    )(tokens, norm_gain.reshape(1, width), probe_signs, here[0], there[0], forward, backward)
+    )(tokens, norm_gain.reshape(1, width), probe_signs, here[0], beside, forward, backward)
     return (hvp, quad.reshape(tok_dev))
 
 
@@ -374,7 +388,8 @@
 
 def local(tokens, norm_gain, probe_signs, cotangent, routes, gates, expert_weights):
     cap = capacity(tokens.shape[0], routes.shape[2], lax.axis_size("expert") // 2)
-    if lax.axis_size("node") == 1 and routes.shape[0] * cap >= tokens.shape[0]:
+    layout = (lax.axis_size("expert"), lax.axis_size("node"))
+    if layout == (16, 1) and routes.shape[0] * cap >= tokens.shape[0]:
         return dense_local(
             tokens, norm_gain, probe_signs, cotangent, routes, gates, expert_weights
         )

time: 77.4 us -> 69.1 us (0.89)
  local copies, waits for them, and re-layouts: 5.1 us -> 0.02 us
  starting transfers between devices: 22.4 us -> 19.8 us
  waiting for transfers between devices: 33.8 us -> 32.7 us
    unnamed x12 -> x6, local copies, waits for them, and re-layouts: 5.1 us -> 0.02 us
    ppermute x15, starting transfers between devices: 22.4 us -> 19.8 us  [moved(): return lax.ppermute(rows, 'expert', pairs)]
    pallas_call x2, Pallas kernels: 9.08 us -> 10.9 us  [experts(): pl.pallas_call(functools.partial(expert_kernel, count, expert_count), out...]
    ppermute x15, waiting for transfers between devices: 33.8 us -> 32.7 us  [moved(): return lax.ppermute(rows, 'expert', pairs)]
  transfers between devices with their start and end apart: 15 -> 15, of which waited for: 9 -> 9; matrix products, arithmetic and copies ran while one was open for 4% -> 0% of each run, Pallas kernels for 12% -> 21%
where the time goes in v5:
time: 69.1 us; the launch traced here: 69 us
  waiting for transfers between devices  32.7 us (47%)
  starting transfers between devices  19.8 us (29%)
  Pallas kernels  15.6 us (23%)
  between operations  0.73 us (1%)
    ppermute x15, waiting for transfers between devices, moved(): return lax.ppermute(rows, 'expert', pairs)  32.7 us
    ppermute x15, starting transfers between devices, moved(): return lax.ppermute(rows, 'expert', pairs)  19.8 us
    pallas_call x2, Pallas kernels, experts(): pl.pallas_call(functools.partial(expert_kernel, count, expert_count), out...  10.9 us
    pallas_call x1, Pallas kernels, joined(): pl.pallas_call(join_kernel, out_shape=pltpu.VMEM((parts, width, 2 * half)...  2.41 us
  transfers between devices with their start and end apart: 15, of which 9 were waited for; matrix products, arithmetic and copies ran while one was open for 0% of the time, Pallas kernels for 21%

profile of v5, /device:TPU:0, one launch (start us, length us, event | category | flops | bytes accessed | tf_op | source)
XLA Modules:
  0.0 69.0 jit_solution(5214437140988973737)
XLA Ops:
  0.6 0.5 collective-permute-start.2
  1.1 1.3 %shard_map.86.refs_0_ = bf16[24,6272]{1,0:T(8,128)(2,1)S(1)} custom-call(bf16[24,2048]{1,0:T(8,128)(2,1)} %tokens.1, f32[1,2048]{1,0:T(1,128)} %bitcast.4, s32[24,2048]{1,0:T(8,128)} %signs.1, bf16[24,2048]{1,0:T(8,128)(2,1)} %refs_3_.1, s32[2,4,24]{2,1,0:T(4,128)} %bitcast.6, f32[2,4,24]{2,1,0:T(4,128)} %bitcast.7), custom_call_target="tpu_custom_call" | custom-call | flops 983040 | bytes 688128 | tf_op jit(solution)/shard_map/pallas_call | solution.py:118
  2.4 2.6 %collective-permute-start.1 = (bf16[24,6272]{1,0:T(8,128)(2,1)S(1)}, bf16[24,6272]{1,0:T(8,128)(2,1)S(1)}, u32[]{:S(2)}, u32[]{:S(2)}) collective-permute-start(bf16[24,6272]{1,0:T(8,128)(2,1)S(1)} %shard_map.86.refs_0_), channel_id=1, source_target_pairs={{0,2},{1,3},{2,0},{3,1},{4,6},{5,7},{6,4},{7,5},{8,10},{9,11},{10,... | collective-permute-start | bytes 903176 | tf_op jit(solution)/shard_map/ppermute | solution.py:279
  5.0 1.6 %collective-permute-start = (bf16[24,6272]{1,0:T(8,128)(2,1)S(1)}, bf16[24,6272]{1,0:T(8,128)(2,1)S(1)}, u32[]{:S(2)}, u32[]{:S(2)}) collective-permute-start(bf16[24,6272]{1,0:T(8,128)(2,1)S(1)} %shard_map.86.refs_0_), channel_id=1, source_target_pairs={{0,4},{1,5},{2,6},{3,7},{4,8},{5,9},{6,10},{7,11},{8,12},{9,13},{1... | collective-permute-start | bytes 903176 | tf_op jit(solution)/shard_map/ppermute | solution.py:279
  6.6 2.3 %collective-permute-done.2.other = bf16[3,2048,384]{2,1,0:T(8,128)(2,1)S(1)} collective-permute-done((bf16[3,2048,384]{2,1,0:T(8,128)(2,1)}, bf16[3,2048,384]{2,1,0:T(8,128)(2,1)S(1)}, u32[]{:S(2)}, u32[]{:S(2)}) %collective-permute-start.2) | collective-permute-done | bytes 4718624 | tf_op jit(solution)/shard_map/ppermute | solution.py:279
  8.9 2.4 %shard_map.87.refs_7_.refs_1_ = bf16[3,2048,768]{2,1,0:T(8,128)(2,1)S(1)} custom-call(bf16[3,2048,384]{2,1,0:T(8,128)(2,1)} %own.1, bf16[3,2048,384]{2,1,0:T(8,128)(2,1)S(1)} %collective-permute-done.2.other), custom_call_target="tpu_custom_call" | custom-call | bytes 18874368 | tf_op jit(solution)/shard_map/pallas_call | solution.py:149
  11.3 1.5 %collective-permute-done.1.refs_4_ = bf16[24,6272]{1,0:T(8,128)(2,1)S(1)} collective-permute-done((bf16[24,6272]{1,0:T(8,128)(2,1)S(1)}, bf16[24,6272]{1,0:T(8,128)(2,1)S(1)}, u32[]{:S(2)}, u32[]{:S(2)}) %collective-permute-start.1) | collective-permute-done | bytes 301088 | tf_op jit(solution)/shard_map/ppermute | solution.py:279
  12.8 3.3 %collective-permute-done.refs_1_ = bf16[24,6272]{1,0:T(8,128)(2,1)S(1)} collective-permute-done((bf16[24,6272]{1,0:T(8,128)(2,1)S(1)}, bf16[24,6272]{1,0:T(8,128)(2,1)S(1)}, u32[]{:S(2)}, u32[]{:S(2)}) %collective-permute-start) | collective-permute-done | bytes 301088 | tf_op jit(solution)/shard_map/ppermute | solution.py:279
  16.1 0.0 collective-permute-start.3
  16.1 3.8 %collective-permute-start.4 = (bf16[24,6272]{1,0:T(8,128)(2,1)S(1)}, bf16[24,6272]{1,0:T(8,128)(2,1)S(1)}, u32[]{:S(2)}, u32[]{:S(2)}) collective-permute-start(bf16[24,6272]{1,0:T(8,128)(2,1)S(1)} %shard_map.86.refs_0_), channel_id=1, source_target_pairs={{0,12},{1,13},{2,14},{3,15},{4,0},{5,1},{6,2},{7,3},{8,4},{9,5},{1... | collective-permute-start | bytes 903176 | tf_op jit(solution)/shard_map/ppermute | solution.py:279
  19.9 0.5 collective-permute-start.5
  20.5 7.5 %collective-permute-done.3.refs_2_ = bf16[24,6272]{1,0:T(8,128)(2,1)S(1)} collective-permute-done((bf16[24,6272]{1,0:T(8,128)(2,1)S(1)}, bf16[24,6272]{1,0:T(8,128)(2,1)S(1)}, u32[]{:S(2)}, u32[]{:S(2)}) %collective-permute-start.3) | collective-permute-done | bytes 301088 | tf_op jit(solution)/shard_map/ppermute | solution.py:279
  28.0 0.5 collective-permute-start.6
  28.5 2.6 %collective-permute-done.4.refs_3_ = bf16[24,6272]{1,0:T(8,128)(2,1)S(1)} collective-permute-done((bf16[24,6272]{1,0:T(8,128)(2,1)S(1)}, bf16[24,6272]{1,0:T(8,128)(2,1)S(1)}, u32[]{:S(2)}, u32[]{:S(2)}) %collective-permute-start.4) | collective-permute-done | bytes 301088 | tf_op jit(solution)/shard_map/ppermute | solution.py:279
  31.1 0.8 %collective-permute-start.7 = (bf16[24,6272]{1,0:T(8,128)(2,1)S(1)}, bf16[24,6272]{1,0:T(8,128)(2,1)S(1)}, u32[]{:S(2)}, u32[]{:S(2)}) collective-permute-start(bf16[24,6272]{1,0:T(8,128)(2,1)S(1)} %collective-permute-done.4.refs_3_), channel_id=1, source_target_pairs={{0,2},{1,3},{2,0},{3,1},{4,6},{5,7},{6,4},{7,5},{8,10},{9,11},{10,... | collective-permute-start | bytes 903176 | tf_op jit(solution)/shard_map/ppermute | solution.py:279
  31.9 0.0 collective-permute-done.5.refs_5_
  31.9 5.6 %collective-permute-done.6.refs_6_ = bf16[24,6272]{1,0:T(8,128)(2,1)S(1)} collective-permute-done((bf16[24,6272]{1,0:T(8,128)(2,1)S(1)}, bf16[24,6272]{1,0:T(8,128)(2,1)S(1)}, u32[]{:S(2)}, u32[]{:S(2)}) %collective-permute-start.6) | collective-permute-done | bytes 301088 | tf_op jit(solution)/shard_map/ppermute | solution.py:279
  37.4 6.9 %shard_map.88 = (f32[24,4096]{1,0:T(8,128)S(1)}, f32[24,4096]{1,0:T(8,128)S(1)}, f32[24,4096]{1,0:T(8,128)S(1)}, bf16[24,4096]{1,0:T(8,128)(2,1)S(1)}, f32[24,40...) custom-call(bf16[24,6272]{1,0:T(8,128)(2,1)S(1)} %shard_map.86.refs_0_, ...), custom_call_target="tpu_custom_call" | custom-call | flops 4756340736 | bytes 9437184 | tf_op jit(solution)/shard_map/pallas_call | solution.py:228
  44.3 0.1 collective-permute-start.11
  44.4 0.0 collective-permute-done.7.refs_0_
  44.4 0.0 copy-start
  44.4 0.0 copy-start.1
  44.4 0.0 copy-start.2
  44.4 4.0 %shard_map.89 = bf16[24,4096]{1,0:T(8,128)(2,1)S(1)} custom-call(bf16[24,6272]{1,0:T(8,128)(2,1)S(1)} %collective-permute-done.7.refs_0_, bf16[3,2048,768]{2,1,0:T(8,128)(2,1)S(1)} %shard_map.87.refs_7_.refs_1_), custom_call_target="tpu_custom_call" | custom-call | flops 679477248 | bytes 9437184 | tf_op jit(solution)/shard_map/pallas_call | solution.py:228
  48.5 0.1 collective-permute-start.8
  48.5 2.0 %collective-permute-start.10 = (bf16[24,4096]{1,0:T(8,128)(2,1)S(1)}, bf16[24,4096]{1,0:T(8,128)(2,1)S(1)}, u32[]{:S(2)}, u32[]{:S(2)}) collective-permute-start(bf16[24,4096]{1,0:T(8,128)(2,1)S(1)} %get-tuple-element.20), channel_id=1, source_target_pairs={{0,2},{1,3},{2,0},{3,1},{4,6},{5,7},{6,4},{7,5},{8,10},{9,11},{10,... | collective-permute-start | bytes 589832 | tf_op jit(solution)/shard_map/ppermute | solution.py:279
  50.6 0.0 collective-permute-start.14
  50.6 0.0 collective-permute-done.11
  50.6 0.1 add_convert_fusion.1
  50.6 3.9 %collective-permute-start.12 = (bf16[24,4096]{1,0:T(8,128)(2,1)S(1)}, bf16[24,4096]{1,0:T(8,128)(2,1)S(1)}, u32[]{:S(2)}, u32[]{:S(2)}) collective-permute-start(bf16[24,4096]{1,0:T(8,128)(2,1)S(1)} %add_convert_fusion.1), channel_id=1, source_target_pairs={{0,12},{1,13},{2,14},{3,15},{4,0},{5,1},{6,2},{7,3},{8,4},{9,5},{1... | collective-permute-start | bytes 589832 | tf_op jit(solution)/shard_map/ppermute | solution.py:279
  54.5 1.6 %collective-permute-done.8 = bf16[24,4096]{1,0:T(8,128)(2,1)S(1)} collective-permute-done((bf16[24,4096]{1,0:T(8,128)(2,1)S(1)}, bf16[24,4096]{1,0:T(8,128)(2,1)S(1)}, u32[]{:S(2)}, u32[]{:S(2)}) %collective-permute-start.8) | collective-permute-done | bytes 196640 | tf_op jit(solution)/shard_map/ppermute | solution.py:279
  56.1 2.3 %collective-permute-start.9 = (bf16[24,4096]{1,0:T(8,128)(2,1)S(1)}, bf16[24,4096]{1,0:T(8,128)(2,1)S(1)}, u32[]{:S(2)}, u32[]{:S(2)}) collective-permute-start(bf16[24,4096]{1,0:T(8,128)(2,1)S(1)} %add_convert_fusion.2), channel_id=1, source_target_pairs={{0,2},{1,3},{2,0},{3,1},{4,6},{5,7},{6,4},{7,5},{8,10},{9,11},{10,... | collective-permute-start | bytes 589832 | tf_op jit(solution)/shard_map/ppermute | solution.py:279
  58.4 0.0 collective-permute-done.10
  58.4 3.8 %collective-permute-done.12 = bf16[24,4096]{1,0:T(8,128)(2,1)S(1)} collective-permute-done((bf16[24,4096]{1,0:T(8,128)(2,1)S(1)}, bf16[24,4096]{1,0:T(8,128)(2,1)S(1)}, u32[]{:S(2)}, u32[]{:S(2)}) %collective-permute-start.12) | collective-permute-done | bytes 196640 | tf_op jit(solution)/shard_map/ppermute | solution.py:279
  62.2 0.1 add_convert_fusion
  62.3 1.2 %collective-permute-start.13 = (bf16[24,4096]{1,0:T(8,128)(2,1)S(1)}, bf16[24,4096]{1,0:T(8,128)(2,1)S(1)}, u32[]{:S(2)}, u32[]{:S(2)}) collective-permute-start(bf16[24,4096]{1,0:T(8,128)(2,1)S(1)} %add_convert_fusion), channel_id=1, source_target_pairs={{0,12},{1,13},{2,14},{3,15},{4,0},{5,1},{6,2},{7,3},{8,4},{9,5},{1... | collective-permute-start | bytes 589832 | tf_op jit(solution)/shard_map/ppermute | solution.py:279
  63.5 0.0 collective-permute-done.14.backward
  63.5 0.0 collective-permute-done.9.there
  63.5 4.5 %collective-permute-done.13.forward = bf16[24,4096]{1,0:T(8,128)(2,1)S(1)} collective-permute-done((bf16[24,4096]{1,0:T(8,128)(2,1)S(1)}, bf16[24,4096]{1,0:T(8,128)(2,1)S(1)}, u32[]{:S(2)}, u32[]{:S(2)}) %collective-permute-start.13) | collective-permute-done | bytes 196640 | tf_op jit(solution)/shard_map/ppermute | solution.py:279
  68.0 0.0 copy-done
  68.0 0.0 copy-done.1
  68.0 0.0 copy-done.2
  68.0 1.0 %shard_map.90 = (f32[24,2048]{1,0:T(8,128)}, f32[1,24]{1,0:T(1,128)}) custom-call(bf16[24,2048]{1,0:T(8,128)(2,1)S(1)} %copy-done.1, f32[1,2048]{1,0:T(1,128)S(1)} %bitcast.5, s32[24,2048]{1,0:T(8,128)S(1)} %copy-done, f32[24,4096]{1,0:T(8,128)S(1)} %get-tuple-element.16.here, bf16[24,4096]{1,0:T(8,128)(2,1)S(1)} %collective-permute-done.9.there, ...), custom_call_target="tpu_custom_call" | custom-call | flops 1966080 | bytes 1277952 | tf_op jit(solution)/shard_map/pallas_call | solution.py:315
  (1 shorter events, 0.0 us)
Async XLA Ops:
  0.6 8.3 %collective-permute-start.2 = (bf16[3,2048,384]{2,1,0:T(8,128)(2,1)}, bf16[3,2048,384]{2,1,0:T(8,128)(2,1)S(1)}, u32[]{:S(2)}, u32[]{:S(2)}) collective-permute-start(bf16[3,2048,384]{2,1,0:T(8,128)(2,1)} %own.1), channel_id=1, source_target_pairs={{0,1},{1,0},{2,3},{3,2},{4,5},{5,4},{6,7},{7,6},{8,9},{9,8},{10,11... | collective-permute-start | bytes 14155784 | tf_op jit(solution)/shard_map/ppermute | solution.py:279
  2.4 10.4 %collective-permute-start.1 = (bf16[24,6272]{1,0:T(8,128)(2,1)S(1)}, bf16[24,6272]{1,0:T(8,128)(2,1)S(1)}, u32[]{:S(2)}, u32[]{:S(2)}) collective-permute-start(bf16[24,6272]{1,0:T(8,128)(2,1)S(1)} %shard_map.86.refs_0_), channel_id=1, source_target_pairs={{0,2},{1,3},{2,0},{3,1},{4,6},{5,7},{6,4},{7,5},{8,10},{9,11},{10,... | collective-permute-start | bytes 903176 | tf_op jit(solution)/shard_map/ppermute | solution.py:279
  5.0 11.1 %collective-permute-start = (bf16[24,6272]{1,0:T(8,128)(2,1)S(1)}, bf16[24,6272]{1,0:T(8,128)(2,1)S(1)}, u32[]{:S(2)}, u32[]{:S(2)}) collective-permute-start(bf16[24,6272]{1,0:T(8,128)(2,1)S(1)} %shard_map.86.refs_0_), channel_id=1, source_target_pairs={{0,4},{1,5},{2,6},{3,7},{4,8},{5,9},{6,10},{7,11},{8,12},{9,13},{1... | collective-permute-start | bytes 903176 | tf_op jit(solution)/shard_map/ppermute | solution.py:279
  16.1 11.9 %collective-permute-start.3 = (bf16[24,6272]{1,0:T(8,128)(2,1)S(1)}, bf16[24,6272]{1,0:T(8,128)(2,1)S(1)}, u32[]{:S(2)}, u32[]{:S(2)}) collective-permute-start(bf16[24,6272]{1,0:T(8,128)(2,1)S(1)} %collective-permute-done.refs_1_), channel_id=1, source_target_pairs={{0,4},{1,5},{2,6},{3,7},{4,8},{5,9},{6,10},{7,11},{8,12},{9,13},{1... | collective-permute-start | bytes 903176 | tf_op jit(solution)/shard_map/ppermute | solution.py:279
  16.1 15.0 %collective-permute-start.4 = (bf16[24,6272]{1,0:T(8,128)(2,1)S(1)}, bf16[24,6272]{1,0:T(8,128)(2,1)S(1)}, u32[]{:S(2)}, u32[]{:S(2)}) collective-permute-start(bf16[24,6272]{1,0:T(8,128)(2,1)S(1)} %shard_map.86.refs_0_), channel_id=1, source_target_pairs={{0,12},{1,13},{2,14},{3,15},{4,0},{5,1},{6,2},{7,3},{8,4},{9,5},{1... | collective-permute-start | bytes 903176 | tf_op jit(solution)/shard_map/ppermute | solution.py:279
  19.9 11.9 %collective-permute-start.5 = (bf16[24,6272]{1,0:T(8,128)(2,1)S(1)}, bf16[24,6272]{1,0:T(8,128)(2,1)S(1)}, u32[]{:S(2)}, u32[]{:S(2)}) collective-permute-start(bf16[24,6272]{1,0:T(8,128)(2,1)S(1)} %collective-permute-done.refs_1_), channel_id=1, source_target_pairs={{0,2},{1,3},{2,0},{3,1},{4,6},{5,7},{6,4},{7,5},{8,10},{9,11},{10,... | collective-permute-start | bytes 903176 | tf_op jit(solution)/shard_map/ppermute | solution.py:279
  28.0 9.4 %collective-permute-start.6 = (bf16[24,6272]{1,0:T(8,128)(2,1)S(1)}, bf16[24,6272]{1,0:T(8,128)(2,1)S(1)}, u32[]{:S(2)}, u32[]{:S(2)}) collective-permute-start(bf16[24,6272]{1,0:T(8,128)(2,1)S(1)} %collective-permute-done.3.refs_2_), channel_id=1, source_target_pairs={{0,2},{1,3},{2,0},{3,1},{4,6},{5,7},{6,4},{7,5},{8,10},{9,11},{10,... | collective-permute-start | bytes 903176 | tf_op jit(solution)/shard_map/ppermute | solution.py:279
  31.1 13.3 %collective-permute-start.7 = (bf16[24,6272]{1,0:T(8,128)(2,1)S(1)}, bf16[24,6272]{1,0:T(8,128)(2,1)S(1)}, u32[]{:S(2)}, u32[]{:S(2)}) collective-permute-start(bf16[24,6272]{1,0:T(8,128)(2,1)S(1)} %collective-permute-done.4.refs_3_), channel_id=1, source_target_pairs={{0,2},{1,3},{2,0},{3,1},{4,6},{5,7},{6,4},{7,5},{8,10},{9,11},{10,... | collective-permute-start | bytes 903176 | tf_op jit(solution)/shard_map/ppermute | solution.py:279
  44.3 6.3 %collective-permute-start.11 = (bf16[24,4096]{1,0:T(8,128)(2,1)S(1)}, bf16[24,4096]{1,0:T(8,128)(2,1)S(1)}, u32[]{:S(2)}, u32[]{:S(2)}) collective-permute-start(bf16[24,4096]{1,0:T(8,128)(2,1)S(1)} %get-tuple-element.22), channel_id=1, source_target_pairs={{0,2},{1,3},{2,0},{3,1},{4,6},{5,7},{6,4},{7,5},{8,10},{9,11},{10,... | collective-permute-start | bytes 589832 | tf_op jit(solution)/shard_map/ppermute | solution.py:279
  44.4 23.6 %copy-start = (s32[24,2048]{1,0:T(8,128)S(1)}, s32[24,2048]{1,0:T(8,128)}, u32[]{:S(2)}) copy-start(s32[24,2048]{1,0:T(8,128)} %signs.1) | copy-start | bytes 589828
  44.4 23.6 %copy-start.1 = (bf16[24,2048]{1,0:T(8,128)(2,1)S(1)}, bf16[24,2048]{1,0:T(8,128)(2,1)}, u32[]{:S(2)}) copy-start(bf16[24,2048]{1,0:T(8,128)(2,1)} %tokens.1) | copy-start | bytes 294916
  44.4 23.6 %copy-start.2 = (f32[2048]{0:T(1024)S(1)}, f32[2048]{0:T(1024)}, u32[]{:S(2)}) copy-start(f32[2048]{0:T(1024)} %param.8) | copy-start | bytes 24580
  48.5 7.6 %collective-permute-start.8 = (bf16[24,4096]{1,0:T(8,128)(2,1)S(1)}, bf16[24,4096]{1,0:T(8,128)(2,1)S(1)}, u32[]{:S(2)}, u32[]{:S(2)}) collective-permute-start(bf16[24,4096]{1,0:T(8,128)(2,1)S(1)} %shard_map.89), channel_id=1, source_target_pairs={{0,4},{1,5},{2,6},{3,7},{4,8},{5,9},{6,10},{7,11},{8,12},{9,13},{1... | collective-permute-start | bytes 589832 | tf_op jit(solution)/shard_map/ppermute | solution.py:279
  48.5 9.9 %collective-permute-start.10 = (bf16[24,4096]{1,0:T(8,128)(2,1)S(1)}, bf16[24,4096]{1,0:T(8,128)(2,1)S(1)}, u32[]{:S(2)}, u32[]{:S(2)}) collective-permute-start(bf16[24,4096]{1,0:T(8,128)(2,1)S(1)} %get-tuple-element.20), channel_id=1, source_target_pairs={{0,2},{1,3},{2,0},{3,1},{4,6},{5,7},{6,4},{7,5},{8,10},{9,11},{10,... | collective-permute-start | bytes 589832 | tf_op jit(solution)/shard_map/ppermute | solution.py:279
  50.6 12.9 %collective-permute-start.14 = (bf16[24,4096]{1,0:T(8,128)(2,1)S(1)}, bf16[24,4096]{1,0:T(8,128)(2,1)S(1)}, u32[]{:S(2)}, u32[]{:S(2)}) collective-permute-start(bf16[24,4096]{1,0:T(8,128)(2,1)S(1)} %get-tuple-element.23), channel_id=1, source_target_pairs={{0,4},{1,5},{2,6},{3,7},{4,8},{5,9},{6,10},{7,11},{8,12},{9,13},{1... | collective-permute-start | bytes 589832 | tf_op jit(solution)/shard_map/ppermute | solution.py:279
  50.6 11.6 %collective-permute-start.12 = (bf16[24,4096]{1,0:T(8,128)(2,1)S(1)}, bf16[24,4096]{1,0:T(8,128)(2,1)S(1)}, u32[]{:S(2)}, u32[]{:S(2)}) collective-permute-start(bf16[24,4096]{1,0:T(8,128)(2,1)S(1)} %add_convert_fusion.1), channel_id=1, source_target_pairs={{0,12},{1,13},{2,14},{3,15},{4,0},{5,1},{6,2},{7,3},{8,4},{9,5},{1... | collective-permute-start | bytes 589832 | tf_op jit(solution)/shard_map/ppermute | solution.py:279
  56.1 7.4 %collective-permute-start.9 = (bf16[24,4096]{1,0:T(8,128)(2,1)S(1)}, bf16[24,4096]{1,0:T(8,128)(2,1)S(1)}, u32[]{:S(2)}, u32[]{:S(2)}) collective-permute-start(bf16[24,4096]{1,0:T(8,128)(2,1)S(1)} %add_convert_fusion.2), channel_id=1, source_target_pairs={{0,2},{1,3},{2,0},{3,1},{4,6},{5,7},{6,4},{7,5},{8,10},{9,11},{10,... | collective-permute-start | bytes 589832 | tf_op jit(solution)/shard_map/ppermute | solution.py:279
  62.3 5.7 %collective-permute-start.13 = (bf16[24,4096]{1,0:T(8,128)(2,1)S(1)}, bf16[24,4096]{1,0:T(8,128)(2,1)S(1)}, u32[]{:S(2)}, u32[]{:S(2)}) collective-permute-start(bf16[24,4096]{1,0:T(8,128)(2,1)S(1)} %add_convert_fusion), channel_id=1, source_target_pairs={{0,12},{1,13},{2,14},{3,15},{4,0},{5,1},{6,2},{7,3},{8,4},{9,5},{1... | collective-permute-start | bytes 589832 | tf_op jit(solution)/shard_map/ppermute | solution.py:279

commit v6 on v5

--- a/solution.py
+++ b/solution.py
@@ -95,6 +95,14 @@
         (((1,), (1,)), ((), ())),
         preferred_element_type=jnp.float32,
     )
+    lane = lax.broadcasted_iota(jnp.int32, (tok_dev, lanes), 1)
+    place = 2 * expert_count
+    for number in (scale, -(scale**3) * along):
+        for _ in range(3):
+            addend = number.astype(jnp.bfloat16).astype(jnp.float32)
+            turned = jnp.where(lane == place, addend, turned)
+            number = number - addend
+            place += 1
     pack[:, 3 * width :] = turned.astype(jnp.bfloat16)
 
 
@@ -105,7 +113,7 @@
 
 def packed(tokens, norm_gain, probe_signs, cotangent, routes, gates, expert_count):
     tok_dev, width = tokens.shape
-    tail = -(-2 * expert_count // 128) * 128
+    tail = -(-(2 * expert_count + 6) // 128) * 128
     token_minor = (0, 2, 1)
     operands = (
         tokens,
@@ -175,8 +183,14 @@
     tail = stacked(3 * width, packs[0].shape[1] - 3 * width)
     mine = lax.axis_index("expert") // 2
     lane = lax.broadcasted_iota(jnp.int32, tail.shape, 1)
-    picked = (lane == mine) | (lane == mine + expert_count)
-    gate_row = jnp.sum(jnp.where(picked, tail, 0.0), axis=1, keepdims=True)
+    after = 2 * expert_count
+
+    def picked(lanes):
+        return jnp.sum(jnp.where(lanes, tail, 0.0), axis=1, keepdims=True)
+
+    gate_row = picked((lane == mine) | (lane == mine + expert_count))
+    scale_row = picked((lane >= after) & (lane < after + 3))
+    slope_row = picked((lane >= after + 3) & (lane < after + 6))
 
     def weights(part, start, size):
         return held[part, :, start : start + size]
@@ -215,8 +229,17 @@
     for n in range(count):
         part = slice(n * tok_dev, (n + 1) * tok_dev)
         later = slice(rows + n * tok_dev, rows + (n + 1) * tok_dev)
-        outs[n][:, :width] = (acc[part] * gate_row[part]).astype(outs[n].dtype)
-        outs[n][:, width:] = (acc[later] * gate_row[part]).astype(outs[n].dtype)
+        grad, tan = (acc[part] * gate_row[part], acc[later] * gate_row[part])
+        scale, slope_r = (scale_row[part], slope_row[part])
+        normed = packs[n][:, :width].astype(jnp.float32)
+        normed_t = packs[n][:, width : 2 * width].astype(jnp.float32)
+        outs[n][:, :width] = (scale * tan + slope_r * grad).astype(outs[n].dtype)
+        first = jnp.mean(normed * grad, axis=1, keepdims=True)
+        second = jnp.mean(normed * tan + normed_t * grad, axis=1, keepdims=True)
+        second = (second - slope_r / scale * first) / scale
+        lane = lax.broadcasted_iota(jnp.int32, (tok_dev, outs[n].shape[1] - width), 1)
+        sums = jnp.where(lane == 0, first / scale, jnp.where(lane == 1, second, 0.0))
+        outs[n][:, width:] = sums.astype(outs[n].dtype)
 
 
 def experts(packs, kinds, held, expert_count):
@@ -227,7 +250,7 @@
     whole = pl.BlockSpec(memory_space=pltpu.VMEM)
     return pl.pallas_call(
         functools.partial(expert_kernel, count, expert_count),
-        out_shape=[jax.ShapeDtypeStruct((tok_dev, 2 * width), kind) for kind in kinds],
+        out_shape=[jax.ShapeDtypeStruct((tok_dev, width + 128), kind) for kind in kinds],
         in_specs=[whole] * (count + 1),
         out_specs=[whole] * count,
         scratch_shapes=[
@@ -253,17 +276,13 @@
     rows = here[...]
     for part in (there, forward, backward):
         rows = rows + part[...].astype(jnp.float32)
-    lifted = gain[...] * rows[:, :width]
-    lifted_t = gain[...] * rows[:, width:]
-    first = jnp.mean(xf * lifted, axis=1, keepdims=True)
-    second = jnp.mean(xf * lifted_t, axis=1, keepdims=True)
-    third = jnp.mean(probe * lifted, axis=1, keepdims=True)
+    first = rows[:, width : width + 1]
+    second = rows[:, width + 1 : width + 2]
     whole = (
-        scale * lifted_t
-        + slope_r * lifted
+        gain[...] * rows[:, :width]
         - 3.0 * scale**2 * slope_r * first * xf
         - scale**3 * first * probe
-        - scale**3 * (second + third) * xf
+        - scale**3 * second * xf
     )
     hvp[...] = whole
     column = jnp.mean(probe * whole, axis=1, keepdims=True)
@@ -293,12 +312,12 @@
     across[1] = moved(same[1], 0, flip_x=True)
     same[3] = moved(lax.optimization_barrier((pack, same[1]))[0], -1)
     across[2] = moved(same[2], 0, flip_x=True)
-    across[3] = moved(same[3], 0, flip_x=True)
+    across[3] = moved(lax.optimization_barrier((across[0], same[2]))[0], -1)
     wide, sent = (jnp.float32, jnp.bfloat16)
     here, there = {}, {}
     here[0], here[1], here[2], here[3], there[0], there[1], there[2] = experts(
         [same[0], same[1], same[2], same[3], across[0], across[1], across[2]],
-        [wide, wide, wide, sent, wide, sent, sent],
+        [wide, wide, wide, wide, sent, sent, sent],
         held,
         expert_count,
     )
@@ -308,10 +327,10 @@
     def total(*parts):
         return sum(part.astype(jnp.float32) for part in parts).astype(jnp.bfloat16)
 
-    backward = moved(here[3], 1)
-    forward = moved(total(here[2], moved(there[2], 0, flip_x=True)), -1)
-    forward = moved(total(here[1], moved(there[1], 0, flip_x=True), forward), -1)
-    beside = moved(total(there[0], moved(there[3], 1)), 0, flip_x=True)
+    beside = {k: moved(there[k], 0, flip_x=True) for k in (2, 1, 3, 0)}
+    backward = moved(total(here[3], beside[3]), 1)
+    forward = moved(total(here[2], beside[2]), -1)
+    forward = moved(total(here[1], beside[1], forward), -1)
     hvp, quad = pl.pallas_call(
         finish_kernel,
         out_shape=[
@@ -322,7 +341,7 @@
         cost_estimate=pl.CostEstimate(
             flops=40 * tok_dev * width, bytes_accessed=26 * tok_dev * width, transcendentals=0
         ),
-    )(tokens, norm_gain.reshape(1, width), probe_signs, here[0], beside, forward, backward)
+    )(tokens, norm_gain.reshape(1, width), probe_signs, here[0], beside[0], forward, backward)
     return (hvp, quad.reshape(tok_dev))
 
 

time: 69.1 us -> 61.2 us (0.89)
  waiting for transfers between devices: 32.7 us -> 27.7 us
  starting transfers between devices: 19.8 us -> 16.8 us
    ppermute x15, waiting for transfers between devices: 32.7 us -> 27.7 us  [moved(): return lax.ppermute(rows, 'expert', pairs)]
    ppermute x15, starting transfers between devices: 19.8 us -> 16.8 us  [moved(): return lax.ppermute(rows, 'expert', pairs)]
  transfers between devices with their start and end apart: 15 -> 15, of which waited for: 9 -> 11; matrix products, arithmetic and copies ran while one was open for 0% -> 0% of each run, Pallas kernels for 21% -> 24%
where the time goes in v6:
time: 61.2 us; the launch traced here: 61 us
  waiting for transfers between devices  27.7 us (45%)
  starting transfers between devices  16.8 us (27%)
  Pallas kernels  15.7 us (26%)
  between operations  0.7 us (1%)
    ppermute x15, waiting for transfers between devices, moved(): return lax.ppermute(rows, 'expert', pairs)  27.7 us
    ppermute x15, starting transfers between devices, moved(): return lax.ppermute(rows, 'expert', pairs)  16.8 us
    pallas_call x2, Pallas kernels, experts(): pl.pallas_call(functools.partial(expert_kernel, count, expert_count), out...  11 us
    pallas_call x1, Pallas kernels, joined(): pl.pallas_call(join_kernel, out_shape=pltpu.VMEM((parts, width, 2 * half)...  2.41 us
    pallas_call x1, Pallas kernels, packed(): pl.pallas_call(functools.partial(pack_kernel, expert_count), out_shape=ja...  1.29 us
  transfers between devices with their start and end apart: 15, of which 11 were waited for; matrix products, arithmetic and copies ran while one was open for 0% of the time, Pallas kernels for 24%

profile of v6, /device:TPU:0, one launch (start us, length us, event | category | flops | bytes accessed | tf_op | source)
XLA Modules:
  0.0 61.0 jit_solution(10022338107344021481)
XLA Ops:
  0.6 0.5 collective-permute-start.2
  1.1 1.3 %shard_map.86.refs_0_ = bf16[24,6272]{1,0:T(8,128)(2,1)S(1)} custom-call(bf16[24,2048]{1,0:T(8,128)(2,1)} %tokens.1, f32[1,2048]{1,0:T(1,128)} %bitcast.4, s32[24,2048]{1,0:T(8,128)} %signs.1, bf16[24,2048]{1,0:T(8,128)(2,1)} %refs_3_.1, s32[2,4,24]{2,1,0:T(4,128)} %bitcast.6, f32[2,4,24]{2,1,0:T(4,128)} %bitcast.7), custom_call_target="tpu_custom_call" | custom-call | flops 983040 | bytes 688128 | tf_op jit(solution)/shard_map/pallas_call | solution.py:126
  2.4 2.6 %collective-permute-start.1 = (bf16[24,6272]{1,0:T(8,128)(2,1)S(1)}, bf16[24,6272]{1,0:T(8,128)(2,1)S(1)}, u32[]{:S(2)}, u32[]{:S(2)}) collective-permute-start(bf16[24,6272]{1,0:T(8,128)(2,1)S(1)} %shard_map.86.refs_0_), channel_id=1, source_target_pairs={{0,2},{1,3},{2,0},{3,1},{4,6},{5,7},{6,4},{7,5},{8,10},{9,11},{10,... | collective-permute-start | bytes 903176 | tf_op jit(solution)/shard_map/ppermute | solution.py:298
  5.0 1.6 %collective-permute-start = (bf16[24,6272]{1,0:T(8,128)(2,1)S(1)}, bf16[24,6272]{1,0:T(8,128)(2,1)S(1)}, u32[]{:S(2)}, u32[]{:S(2)}) collective-permute-start(bf16[24,6272]{1,0:T(8,128)(2,1)S(1)} %shard_map.86.refs_0_), channel_id=1, source_target_pairs={{0,4},{1,5},{2,6},{3,7},{4,8},{5,9},{6,10},{7,11},{8,12},{9,13},{1... | collective-permute-start | bytes 903176 | tf_op jit(solution)/shard_map/ppermute | solution.py:298
  6.6 2.3 %collective-permute-done.2.other = bf16[3,2048,384]{2,1,0:T(8,128)(2,1)S(1)} collective-permute-done((bf16[3,2048,384]{2,1,0:T(8,128)(2,1)}, bf16[3,2048,384]{2,1,0:T(8,128)(2,1)S(1)}, u32[]{:S(2)}, u32[]{:S(2)}) %collective-permute-start.2) | collective-permute-done | bytes 4718624 | tf_op jit(solution)/shard_map/ppermute | solution.py:298
  8.9 2.4 %shard_map.87.refs_7_.refs_1_ = bf16[3,2048,768]{2,1,0:T(8,128)(2,1)S(1)} custom-call(bf16[3,2048,384]{2,1,0:T(8,128)(2,1)} %own.1, bf16[3,2048,384]{2,1,0:T(8,128)(2,1)S(1)} %collective-permute-done.2.other), custom_call_target="tpu_custom_call" | custom-call | bytes 18874368 | tf_op jit(solution)/shard_map/pallas_call | solution.py:157
  11.3 1.5 %collective-permute-done.1.refs_4_ = bf16[24,6272]{1,0:T(8,128)(2,1)S(1)} collective-permute-done((bf16[24,6272]{1,0:T(8,128)(2,1)S(1)}, bf16[24,6272]{1,0:T(8,128)(2,1)S(1)}, u32[]{:S(2)}, u32[]{:S(2)}) %collective-permute-start.1) | collective-permute-done | bytes 301088 | tf_op jit(solution)/shard_map/ppermute | solution.py:298
  12.8 3.3 %collective-permute-done.refs_1_ = bf16[24,6272]{1,0:T(8,128)(2,1)S(1)} collective-permute-done((bf16[24,6272]{1,0:T(8,128)(2,1)S(1)}, bf16[24,6272]{1,0:T(8,128)(2,1)S(1)}, u32[]{:S(2)}, u32[]{:S(2)}) %collective-permute-start) | collective-permute-done | bytes 301088 | tf_op jit(solution)/shard_map/ppermute | solution.py:298
  16.1 0.0 collective-permute-start.3
  16.1 0.5 collective-permute-start.5
  16.7 3.8 %collective-permute-start.4 = (bf16[24,6272]{1,0:T(8,128)(2,1)S(1)}, bf16[24,6272]{1,0:T(8,128)(2,1)S(1)}, u32[]{:S(2)}, u32[]{:S(2)}) collective-permute-start(bf16[24,6272]{1,0:T(8,128)(2,1)S(1)} %shard_map.86.refs_0_), channel_id=1, source_target_pairs={{0,12},{1,13},{2,14},{3,15},{4,0},{5,1},{6,2},{7,3},{8,4},{9,5},{1... | collective-permute-start | bytes 903176 | tf_op jit(solution)/shard_map/ppermute | solution.py:298
  20.5 7.5 %collective-permute-done.3.refs_2_ = bf16[24,6272]{1,0:T(8,128)(2,1)S(1)} collective-permute-done((bf16[24,6272]{1,0:T(8,128)(2,1)S(1)}, bf16[24,6272]{1,0:T(8,128)(2,1)S(1)}, u32[]{:S(2)}, u32[]{:S(2)}) %collective-permute-start.3) | collective-permute-done | bytes 301088 | tf_op jit(solution)/shard_map/ppermute | solution.py:298
  28.0 0.5 collective-permute-start.6
  28.5 0.0 collective-permute-start.12
  28.5 4.5 %collective-permute-done.4.refs_3_ = bf16[24,6272]{1,0:T(8,128)(2,1)S(1)} collective-permute-done((bf16[24,6272]{1,0:T(8,128)(2,1)S(1)}, bf16[24,6272]{1,0:T(8,128)(2,1)S(1)}, u32[]{:S(2)}, u32[]{:S(2)}) %collective-permute-start.4) | collective-permute-done | bytes 301088 | tf_op jit(solution)/shard_map/ppermute | solution.py:298
  33.1 0.0 collective-permute-done.5.refs_5_
  33.1 1.7 %collective-permute-done.6.refs_6_ = bf16[24,6272]{1,0:T(8,128)(2,1)S(1)} collective-permute-done((bf16[24,6272]{1,0:T(8,128)(2,1)S(1)}, bf16[24,6272]{1,0:T(8,128)(2,1)S(1)}, u32[]{:S(2)}, u32[]{:S(2)}) %collective-permute-start.6) | collective-permute-done | bytes 301088 | tf_op jit(solution)/shard_map/ppermute | solution.py:298
  34.8 6.9 %shard_map.88 = (f32[24,2176]{1,0:T(8,128)S(1)}, f32[24,2176]{1,0:T(8,128)S(1)}, f32[24,2176]{1,0:T(8,128)S(1)}, f32[24,2176]{1,0:T(8,128)S(1)}, bf16[24,2176]{1...) custom-call(bf16[24,6272]{1,0:T(8,128)(2,1)S(1)} %shard_map.86.refs_0_, ...), custom_call_target="tpu_custom_call" | custom-call | flops 4756340736 | bytes 9437184 | tf_op jit(solution)/shard_map/pallas_call | solution.py:251
  41.7 0.6 collective-permute-start.9
  42.2 0.0 collective-permute-done.12.refs_0_
  42.2 0.0 copy-start
  42.2 0.0 copy-start.1
  42.2 0.0 copy-start.2
  42.3 4.1 %shard_map.89 = bf16[24,2176]{1,0:T(8,128)(2,1)S(1)} custom-call(bf16[24,6272]{1,0:T(8,128)(2,1)S(1)} %collective-permute-done.12.refs_0_, bf16[3,2048,768]{2,1,0:T(8,128)(2,1)S(1)} %shard_map.87.refs_7_.refs_1_), custom_call_target="tpu_custom_call" | custom-call | flops 679477248 | bytes 9437184 | tf_op jit(solution)/shard_map/pallas_call | solution.py:251
  46.4 1.6 %collective-permute-start.13 = (bf16[24,2176]{1,0:T(8,128)(2,1)S(1)}, bf16[24,2176]{1,0:T(8,128)(2,1)S(1)}, u32[]{:S(2)}, u32[]{:S(2)}) collective-permute-start(bf16[24,2176]{1,0:T(8,128)(2,1)S(1)} %shard_map.89), channel_id=1, source_target_pairs={{0,2},{1,3},{2,0},{3,1},{4,6},{5,7},{6,4},{7,5},{8,10},{9,11},{10,... | collective-permute-start | bytes 313352 | tf_op jit(solution)/shard_map/ppermute | solution.py:298
  48.0 0.5 collective-permute-start.7
  48.5 1.5 %collective-permute-start.8 = (bf16[24,2176]{1,0:T(8,128)(2,1)S(1)}, bf16[24,2176]{1,0:T(8,128)(2,1)S(1)}, u32[]{:S(2)}, u32[]{:S(2)}) collective-permute-start(bf16[24,2176]{1,0:T(8,128)(2,1)S(1)} %get-tuple-element.20), channel_id=1, source_target_pairs={{0,2},{1,3},{2,0},{3,1},{4,6},{5,7},{6,4},{7,5},{8,10},{9,11},{10,... | collective-permute-start | bytes 313352 | tf_op jit(solution)/shard_map/ppermute | solution.py:298
  50.0 0.0 collective-permute-done.9
  50.1 0.1 collective-permute-start.10
  50.1 1.0 %collective-permute-done.13 = bf16[24,2176]{1,0:T(8,128)(2,1)S(1)} collective-permute-done((bf16[24,2176]{1,0:T(8,128)(2,1)S(1)}, bf16[24,2176]{1,0:T(8,128)(2,1)S(1)}, u32[]{:S(2)}, u32[]{:S(2)}) %collective-permute-start.13) | collective-permute-done | bytes 104480 | tf_op jit(solution)/shard_map/ppermute | solution.py:298
  51.2 1.0 %collective-permute-start.14 = (bf16[24,2176]{1,0:T(8,128)(2,1)S(1)}, bf16[24,2176]{1,0:T(8,128)(2,1)S(1)}, u32[]{:S(2)}, u32[]{:S(2)}) collective-permute-start(bf16[24,2176]{1,0:T(8,128)(2,1)S(1)} %add_convert_fusion), channel_id=1, source_target_pairs={{0,4},{1,5},{2,6},{3,7},{4,8},{5,9},{6,10},{7,11},{8,12},{9,13},{1... | collective-permute-start | bytes 313352 | tf_op jit(solution)/shard_map/ppermute | solution.py:298
  52.2 1.6 %collective-permute-done.8 = bf16[24,2176]{1,0:T(8,128)(2,1)S(1)} collective-permute-done((bf16[24,2176]{1,0:T(8,128)(2,1)S(1)}, bf16[24,2176]{1,0:T(8,128)(2,1)S(1)}, u32[]{:S(2)}, u32[]{:S(2)}) %collective-permute-start.8) | collective-permute-done | bytes 104480 | tf_op jit(solution)/shard_map/ppermute | solution.py:298
  53.8 1.5 %collective-permute-done.10 = bf16[24,2176]{1,0:T(8,128)(2,1)S(1)} collective-permute-done((bf16[24,2176]{1,0:T(8,128)(2,1)S(1)}, bf16[24,2176]{1,0:T(8,128)(2,1)S(1)}, u32[]{:S(2)}, u32[]{:S(2)}) %collective-permute-start.10) | collective-permute-done | bytes 104480 | tf_op jit(solution)/shard_map/ppermute | solution.py:298
  55.3 2.0 %collective-permute-start.11 = (bf16[24,2176]{1,0:T(8,128)(2,1)S(1)}, bf16[24,2176]{1,0:T(8,128)(2,1)S(1)}, u32[]{:S(2)}, u32[]{:S(2)}) collective-permute-start(bf16[24,2176]{1,0:T(8,128)(2,1)S(1)} %add_convert_fusion.1), channel_id=1, source_target_pairs={{0,12},{1,13},{2,14},{3,15},{4,0},{5,1},{6,2},{7,3},{8,4},{9,5},{1... | collective-permute-start | bytes 313352 | tf_op jit(solution)/shard_map/ppermute | solution.py:298
  57.3 0.0 collective-permute-done.7.there
  57.3 0.4 collective-permute-done.14.backward
  57.7 2.3 %collective-permute-done.11.forward = bf16[24,2176]{1,0:T(8,128)(2,1)S(1)} collective-permute-done((bf16[24,2176]{1,0:T(8,128)(2,1)S(1)}, bf16[24,2176]{1,0:T(8,128)(2,1)S(1)}, u32[]{:S(2)}, u32[]{:S(2)}) %collective-permute-start.11) | collective-permute-done | bytes 104480 | tf_op jit(solution)/shard_map/ppermute | solution.py:298
  60.1 0.0 copy-done
  60.1 0.0 copy-done.1
  60.1 0.0 copy-done.2
  60.1 0.9 %shard_map.90 = (f32[24,2048]{1,0:T(8,128)}, f32[1,24]{1,0:T(1,128)}) custom-call(bf16[24,2048]{1,0:T(8,128)(2,1)S(1)} %copy-done.1, f32[1,2048]{1,0:T(1,128)S(1)} %bitcast.5, s32[24,2048]{1,0:T(8,128)S(1)} %copy-done, f32[24,2176]{1,0:T(8,128)S(1)} %get-tuple-element.17.here, bf16[24,2176]{1,0:T(8,128)(2,1)S(1)} %collective-permute-done.7.there, ...), custom_call_target="tpu_custom_call" | custom-call | flops 1966080 | bytes 1277952 | tf_op jit(solution)/shard_map/pallas_call | solution.py:334
  (3 shorter events, 0.1 us)
Async XLA Ops:
  0.6 8.3 %collective-permute-start.2 = (bf16[3,2048,384]{2,1,0:T(8,128)(2,1)}, bf16[3,2048,384]{2,1,0:T(8,128)(2,1)S(1)}, u32[]{:S(2)}, u32[]{:S(2)}) collective-permute-start(bf16[3,2048,384]{2,1,0:T(8,128)(2,1)} %own.1), channel_id=1, source_target_pairs={{0,1},{1,0},{2,3},{3,2},{4,5},{5,4},{6,7},{7,6},{8,9},{9,8},{10,11... | collective-permute-start | bytes 14155784 | tf_op jit(solution)/shard_map/ppermute | solution.py:298
  2.4 10.4 %collective-permute-start.1 = (bf16[24,6272]{1,0:T(8,128)(2,1)S(1)}, bf16[24,6272]{1,0:T(8,128)(2,1)S(1)}, u32[]{:S(2)}, u32[]{:S(2)}) collective-permute-start(bf16[24,6272]{1,0:T(8,128)(2,1)S(1)} %shard_map.86.refs_0_), channel_id=1, source_target_pairs={{0,2},{1,3},{2,0},{3,1},{4,6},{5,7},{6,4},{7,5},{8,10},{9,11},{10,... | collective-permute-start | bytes 903176 | tf_op jit(solution)/shard_map/ppermute | solution.py:298
  5.0 11.1 %collective-permute-start = (bf16[24,6272]{1,0:T(8,128)(2,1)S(1)}, bf16[24,6272]{1,0:T(8,128)(2,1)S(1)}, u32[]{:S(2)}, u32[]{:S(2)}) collective-permute-start(bf16[24,6272]{1,0:T(8,128)(2,1)S(1)} %shard_map.86.refs_0_), channel_id=1, source_target_pairs={{0,4},{1,5},{2,6},{3,7},{4,8},{5,9},{6,10},{7,11},{8,12},{9,13},{1... | collective-permute-start | bytes 903176 | tf_op jit(solution)/shard_map/ppermute | solution.py:298
  16.1 11.9 %collective-permute-start.3 = (bf16[24,6272]{1,0:T(8,128)(2,1)S(1)}, bf16[24,6272]{1,0:T(8,128)(2,1)S(1)}, u32[]{:S(2)}, u32[]{:S(2)}) collective-permute-start(bf16[24,6272]{1,0:T(8,128)(2,1)S(1)} %collective-permute-done.refs_1_), channel_id=1, source_target_pairs={{0,4},{1,5},{2,6},{3,7},{4,8},{5,9},{6,10},{7,11},{8,12},{9,13},{1... | collective-permute-start | bytes 903176 | tf_op jit(solution)/shard_map/ppermute | solution.py:298
  16.1 16.9 %collective-permute-start.5 = (bf16[24,6272]{1,0:T(8,128)(2,1)S(1)}, bf16[24,6272]{1,0:T(8,128)(2,1)S(1)}, u32[]{:S(2)}, u32[]{:S(2)}) collective-permute-start(bf16[24,6272]{1,0:T(8,128)(2,1)S(1)} %collective-permute-done.refs_1_), channel_id=1, source_target_pairs={{0,2},{1,3},{2,0},{3,1},{4,6},{5,7},{6,4},{7,5},{8,10},{9,11},{10,... | collective-permute-start | bytes 903176 | tf_op jit(solution)/shard_map/ppermute | solution.py:298
  16.7 16.4 %collective-permute-start.4 = (bf16[24,6272]{1,0:T(8,128)(2,1)S(1)}, bf16[24,6272]{1,0:T(8,128)(2,1)S(1)}, u32[]{:S(2)}, u32[]{:S(2)}) collective-permute-start(bf16[24,6272]{1,0:T(8,128)(2,1)S(1)} %shard_map.86.refs_0_), channel_id=1, source_target_pairs={{0,12},{1,13},{2,14},{3,15},{4,0},{5,1},{6,2},{7,3},{8,4},{9,5},{1... | collective-permute-start | bytes 903176 | tf_op jit(solution)/shard_map/ppermute | solution.py:298
  28.0 6.8 %collective-permute-start.6 = (bf16[24,6272]{1,0:T(8,128)(2,1)S(1)}, bf16[24,6272]{1,0:T(8,128)(2,1)S(1)}, u32[]{:S(2)}, u32[]{:S(2)}) collective-permute-start(bf16[24,6272]{1,0:T(8,128)(2,1)S(1)} %collective-permute-done.3.refs_2_), channel_id=1, source_target_pairs={{0,2},{1,3},{2,0},{3,1},{4,6},{5,7},{6,4},{7,5},{8,10},{9,11},{10,... | collective-permute-start | bytes 903176 | tf_op jit(solution)/shard_map/ppermute | solution.py:298
  28.5 13.7 %collective-permute-start.12 = (bf16[24,6272]{1,0:T(8,128)(2,1)S(1)}, bf16[24,6272]{1,0:T(8,128)(2,1)S(1)}, u32[]{:S(2)}, u32[]{:S(2)}) collective-permute-start(bf16[24,6272]{1,0:T(8,128)(2,1)S(1)} %collective-permute-done.1.refs_4_), channel_id=1, source_target_pairs={{0,12},{1,13},{2,14},{3,15},{4,0},{5,1},{6,2},{7,3},{8,4},{9,5},{1... | collective-permute-start | bytes 903176 | tf_op jit(solution)/shard_map/ppermute | solution.py:298
  41.7 8.3 %collective-permute-start.9 = (bf16[24,2176]{1,0:T(8,128)(2,1)S(1)}, bf16[24,2176]{1,0:T(8,128)(2,1)S(1)}, u32[]{:S(2)}, u32[]{:S(2)}) collective-permute-start(bf16[24,2176]{1,0:T(8,128)(2,1)S(1)} %get-tuple-element.22), channel_id=1, source_target_pairs={{0,2},{1,3},{2,0},{3,1},{4,6},{5,7},{6,4},{7,5},{8,10},{9,11},{10,... | collective-permute-start | bytes 313352 | tf_op jit(solution)/shard_map/ppermute | solution.py:298
  42.2 17.8 %copy-start = (s32[24,2048]{1,0:T(8,128)S(1)}, s32[24,2048]{1,0:T(8,128)}, u32[]{:S(2)}) copy-start(s32[24,2048]{1,0:T(8,128)} %signs.1) | copy-start | bytes 589828
  42.2 17.8 %copy-start.1 = (bf16[24,2048]{1,0:T(8,128)(2,1)S(1)}, bf16[24,2048]{1,0:T(8,128)(2,1)}, u32[]{:S(2)}) copy-start(bf16[24,2048]{1,0:T(8,128)(2,1)} %tokens.1) | copy-start | bytes 294916
  42.2 17.8 %copy-start.2 = (f32[2048]{0:T(1024)S(1)}, f32[2048]{0:T(1024)}, u32[]{:S(2)}) copy-start(f32[2048]{0:T(1024)} %param.8) | copy-start | bytes 24580
  46.4 4.7 %collective-permute-start.13 = (bf16[24,2176]{1,0:T(8,128)(2,1)S(1)}, bf16[24,2176]{1,0:T(8,128)(2,1)S(1)}, u32[]{:S(2)}, u32[]{:S(2)}) collective-permute-start(bf16[24,2176]{1,0:T(8,128)(2,1)S(1)} %shard_map.89), channel_id=1, source_target_pairs={{0,2},{1,3},{2,0},{3,1},{4,6},{5,7},{6,4},{7,5},{8,10},{9,11},{10,... | collective-permute-start | bytes 313352 | tf_op jit(solution)/shard_map/ppermute | solution.py:298
  48.0 9.3 %collective-permute-start.7 = (bf16[24,2176]{1,0:T(8,128)(2,1)S(1)}, bf16[24,2176]{1,0:T(8,128)(2,1)S(1)}, u32[]{:S(2)}, u32[]{:S(2)}) collective-permute-start(bf16[24,2176]{1,0:T(8,128)(2,1)S(1)} %get-tuple-element.18), channel_id=1, source_target_pairs={{0,2},{1,3},{2,0},{3,1},{4,6},{5,7},{6,4},{7,5},{8,10},{9,11},{10,... | collective-permute-start | bytes 313352 | tf_op jit(solution)/shard_map/ppermute | solution.py:298
  48.5 5.3 %collective-permute-start.8 = (bf16[24,2176]{1,0:T(8,128)(2,1)S(1)}, bf16[24,2176]{1,0:T(8,128)(2,1)S(1)}, u32[]{:S(2)}, u32[]{:S(2)}) collective-permute-start(bf16[24,2176]{1,0:T(8,128)(2,1)S(1)} %get-tuple-element.20), channel_id=1, source_target_pairs={{0,2},{1,3},{2,0},{3,1},{4,6},{5,7},{6,4},{7,5},{8,10},{9,11},{10,... | collective-permute-start | bytes 313352 | tf_op jit(solution)/shard_map/ppermute | solution.py:298
  50.1 5.2 %collective-permute-start.10 = (bf16[24,2176]{1,0:T(8,128)(2,1)S(1)}, bf16[24,2176]{1,0:T(8,128)(2,1)S(1)}, u32[]{:S(2)}, u32[]{:S(2)}) collective-permute-start(bf16[24,2176]{1,0:T(8,128)(2,1)S(1)} %add_convert_fusion.2), channel_id=1, source_target_pairs={{0,12},{1,13},{2,14},{3,15},{4,0},{5,1},{6,2},{7,3},{8,4},{9,5},{1... | collective-permute-start | bytes 313352 | tf_op jit(solution)/shard_map/ppermute | solution.py:298
  51.2 6.5 %collective-permute-start.14 = (bf16[24,2176]{1,0:T(8,128)(2,1)S(1)}, bf16[24,2176]{1,0:T(8,128)(2,1)S(1)}, u32[]{:S(2)}, u32[]{:S(2)}) collective-permute-start(bf16[24,2176]{1,0:T(8,128)(2,1)S(1)} %add_convert_fusion), channel_id=1, source_target_pairs={{0,4},{1,5},{2,6},{3,7},{4,8},{5,9},{6,10},{7,11},{8,12},{9,13},{1... | collective-permute-start | bytes 313352 | tf_op jit(solution)/shard_map/ppermute | solution.py:298
  55.3 4.7 %collective-permute-start.11 = (bf16[24,2176]{1,0:T(8,128)(2,1)S(1)}, bf16[24,2176]{1,0:T(8,128)(2,1)S(1)}, u32[]{:S(2)}, u32[]{:S(2)}) collective-permute-start(bf16[24,2176]{1,0:T(8,128)(2,1)S(1)} %add_convert_fusion.1), channel_id=1, source_target_pairs={{0,12},{1,13},{2,14},{3,15},{4,0},{5,1},{6,2},{7,3},{8,4},{9,5},{1... | collective-permute-start | bytes 313352 | tf_op jit(solution)/shard_map/ppermute | solution.py:298

commit v7 on v6

--- a/solution.py
+++ b/solution.py
@@ -267,15 +267,14 @@
     )(*packs, pltpu.with_memory_space_constraint(held, pltpu.VMEM))
 
 
-def finish_kernel(tokens, gain, signs, here, there, forward, backward, hvp, quad):
+def finish_kernel(tokens, gain, signs, *refs):
+    arrived, hvp, quad = (refs[:-2], refs[-2], refs[-1])
     width = tokens.shape[1]
     xf = tokens[...].astype(jnp.float32)
     probe = (2 * signs[...] - 1).astype(jnp.float32)
     scale, along = rms_terms(xf, probe)
     slope_r = -(scale**3) * along
-    rows = here[...]
-    for part in (there, forward, backward):
-        rows = rows + part[...].astype(jnp.float32)
+    rows = sum(part[...].astype(jnp.float32) for part in arrived)
     first = rows[:, width : width + 1]
     second = rows[:, width + 1 : width + 2]
     whole = (
@@ -315,22 +314,30 @@
     across[3] = moved(lax.optimization_barrier((across[0], same[2]))[0], -1)
     wide, sent = (jnp.float32, jnp.bfloat16)
     here, there = {}, {}
-    here[0], here[1], here[2], here[3], there[0], there[1], there[2] = experts(
-        [same[0], same[1], same[2], same[3], across[0], across[1], across[2]],
-        [wide, wide, wide, wide, sent, sent, sent],
-        held,
-        expert_count,
-    )
-    last = lax.optimization_barrier((across[3], here[1]))[0]
+    here[0], here[1], there[0], there[1] = experts(
+        [same[0], same[1], across[0], across[1]], [wide, wide, sent, sent], held, expert_count
+    )
+    far = lax.optimization_barrier((across[2], here[1]))[0]
+    here[2], here[3], there[2] = experts(
+        [same[2], same[3], far], [wide, sent, sent], held, expert_count
+    )
+    last = lax.optimization_barrier((across[3], here[2]))[0]
     (there[3],) = experts([last], [sent], held, expert_count)
+
+    def flipped(rows):
+        return moved(rows, 0, flip_x=True)
 
     def total(*parts):
         return sum(part.astype(jnp.float32) for part in parts).astype(jnp.bfloat16)
 
-    beside = {k: moved(there[k], 0, flip_x=True) for k in (2, 1, 3, 0)}
-    backward = moved(total(here[3], beside[3]), 1)
-    forward = moved(total(here[2], beside[2]), -1)
-    forward = moved(total(here[1], beside[1], forward), -1)
+    arrived = [
+        here[0],
+        flipped(there[0]),
+        moved(total(here[1], flipped(there[1])), -1),
+        moved(total(here[2], flipped(there[2])), 2),
+        moved(here[3], 1),
+        moved(there[3], 1, flip_x=True),
+    ]
     hvp, quad = pl.pallas_call(
         finish_kernel,
         out_shape=[
@@ -341,7 +348,7 @@
         cost_estimate=pl.CostEstimate(
             flops=40 * tok_dev * width, bytes_accessed=26 * tok_dev * width, transcendentals=0
         ),
-    )(tokens, norm_gain.reshape(1, width), probe_signs, here[0], beside[0], forward, backward)
+    )(tokens, norm_gain.reshape(1, width), probe_signs, *arrived)
     return (hvp, quad.reshape(tok_dev))
 
 

time: 61.2 us -> 60.4 us (0.987)
  waiting for transfers between devices: 27.7 us -> 25.2 us
  Pallas kernels: 15.7 us -> 18.1 us
    ppermute x15, waiting for transfers between devices: 27.7 us -> 25.2 us  [moved(): return lax.ppermute(rows, 'expert', pairs)]
    pallas_call x2 -> x3, Pallas kernels: 11 us -> 13.5 us  [experts(): pl.pallas_call(functools.partial(expert_kernel, count, expert_count), out...]
  transfers between devices with their start and end apart: 15 -> 15, of which waited for: 11 -> 9; matrix products, arithmetic and copies ran while one was open for 0% -> 0% of each run, Pallas kernels for 24% -> 28%
where the time goes in v7:
time: 60.4 us; the launch traced here: 60.3 us
  waiting for transfers between devices  25.2 us (42%)
  Pallas kernels  18.1 us (30%)
  starting transfers between devices  16.2 us (27%)
  between operations  0.7 us (1%)
    ppermute x15, waiting for transfers between devices, moved(): return lax.ppermute(rows, 'expert', pairs)  25.2 us
    ppermute x15, starting transfers between devices, moved(): return lax.ppermute(rows, 'expert', pairs)  16.2 us
    pallas_call x3, Pallas kernels, experts(): pl.pallas_call(functools.partial(expert_kernel, count, expert_count), out...  13.5 us
    pallas_call x1, Pallas kernels, joined(): pl.pallas_call(join_kernel, out_shape=pltpu.VMEM((parts, width, 2 * half)...  2.41 us
    pallas_call x1, Pallas kernels, packed(): pl.pallas_call(functools.partial(pack_kernel, expert_count), out_shape=ja...  1.29 us
  transfers between devices with their start and end apart: 15, of which 9 were waited for; matrix products, arithmetic and copies ran while one was open for 0% of the time, Pallas kernels for 28%

profile of v7, /device:TPU:0, one launch (start us, length us, event | category | flops | bytes accessed | tf_op | source)
XLA Modules:
  0.0 60.3 jit_solution(12238110567915986105)
XLA Ops:
  0.6 0.5 collective-permute-start.2
  1.1 1.3 %shard_map.86.refs_0_ = bf16[24,6272]{1,0:T(8,128)(2,1)S(1)} custom-call(bf16[24,2048]{1,0:T(8,128)(2,1)} %tokens.1, f32[1,2048]{1,0:T(1,128)} %bitcast.4, s32[24,2048]{1,0:T(8,128)} %signs.1, bf16[24,2048]{1,0:T(8,128)(2,1)} %refs_3_.1, s32[2,4,24]{2,1,0:T(4,128)} %bitcast.6, f32[2,4,24]{2,1,0:T(4,128)} %bitcast.7), custom_call_target="tpu_custom_call" | custom-call | flops 983040 | bytes 688128 | tf_op jit(solution)/shard_map/pallas_call | solution.py:126
  2.4 2.6 %collective-permute-start.1 = (bf16[24,6272]{1,0:T(8,128)(2,1)S(1)}, bf16[24,6272]{1,0:T(8,128)(2,1)S(1)}, u32[]{:S(2)}, u32[]{:S(2)}) collective-permute-start(bf16[24,6272]{1,0:T(8,128)(2,1)S(1)} %shard_map.86.refs_0_), channel_id=1, source_target_pairs={{0,2},{1,3},{2,0},{3,1},{4,6},{5,7},{6,4},{7,5},{8,10},{9,11},{10,... | collective-permute-start | bytes 903176 | tf_op jit(solution)/shard_map/ppermute | solution.py:297
  5.0 1.6 %collective-permute-start = (bf16[24,6272]{1,0:T(8,128)(2,1)S(1)}, bf16[24,6272]{1,0:T(8,128)(2,1)S(1)}, u32[]{:S(2)}, u32[]{:S(2)}) collective-permute-start(bf16[24,6272]{1,0:T(8,128)(2,1)S(1)} %shard_map.86.refs_0_), channel_id=1, source_target_pairs={{0,4},{1,5},{2,6},{3,7},{4,8},{5,9},{6,10},{7,11},{8,12},{9,13},{1... | collective-permute-start | bytes 903176 | tf_op jit(solution)/shard_map/ppermute | solution.py:297
  6.6 2.3 %collective-permute-done.2.other = bf16[3,2048,384]{2,1,0:T(8,128)(2,1)S(1)} collective-permute-done((bf16[3,2048,384]{2,1,0:T(8,128)(2,1)}, bf16[3,2048,384]{2,1,0:T(8,128)(2,1)S(1)}, u32[]{:S(2)}, u32[]{:S(2)}) %collective-permute-start.2) | collective-permute-done | bytes 4718624 | tf_op jit(solution)/shard_map/ppermute | solution.py:297
  8.9 2.4 %shard_map.87.refs_4_.refs_3_.refs_1_ = bf16[3,2048,768]{2,1,0:T(8,128)(2,1)S(1)} custom-call(bf16[3,2048,384]{2,1,0:T(8,128)(2,1)} %own.1, bf16[3,2048,384]{2,1,0:T(8,128)(2,1)S(1)} %collective-permute-done.2.other), custom_call_target="tpu_custom_call" | custom-call | bytes 18874368 | tf_op jit(solution)/shard_map/pallas_call | solution.py:157
  11.3 1.5 %collective-permute-done.1.refs_2_ = bf16[24,6272]{1,0:T(8,128)(2,1)S(1)} collective-permute-done((bf16[24,6272]{1,0:T(8,128)(2,1)S(1)}, bf16[24,6272]{1,0:T(8,128)(2,1)S(1)}, u32[]{:S(2)}, u32[]{:S(2)}) %collective-permute-start.1) | collective-permute-done | bytes 301088 | tf_op jit(solution)/shard_map/ppermute | solution.py:297
  12.8 3.3 %collective-permute-done.refs_1_ = bf16[24,6272]{1,0:T(8,128)(2,1)S(1)} collective-permute-done((bf16[24,6272]{1,0:T(8,128)(2,1)S(1)}, bf16[24,6272]{1,0:T(8,128)(2,1)S(1)}, u32[]{:S(2)}, u32[]{:S(2)}) %collective-permute-start) | collective-permute-done | bytes 301088 | tf_op jit(solution)/shard_map/ppermute | solution.py:297
  16.1 0.0 collective-permute-start.7
  16.1 0.5 collective-permute-start.3
  16.7 9.8 %collective-permute-done.7.refs_0_ = bf16[24,6272]{1,0:T(8,128)(2,1)S(1)} collective-permute-done((bf16[24,6272]{1,0:T(8,128)(2,1)S(1)}, bf16[24,6272]{1,0:T(8,128)(2,1)S(1)}, u32[]{:S(2)}, u32[]{:S(2)}) %collective-permute-start.7) | collective-permute-done | bytes 301088 | tf_op jit(solution)/shard_map/ppermute | solution.py:297
  26.4 0.8 %collective-permute-start.9 = (bf16[24,6272]{1,0:T(8,128)(2,1)S(1)}, bf16[24,6272]{1,0:T(8,128)(2,1)S(1)}, u32[]{:S(2)}, u32[]{:S(2)}) collective-permute-start(bf16[24,6272]{1,0:T(8,128)(2,1)S(1)} %collective-permute-done.7.refs_0_), channel_id=1, source_target_pairs={{0,2},{1,3},{2,0},{3,1},{4,6},{5,7},{6,4},{7,5},{8,10},{9,11},{10,... | collective-permute-start | bytes 903176 | tf_op jit(solution)/shard_map/ppermute | solution.py:297
  27.2 0.0 collective-permute-start.8
  27.2 0.3 collective-permute-start.13
  27.5 0.0 collective-permute-done.3.refs_3_
  27.5 4.8 %shard_map.88 = (f32[24,2176]{1,0:T(8,128)S(1)}, f32[24,2176]{1,0:T(8,128)S(1)}, bf16[24,2176]{1,0:T(8,128)(2,1)S(1)}, bf16[24,2176]{1,0:T(8,128)(2,1)S(1)}) custom-call(bf16[24,6272]{1,0:T(8,128)(2,1)S(1)} %shard_map.86.refs_0_, bf16[24,6272]{1,0:T(8,128)(2,1)S(1)} %collective-permute-done.refs_1_, bf16[24,6272]{1,0:T(8,128)(2,1)S(1)} %collective-permute-done.1.refs_2_, ...), custom_call_target="tpu_custom_call" | custom-call | flops 2717908992 | bytes 9437184 | tf_op jit(solution)/shard_map/pallas_call | solution.py:251
  32.3 1.4 %collective-permute-start.4 = (bf16[24,2176]{1,0:T(8,128)(2,1)S(1)}, bf16[24,2176]{1,0:T(8,128)(2,1)S(1)}, u32[]{:S(2)}, u32[]{:S(2)}) collective-permute-start(bf16[24,2176]{1,0:T(8,128)(2,1)S(1)} %get-tuple-element.18), channel_id=1, source_target_pairs={{0,2},{1,3},{2,0},{3,1},{4,6},{5,7},{6,4},{7,5},{8,10},{9,11},{10,... | collective-permute-start | bytes 313352 | tf_op jit(solution)/shard_map/ppermute | solution.py:297
  33.7 0.7 %collective-permute-start.5 = (bf16[24,2176]{1,0:T(8,128)(2,1)S(1)}, bf16[24,2176]{1,0:T(8,128)(2,1)S(1)}, u32[]{:S(2)}, u32[]{:S(2)}) collective-permute-start(bf16[24,2176]{1,0:T(8,128)(2,1)S(1)} %get-tuple-element.20), channel_id=1, source_target_pairs={{0,2},{1,3},{2,0},{3,1},{4,6},{5,7},{6,4},{7,5},{8,10},{9,11},{10,... | collective-permute-start | bytes 313352 | tf_op jit(solution)/shard_map/ppermute | solution.py:297
  34.4 0.4 collective-permute-done.9.refs_2_
  34.7 2.6 %collective-permute-done.8.refs_1_ = bf16[24,6272]{1,0:T(8,128)(2,1)S(1)} collective-permute-done((bf16[24,6272]{1,0:T(8,128)(2,1)S(1)}, bf16[24,6272]{1,0:T(8,128)(2,1)S(1)}, u32[]{:S(2)}, u32[]{:S(2)}) %collective-permute-start.8) | collective-permute-done | bytes 301088 | tf_op jit(solution)/shard_map/ppermute | solution.py:297
  37.3 4.5 %shard_map.89 = (f32[24,2176]{1,0:T(8,128)S(1)}, bf16[24,2176]{1,0:T(8,128)(2,1)S(1)}, bf16[24,2176]{1,0:T(8,128)(2,1)S(1)}) custom-call(bf16[24,6272]{1,0:T(8,128)(2,1)S(1)} %collective-permute-done.7.refs_0_, bf16[24,6272]{1,0:T(8,128)(2,1)S(1)} %collective-permute-done.8.refs_1_, bf16[24,6272]{1,0:T(8,128)(2,1)S(1)} %collective-permute-done.9.refs_2_, ...), custom_call_target="tpu_custom_call" | custom-call | flops 2038431744 | bytes 9437184 | tf_op jit(solution)/shard_map/pallas_call | solution.py:251
  41.8 1.3 %collective-permute-start.10 = (bf16[24,2176]{1,0:T(8,128)(2,1)S(1)}, bf16[24,2176]{1,0:T(8,128)(2,1)S(1)}, u32[]{:S(2)}, u32[]{:S(2)}) collective-permute-start(bf16[24,2176]{1,0:T(8,128)(2,1)S(1)} %get-tuple-element.24), channel_id=1, source_target_pairs={{0,2},{1,3},{2,0},{3,1},{4,6},{5,7},{6,4},{7,5},{8,10},{9,11},{10,... | collective-permute-start | bytes 313352 | tf_op jit(solution)/shard_map/ppermute | solution.py:297
  43.1 0.0 collective-permute-done.5
  43.2 1.9 %collective-permute-start.6 = (bf16[24,2176]{1,0:T(8,128)(2,1)S(1)}, bf16[24,2176]{1,0:T(8,128)(2,1)S(1)}, u32[]{:S(2)}, u32[]{:S(2)}) collective-permute-start(bf16[24,2176]{1,0:T(8,128)(2,1)S(1)} %add_convert_fusion.1), channel_id=1, source_target_pairs={{0,12},{1,13},{2,14},{3,15},{4,0},{5,1},{6,2},{7,3},{8,4},{9,5},{1... | collective-permute-start | bytes 313352 | tf_op jit(solution)/shard_map/ppermute | solution.py:297
  45.0 0.0 collective-permute-done.13.refs_0_
  45.0 0.0 copy-start
  45.0 0.0 copy-start.1
  45.0 0.0 copy-start.2
  45.0 4.1 %shard_map.90 = bf16[24,2176]{1,0:T(8,128)(2,1)S(1)} custom-call(bf16[24,6272]{1,0:T(8,128)(2,1)S(1)} %collective-permute-done.13.refs_0_, bf16[3,2048,768]{2,1,0:T(8,128)(2,1)S(1)} %shard_map.87.refs_4_.refs_3_.refs_1_), custom_call_target="tpu_custom_call" | custom-call | flops 679477248 | bytes 9437184 | tf_op jit(solution)/shard_map/pallas_call | solution.py:251
  49.2 0.5 collective-permute-start.14
  49.7 0.0 collective-permute-start.12
  49.7 0.0 collective-permute-done.10
  49.7 4.2 %collective-permute-start.11 = (bf16[24,2176]{1,0:T(8,128)(2,1)S(1)}, bf16[24,2176]{1,0:T(8,128)(2,1)S(1)}, u32[]{:S(2)}, u32[]{:S(2)}) collective-permute-start(bf16[24,2176]{1,0:T(8,128)(2,1)S(1)} %add_convert_fusion), channel_id=1, source_target_pairs={{0,8},{1,9},{2,10},{3,11},{4,12},{5,13},{6,14},{7,15},{8,0},{9,1},... | collective-permute-start | bytes 313352 | tf_op jit(solution)/shard_map/ppermute | solution.py:297
  54.0 0.0 collective-permute-done.4.refs_1_
  54.0 0.0 collective-permute-done.6.refs_2_
  54.0 2.7 %collective-permute-done.14.refs_5_ = bf16[24,2176]{1,0:T(8,128)(2,1)S(1)} collective-permute-done((bf16[24,2176]{1,0:T(8,128)(2,1)S(1)}, bf16[24,2176]{1,0:T(8,128)(2,1)S(1)}, u32[]{:S(2)}, u32[]{:S(2)}) %collective-permute-start.14) | collective-permute-done | bytes 104480 | tf_op jit(solution)/shard_map/ppermute | solution.py:297
  56.7 0.5 collective-permute-done.12.refs_4_
  57.2 2.1 %collective-permute-done.11.refs_3_ = bf16[24,2176]{1,0:T(8,128)(2,1)S(1)} collective-permute-done((bf16[24,2176]{1,0:T(8,128)(2,1)S(1)}, bf16[24,2176]{1,0:T(8,128)(2,1)S(1)}, u32[]{:S(2)}, u32[]{:S(2)}) %collective-permute-start.11) | collective-permute-done | bytes 104480 | tf_op jit(solution)/shard_map/ppermute | solution.py:297
  59.3 0.0 copy-done
  59.3 0.0 copy-done.1
  59.3 0.0 copy-done.2
  59.3 1.0 %shard_map.91 = (f32[24,2048]{1,0:T(8,128)}, f32[1,24]{1,0:T(1,128)}) custom-call(bf16[24,2048]{1,0:T(8,128)(2,1)S(1)} %copy-done.1, f32[1,2048]{1,0:T(1,128)S(1)} %bitcast.5, s32[24,2048]{1,0:T(8,128)S(1)} %copy-done, f32[24,2176]{1,0:T(8,128)S(1)} %get-tuple-element.17.refs_0_, bf16[24,2176]{1,0:T(8,128)(2,1)S(1)} %collective-permute-done.4.refs_1_, ...), custom_call_target="tpu_custom_call" | custom-call | flops 1966080 | bytes 1277952 | tf_op jit(solution)/shard_map/pallas_call | solution.py:341
  (2 shorter events, 0.1 us)
Async XLA Ops:
  0.6 8.3 %collective-permute-start.2 = (bf16[3,2048,384]{2,1,0:T(8,128)(2,1)}, bf16[3,2048,384]{2,1,0:T(8,128)(2,1)S(1)}, u32[]{:S(2)}, u32[]{:S(2)}) collective-permute-start(bf16[3,2048,384]{2,1,0:T(8,128)(2,1)} %own.1), channel_id=1, source_target_pairs={{0,1},{1,0},{2,3},{3,2},{4,5},{5,4},{6,7},{7,6},{8,9},{9,8},{10,11... | collective-permute-start | bytes 14155784 | tf_op jit(solution)/shard_map/ppermute | solution.py:297
  2.4 10.4 %collective-permute-start.1 = (bf16[24,6272]{1,0:T(8,128)(2,1)S(1)}, bf16[24,6272]{1,0:T(8,128)(2,1)S(1)}, u32[]{:S(2)}, u32[]{:S(2)}) collective-permute-start(bf16[24,6272]{1,0:T(8,128)(2,1)S(1)} %shard_map.86.refs_0_), channel_id=1, source_target_pairs={{0,2},{1,3},{2,0},{3,1},{4,6},{5,7},{6,4},{7,5},{8,10},{9,11},{10,... | collective-permute-start | bytes 903176 | tf_op jit(solution)/shard_map/ppermute | solution.py:297
  5.0 11.1 %collective-permute-start = (bf16[24,6272]{1,0:T(8,128)(2,1)S(1)}, bf16[24,6272]{1,0:T(8,128)(2,1)S(1)}, u32[]{:S(2)}, u32[]{:S(2)}) collective-permute-start(bf16[24,6272]{1,0:T(8,128)(2,1)S(1)} %shard_map.86.refs_0_), channel_id=1, source_target_pairs={{0,4},{1,5},{2,6},{3,7},{4,8},{5,9},{6,10},{7,11},{8,12},{9,13},{1... | collective-permute-start | bytes 903176 | tf_op jit(solution)/shard_map/ppermute | solution.py:297
  16.1 10.3 %collective-permute-start.7 = (bf16[24,6272]{1,0:T(8,128)(2,1)S(1)}, bf16[24,6272]{1,0:T(8,128)(2,1)S(1)}, u32[]{:S(2)}, u32[]{:S(2)}) collective-permute-start(bf16[24,6272]{1,0:T(8,128)(2,1)S(1)} %collective-permute-done.refs_1_), channel_id=1, source_target_pairs={{0,4},{1,5},{2,6},{3,7},{4,8},{5,9},{6,10},{7,11},{8,12},{9,13},{1... | collective-permute-start | bytes 903176 | tf_op jit(solution)/shard_map/ppermute | solution.py:297
  16.1 11.3 %collective-permute-start.3 = (bf16[24,6272]{1,0:T(8,128)(2,1)S(1)}, bf16[24,6272]{1,0:T(8,128)(2,1)S(1)}, u32[]{:S(2)}, u32[]{:S(2)}) collective-permute-start(bf16[24,6272]{1,0:T(8,128)(2,1)S(1)} %collective-permute-done.refs_1_), channel_id=1, source_target_pairs={{0,2},{1,3},{2,0},{3,1},{4,6},{5,7},{6,4},{7,5},{8,10},{9,11},{10,... | collective-permute-start | bytes 903176 | tf_op jit(solution)/shard_map/ppermute | solution.py:297
  26.4 8.3 %collective-permute-start.9 = (bf16[24,6272]{1,0:T(8,128)(2,1)S(1)}, bf16[24,6272]{1,0:T(8,128)(2,1)S(1)}, u32[]{:S(2)}, u32[]{:S(2)}) collective-permute-start(bf16[24,6272]{1,0:T(8,128)(2,1)S(1)} %collective-permute-done.7.refs_0_), channel_id=1, source_target_pairs={{0,2},{1,3},{2,0},{3,1},{4,6},{5,7},{6,4},{7,5},{8,10},{9,11},{10,... | collective-permute-start | bytes 903176 | tf_op jit(solution)/shard_map/ppermute | solution.py:297
  27.2 10.1 %collective-permute-start.8 = (bf16[24,6272]{1,0:T(8,128)(2,1)S(1)}, bf16[24,6272]{1,0:T(8,128)(2,1)S(1)}, u32[]{:S(2)}, u32[]{:S(2)}) collective-permute-start(bf16[24,6272]{1,0:T(8,128)(2,1)S(1)} %shard_map.86.refs_0_), channel_id=1, source_target_pairs={{0,12},{1,13},{2,14},{3,15},{4,0},{5,1},{6,2},{7,3},{8,4},{9,5},{1... | collective-permute-start | bytes 903176 | tf_op jit(solution)/shard_map/ppermute | solution.py:297
  27.2 17.8 %collective-permute-start.13 = (bf16[24,6272]{1,0:T(8,128)(2,1)S(1)}, bf16[24,6272]{1,0:T(8,128)(2,1)S(1)}, u32[]{:S(2)}, u32[]{:S(2)}) collective-permute-start(bf16[24,6272]{1,0:T(8,128)(2,1)S(1)} %collective-permute-done.1.refs_2_), channel_id=1, source_target_pairs={{0,12},{1,13},{2,14},{3,15},{4,0},{5,1},{6,2},{7,3},{8,4},{9,5},{1... | collective-permute-start | bytes 903176 | tf_op jit(solution)/shard_map/ppermute | solution.py:297
  32.3 21.7 %collective-permute-start.4 = (bf16[24,2176]{1,0:T(8,128)(2,1)S(1)}, bf16[24,2176]{1,0:T(8,128)(2,1)S(1)}, u32[]{:S(2)}, u32[]{:S(2)}) collective-permute-start(bf16[24,2176]{1,0:T(8,128)(2,1)S(1)} %get-tuple-element.18), channel_id=1, source_target_pairs={{0,2},{1,3},{2,0},{3,1},{4,6},{5,7},{6,4},{7,5},{8,10},{9,11},{10,... | collective-permute-start | bytes 313352 | tf_op jit(solution)/shard_map/ppermute | solution.py:297
  33.7 9.5 %collective-permute-start.5 = (bf16[24,2176]{1,0:T(8,128)(2,1)S(1)}, bf16[24,2176]{1,0:T(8,128)(2,1)S(1)}, u32[]{:S(2)}, u32[]{:S(2)}) collective-permute-start(bf16[24,2176]{1,0:T(8,128)(2,1)S(1)} %get-tuple-element.20), channel_id=1, source_target_pairs={{0,2},{1,3},{2,0},{3,1},{4,6},{5,7},{6,4},{7,5},{8,10},{9,11},{10,... | collective-permute-start | bytes 313352 | tf_op jit(solution)/shard_map/ppermute | solution.py:297
  41.8 7.9 %collective-permute-start.10 = (bf16[24,2176]{1,0:T(8,128)(2,1)S(1)}, bf16[24,2176]{1,0:T(8,128)(2,1)S(1)}, u32[]{:S(2)}, u32[]{:S(2)}) collective-permute-start(bf16[24,2176]{1,0:T(8,128)(2,1)S(1)} %get-tuple-element.24), channel_id=1, source_target_pairs={{0,2},{1,3},{2,0},{3,1},{4,6},{5,7},{6,4},{7,5},{8,10},{9,11},{10,... | collective-permute-start | bytes 313352 | tf_op jit(solution)/shard_map/ppermute | solution.py:297
  43.2 10.8 %collective-permute-start.6 = (bf16[24,2176]{1,0:T(8,128)(2,1)S(1)}, bf16[24,2176]{1,0:T(8,128)(2,1)S(1)}, u32[]{:S(2)}, u32[]{:S(2)}) collective-permute-start(bf16[24,2176]{1,0:T(8,128)(2,1)S(1)} %add_convert_fusion.1), channel_id=1, source_target_pairs={{0,12},{1,13},{2,14},{3,15},{4,0},{5,1},{6,2},{7,3},{8,4},{9,5},{1... | collective-permute-start | bytes 313352 | tf_op jit(solution)/shard_map/ppermute | solution.py:297
  45.0 14.3 %copy-start = (s32[24,2048]{1,0:T(8,128)S(1)}, s32[24,2048]{1,0:T(8,128)}, u32[]{:S(2)}) copy-start(s32[24,2048]{1,0:T(8,128)} %signs.1) | copy-start | bytes 589828
  45.0 14.3 %copy-start.1 = (bf16[24,2048]{1,0:T(8,128)(2,1)S(1)}, bf16[24,2048]{1,0:T(8,128)(2,1)}, u32[]{:S(2)}) copy-start(bf16[24,2048]{1,0:T(8,128)(2,1)} %tokens.1) | copy-start | bytes 294916
  45.0 14.3 %copy-start.2 = (f32[2048]{0:T(1024)S(1)}, f32[2048]{0:T(1024)}, u32[]{:S(2)}) copy-start(f32[2048]{0:T(1024)} %param.8) | copy-start | bytes 24580
  49.2 7.5 %collective-permute-start.14 = (bf16[24,2176]{1,0:T(8,128)(2,1)S(1)}, bf16[24,2176]{1,0:T(8,128)(2,1)S(1)}, u32[]{:S(2)}, u32[]{:S(2)}) collective-permute-start(bf16[24,2176]{1,0:T(8,128)(2,1)S(1)} %shard_map.90), channel_id=1, source_target_pairs={{0,6},{1,7},{2,4},{3,5},{4,10},{5,11},{6,8},{7,9},{8,14},{9,15},{1... | collective-permute-start | bytes 313352 | tf_op jit(solution)/shard_map/ppermute | solution.py:297
  49.7 7.5 %collective-permute-start.12 = (bf16[24,2176]{1,0:T(8,128)(2,1)S(1)}, bf16[24,2176]{1,0:T(8,128)(2,1)S(1)}, u32[]{:S(2)}, u32[]{:S(2)}) collective-permute-start(bf16[24,2176]{1,0:T(8,128)(2,1)S(1)} %get-tuple-element.25), channel_id=1, source_target_pairs={{0,4},{1,5},{2,6},{3,7},{4,8},{5,9},{6,10},{7,11},{8,12},{9,13},{1... | collective-permute-start | bytes 313352 | tf_op jit(solution)/shard_map/ppermute | solution.py:297
  49.7 9.6 %collective-permute-start.11 = (bf16[24,2176]{1,0:T(8,128)(2,1)S(1)}, bf16[24,2176]{1,0:T(8,128)(2,1)S(1)}, u32[]{:S(2)}, u32[]{:S(2)}) collective-permute-start(bf16[24,2176]{1,0:T(8,128)(2,1)S(1)} %add_convert_fusion), channel_id=1, source_target_pairs={{0,8},{1,9},{2,10},{3,11},{4,12},{5,13},{6,14},{7,15},{8,0},{9,1},... | collective-permute-start | bytes 313352 | tf_op jit(solution)/shard_map/ppermute | solution.py:297

commit v8 on v7

--- a/solution.py
+++ b/solution.py
@@ -307,22 +307,21 @@
     same[1] = moved(pack, 1)
     across[0] = moved(pack, 0, flip_x=True)
     same[1] = lax.optimization_barrier((same[1], across[0], held))[0]
+    same[3] = moved(pack, -1)
     same[2] = moved(same[1], 1)
     across[1] = moved(same[1], 0, flip_x=True)
-    same[3] = moved(lax.optimization_barrier((pack, same[1]))[0], -1)
-    across[2] = moved(same[2], 0, flip_x=True)
-    across[3] = moved(lax.optimization_barrier((across[0], same[2]))[0], -1)
+    across[3] = moved(same[3], 0, flip_x=True)
+    across[2] = moved(across[1], 1)
     wide, sent = (jnp.float32, jnp.bfloat16)
     here, there = {}, {}
-    here[0], here[1], there[0], there[1] = experts(
-        [same[0], same[1], across[0], across[1]], [wide, wide, sent, sent], held, expert_count
-    )
-    far = lax.optimization_barrier((across[2], here[1]))[0]
-    here[2], here[3], there[2] = experts(
-        [same[2], same[3], far], [wide, sent, sent], held, expert_count
-    )
-    last = lax.optimization_barrier((across[3], here[2]))[0]
-    (there[3],) = experts([last], [sent], held, expert_count)
+    here[0], here[1], here[2], here[3], there[0], there[1] = experts(
+        [same[0], same[1], same[2], same[3], across[0], across[1]],
+        [wide, wide, sent, sent, sent, sent],
+        held,
+        expert_count,
+    )
+    late = lax.optimization_barrier((across[2], across[3], here[1]))[:2]
+    there[2], there[3] = experts(late, [sent, sent], held, expert_count)
 
     def flipped(rows):
         return moved(rows, 0, flip_x=True)
@@ -330,13 +329,16 @@
     def total(*parts):
         return sum(part.astype(jnp.float32) for part in parts).astype(jnp.bfloat16)
 
+    beside = flipped(there[1])
+    kept = lax.optimization_barrier((here[1], there[2]))[0]
     arrived = [
         here[0],
         flipped(there[0]),
-        moved(total(here[1], flipped(there[1])), -1),
-        moved(total(here[2], flipped(there[2])), 2),
+        moved(here[2], 2),
         moved(here[3], 1),
+        moved(there[2], 2, flip_x=True),
         moved(there[3], 1, flip_x=True),
+        moved(total(kept, beside), -1),
     ]
     hvp, quad = pl.pallas_call(
         finish_kernel,

time: 60.4 us -> 59.4 us (0.983)
  Pallas kernels: 18.1 us -> 15.1 us
  waiting for transfers between devices: 25.2 us -> 26.3 us
  starting transfers between devices: 16.2 us -> 17.2 us
    pallas_call x3 -> x2, Pallas kernels: 13.5 us -> 10.4 us  [experts(): pl.pallas_call(functools.partial(expert_kernel, count, expert_count), out...]
    ppermute x15, waiting for transfers between devices: 25.2 us -> 26.3 us  [moved(): return lax.ppermute(rows, 'expert', pairs)]
    ppermute x15, starting transfers between devices: 16.2 us -> 17.2 us  [moved(): return lax.ppermute(rows, 'expert', pairs)]
  transfers between devices with their start and end apart: 15 -> 15, of which waited for: 9 -> 8; matrix products, arithmetic and copies ran while one was open for 0% -> 0% of each run, Pallas kernels for 28% -> 24%
where the time goes in v8:
time: 59.4 us; the launch traced here: 59.3 us
  waiting for transfers between devices  26.3 us (44%)
  starting transfers between devices  17.2 us (29%)
  Pallas kernels  15.1 us (25%)
  between operations  0.69 us (1%)
    ppermute x15, waiting for transfers between devices, moved(): return lax.ppermute(rows, 'expert', pairs)  26.3 us
    ppermute x15, starting transfers between devices, moved(): return lax.ppermute(rows, 'expert', pairs)  17.2 us
    pallas_call x2, Pallas kernels, experts(): pl.pallas_call(functools.partial(expert_kernel, count, expert_count), out...  10.4 us
    pallas_call x1, Pallas kernels, joined(): pl.pallas_call(join_kernel, out_shape=pltpu.VMEM((parts, width, 2 * half)...  2.41 us
    pallas_call x1, Pallas kernels, packed(): pl.pallas_call(functools.partial(pack_kernel, expert_count), out_shape=ja...  1.29 us
  transfers between devices with their start and end apart: 15, of which 8 were waited for; matrix products, arithmetic and copies ran while one was open for 0% of the time, Pallas kernels for 24%

profile of v8, /device:TPU:0, one launch (start us, length us, event | category | flops | bytes accessed | tf_op | source)
XLA Modules:
  0.0 59.3 jit_solution(866140965417616235)
XLA Ops:
  0.6 0.5 collective-permute-start.2
  1.1 1.3 %shard_map.86.refs_0_ = bf16[24,6272]{1,0:T(8,128)(2,1)S(1)} custom-call(bf16[24,2048]{1,0:T(8,128)(2,1)} %tokens.1, f32[1,2048]{1,0:T(1,128)} %bitcast.4, s32[24,2048]{1,0:T(8,128)} %signs.1, bf16[24,2048]{1,0:T(8,128)(2,1)} %refs_3_.1, s32[2,4,24]{2,1,0:T(4,128)} %bitcast.6, f32[2,4,24]{2,1,0:T(4,128)} %bitcast.7), custom_call_target="tpu_custom_call" | custom-call | flops 983040 | bytes 688128 | tf_op jit(solution)/shard_map/pallas_call | solution.py:126
  2.4 2.6 %collective-permute-start.1 = (bf16[24,6272]{1,0:T(8,128)(2,1)S(1)}, bf16[24,6272]{1,0:T(8,128)(2,1)S(1)}, u32[]{:S(2)}, u32[]{:S(2)}) collective-permute-start(bf16[24,6272]{1,0:T(8,128)(2,1)S(1)} %shard_map.86.refs_0_), channel_id=1, source_target_pairs={{0,2},{1,3},{2,0},{3,1},{4,6},{5,7},{6,4},{7,5},{8,10},{9,11},{10,... | collective-permute-start | bytes 903176 | tf_op jit(solution)/shard_map/ppermute | solution.py:297
  5.0 1.6 %collective-permute-start = (bf16[24,6272]{1,0:T(8,128)(2,1)S(1)}, bf16[24,6272]{1,0:T(8,128)(2,1)S(1)}, u32[]{:S(2)}, u32[]{:S(2)}) collective-permute-start(bf16[24,6272]{1,0:T(8,128)(2,1)S(1)} %shard_map.86.refs_0_), channel_id=1, source_target_pairs={{0,4},{1,5},{2,6},{3,7},{4,8},{5,9},{6,10},{7,11},{8,12},{9,13},{1... | collective-permute-start | bytes 903176 | tf_op jit(solution)/shard_map/ppermute | solution.py:297
  6.6 2.2 %collective-permute-start.4 = (bf16[24,6272]{1,0:T(8,128)(2,1)S(1)}, bf16[24,6272]{1,0:T(8,128)(2,1)S(1)}, u32[]{:S(2)}, u32[]{:S(2)}) collective-permute-start(bf16[24,6272]{1,0:T(8,128)(2,1)S(1)} %shard_map.86.refs_0_), channel_id=1, source_target_pairs={{0,12},{1,13},{2,14},{3,15},{4,0},{5,1},{6,2},{7,3},{8,4},{9,5},{1... | collective-permute-start | bytes 903176 | tf_op jit(solution)/shard_map/ppermute | solution.py:297
  8.8 0.0 collective-permute-done.2.other
  8.9 2.4 %shard_map.87.refs_6_.refs_2_ = bf16[3,2048,768]{2,1,0:T(8,128)(2,1)S(1)} custom-call(bf16[3,2048,384]{2,1,0:T(8,128)(2,1)} %own.1, bf16[3,2048,384]{2,1,0:T(8,128)(2,1)S(1)} %collective-permute-done.2.other), custom_call_target="tpu_custom_call" | custom-call | bytes 18874368 | tf_op jit(solution)/shard_map/pallas_call | solution.py:157
  11.3 1.5 %collective-permute-done.1.refs_4_ = bf16[24,6272]{1,0:T(8,128)(2,1)S(1)} collective-permute-done((bf16[24,6272]{1,0:T(8,128)(2,1)S(1)}, bf16[24,6272]{1,0:T(8,128)(2,1)S(1)}, u32[]{:S(2)}, u32[]{:S(2)}) %collective-permute-start.1) | collective-permute-done | bytes 301088 | tf_op jit(solution)/shard_map/ppermute | solution.py:297
  12.8 4.0 %collective-permute-done.refs_1_ = bf16[24,6272]{1,0:T(8,128)(2,1)S(1)} collective-permute-done((bf16[24,6272]{1,0:T(8,128)(2,1)S(1)}, bf16[24,6272]{1,0:T(8,128)(2,1)S(1)}, u32[]{:S(2)}, u32[]{:S(2)}) %collective-permute-start) | collective-permute-done | bytes 301088 | tf_op jit(solution)/shard_map/ppermute | solution.py:297
  16.8 0.3 collective-permute-start.5
  17.1 0.0 collective-permute-start.3
  17.1 4.9 %collective-permute-done.4.refs_3_ = bf16[24,6272]{1,0:T(8,128)(2,1)S(1)} collective-permute-done((bf16[24,6272]{1,0:T(8,128)(2,1)S(1)}, bf16[24,6272]{1,0:T(8,128)(2,1)S(1)}, u32[]{:S(2)}, u32[]{:S(2)}) %collective-permute-start.4) | collective-permute-done | bytes 301088 | tf_op jit(solution)/shard_map/ppermute | solution.py:297
  22.1 0.5 collective-permute-start.10
  22.6 2.7 %collective-permute-done.5.refs_5_ = bf16[24,6272]{1,0:T(8,128)(2,1)S(1)} collective-permute-done((bf16[24,6272]{1,0:T(8,128)(2,1)S(1)}, bf16[24,6272]{1,0:T(8,128)(2,1)S(1)}, u32[]{:S(2)}, u32[]{:S(2)}) %collective-permute-start.5) | collective-permute-done | bytes 301088 | tf_op jit(solution)/shard_map/ppermute | solution.py:297
  25.2 0.0 collective-permute-start.9
  25.2 6.0 %collective-permute-done.3.refs_2_ = bf16[24,6272]{1,0:T(8,128)(2,1)S(1)} collective-permute-done((bf16[24,6272]{1,0:T(8,128)(2,1)S(1)}, bf16[24,6272]{1,0:T(8,128)(2,1)S(1)}, u32[]{:S(2)}, u32[]{:S(2)}) %collective-permute-start.3) | collective-permute-done | bytes 301088 | tf_op jit(solution)/shard_map/ppermute | solution.py:297
  31.2 6.2 %shard_map.88 = (f32[24,2176]{1,0:T(8,128)S(1)}, f32[24,2176]{1,0:T(8,128)S(1)}, bf16[24,2176]{1,0:T(8,128)(2,1)S(1)}, bf16[24,2176]{1,0:T(8,128)(2,1)S(1)}, bf1...) custom-call(bf16[24,6272]{1,0:T(8,128)(2,1)S(1)} %shard_map.86.refs_0_, ...), custom_call_target="tpu_custom_call" | custom-call | flops 4076863488 | bytes 9437184 | tf_op jit(solution)/shard_map/pallas_call | solution.py:251
  37.4 1.8 %collective-permute-start.13 = (bf16[24,2176]{1,0:T(8,128)(2,1)S(1)}, bf16[24,2176]{1,0:T(8,128)(2,1)S(1)}, u32[]{:S(2)}, u32[]{:S(2)}) collective-permute-start(bf16[24,2176]{1,0:T(8,128)(2,1)S(1)} %get-tuple-element.27), channel_id=1, source_target_pairs={{0,2},{1,3},{2,0},{3,1},{4,6},{5,7},{6,4},{7,5},{8,10},{9,11},{10,... | collective-permute-start | bytes 313352 | tf_op jit(solution)/shard_map/ppermute | solution.py:297
  39.2 0.3 collective-permute-start.6
  39.5 1.9 %collective-permute-start.7 = (bf16[24,2176]{1,0:T(8,128)(2,1)S(1)}, bf16[24,2176]{1,0:T(8,128)(2,1)S(1)}, u32[]{:S(2)}, u32[]{:S(2)}) collective-permute-start(bf16[24,2176]{1,0:T(8,128)(2,1)S(1)} %get-tuple-element.19), channel_id=1, source_target_pairs={{0,8},{1,9},{2,10},{3,11},{4,12},{5,13},{6,14},{7,15},{8,0},{9,1},... | collective-permute-start | bytes 313352 | tf_op jit(solution)/shard_map/ppermute | solution.py:297
  41.4 0.0 collective-permute-done.10.refs_1_
  41.4 1.4 %collective-permute-start.8 = (bf16[24,2176]{1,0:T(8,128)(2,1)S(1)}, bf16[24,2176]{1,0:T(8,128)(2,1)S(1)}, u32[]{:S(2)}, u32[]{:S(2)}) collective-permute-start(bf16[24,2176]{1,0:T(8,128)(2,1)S(1)} %get-tuple-element.20), channel_id=1, source_target_pairs={{0,4},{1,5},{2,6},{3,7},{4,8},{5,9},{6,10},{7,11},{8,12},{9,13},{1... | collective-permute-start | bytes 313352 | tf_op jit(solution)/shard_map/ppermute | solution.py:297
  42.9 0.0 collective-permute-done.9.refs_0_
  42.9 0.0 copy-start
  42.9 0.0 copy-start.1
  42.9 0.0 copy-start.2
  42.9 4.2 %shard_map.89 = (bf16[24,2176]{1,0:T(8,128)(2,1)S(1)}, bf16[24,2176]{1,0:T(8,128)(2,1)S(1)}) custom-call(bf16[24,6272]{1,0:T(8,128)(2,1)S(1)} %collective-permute-done.9.refs_0_, bf16[24,6272]{1,0:T(8,128)(2,1)S(1)} %collective-permute-done.10.refs_1_, bf16[3,2048,768]{2,1,0:T(8,128)(2,1)S(1)} %shard_map.87.refs_6_.refs_2_), custom_call_target="tpu_custom_call" | custom-call | flops 1358954496 | bytes 9437184 | tf_op jit(solution)/shard_map/pallas_call | solution.py:251
  47.1 0.9 %collective-permute-start.11 = (bf16[24,2176]{1,0:T(8,128)(2,1)S(1)}, bf16[24,2176]{1,0:T(8,128)(2,1)S(1)}, u32[]{:S(2)}, u32[]{:S(2)}) collective-permute-start(bf16[24,2176]{1,0:T(8,128)(2,1)S(1)} %get-tuple-element.24), channel_id=1, source_target_pairs={{0,10},{1,11},{2,8},{3,9},{4,14},{5,15},{6,12},{7,13},{8,2},{9,3},... | collective-permute-start | bytes 313352 | tf_op jit(solution)/shard_map/ppermute | solution.py:297
  48.0 0.0 collective-permute-done.13
  48.0 2.9 %collective-permute-start.14 = (bf16[24,2176]{1,0:T(8,128)(2,1)S(1)}, bf16[24,2176]{1,0:T(8,128)(2,1)S(1)}, u32[]{:S(2)}, u32[]{:S(2)}) collective-permute-start(bf16[24,2176]{1,0:T(8,128)(2,1)S(1)} %add_convert_fusion), channel_id=1, source_target_pairs={{0,12},{1,13},{2,14},{3,15},{4,0},{5,1},{6,2},{7,3},{8,4},{9,5},{1... | collective-permute-start | bytes 313352 | tf_op jit(solution)/shard_map/ppermute | solution.py:297
  50.9 0.0 collective-permute-done.6.refs_1_
  50.9 0.3 collective-permute-start.12
  51.2 0.0 collective-permute-done.7.refs_2_
  51.2 0.0 collective-permute-done.8.refs_3_
  51.2 2.4 %collective-permute-done.14.refs_6_ = bf16[24,2176]{1,0:T(8,128)(2,1)S(1)} collective-permute-done((bf16[24,2176]{1,0:T(8,128)(2,1)S(1)}, bf16[24,2176]{1,0:T(8,128)(2,1)S(1)}, u32[]{:S(2)}, u32[]{:S(2)}) %collective-permute-start.14) | collective-permute-done | bytes 104480 | tf_op jit(solution)/shard_map/ppermute | solution.py:297
  53.6 1.0 %collective-permute-done.11.refs_4_ = bf16[24,2176]{1,0:T(8,128)(2,1)S(1)} collective-permute-done((bf16[24,2176]{1,0:T(8,128)(2,1)S(1)}, bf16[24,2176]{1,0:T(8,128)(2,1)S(1)}, u32[]{:S(2)}, u32[]{:S(2)}) %collective-permute-start.11) | collective-permute-done | bytes 104480 | tf_op jit(solution)/shard_map/ppermute | solution.py:297
  54.6 3.7 %collective-permute-done.12.refs_5_ = bf16[24,2176]{1,0:T(8,128)(2,1)S(1)} collective-permute-done((bf16[24,2176]{1,0:T(8,128)(2,1)S(1)}, bf16[24,2176]{1,0:T(8,128)(2,1)S(1)}, u32[]{:S(2)}, u32[]{:S(2)}) %collective-permute-start.12) | collective-permute-done | bytes 104480 | tf_op jit(solution)/shard_map/ppermute | solution.py:297
  58.3 0.0 copy-done
  58.3 0.0 copy-done.1
  58.3 0.0 copy-done.2
  58.3 1.0 %shard_map.90 = (f32[24,2048]{1,0:T(8,128)}, f32[1,24]{1,0:T(1,128)}) custom-call(bf16[24,2048]{1,0:T(8,128)(2,1)S(1)} %copy-done.1, f32[1,2048]{1,0:T(1,128)S(1)} %bitcast.5, s32[24,2048]{1,0:T(8,128)S(1)} %copy-done, f32[24,2176]{1,0:T(8,128)S(1)} %get-tuple-element.17.refs_0_, bf16[24,2176]{1,0:T(8,128)(2,1)S(1)} %collective-permute-done.6.refs_1_, ...), custom_call_target="tpu_custom_call" | custom-call | flops 1966080 | bytes 1277952 | tf_op jit(solution)/shard_map/pallas_call | solution.py:343
  (1 shorter events, 0.0 us)
Async XLA Ops:
  0.6 8.3 %collective-permute-start.2 = (bf16[3,2048,384]{2,1,0:T(8,128)(2,1)}, bf16[3,2048,384]{2,1,0:T(8,128)(2,1)S(1)}, u32[]{:S(2)}, u32[]{:S(2)}) collective-permute-start(bf16[3,2048,384]{2,1,0:T(8,128)(2,1)} %own.1), channel_id=1, source_target_pairs={{0,1},{1,0},{2,3},{3,2},{4,5},{5,4},{6,7},{7,6},{8,9},{9,8},{10,11... | collective-permute-start | bytes 14155784 | tf_op jit(solution)/shard_map/ppermute | solution.py:297
  2.4 10.4 %collective-permute-start.1 = (bf16[24,6272]{1,0:T(8,128)(2,1)S(1)}, bf16[24,6272]{1,0:T(8,128)(2,1)S(1)}, u32[]{:S(2)}, u32[]{:S(2)}) collective-permute-start(bf16[24,6272]{1,0:T(8,128)(2,1)S(1)} %shard_map.86.refs_0_), channel_id=1, source_target_pairs={{0,2},{1,3},{2,0},{3,1},{4,6},{5,7},{6,4},{7,5},{8,10},{9,11},{10,... | collective-permute-start | bytes 903176 | tf_op jit(solution)/shard_map/ppermute | solution.py:297
  5.0 11.8 %collective-permute-start = (bf16[24,6272]{1,0:T(8,128)(2,1)S(1)}, bf16[24,6272]{1,0:T(8,128)(2,1)S(1)}, u32[]{:S(2)}, u32[]{:S(2)}) collective-permute-start(bf16[24,6272]{1,0:T(8,128)(2,1)S(1)} %shard_map.86.refs_0_), channel_id=1, source_target_pairs={{0,4},{1,5},{2,6},{3,7},{4,8},{5,9},{6,10},{7,11},{8,12},{9,13},{1... | collective-permute-start | bytes 903176 | tf_op jit(solution)/shard_map/ppermute | solution.py:297
  6.6 15.5 %collective-permute-start.4 = (bf16[24,6272]{1,0:T(8,128)(2,1)S(1)}, bf16[24,6272]{1,0:T(8,128)(2,1)S(1)}, u32[]{:S(2)}, u32[]{:S(2)}) collective-permute-start(bf16[24,6272]{1,0:T(8,128)(2,1)S(1)} %shard_map.86.refs_0_), channel_id=1, source_target_pairs={{0,12},{1,13},{2,14},{3,15},{4,0},{5,1},{6,2},{7,3},{8,4},{9,5},{1... | collective-permute-start | bytes 903176 | tf_op jit(solution)/shard_map/ppermute | solution.py:297
  16.8 8.4 %collective-permute-start.5 = (bf16[24,6272]{1,0:T(8,128)(2,1)S(1)}, bf16[24,6272]{1,0:T(8,128)(2,1)S(1)}, u32[]{:S(2)}, u32[]{:S(2)}) collective-permute-start(bf16[24,6272]{1,0:T(8,128)(2,1)S(1)} %collective-permute-done.refs_1_), channel_id=1, source_target_pairs={{0,2},{1,3},{2,0},{3,1},{4,6},{5,7},{6,4},{7,5},{8,10},{9,11},{10,... | collective-permute-start | bytes 903176 | tf_op jit(solution)/shard_map/ppermute | solution.py:297
  17.1 14.1 %collective-permute-start.3 = (bf16[24,6272]{1,0:T(8,128)(2,1)S(1)}, bf16[24,6272]{1,0:T(8,128)(2,1)S(1)}, u32[]{:S(2)}, u32[]{:S(2)}) collective-permute-start(bf16[24,6272]{1,0:T(8,128)(2,1)S(1)} %collective-permute-done.refs_1_), channel_id=1, source_target_pairs={{0,4},{1,5},{2,6},{3,7},{4,8},{5,9},{6,10},{7,11},{8,12},{9,13},{1... | collective-permute-start | bytes 903176 | tf_op jit(solution)/shard_map/ppermute | solution.py:297
  22.1 19.4 %collective-permute-start.10 = (bf16[24,6272]{1,0:T(8,128)(2,1)S(1)}, bf16[24,6272]{1,0:T(8,128)(2,1)S(1)}, u32[]{:S(2)}, u32[]{:S(2)}) collective-permute-start(bf16[24,6272]{1,0:T(8,128)(2,1)S(1)} %collective-permute-done.4.refs_3_), channel_id=1, source_target_pairs={{0,2},{1,3},{2,0},{3,1},{4,6},{5,7},{6,4},{7,5},{8,10},{9,11},{10,... | collective-permute-start | bytes 903176 | tf_op jit(solution)/shard_map/ppermute | solution.py:297
  25.2 17.6 %collective-permute-start.9 = (bf16[24,6272]{1,0:T(8,128)(2,1)S(1)}, bf16[24,6272]{1,0:T(8,128)(2,1)S(1)}, u32[]{:S(2)}, u32[]{:S(2)}) collective-permute-start(bf16[24,6272]{1,0:T(8,128)(2,1)S(1)} %collective-permute-done.5.refs_5_), channel_id=1, source_target_pairs={{0,4},{1,5},{2,6},{3,7},{4,8},{5,9},{6,10},{7,11},{8,12},{9,13},{1... | collective-permute-start | bytes 903176 | tf_op jit(solution)/shard_map/ppermute | solution.py:297
  37.4 10.6 %collective-permute-start.13 = (bf16[24,2176]{1,0:T(8,128)(2,1)S(1)}, bf16[24,2176]{1,0:T(8,128)(2,1)S(1)}, u32[]{:S(2)}, u32[]{:S(2)}) collective-permute-start(bf16[24,2176]{1,0:T(8,128)(2,1)S(1)} %get-tuple-element.27), channel_id=1, source_target_pairs={{0,2},{1,3},{2,0},{3,1},{4,6},{5,7},{6,4},{7,5},{8,10},{9,11},{10,... | collective-permute-start | bytes 313352 | tf_op jit(solution)/shard_map/ppermute | solution.py:297
  39.2 11.7 %collective-permute-start.6 = (bf16[24,2176]{1,0:T(8,128)(2,1)S(1)}, bf16[24,2176]{1,0:T(8,128)(2,1)S(1)}, u32[]{:S(2)}, u32[]{:S(2)}) collective-permute-start(bf16[24,2176]{1,0:T(8,128)(2,1)S(1)} %get-tuple-element.18), channel_id=1, source_target_pairs={{0,2},{1,3},{2,0},{3,1},{4,6},{5,7},{6,4},{7,5},{8,10},{9,11},{10,... | collective-permute-start | bytes 313352 | tf_op jit(solution)/shard_map/ppermute | solution.py:297
  39.5 11.7 %collective-permute-start.7 = (bf16[24,2176]{1,0:T(8,128)(2,1)S(1)}, bf16[24,2176]{1,0:T(8,128)(2,1)S(1)}, u32[]{:S(2)}, u32[]{:S(2)}) collective-permute-start(bf16[24,2176]{1,0:T(8,128)(2,1)S(1)} %get-tuple-element.19), channel_id=1, source_target_pairs={{0,8},{1,9},{2,10},{3,11},{4,12},{5,13},{6,14},{7,15},{8,0},{9,1},... | collective-permute-start | bytes 313352 | tf_op jit(solution)/shard_map/ppermute | solution.py:297
  41.4 9.7 %collective-permute-start.8 = (bf16[24,2176]{1,0:T(8,128)(2,1)S(1)}, bf16[24,2176]{1,0:T(8,128)(2,1)S(1)}, u32[]{:S(2)}, u32[]{:S(2)}) collective-permute-start(bf16[24,2176]{1,0:T(8,128)(2,1)S(1)} %get-tuple-element.20), channel_id=1, source_target_pairs={{0,4},{1,5},{2,6},{3,7},{4,8},{5,9},{6,10},{7,11},{8,12},{9,13},{1... | collective-permute-start | bytes 313352 | tf_op jit(solution)/shard_map/ppermute | solution.py:297
  42.9 15.4 %copy-start = (s32[24,2048]{1,0:T(8,128)S(1)}, s32[24,2048]{1,0:T(8,128)}, u32[]{:S(2)}) copy-start(s32[24,2048]{1,0:T(8,128)} %signs.1) | copy-start | bytes 589828
  42.9 15.4 %copy-start.1 = (bf16[24,2048]{1,0:T(8,128)(2,1)S(1)}, bf16[24,2048]{1,0:T(8,128)(2,1)}, u32[]{:S(2)}) copy-start(bf16[24,2048]{1,0:T(8,128)(2,1)} %tokens.1) | copy-start | bytes 294916
  42.9 15.4 %copy-start.2 = (f32[2048]{0:T(1024)S(1)}, f32[2048]{0:T(1024)}, u32[]{:S(2)}) copy-start(f32[2048]{0:T(1024)} %param.8) | copy-start | bytes 24580
  47.1 7.5 %collective-permute-start.11 = (bf16[24,2176]{1,0:T(8,128)(2,1)S(1)}, bf16[24,2176]{1,0:T(8,128)(2,1)S(1)}, u32[]{:S(2)}, u32[]{:S(2)}) collective-permute-start(bf16[24,2176]{1,0:T(8,128)(2,1)S(1)} %get-tuple-element.24), channel_id=1, source_target_pairs={{0,10},{1,11},{2,8},{3,9},{4,14},{5,15},{6,12},{7,13},{8,2},{9,3},... | collective-permute-start | bytes 313352 | tf_op jit(solution)/shard_map/ppermute | solution.py:297
  48.0 5.5 %collective-permute-start.14 = (bf16[24,2176]{1,0:T(8,128)(2,1)S(1)}, bf16[24,2176]{1,0:T(8,128)(2,1)S(1)}, u32[]{:S(2)}, u32[]{:S(2)}) collective-permute-start(bf16[24,2176]{1,0:T(8,128)(2,1)S(1)} %add_convert_fusion), channel_id=1, source_target_pairs={{0,12},{1,13},{2,14},{3,15},{4,0},{5,1},{6,2},{7,3},{8,4},{9,5},{1... | collective-permute-start | bytes 313352 | tf_op jit(solution)/shard_map/ppermute | solution.py:297
  50.9 7.4 %collective-permute-start.12 = (bf16[24,2176]{1,0:T(8,128)(2,1)S(1)}, bf16[24,2176]{1,0:T(8,128)(2,1)S(1)}, u32[]{:S(2)}, u32[]{:S(2)}) collective-permute-start(bf16[24,2176]{1,0:T(8,128)(2,1)S(1)} %get-tuple-element.25), channel_id=1, source_target_pairs={{0,6},{1,7},{2,4},{3,5},{4,10},{5,11},{6,8},{7,9},{8,14},{9,15},{1... | collective-permute-start | bytes 313352 | tf_op jit(solution)/shard_map/ppermute | solution.py:297

commit v9 on v7

--- a/solution.py
+++ b/solution.py
@@ -167,20 +167,28 @@
     )(pltpu.with_memory_space_constraint(own, pltpu.HBM), other)
 
 
-def expert_kernel(count, expert_count, *refs):
-    packs, held, outs = (refs[:count], refs[count], refs[count + 1 : 2 * count + 1])
-    both, cotan, acc = refs[2 * count + 1 :]
-    tok_dev = packs[0].shape[0]
+def expert_kernel(expert_count, gathered, held, *refs):
+    count, tok_dev, lanes = gathered.shape
+    outs, both, cotan, acc = (refs[:count], *refs[count:])
     _, width, hidden = held.shape
+    turns = count // 2
+    place = lax.axis_index("expert") // 2
+    places = [
+        lax.rem(place // 2 + turns - k, turns) * 2 + (lax.rem(place, 2) + flip) % 2
+        for flip in range(2)
+        for k in range(turns)
+    ]
     rows = count * tok_dev
 
     def stacked(start, size):
-        return jnp.concatenate([p[:, start : start + size].astype(jnp.float32) for p in packs], 0)
+        return jnp.concatenate(
+            [gathered[place, :, start : start + size].astype(jnp.float32) for place in places], 0
+        )
 
     both[:rows, :] = stacked(0, width).astype(jnp.bfloat16)
     both[rows:, :] = stacked(width, width).astype(jnp.bfloat16)
     cotan[...] = stacked(2 * width, width).astype(jnp.bfloat16)
-    tail = stacked(3 * width, packs[0].shape[1] - 3 * width)
+    tail = stacked(3 * width, lanes - 3 * width)
     mine = lax.axis_index("expert") // 2
     lane = lax.broadcasted_iota(jnp.int32, tail.shape, 1)
     after = 2 * expert_count
@@ -231,8 +239,8 @@
         later = slice(rows + n * tok_dev, rows + (n + 1) * tok_dev)
         grad, tan = (acc[part] * gate_row[part], acc[later] * gate_row[part])
         scale, slope_r = (scale_row[part], slope_row[part])
-        normed = packs[n][:, :width].astype(jnp.float32)
-        normed_t = packs[n][:, width : 2 * width].astype(jnp.float32)
+        normed = gathered[places[n], :, :width].astype(jnp.float32)
+        normed_t = gathered[places[n], :, width : 2 * width].astype(jnp.float32)
         outs[n][:, :width] = (scale * tan + slope_r * grad).astype(outs[n].dtype)
         first = jnp.mean(normed * grad, axis=1, keepdims=True)
         second = jnp.mean(normed * tan + normed_t * grad, axis=1, keepdims=True)
@@ -242,16 +250,15 @@
         outs[n][:, width:] = sums.astype(outs[n].dtype)
 
 
-def experts(packs, kinds, held, expert_count):
-    count = len(packs)
-    tok_dev = packs[0].shape[0]
+def experts(gathered, kinds, held, expert_count):
+    count, tok_dev, _ = gathered.shape
     _, width, hidden = held.shape
     rows = count * tok_dev
     whole = pl.BlockSpec(memory_space=pltpu.VMEM)
     return pl.pallas_call(
-        functools.partial(expert_kernel, count, expert_count),
+        functools.partial(expert_kernel, expert_count),
         out_shape=[jax.ShapeDtypeStruct((tok_dev, width + 128), kind) for kind in kinds],
-        in_specs=[whole] * (count + 1),
+        in_specs=[whole] * 2,
         out_specs=[whole] * count,
         scratch_shapes=[
             pltpu.VMEM((2 * rows, width), jnp.bfloat16),
@@ -264,7 +271,7 @@
             bytes_accessed=6 * width * hidden,
             transcendentals=rows * hidden,
         ),
-    )(*packs, pltpu.with_memory_space_constraint(held, pltpu.VMEM))
+    )(gathered, pltpu.with_memory_space_constraint(held, pltpu.VMEM))
 
 
 def finish_kernel(tokens, gain, signs, *refs):
@@ -303,40 +310,22 @@
     expert_count = n_exp // 2
     pack = packed(tokens, norm_gain, probe_signs, cotangent, routes, gates, expert_count)
     held = joined(weights, moved(weights, 0, flip_core=True))
-    same, across = {0: pack}, {}
-    same[1] = moved(pack, 1)
-    across[0] = moved(pack, 0, flip_x=True)
-    same[1] = lax.optimization_barrier((same[1], across[0], held))[0]
-    same[2] = moved(same[1], 1)
-    across[1] = moved(same[1], 0, flip_x=True)
-    same[3] = moved(lax.optimization_barrier((pack, same[1]))[0], -1)
-    across[2] = moved(same[2], 0, flip_x=True)
-    across[3] = moved(lax.optimization_barrier((across[0], same[2]))[0], -1)
+    parity = [list(range(core, n_exp, 2)) for core in range(2)]
+    gathered = lax.all_gather(pack, "expert", axis_index_groups=parity)
     wide, sent = (jnp.float32, jnp.bfloat16)
-    here, there = {}, {}
-    here[0], here[1], there[0], there[1] = experts(
-        [same[0], same[1], across[0], across[1]], [wide, wide, sent, sent], held, expert_count
-    )
-    far = lax.optimization_barrier((across[2], here[1]))[0]
-    here[2], here[3], there[2] = experts(
-        [same[2], same[3], far], [wide, sent, sent], held, expert_count
-    )
-    last = lax.optimization_barrier((across[3], here[2]))[0]
-    (there[3],) = experts([last], [sent], held, expert_count)
-
-    def flipped(rows):
-        return moved(rows, 0, flip_x=True)
+    results = experts(gathered, [wide] * 4 + [sent] * 4, held, expert_count)
+    here, there = (results[:4], results[4:])
 
     def total(*parts):
         return sum(part.astype(jnp.float32) for part in parts).astype(jnp.bfloat16)
 
+    beside = {k: moved(there[k], 0, flip_x=True) for k in (2, 1, 3, 0)}
+    forward = moved(total(here[2], beside[2]), -1)
     arrived = [
         here[0],
-        flipped(there[0]),
-        moved(total(here[1], flipped(there[1])), -1),
-        moved(total(here[2], flipped(there[2])), 2),
-        moved(here[3], 1),
-        moved(there[3], 1, flip_x=True),
+        beside[0],
+        moved(total(here[1], beside[1], forward), -1),
+        moved(total(here[3], beside[3]), 1),
     ]
     hvp, quad = pl.pallas_call(
         finish_kernel,

time: 60.4 us -> 105 us (1.74)
  waiting for transfers between devices: 25.2 us -> 55.8 us
  between operations: 0.7 us -> 14.1 us
  local copies, waits for them, and re-layouts: 0.01 us -> 9.02 us
  starting transfers between devices: 16.2 us -> 10.8 us
  Pallas kernels: 18.1 us -> 14.5 us
    all_gather x0 -> x1, waiting for transfers between devices: none -> 42.5 us  [dense_local(): gathered = lax.all_gather(pack, 'expert', axis_index_groups=parity)]
    ppermute x15 -> x8, waiting for transfers between devices: 25.2 us -> 13.3 us  [moved(): return lax.ppermute(rows, 'expert', pairs)]
    unnamed x6 -> x12, local copies, waits for them, and re-layouts: 0.01 us -> 9.02 us
    pallas_call x3 -> x1, Pallas kernels: 13.5 us -> 7.79 us  [experts(): pl.pallas_call(functools.partial(expert_kernel, expert_count), out_shape=...]
    ppermute x15 -> x8, starting transfers between devices: 16.2 us -> 10.8 us  [moved(): return lax.ppermute(rows, 'expert', pairs)]
    pallas_call x1, Pallas kernels: 2.41 us -> 3.79 us  [joined(): pl.pallas_call(join_kernel, out_shape=pltpu.VMEM((parts, width, 2 * half)...]
  transfers between devices with their start and end apart: 15 -> 9, of which waited for: 9 -> 6; matrix products, arithmetic and copies ran while one was open for 0% -> 0% of each run, Pallas kernels for 28% -> 6%
where the time goes in v9:
time: 105 us; the launch traced here: 104 us
  waiting for transfers between devices  55.8 us (53%)
  Pallas kernels  14.5 us (14%)
  between operations  14.1 us (13%)
  starting transfers between devices  10.8 us (10%)
  local copies, waits for them, and re-layouts  9.02 us (9%)
    all_gather x1, waiting for transfers between devices, dense_local(): gathered = lax.all_gather(pack, 'expert', axis_index_groups=parity)  42.5 us
    ppermute x8, waiting for transfers between devices, moved(): return lax.ppermute(rows, 'expert', pairs)  13.3 us
    ppermute x8, starting transfers between devices, moved(): return lax.ppermute(rows, 'expert', pairs)  10.8 us
    unnamed x12, local copies, waits for them, and re-layouts  9.02 us
    pallas_call x1, Pallas kernels, experts(): pl.pallas_call(functools.partial(expert_kernel, expert_count), out_shape=...  7.79 us
    pallas_call x1, Pallas kernels, joined(): pl.pallas_call(join_kernel, out_shape=pltpu.VMEM((parts, width, 2 * half)...  3.79 us
  transfers between devices with their start and end apart: 9, of which 6 were waited for; matrix products, arithmetic and copies ran while one was open for 0% of the time, Pallas kernels for 6%

profile of v9, /device:TPU:0, one launch (start us, length us, event | category | flops | bytes accessed | tf_op | source)
XLA Modules:
  0.0 104.3 jit_solution(9650258655561700449)
XLA Ops:
  7.2 0.0 all-gather.3.cloned.1.call-start
  7.2 0.5 collective-permute-start
  7.7 2.0 %shard_map.86 = bf16[24,6272]{1,0:T(8,128)(2,1)} custom-call(bf16[24,2048]{1,0:T(8,128)(2,1)} %tokens.1, f32[1,2048]{1,0:T(1,128)} %bitcast.5, s32[24,2048]{1,0:T(8,128)} %signs.1, bf16[24,2048]{1,0:T(8,128)(2,1)} %refs_3_.1, s32[2,4,24]{2,1,0:T(4,128)} %bitcast.8, f32[2,4,24]{2,1,0:T(4,128)} %bitcast.9), custom_call_target="tpu_custom_call" | custom-call | flops 983040 | bytes 688128 | tf_op jit(solution)/shard_map/pallas_call | solution.py:126
  9.7 0.0 all-gather.3.cloned.1.call-update
  9.7 5.9 %collective-permute-done.other = bf16[3,2048,384]{2,1,0:T(8,128)(2,1)} collective-permute-done((bf16[3,2048,384]{2,1,0:T(8,128)(2,1)}, bf16[3,2048,384]{2,1,0:T(8,128)(2,1)}, u32[]{:S(2)}, u32[]{:S(2)}) %collective-permute-start) | collective-permute-done | bytes 4718624 | tf_op jit(solution)/shard_map/ppermute | solution.py:304
  15.6 3.8 %shard_map.87.held = bf16[3,2048,768]{2,1,0:T(8,128)(2,1)S(1)} custom-call(bf16[3,2048,384]{2,1,0:T(8,128)(2,1)} %own.1, bf16[3,2048,384]{2,1,0:T(8,128)(2,1)} %collective-permute-done.other), custom_call_target="tpu_custom_call" | custom-call | bytes 18874368 | tf_op jit(solution)/shard_map/pallas_call | solution.py:157
  19.4 0.0 copy-start
  19.4 3.6 %copy-done = bf16[3,2048,768]{2,1,0:T(8,128)(2,1)} copy-done((bf16[3,2048,768]{2,1,0:T(8,128)(2,1)}, bf16[3,2048,768]{2,1,0:T(8,128)(2,1)S(1)}, u32[]{:S(2)}) %copy-start) | copy-done | bytes 9437208
  23.1 42.5 %all-gather.3.cloned.1.call-done = bf16[192,6272]{1,0:T(8,128)(2,1)} async-done(((bf16[24,6272]{1,0:T(8,128)(2,1)}), bf16[192,6272]{1,0:T(8,128)(2,1)}) %all-gather.3.cloned.1.call-update) | async-done | bytes 2408464 | tf_op jit(solution)/shard_map/all_gather | solution.py:314
  65.5 0.0 copy-start.1
  65.5 3.7 %copy-done.1 = bf16[3,2048,768]{2,1,0:T(8,128)(2,1)S(1)} copy-done((bf16[3,2048,768]{2,1,0:T(8,128)(2,1)S(1)}, bf16[3,2048,768]{2,1,0:T(8,128)(2,1)}, u32[]{:S(2)}) %copy-start.1) | copy-done | bytes 9437208
  69.2 0.0 copy-start.5
  69.2 1.7 %copy-done.5 = bf16[192,6272]{1,0:T(8,128)(2,1)S(1)} copy-done((bf16[192,6272]{1,0:T(8,128)(2,1)S(1)}, bf16[192,6272]{1,0:T(8,128)(2,1)}, u32[]{:S(2)}) %copy-start.5) | copy-done | bytes 2408472
  70.9 0.0 copy-start.2
  70.9 0.0 copy-start.3
  70.9 0.0 copy-start.4
  70.9 7.8 %shard_map.88 = (f32[24,2176]{1,0:T(8,128)S(1)}, f32[24,2176]{1,0:T(8,128)S(1)}, f32[24,2176]{1,0:T(8,128)S(1)}, f32[24,2176]{1,0:T(8,128)S(1)}, bf16[24,2176]{1...) custom-call(bf16[8,24,6272]{2,1,0:T(8,128)(2,1)S(1)} %bitcast.7, ...), custom_call_target="tpu_custom_call" | custom-call | flops 5435817984 | bytes 9437184 | tf_op jit(solution)/shard_map/pallas_call | solution.py:258
  78.7 0.6 collective-permute-start.3
  79.3 1.5 %collective-permute-start.1 = (bf16[24,2176]{1,0:T(8,128)(2,1)S(1)}, bf16[24,2176]{1,0:T(8,128)(2,1)S(1)}, u32[]{:S(2)}, u32[]{:S(2)}) collective-permute-start(bf16[24,2176]{1,0:T(8,128)(2,1)S(1)} %get-tuple-element.13), channel_id=1, source_target_pairs={{0,2},{1,3},{2,0},{3,1},{4,6},{5,7},{6,4},{7,5},{8,10},{9,11},{10,... | collective-permute-start | bytes 313352 | tf_op jit(solution)/shard_map/ppermute | solution.py:304
  80.8 0.5 collective-permute-start.2
  81.3 1.5 %collective-permute-start.6 = (bf16[24,2176]{1,0:T(8,128)(2,1)S(1)}, bf16[24,2176]{1,0:T(8,128)(2,1)S(1)}, u32[]{:S(2)}, u32[]{:S(2)}) collective-permute-start(bf16[24,2176]{1,0:T(8,128)(2,1)S(1)} %get-tuple-element.19), channel_id=1, source_target_pairs={{0,2},{1,3},{2,0},{3,1},{4,6},{5,7},{6,4},{7,5},{8,10},{9,11},{10,... | collective-permute-start | bytes 313352 | tf_op jit(solution)/shard_map/ppermute | solution.py:304
  82.8 1.8 %collective-permute-done.3 = bf16[24,2176]{1,0:T(8,128)(2,1)S(1)} collective-permute-done((bf16[24,2176]{1,0:T(8,128)(2,1)S(1)}, bf16[24,2176]{1,0:T(8,128)(2,1)S(1)}, u32[]{:S(2)}, u32[]{:S(2)}) %collective-permute-start.3) | collective-permute-done | bytes 104480 | tf_op jit(solution)/shard_map/ppermute | solution.py:304
  84.7 1.9 %collective-permute-start.4 = (bf16[24,2176]{1,0:T(8,128)(2,1)S(1)}, bf16[24,2176]{1,0:T(8,128)(2,1)S(1)}, u32[]{:S(2)}, u32[]{:S(2)}) collective-permute-start(bf16[24,2176]{1,0:T(8,128)(2,1)S(1)} %add_convert_fusion.2), channel_id=1, source_target_pairs={{0,12},{1,13},{2,14},{3,15},{4,0},{5,1},{6,2},{7,3},{8,4},{9,5},{1... | collective-permute-start | bytes 313352 | tf_op jit(solution)/shard_map/ppermute | solution.py:304
  86.5 2.4 %collective-permute-done.6 = bf16[24,2176]{1,0:T(8,128)(2,1)S(1)} collective-permute-done((bf16[24,2176]{1,0:T(8,128)(2,1)S(1)}, bf16[24,2176]{1,0:T(8,128)(2,1)S(1)}, u32[]{:S(2)}, u32[]{:S(2)}) %collective-permute-start.6) | collective-permute-done | bytes 104480 | tf_op jit(solution)/shard_map/ppermute | solution.py:304
  89.0 1.6 %collective-permute-start.7 = (bf16[24,2176]{1,0:T(8,128)(2,1)S(1)}, bf16[24,2176]{1,0:T(8,128)(2,1)S(1)}, u32[]{:S(2)}, u32[]{:S(2)}) collective-permute-start(bf16[24,2176]{1,0:T(8,128)(2,1)S(1)} %add_convert_fusion), channel_id=1, source_target_pairs={{0,4},{1,5},{2,6},{3,7},{4,8},{5,9},{6,10},{7,11},{8,12},{9,13},{1... | collective-permute-start | bytes 313352 | tf_op jit(solution)/shard_map/ppermute | solution.py:304
  90.6 0.0 collective-permute-done.2
  90.6 0.0 collective-permute-done.4
  90.7 2.6 %collective-permute-start.5 = (bf16[24,2176]{1,0:T(8,128)(2,1)S(1)}, bf16[24,2176]{1,0:T(8,128)(2,1)S(1)}, u32[]{:S(2)}, u32[]{:S(2)}) collective-permute-start(bf16[24,2176]{1,0:T(8,128)(2,1)S(1)} %add_convert_fusion.1), channel_id=1, source_target_pairs={{0,12},{1,13},{2,14},{3,15},{4,0},{5,1},{6,2},{7,3},{8,4},{9,5},{1... | collective-permute-start | bytes 313352 | tf_op jit(solution)/shard_map/ppermute | solution.py:304
  93.3 0.0 collective-permute-done.1.refs_1_
  93.3 2.4 %collective-permute-done.7.refs_3_ = bf16[24,2176]{1,0:T(8,128)(2,1)S(1)} collective-permute-done((bf16[24,2176]{1,0:T(8,128)(2,1)S(1)}, bf16[24,2176]{1,0:T(8,128)(2,1)S(1)}, u32[]{:S(2)}, u32[]{:S(2)}) %collective-permute-start.7) | collective-permute-done | bytes 104480 | tf_op jit(solution)/shard_map/ppermute | solution.py:304
  95.7 0.9 collective-permute-done.5.refs_2_
  96.5 0.0 copy-done.2
  96.5 0.0 copy-done.3
  96.5 0.0 copy-done.4
  96.5 0.9 shard_map.89
  (3 shorter events, 0.1 us)
Async XLA Ops:
  7.2 58.4 %all-gather.3.cloned.1.call-start = ((), (), s32[]{:S(2)}) async-start(), calls=%async_computation | async-start | bytes 2709504 | tf_op jit(solution)/shard_map/all_gather | solution.py:314
  7.2 8.4 %collective-permute-start = (bf16[3,2048,384]{2,1,0:T(8,128)(2,1)}, bf16[3,2048,384]{2,1,0:T(8,128)(2,1)}, u32[]{:S(2)}, u32[]{:S(2)}) collective-permute-start(bf16[3,2048,384]{2,1,0:T(8,128)(2,1)} %own.1), channel_id=1, source_target_pairs={{0,1},{1,0},{2,3},{3,2},{4,5},{5,4},{6,7},{7,6},{8,9},{9,8},{10,11... | collective-permute-start | bytes 14155784 | tf_op jit(solution)/shard_map/ppermute | solution.py:304
  19.4 3.7 %copy-start = (bf16[3,2048,768]{2,1,0:T(8,128)(2,1)}, bf16[3,2048,768]{2,1,0:T(8,128)(2,1)S(1)}, u32[]{:S(2)}) copy-start(bf16[3,2048,768]{2,1,0:T(8,128)(2,1)S(1)} %shard_map.87.held) | copy-start | bytes 28311556
  65.5 3.7 %copy-start.1 = (bf16[3,2048,768]{2,1,0:T(8,128)(2,1)S(1)}, bf16[3,2048,768]{2,1,0:T(8,128)(2,1)}, u32[]{:S(2)}) copy-start(bf16[3,2048,768]{2,1,0:T(8,128)(2,1)} %copy-done) | copy-start | bytes 28311556
  69.2 1.7 %copy-start.5 = (bf16[192,6272]{1,0:T(8,128)(2,1)S(1)}, bf16[192,6272]{1,0:T(8,128)(2,1)}, u32[]{:S(2)}) copy-start(bf16[192,6272]{1,0:T(8,128)(2,1)} %all-gather.3.cloned.1.call-done) | copy-start | bytes 7225348
  70.9 25.6 %copy-start.2 = (s32[24,2048]{1,0:T(8,128)S(1)}, s32[24,2048]{1,0:T(8,128)}, u32[]{:S(2)}) copy-start(s32[24,2048]{1,0:T(8,128)} %signs.1) | copy-start | bytes 589828
  70.9 25.6 %copy-start.3 = (bf16[24,2048]{1,0:T(8,128)(2,1)S(1)}, bf16[24,2048]{1,0:T(8,128)(2,1)}, u32[]{:S(2)}) copy-start(bf16[24,2048]{1,0:T(8,128)(2,1)} %tokens.1) | copy-start | bytes 294916
  70.9 25.6 %copy-start.4 = (f32[2048]{0:T(1024)S(1)}, f32[2048]{0:T(1024)}, u32[]{:S(2)}) copy-start(f32[2048]{0:T(1024)} %param.8) | copy-start | bytes 24580
  78.7 5.9 %collective-permute-start.3 = (bf16[24,2176]{1,0:T(8,128)(2,1)S(1)}, bf16[24,2176]{1,0:T(8,128)(2,1)S(1)}, u32[]{:S(2)}, u32[]{:S(2)}) collective-permute-start(bf16[24,2176]{1,0:T(8,128)(2,1)S(1)} %get-tuple-element.17), channel_id=1, source_target_pairs={{0,2},{1,3},{2,0},{3,1},{4,6},{5,7},{6,4},{7,5},{8,10},{9,11},{10,... | collective-permute-start | bytes 313352 | tf_op jit(solution)/shard_map/ppermute | solution.py:304
  79.3 14.0 %collective-permute-start.1 = (bf16[24,2176]{1,0:T(8,128)(2,1)S(1)}, bf16[24,2176]{1,0:T(8,128)(2,1)S(1)}, u32[]{:S(2)}, u32[]{:S(2)}) collective-permute-start(bf16[24,2176]{1,0:T(8,128)(2,1)S(1)} %get-tuple-element.13), channel_id=1, source_target_pairs={{0,2},{1,3},{2,0},{3,1},{4,6},{5,7},{6,4},{7,5},{8,10},{9,11},{10,... | collective-permute-start | bytes 313352 | tf_op jit(solution)/shard_map/ppermute | solution.py:304
  80.8 9.8 %collective-permute-start.2 = (bf16[24,2176]{1,0:T(8,128)(2,1)S(1)}, bf16[24,2176]{1,0:T(8,128)(2,1)S(1)}, u32[]{:S(2)}, u32[]{:S(2)}) collective-permute-start(bf16[24,2176]{1,0:T(8,128)(2,1)S(1)} %get-tuple-element.15), channel_id=1, source_target_pairs={{0,2},{1,3},{2,0},{3,1},{4,6},{5,7},{6,4},{7,5},{8,10},{9,11},{10,... | collective-permute-start | bytes 313352 | tf_op jit(solution)/shard_map/ppermute | solution.py:304
  81.3 7.6 %collective-permute-start.6 = (bf16[24,2176]{1,0:T(8,128)(2,1)S(1)}, bf16[24,2176]{1,0:T(8,128)(2,1)S(1)}, u32[]{:S(2)}, u32[]{:S(2)}) collective-permute-start(bf16[24,2176]{1,0:T(8,128)(2,1)S(1)} %get-tuple-element.19), channel_id=1, source_target_pairs={{0,2},{1,3},{2,0},{3,1},{4,6},{5,7},{6,4},{7,5},{8,10},{9,11},{10,... | collective-permute-start | bytes 313352 | tf_op jit(solution)/shard_map/ppermute | solution.py:304
  84.7 6.0 %collective-permute-start.4 = (bf16[24,2176]{1,0:T(8,128)(2,1)S(1)}, bf16[24,2176]{1,0:T(8,128)(2,1)S(1)}, u32[]{:S(2)}, u32[]{:S(2)}) collective-permute-start(bf16[24,2176]{1,0:T(8,128)(2,1)S(1)} %add_convert_fusion.2), channel_id=1, source_target_pairs={{0,12},{1,13},{2,14},{3,15},{4,0},{5,1},{6,2},{7,3},{8,4},{9,5},{1... | collective-permute-start | bytes 313352 | tf_op jit(solution)/shard_map/ppermute | solution.py:304
  89.0 6.7 %collective-permute-start.7 = (bf16[24,2176]{1,0:T(8,128)(2,1)S(1)}, bf16[24,2176]{1,0:T(8,128)(2,1)S(1)}, u32[]{:S(2)}, u32[]{:S(2)}) collective-permute-start(bf16[24,2176]{1,0:T(8,128)(2,1)S(1)} %add_convert_fusion), channel_id=1, source_target_pairs={{0,4},{1,5},{2,6},{3,7},{4,8},{5,9},{6,10},{7,11},{8,12},{9,13},{1... | collective-permute-start | bytes 313352 | tf_op jit(solution)/shard_map/ppermute | solution.py:304
  90.7 5.9 %collective-permute-start.5 = (bf16[24,2176]{1,0:T(8,128)(2,1)S(1)}, bf16[24,2176]{1,0:T(8,128)(2,1)S(1)}, u32[]{:S(2)}, u32[]{:S(2)}) collective-permute-start(bf16[24,2176]{1,0:T(8,128)(2,1)S(1)} %add_convert_fusion.1), channel_id=1, source_target_pairs={{0,12},{1,13},{2,14},{3,15},{4,0},{5,1},{6,2},{7,3},{8,4},{9,5},{1... | collective-permute-start | bytes 313352 | tf_op jit(solution)/shard_map/ppermute | solution.py:304
Sparse Core Ops, SparseCore 0:
  10.2 55.3 all-gather.2

commit v10 on v8

--- a/solution.py
+++ b/solution.py
@@ -306,12 +306,13 @@
     same, across = {0: pack}, {}
     same[1] = moved(pack, 1)
     across[0] = moved(pack, 0, flip_x=True)
-    same[1] = lax.optimization_barrier((same[1], across[0], held))[0]
+    same[1] = lax.optimization_barrier((same[1], across[0]))[0]
     same[3] = moved(pack, -1)
     same[2] = moved(same[1], 1)
     across[1] = moved(same[1], 0, flip_x=True)
+    same[3] = lax.optimization_barrier((same[3], held))[0]
     across[3] = moved(same[3], 0, flip_x=True)
-    across[2] = moved(across[1], 1)
+    across[2] = moved(same[2], 0, flip_x=True)
     wide, sent = (jnp.float32, jnp.bfloat16)
     here, there = {}, {}
     here[0], here[1], here[2], here[3], there[0], there[1] = experts(

time: 59.4 us -> 60.1 us (1.012)
  starting transfers between devices: 17.2 us -> 25.6 us
  waiting for transfers between devices: 26.3 us -> 18.6 us
    ppermute x15, starting transfers between devices: 17.2 us -> 25.6 us  [moved(): return lax.ppermute(rows, 'expert', pairs)]
    ppermute x15, waiting for transfers between devices: 26.3 us -> 18.6 us  [moved(): return lax.ppermute(rows, 'expert', pairs)]
  transfers between devices with their start and end apart: 15 -> 15, of which waited for: 8 -> 5; matrix products, arithmetic and copies ran while one was open for 0% -> 0% of each run, Pallas kernels for 24% -> 23%
where the time goes in v10:
time: 60.1 us; the launch traced here: 60 us
  starting transfers between devices  25.6 us (43%)
  waiting for transfers between devices  18.6 us (31%)
  Pallas kernels  15.1 us (25%)
  between operations  0.7 us (1%)
    ppermute x15, starting transfers between devices, moved(): return lax.ppermute(rows, 'expert', pairs)  25.6 us
    ppermute x15, waiting for transfers between devices, moved(): return lax.ppermute(rows, 'expert', pairs)  18.6 us
    pallas_call x2, Pallas kernels, experts(): pl.pallas_call(functools.partial(expert_kernel, count, expert_count), out...  10.4 us
    pallas_call x1, Pallas kernels, joined(): pl.pallas_call(join_kernel, out_shape=pltpu.VMEM((parts, width, 2 * half)...  2.41 us
    pallas_call x1, Pallas kernels, packed(): pl.pallas_call(functools.partial(pack_kernel, expert_count), out_shape=ja...  1.29 us
  transfers between devices with their start and end apart: 15, of which 5 were waited for; matrix products, arithmetic and copies ran while one was open for 0% of the time, Pallas kernels for 23%

profile of v10, /device:TPU:0, one launch (start us, length us, event | category | flops | bytes accessed | tf_op | source)
XLA Modules:
  0.0 60.0 jit_solution(11248337634196058082)
XLA Ops:
  0.6 0.5 collective-permute-start.4
  1.1 1.3 %shard_map.86.refs_0_ = bf16[24,6272]{1,0:T(8,128)(2,1)S(1)} custom-call(bf16[24,2048]{1,0:T(8,128)(2,1)} %tokens.1, f32[1,2048]{1,0:T(1,128)} %bitcast.4, s32[24,2048]{1,0:T(8,128)} %signs.1, bf16[24,2048]{1,0:T(8,128)(2,1)} %refs_3_.1, s32[2,4,24]{2,1,0:T(4,128)} %bitcast.6, f32[2,4,24]{2,1,0:T(4,128)} %bitcast.7), custom_call_target="tpu_custom_call" | custom-call | flops 983040 | bytes 688128 | tf_op jit(solution)/shard_map/pallas_call | solution.py:126
  2.4 2.6 %collective-permute-start = (bf16[24,6272]{1,0:T(8,128)(2,1)S(1)}, bf16[24,6272]{1,0:T(8,128)(2,1)S(1)}, u32[]{:S(2)}, u32[]{:S(2)}) collective-permute-start(bf16[24,6272]{1,0:T(8,128)(2,1)S(1)} %shard_map.86.refs_0_), channel_id=1, source_target_pairs={{0,4},{1,5},{2,6},{3,7},{4,8},{5,9},{6,10},{7,11},{8,12},{9,13},{1... | collective-permute-start | bytes 903176 | tf_op jit(solution)/shard_map/ppermute | solution.py:297
  5.1 1.5 %collective-permute-start.1 = (bf16[24,6272]{1,0:T(8,128)(2,1)S(1)}, bf16[24,6272]{1,0:T(8,128)(2,1)S(1)}, u32[]{:S(2)}, u32[]{:S(2)}) collective-permute-start(bf16[24,6272]{1,0:T(8,128)(2,1)S(1)} %shard_map.86.refs_0_), channel_id=1, source_target_pairs={{0,2},{1,3},{2,0},{3,1},{4,6},{5,7},{6,4},{7,5},{8,10},{9,11},{10,... | collective-permute-start | bytes 903176 | tf_op jit(solution)/shard_map/ppermute | solution.py:297
  6.6 8.3 %collective-permute-done.refs_1_ = bf16[24,6272]{1,0:T(8,128)(2,1)S(1)} collective-permute-done((bf16[24,6272]{1,0:T(8,128)(2,1)S(1)}, bf16[24,6272]{1,0:T(8,128)(2,1)S(1)}, u32[]{:S(2)}, u32[]{:S(2)}) %collective-permute-start) | collective-permute-done | bytes 301088 | tf_op jit(solution)/shard_map/ppermute | solution.py:297
  14.9 0.0 collective-permute-done.1.refs_4_
  14.9 1.0 %collective-permute-start.2 = (bf16[24,6272]{1,0:T(8,128)(2,1)S(1)}, bf16[24,6272]{1,0:T(8,128)(2,1)S(1)}, u32[]{:S(2)}, u32[]{:S(2)}) collective-permute-start(bf16[24,6272]{1,0:T(8,128)(2,1)S(1)} %collective-permute-done.refs_1_), channel_id=1, source_target_pairs={{0,4},{1,5},{2,6},{3,7},{4,8},{5,9},{6,10},{7,11},{8,12},{9,13},{1... | collective-permute-start | bytes 903176 | tf_op jit(solution)/shard_map/ppermute | solution.py:297
  15.9 2.8 %collective-permute-start.3 = (bf16[24,6272]{1,0:T(8,128)(2,1)S(1)}, bf16[24,6272]{1,0:T(8,128)(2,1)S(1)}, u32[]{:S(2)}, u32[]{:S(2)}) collective-permute-start(bf16[24,6272]{1,0:T(8,128)(2,1)S(1)} %shard_map.86.refs_0_), channel_id=1, source_target_pairs={{0,12},{1,13},{2,14},{3,15},{4,0},{5,1},{6,2},{7,3},{8,4},{9,5},{1... | collective-permute-start | bytes 903176 | tf_op jit(solution)/shard_map/ppermute | solution.py:297
  18.7 1.5 %collective-permute-start.5 = (bf16[24,6272]{1,0:T(8,128)(2,1)S(1)}, bf16[24,6272]{1,0:T(8,128)(2,1)S(1)}, u32[]{:S(2)}, u32[]{:S(2)}) collective-permute-start(bf16[24,6272]{1,0:T(8,128)(2,1)S(1)} %collective-permute-done.refs_1_), channel_id=1, source_target_pairs={{0,2},{1,3},{2,0},{3,1},{4,6},{5,7},{6,4},{7,5},{8,10},{9,11},{10,... | collective-permute-start | bytes 903176 | tf_op jit(solution)/shard_map/ppermute | solution.py:297
  20.2 6.5 %collective-permute-done.2.refs_2_ = bf16[24,6272]{1,0:T(8,128)(2,1)S(1)} collective-permute-done((bf16[24,6272]{1,0:T(8,128)(2,1)S(1)}, bf16[24,6272]{1,0:T(8,128)(2,1)S(1)}, u32[]{:S(2)}, u32[]{:S(2)}) %collective-permute-start.2) | collective-permute-done | bytes 301088 | tf_op jit(solution)/shard_map/ppermute | solution.py:297
  26.7 1.5 %collective-permute-start.9 = (bf16[24,6272]{1,0:T(8,128)(2,1)S(1)}, bf16[24,6272]{1,0:T(8,128)(2,1)S(1)}, u32[]{:S(2)}, u32[]{:S(2)}) collective-permute-start(bf16[24,6272]{1,0:T(8,128)(2,1)S(1)} %collective-permute-done.2.refs_2_), channel_id=1, source_target_pairs={{0,2},{1,3},{2,0},{3,1},{4,6},{5,7},{6,4},{7,5},{8,10},{9,11},{10,... | collective-permute-start | bytes 903176 | tf_op jit(solution)/shard_map/ppermute | solution.py:297
  28.2 0.0 collective-permute-done.4.other
  28.2 2.4 %shard_map.87.refs_6_.refs_2_ = bf16[3,2048,768]{2,1,0:T(8,128)(2,1)S(1)} custom-call(bf16[3,2048,384]{2,1,0:T(8,128)(2,1)} %own.1, bf16[3,2048,384]{2,1,0:T(8,128)(2,1)S(1)} %collective-permute-done.4.other), custom_call_target="tpu_custom_call" | custom-call | bytes 18874368 | tf_op jit(solution)/shard_map/pallas_call | solution.py:157
  30.7 0.0 collective-permute-done.3.refs_3_
  30.7 1.3 %collective-permute-start.10 = (bf16[24,6272]{1,0:T(8,128)(2,1)S(1)}, bf16[24,6272]{1,0:T(8,128)(2,1)S(1)}, u32[]{:S(2)}, u32[]{:S(2)}) collective-permute-start(bf16[24,6272]{1,0:T(8,128)(2,1)S(1)} %collective-permute-done.3.refs_3_), channel_id=1, source_target_pairs={{0,2},{1,3},{2,0},{3,1},{4,6},{5,7},{6,4},{7,5},{8,10},{9,11},{10,... | collective-permute-start | bytes 903176 | tf_op jit(solution)/shard_map/ppermute | solution.py:297
  32.0 0.0 collective-permute-done.5.refs_5_
  32.0 6.2 %shard_map.88 = (f32[24,2176]{1,0:T(8,128)S(1)}, f32[24,2176]{1,0:T(8,128)S(1)}, bf16[24,2176]{1,0:T(8,128)(2,1)S(1)}, bf16[24,2176]{1,0:T(8,128)(2,1)S(1)}, bf1...) custom-call(bf16[24,6272]{1,0:T(8,128)(2,1)S(1)} %shard_map.86.refs_0_, ...), custom_call_target="tpu_custom_call" | custom-call | flops 4076863488 | bytes 9437184 | tf_op jit(solution)/shard_map/pallas_call | solution.py:251
  38.2 0.8 %collective-permute-start.6 = (bf16[24,2176]{1,0:T(8,128)(2,1)S(1)}, bf16[24,2176]{1,0:T(8,128)(2,1)S(1)}, u32[]{:S(2)}, u32[]{:S(2)}) collective-permute-start(bf16[24,2176]{1,0:T(8,128)(2,1)S(1)} %get-tuple-element.20), channel_id=1, source_target_pairs={{0,2},{1,3},{2,0},{3,1},{4,6},{5,7},{6,4},{7,5},{8,10},{9,11},{10,... | collective-permute-start | bytes 313352 | tf_op jit(solution)/shard_map/ppermute | solution.py:297
  39.0 5.1 %collective-permute-start.7 = (bf16[24,2176]{1,0:T(8,128)(2,1)S(1)}, bf16[24,2176]{1,0:T(8,128)(2,1)S(1)}, u32[]{:S(2)}, u32[]{:S(2)}) collective-permute-start(bf16[24,2176]{1,0:T(8,128)(2,1)S(1)} %get-tuple-element.21), channel_id=1, source_target_pairs={{0,8},{1,9},{2,10},{3,11},{4,12},{5,13},{6,14},{7,15},{8,0},{9,1},... | collective-permute-start | bytes 313352 | tf_op jit(solution)/shard_map/ppermute | solution.py:297
  44.1 0.0 collective-permute-start.8
  44.1 0.0 collective-permute-done.9.refs_0_
  44.1 0.5 collective-permute-start.13
  44.7 0.0 collective-permute-done.10.refs_1_
  44.7 0.0 copy-start
  44.7 0.0 copy-start.1
  44.7 0.0 copy-start.2
  44.7 4.2 %shard_map.89 = (bf16[24,2176]{1,0:T(8,128)(2,1)S(1)}, bf16[24,2176]{1,0:T(8,128)(2,1)S(1)}) custom-call(bf16[24,6272]{1,0:T(8,128)(2,1)S(1)} %collective-permute-done.9.refs_0_, bf16[24,6272]{1,0:T(8,128)(2,1)S(1)} %collective-permute-done.10.refs_1_, bf16[3,2048,768]{2,1,0:T(8,128)(2,1)S(1)} %shard_map.87.refs_6_.refs_2_), custom_call_target="tpu_custom_call" | custom-call | flops 1358954496 | bytes 9437184 | tf_op jit(solution)/shard_map/pallas_call | solution.py:251
  48.9 1.8 %collective-permute-start.11 = (bf16[24,2176]{1,0:T(8,128)(2,1)S(1)}, bf16[24,2176]{1,0:T(8,128)(2,1)S(1)}, u32[]{:S(2)}, u32[]{:S(2)}) collective-permute-start(bf16[24,2176]{1,0:T(8,128)(2,1)S(1)} %get-tuple-element.26), channel_id=1, source_target_pairs={{0,10},{1,11},{2,8},{3,9},{4,14},{5,15},{6,12},{7,13},{8,2},{9,3},... | collective-permute-start | bytes 313352 | tf_op jit(solution)/shard_map/ppermute | solution.py:297
  50.7 0.0 collective-permute-done.13
  50.7 3.5 %collective-permute-start.12 = (bf16[24,2176]{1,0:T(8,128)(2,1)S(1)}, bf16[24,2176]{1,0:T(8,128)(2,1)S(1)}, u32[]{:S(2)}, u32[]{:S(2)}) collective-permute-start(bf16[24,2176]{1,0:T(8,128)(2,1)S(1)} %get-tuple-element.27), channel_id=1, source_target_pairs={{0,6},{1,7},{2,4},{3,5},{4,10},{5,11},{6,8},{7,9},{8,14},{9,15},{1... | collective-permute-start | bytes 313352 | tf_op jit(solution)/shard_map/ppermute | solution.py:297
  54.3 0.0 collective-permute-done.6.refs_1_
  54.3 1.0 %collective-permute-start.14 = (bf16[24,2176]{1,0:T(8,128)(2,1)S(1)}, bf16[24,2176]{1,0:T(8,128)(2,1)S(1)}, u32[]{:S(2)}, u32[]{:S(2)}) collective-permute-start(bf16[24,2176]{1,0:T(8,128)(2,1)S(1)} %add_convert_fusion), channel_id=1, source_target_pairs={{0,12},{1,13},{2,14},{3,15},{4,0},{5,1},{6,2},{7,3},{8,4},{9,5},{1... | collective-permute-start | bytes 313352 | tf_op jit(solution)/shard_map/ppermute | solution.py:297
  55.3 0.0 collective-permute-done.7.refs_2_
  55.3 0.0 collective-permute-done.8.refs_3_
  55.3 1.5 %collective-permute-done.11.refs_4_ = bf16[24,2176]{1,0:T(8,128)(2,1)S(1)} collective-permute-done((bf16[24,2176]{1,0:T(8,128)(2,1)S(1)}, bf16[24,2176]{1,0:T(8,128)(2,1)S(1)}, u32[]{:S(2)}, u32[]{:S(2)}) %collective-permute-start.11) | collective-permute-done | bytes 104480 | tf_op jit(solution)/shard_map/ppermute | solution.py:297
  56.8 1.3 %collective-permute-done.12.refs_5_ = bf16[24,2176]{1,0:T(8,128)(2,1)S(1)} collective-permute-done((bf16[24,2176]{1,0:T(8,128)(2,1)S(1)}, bf16[24,2176]{1,0:T(8,128)(2,1)S(1)}, u32[]{:S(2)}, u32[]{:S(2)}) %collective-permute-start.12) | collective-permute-done | bytes 104480 | tf_op jit(solution)/shard_map/ppermute | solution.py:297
  58.1 0.9 %collective-permute-done.14.refs_6_ = bf16[24,2176]{1,0:T(8,128)(2,1)S(1)} collective-permute-done((bf16[24,2176]{1,0:T(8,128)(2,1)S(1)}, bf16[24,2176]{1,0:T(8,128)(2,1)S(1)}, u32[]{:S(2)}, u32[]{:S(2)}) %collective-permute-start.14) | collective-permute-done | bytes 104480 | tf_op jit(solution)/shard_map/ppermute | solution.py:297
  59.0 0.0 copy-done
  59.0 0.0 copy-done.1
  59.0 0.0 copy-done.2
  59.0 1.0 %shard_map.90 = (f32[24,2048]{1,0:T(8,128)}, f32[1,24]{1,0:T(1,128)}) custom-call(bf16[24,2048]{1,0:T(8,128)(2,1)S(1)} %copy-done.1, f32[1,2048]{1,0:T(1,128)S(1)} %bitcast.5, s32[24,2048]{1,0:T(8,128)S(1)} %copy-done, f32[24,2176]{1,0:T(8,128)S(1)} %get-tuple-element.19.refs_0_, bf16[24,2176]{1,0:T(8,128)(2,1)S(1)} %collective-permute-done.6.refs_1_, ...), custom_call_target="tpu_custom_call" | custom-call | flops 1966080 | bytes 1277952 | tf_op jit(solution)/shard_map/pallas_call | solution.py:344
  (1 shorter events, 0.0 us)
Async XLA Ops:
  0.6 27.6 %collective-permute-start.4 = (bf16[3,2048,384]{2,1,0:T(8,128)(2,1)}, bf16[3,2048,384]{2,1,0:T(8,128)(2,1)S(1)}, u32[]{:S(2)}, u32[]{:S(2)}) collective-permute-start(bf16[3,2048,384]{2,1,0:T(8,128)(2,1)} %own.1), channel_id=1, source_target_pairs={{0,1},{1,0},{2,3},{3,2},{4,5},{5,4},{6,7},{7,6},{8,9},{9,8},{10,11... | collective-permute-start | bytes 14155784 | tf_op jit(solution)/shard_map/ppermute | solution.py:297
  2.4 12.5 %collective-permute-start = (bf16[24,6272]{1,0:T(8,128)(2,1)S(1)}, bf16[24,6272]{1,0:T(8,128)(2,1)S(1)}, u32[]{:S(2)}, u32[]{:S(2)}) collective-permute-start(bf16[24,6272]{1,0:T(8,128)(2,1)S(1)} %shard_map.86.refs_0_), channel_id=1, source_target_pairs={{0,4},{1,5},{2,6},{3,7},{4,8},{5,9},{6,10},{7,11},{8,12},{9,13},{1... | collective-permute-start | bytes 903176 | tf_op jit(solution)/shard_map/ppermute | solution.py:297
  5.1 9.8 %collective-permute-start.1 = (bf16[24,6272]{1,0:T(8,128)(2,1)S(1)}, bf16[24,6272]{1,0:T(8,128)(2,1)S(1)}, u32[]{:S(2)}, u32[]{:S(2)}) collective-permute-start(bf16[24,6272]{1,0:T(8,128)(2,1)S(1)} %shard_map.86.refs_0_), channel_id=1, source_target_pairs={{0,2},{1,3},{2,0},{3,1},{4,6},{5,7},{6,4},{7,5},{8,10},{9,11},{10,... | collective-permute-start | bytes 903176 | tf_op jit(solution)/shard_map/ppermute | solution.py:297
  14.9 11.8 %collective-permute-start.2 = (bf16[24,6272]{1,0:T(8,128)(2,1)S(1)}, bf16[24,6272]{1,0:T(8,128)(2,1)S(1)}, u32[]{:S(2)}, u32[]{:S(2)}) collective-permute-start(bf16[24,6272]{1,0:T(8,128)(2,1)S(1)} %collective-permute-done.refs_1_), channel_id=1, source_target_pairs={{0,4},{1,5},{2,6},{3,7},{4,8},{5,9},{6,10},{7,11},{8,12},{9,13},{1... | collective-permute-start | bytes 903176 | tf_op jit(solution)/shard_map/ppermute | solution.py:297
  15.9 14.7 %collective-permute-start.3 = (bf16[24,6272]{1,0:T(8,128)(2,1)S(1)}, bf16[24,6272]{1,0:T(8,128)(2,1)S(1)}, u32[]{:S(2)}, u32[]{:S(2)}) collective-permute-start(bf16[24,6272]{1,0:T(8,128)(2,1)S(1)} %shard_map.86.refs_0_), channel_id=1, source_target_pairs={{0,12},{1,13},{2,14},{3,15},{4,0},{5,1},{6,2},{7,3},{8,4},{9,5},{1... | collective-permute-start | bytes 903176 | tf_op jit(solution)/shard_map/ppermute | solution.py:297
  18.7 13.3 %collective-permute-start.5 = (bf16[24,6272]{1,0:T(8,128)(2,1)S(1)}, bf16[24,6272]{1,0:T(8,128)(2,1)S(1)}, u32[]{:S(2)}, u32[]{:S(2)}) collective-permute-start(bf16[24,6272]{1,0:T(8,128)(2,1)S(1)} %collective-permute-done.refs_1_), channel_id=1, source_target_pairs={{0,2},{1,3},{2,0},{3,1},{4,6},{5,7},{6,4},{7,5},{8,10},{9,11},{10,... | collective-permute-start | bytes 903176 | tf_op jit(solution)/shard_map/ppermute | solution.py:297
  26.7 17.4 %collective-permute-start.9 = (bf16[24,6272]{1,0:T(8,128)(2,1)S(1)}, bf16[24,6272]{1,0:T(8,128)(2,1)S(1)}, u32[]{:S(2)}, u32[]{:S(2)}) collective-permute-start(bf16[24,6272]{1,0:T(8,128)(2,1)S(1)} %collective-permute-done.2.refs_2_), channel_id=1, source_target_pairs={{0,2},{1,3},{2,0},{3,1},{4,6},{5,7},{6,4},{7,5},{8,10},{9,11},{10,... | collective-permute-start | bytes 903176 | tf_op jit(solution)/shard_map/ppermute | solution.py:297
  30.7 14.0 %collective-permute-start.10 = (bf16[24,6272]{1,0:T(8,128)(2,1)S(1)}, bf16[24,6272]{1,0:T(8,128)(2,1)S(1)}, u32[]{:S(2)}, u32[]{:S(2)}) collective-permute-start(bf16[24,6272]{1,0:T(8,128)(2,1)S(1)} %collective-permute-done.3.refs_3_), channel_id=1, source_target_pairs={{0,2},{1,3},{2,0},{3,1},{4,6},{5,7},{6,4},{7,5},{8,10},{9,11},{10,... | collective-permute-start | bytes 903176 | tf_op jit(solution)/shard_map/ppermute | solution.py:297
  38.2 16.0 %collective-permute-start.6 = (bf16[24,2176]{1,0:T(8,128)(2,1)S(1)}, bf16[24,2176]{1,0:T(8,128)(2,1)S(1)}, u32[]{:S(2)}, u32[]{:S(2)}) collective-permute-start(bf16[24,2176]{1,0:T(8,128)(2,1)S(1)} %get-tuple-element.20), channel_id=1, source_target_pairs={{0,2},{1,3},{2,0},{3,1},{4,6},{5,7},{6,4},{7,5},{8,10},{9,11},{10,... | collective-permute-start | bytes 313352 | tf_op jit(solution)/shard_map/ppermute | solution.py:297
  39.0 16.2 %collective-permute-start.7 = (bf16[24,2176]{1,0:T(8,128)(2,1)S(1)}, bf16[24,2176]{1,0:T(8,128)(2,1)S(1)}, u32[]{:S(2)}, u32[]{:S(2)}) collective-permute-start(bf16[24,2176]{1,0:T(8,128)(2,1)S(1)} %get-tuple-element.21), channel_id=1, source_target_pairs={{0,8},{1,9},{2,10},{3,11},{4,12},{5,13},{6,14},{7,15},{8,0},{9,1},... | collective-permute-start | bytes 313352 | tf_op jit(solution)/shard_map/ppermute | solution.py:297
  44.1 11.2 %collective-permute-start.8 = (bf16[24,2176]{1,0:T(8,128)(2,1)S(1)}, bf16[24,2176]{1,0:T(8,128)(2,1)S(1)}, u32[]{:S(2)}, u32[]{:S(2)}) collective-permute-start(bf16[24,2176]{1,0:T(8,128)(2,1)S(1)} %get-tuple-element.22), channel_id=1, source_target_pairs={{0,4},{1,5},{2,6},{3,7},{4,8},{5,9},{6,10},{7,11},{8,12},{9,13},{1... | collective-permute-start | bytes 313352 | tf_op jit(solution)/shard_map/ppermute | solution.py:297
  44.1 6.6 %collective-permute-start.13 = (bf16[24,2176]{1,0:T(8,128)(2,1)S(1)}, bf16[24,2176]{1,0:T(8,128)(2,1)S(1)}, u32[]{:S(2)}, u32[]{:S(2)}) collective-permute-start(bf16[24,2176]{1,0:T(8,128)(2,1)S(1)} %get-tuple-element.29), channel_id=1, source_target_pairs={{0,2},{1,3},{2,0},{3,1},{4,6},{5,7},{6,4},{7,5},{8,10},{9,11},{10,... | collective-permute-start | bytes 313352 | tf_op jit(solution)/shard_map/ppermute | solution.py:297
  44.7 14.4 %copy-start = (s32[24,2048]{1,0:T(8,128)S(1)}, s32[24,2048]{1,0:T(8,128)}, u32[]{:S(2)}) copy-start(s32[24,2048]{1,0:T(8,128)} %signs.1) | copy-start | bytes 589828
  44.7 14.4 %copy-start.1 = (bf16[24,2048]{1,0:T(8,128)(2,1)S(1)}, bf16[24,2048]{1,0:T(8,128)(2,1)}, u32[]{:S(2)}) copy-start(bf16[24,2048]{1,0:T(8,128)(2,1)} %tokens.1) | copy-start | bytes 294916
  44.7 14.4 %copy-start.2 = (f32[2048]{0:T(1024)S(1)}, f32[2048]{0:T(1024)}, u32[]{:S(2)}) copy-start(f32[2048]{0:T(1024)} %param.8) | copy-start | bytes 24580
  48.9 7.9 %collective-permute-start.11 = (bf16[24,2176]{1,0:T(8,128)(2,1)S(1)}, bf16[24,2176]{1,0:T(8,128)(2,1)S(1)}, u32[]{:S(2)}, u32[]{:S(2)}) collective-permute-start(bf16[24,2176]{1,0:T(8,128)(2,1)S(1)} %get-tuple-element.26), channel_id=1, source_target_pairs={{0,10},{1,11},{2,8},{3,9},{4,14},{5,15},{6,12},{7,13},{8,2},{9,3},... | collective-permute-start | bytes 313352 | tf_op jit(solution)/shard_map/ppermute | solution.py:297
  50.7 7.4 %collective-permute-start.12 = (bf16[24,2176]{1,0:T(8,128)(2,1)S(1)}, bf16[24,2176]{1,0:T(8,128)(2,1)S(1)}, u32[]{:S(2)}, u32[]{:S(2)}) collective-permute-start(bf16[24,2176]{1,0:T(8,128)(2,1)S(1)} %get-tuple-element.27), channel_id=1, source_target_pairs={{0,6},{1,7},{2,4},{3,5},{4,10},{5,11},{6,8},{7,9},{8,14},{9,15},{1... | collective-permute-start | bytes 313352 | tf_op jit(solution)/shard_map/ppermute | solution.py:297
  54.3 4.7 %collective-permute-start.14 = (bf16[24,2176]{1,0:T(8,128)(2,1)S(1)}, bf16[24,2176]{1,0:T(8,128)(2,1)S(1)}, u32[]{:S(2)}, u32[]{:S(2)}) collective-permute-start(bf16[24,2176]{1,0:T(8,128)(2,1)S(1)} %add_convert_fusion), channel_id=1, source_target_pairs={{0,12},{1,13},{2,14},{3,15},{4,0},{5,1},{6,2},{7,3},{8,4},{9,5},{1... | collective-permute-start | bytes 313352 | tf_op jit(solution)/shard_map/ppermute | solution.py:297

commit v11 on v8

--- a/solution.py
+++ b/solution.py
@@ -307,21 +307,23 @@
     same[1] = moved(pack, 1)
     across[0] = moved(pack, 0, flip_x=True)
     same[1] = lax.optimization_barrier((same[1], across[0], held))[0]
-    same[3] = moved(pack, -1)
     same[2] = moved(same[1], 1)
     across[1] = moved(same[1], 0, flip_x=True)
-    across[3] = moved(same[3], 0, flip_x=True)
-    across[2] = moved(across[1], 1)
+    across[2] = moved(same[2], 0, flip_x=True)
+    same[3] = moved(lax.optimization_barrier((pack, same[2]))[0], -1)
     wide, sent = (jnp.float32, jnp.bfloat16)
     here, there = {}, {}
-    here[0], here[1], here[2], here[3], there[0], there[1] = experts(
-        [same[0], same[1], same[2], same[3], across[0], across[1]],
-        [wide, wide, sent, sent, sent, sent],
+    here[0], here[1], here[2], there[0], there[1] = experts(
+        [same[0], same[1], same[2], across[0], across[1]],
+        [wide, wide, sent, sent, sent],
         held,
         expert_count,
     )
-    late = lax.optimization_barrier((across[2], across[3], here[1]))[:2]
-    there[2], there[3] = experts(late, [sent, sent], held, expert_count)
+    near, far, _ = lax.optimization_barrier((same[3], across[2], here[1]))
+    across[3] = moved(near, 0, flip_x=True)
+    here[3], there[2] = experts([near, far], [sent, sent], held, expert_count)
+    last = lax.optimization_barrier((across[3], there[2]))[0]
+    (there[3],) = experts([last], [sent], held, expert_count)
 
     def flipped(rows):
         return moved(rows, 0, flip_x=True)
@@ -329,16 +331,15 @@
     def total(*parts):
         return sum(part.astype(jnp.float32) for part in parts).astype(jnp.bfloat16)
 
-    beside = flipped(there[1])
-    kept = lax.optimization_barrier((here[1], there[2]))[0]
+    beside, forward = (flipped(there[1]), moved(here[2], -1))
+    kept = lax.optimization_barrier((here[1], there[3]))[0]
     arrived = [
         here[0],
         flipped(there[0]),
-        moved(here[2], 2),
         moved(here[3], 1),
         moved(there[2], 2, flip_x=True),
         moved(there[3], 1, flip_x=True),
-        moved(total(kept, beside), -1),
+        moved(total(kept, beside, forward), -1),
     ]
     hvp, quad = pl.pallas_call(
         finish_kernel,

time: 59.4 us -> 61.1 us (1.029)
  Pallas kernels: 15.1 us -> 18.2 us
  starting transfers between devices: 17.2 us -> 16.3 us
  waiting for transfers between devices: 26.3 us -> 25.6 us
    pallas_call x2 -> x3, Pallas kernels: 10.4 us -> 13.6 us  [experts(): pl.pallas_call(functools.partial(expert_kernel, count, expert_count), out...]
    ppermute x15, starting transfers between devices: 17.2 us -> 16.3 us  [moved(): return lax.ppermute(rows, 'expert', pairs)]
    ppermute x15, waiting for transfers between devices: 26.3 us -> 25.6 us  [moved(): return lax.ppermute(rows, 'expert', pairs)]
  transfers between devices with their start and end apart: 15 -> 15, of which waited for: 8 -> 8; matrix products, arithmetic and copies ran while one was open for 0% -> 0% of each run, Pallas kernels for 24% -> 28%
where the time goes in v11:
time: 61.1 us; the launch traced here: 61 us
  waiting for transfers between devices  25.6 us (42%)
  Pallas kernels  18.2 us (30%)
  starting transfers between devices  16.3 us (27%)
  between operations  0.74 us (1%)
    ppermute x15, waiting for transfers between devices, moved(): return lax.ppermute(rows, 'expert', pairs)  25.6 us
    ppermute x15, starting transfers between devices, moved(): return lax.ppermute(rows, 'expert', pairs)  16.3 us
    pallas_call x3, Pallas kernels, experts(): pl.pallas_call(functools.partial(expert_kernel, count, expert_count), out...  13.6 us
    pallas_call x1, Pallas kernels, joined(): pl.pallas_call(join_kernel, out_shape=pltpu.VMEM((parts, width, 2 * half)...  2.41 us
    pallas_call x1, Pallas kernels, packed(): pl.pallas_call(functools.partial(pack_kernel, expert_count), out_shape=ja...  1.29 us
  transfers between devices with their start and end apart: 15, of which 8 were waited for; matrix products, arithmetic and copies ran while one was open for 0% of the time, Pallas kernels for 28%

profile of v11, /device:TPU:0, one launch (start us, length us, event | category | flops | bytes accessed | tf_op | source)
XLA Modules:
  0.0 61.0 jit_solution(7426761071918673926)
XLA Ops:
  0.6 0.5 collective-permute-start.2
  1.1 1.3 %shard_map.86.refs_0_ = bf16[24,6272]{1,0:T(8,128)(2,1)S(1)} custom-call(bf16[24,2048]{1,0:T(8,128)(2,1)} %tokens.1, f32[1,2048]{1,0:T(1,128)} %bitcast.4, s32[24,2048]{1,0:T(8,128)} %signs.1, bf16[24,2048]{1,0:T(8,128)(2,1)} %refs_3_.1, s32[2,4,24]{2,1,0:T(4,128)} %bitcast.6, f32[2,4,24]{2,1,0:T(4,128)} %bitcast.7), custom_call_target="tpu_custom_call" | custom-call | flops 983040 | bytes 688128 | tf_op jit(solution)/shard_map/pallas_call | solution.py:126
  2.4 2.6 %collective-permute-start.1 = (bf16[24,6272]{1,0:T(8,128)(2,1)S(1)}, bf16[24,6272]{1,0:T(8,128)(2,1)S(1)}, u32[]{:S(2)}, u32[]{:S(2)}) collective-permute-start(bf16[24,6272]{1,0:T(8,128)(2,1)S(1)} %shard_map.86.refs_0_), channel_id=1, source_target_pairs={{0,2},{1,3},{2,0},{3,1},{4,6},{5,7},{6,4},{7,5},{8,10},{9,11},{10,... | collective-permute-start | bytes 903176 | tf_op jit(solution)/shard_map/ppermute | solution.py:297
  5.0 1.6 %collective-permute-start = (bf16[24,6272]{1,0:T(8,128)(2,1)S(1)}, bf16[24,6272]{1,0:T(8,128)(2,1)S(1)}, u32[]{:S(2)}, u32[]{:S(2)}) collective-permute-start(bf16[24,6272]{1,0:T(8,128)(2,1)S(1)} %shard_map.86.refs_0_), channel_id=1, source_target_pairs={{0,4},{1,5},{2,6},{3,7},{4,8},{5,9},{6,10},{7,11},{8,12},{9,13},{1... | collective-permute-start | bytes 903176 | tf_op jit(solution)/shard_map/ppermute | solution.py:297
  6.6 2.3 %collective-permute-done.2.other = bf16[3,2048,384]{2,1,0:T(8,128)(2,1)S(1)} collective-permute-done((bf16[3,2048,384]{2,1,0:T(8,128)(2,1)}, bf16[3,2048,384]{2,1,0:T(8,128)(2,1)S(1)}, u32[]{:S(2)}, u32[]{:S(2)}) %collective-permute-start.2) | collective-permute-done | bytes 4718624 | tf_op jit(solution)/shard_map/ppermute | solution.py:297
  8.9 2.4 %shard_map.87.refs_5_.refs_2_.refs_1_ = bf16[3,2048,768]{2,1,0:T(8,128)(2,1)S(1)} custom-call(bf16[3,2048,384]{2,1,0:T(8,128)(2,1)} %own.1, bf16[3,2048,384]{2,1,0:T(8,128)(2,1)S(1)} %collective-permute-done.2.other), custom_call_target="tpu_custom_call" | custom-call | bytes 18874368 | tf_op jit(solution)/shard_map/pallas_call | solution.py:157
  11.3 1.5 %collective-permute-done.1.refs_3_ = bf16[24,6272]{1,0:T(8,128)(2,1)S(1)} collective-permute-done((bf16[24,6272]{1,0:T(8,128)(2,1)S(1)}, bf16[24,6272]{1,0:T(8,128)(2,1)S(1)}, u32[]{:S(2)}, u32[]{:S(2)}) %collective-permute-start.1) | collective-permute-done | bytes 301088 | tf_op jit(solution)/shard_map/ppermute | solution.py:297
  12.8 3.3 %collective-permute-done.refs_1_ = bf16[24,6272]{1,0:T(8,128)(2,1)S(1)} collective-permute-done((bf16[24,6272]{1,0:T(8,128)(2,1)S(1)}, bf16[24,6272]{1,0:T(8,128)(2,1)S(1)}, u32[]{:S(2)}, u32[]{:S(2)}) %collective-permute-start) | collective-permute-done | bytes 301088 | tf_op jit(solution)/shard_map/ppermute | solution.py:297
  16.1 0.0 collective-permute-start.3
  16.1 0.5 collective-permute-start.4
  16.7 10.3 %collective-permute-done.3.refs_2_ = bf16[24,6272]{1,0:T(8,128)(2,1)S(1)} collective-permute-done((bf16[24,6272]{1,0:T(8,128)(2,1)S(1)}, bf16[24,6272]{1,0:T(8,128)(2,1)S(1)}, u32[]{:S(2)}, u32[]{:S(2)}) %collective-permute-start.3) | collective-permute-done | bytes 301088 | tf_op jit(solution)/shard_map/ppermute | solution.py:297
  27.0 0.0 collective-permute-start.6
  27.0 0.7 %collective-permute-start.7 = (bf16[24,6272]{1,0:T(8,128)(2,1)S(1)}, bf16[24,6272]{1,0:T(8,128)(2,1)S(1)}, u32[]{:S(2)}, u32[]{:S(2)}) collective-permute-start(bf16[24,6272]{1,0:T(8,128)(2,1)S(1)} %collective-permute-done.3.refs_2_), channel_id=1, source_target_pairs={{0,2},{1,3},{2,0},{3,1},{4,6},{5,7},{6,4},{7,5},{8,10},{9,11},{10,... | collective-permute-start | bytes 903176 | tf_op jit(solution)/shard_map/ppermute | solution.py:297
  27.7 0.0 collective-permute-done.4.refs_4_
  27.7 5.2 %shard_map.88 = (f32[24,2176]{1,0:T(8,128)S(1)}, f32[24,2176]{1,0:T(8,128)S(1)}, bf16[24,2176]{1,0:T(8,128)(2,1)S(1)}, bf16[24,2176]{1,0:T(8,128)(2,1)S(1)}, bf16[24,2176]{1,0:T(8,128)(2,1)S(1)}) custom-call(bf16[24,6272]{1,0:T(8,128)(2,1)S(1)} %shard_map.86.refs_0_, bf16[24,6272]{1,0:T(8,128)(2,1)S(1)} %collective-permute-done.refs_1_, ...), custom_call_target="tpu_custom_call" | custom-call | flops 3397386240 | bytes 9437184 | tf_op jit(solution)/shard_map/pallas_call | solution.py:251
  32.9 1.1 %collective-permute-done.6.refs_0_ = bf16[24,6272]{1,0:T(8,128)(2,1)S(1)} collective-permute-done((bf16[24,6272]{1,0:T(8,128)(2,1)S(1)}, bf16[24,6272]{1,0:T(8,128)(2,1)S(1)}, u32[]{:S(2)}, u32[]{:S(2)}) %collective-permute-start.6) | collective-permute-done | bytes 301088 | tf_op jit(solution)/shard_map/ppermute | solution.py:297
  34.0 0.3 collective-permute-done.7.refs_1_
  34.3 0.8 %collective-permute-start.10 = (bf16[24,6272]{1,0:T(8,128)(2,1)S(1)}, bf16[24,6272]{1,0:T(8,128)(2,1)S(1)}, u32[]{:S(2)}, u32[]{:S(2)}) collective-permute-start(bf16[24,6272]{1,0:T(8,128)(2,1)S(1)} %collective-permute-done.6.refs_0_), channel_id=1, source_target_pairs={{0,2},{1,3},{2,0},{3,1},{4,6},{5,7},{6,4},{7,5},{8,10},{9,11},{10,... | collective-permute-start | bytes 903176 | tf_op jit(solution)/shard_map/ppermute | solution.py:297
  35.1 1.2 %collective-permute-start.5 = (bf16[24,2176]{1,0:T(8,128)(2,1)S(1)}, bf16[24,2176]{1,0:T(8,128)(2,1)S(1)}, u32[]{:S(2)}, u32[]{:S(2)}) collective-permute-start(bf16[24,2176]{1,0:T(8,128)(2,1)S(1)} %get-tuple-element.19), channel_id=1, source_target_pairs={{0,2},{1,3},{2,0},{3,1},{4,6},{5,7},{6,4},{7,5},{8,10},{9,11},{10,... | collective-permute-start | bytes 313352 | tf_op jit(solution)/shard_map/ppermute | solution.py:297
  36.3 0.8 %collective-permute-start.12 = (bf16[24,2176]{1,0:T(8,128)(2,1)S(1)}, bf16[24,2176]{1,0:T(8,128)(2,1)S(1)}, u32[]{:S(2)}, u32[]{:S(2)}) collective-permute-start(bf16[24,2176]{1,0:T(8,128)(2,1)S(1)} %get-tuple-element.28), channel_id=1, source_target_pairs={{0,2},{1,3},{2,0},{3,1},{4,6},{5,7},{6,4},{7,5},{8,10},{9,11},{10,... | collective-permute-start | bytes 313352 | tf_op jit(solution)/shard_map/ppermute | solution.py:297
  37.1 2.1 %collective-permute-start.13 = (bf16[24,2176]{1,0:T(8,128)(2,1)S(1)}, bf16[24,2176]{1,0:T(8,128)(2,1)S(1)}, u32[]{:S(2)}, u32[]{:S(2)}) collective-permute-start(bf16[24,2176]{1,0:T(8,128)(2,1)S(1)} %get-tuple-element.29), channel_id=1, source_target_pairs={{0,12},{1,13},{2,14},{3,15},{4,0},{5,1},{6,2},{7,3},{8,4},{9,5},{1... | collective-permute-start | bytes 313352 | tf_op jit(solution)/shard_map/ppermute | solution.py:297
  39.2 4.2 %shard_map.89 = (bf16[24,2176]{1,0:T(8,128)(2,1)S(1)}, bf16[24,2176]{1,0:T(8,128)(2,1)S(1)}) custom-call(bf16[24,6272]{1,0:T(8,128)(2,1)S(1)} %collective-permute-done.6.refs_0_, bf16[24,6272]{1,0:T(8,128)(2,1)S(1)} %collective-permute-done.7.refs_1_, bf16[3,2048,768]{2,1,0:T(8,128)(2,1)S(1)} %shard_map.87.refs_5_.refs_2_.refs_1_), custom_call_target="tpu_custom_call" | custom-call | flops 1358954496 | bytes 9437184 | tf_op jit(solution)/shard_map/pallas_call | solution.py:251
  43.4 0.1 collective-permute-start.8
  43.5 0.0 collective-permute-done.10.refs_0_
  43.5 0.0 copy-start
  43.5 0.0 copy-start.1
  43.5 0.0 copy-start.2
  43.5 1.9 %collective-permute-start.9 = (bf16[24,2176]{1,0:T(8,128)(2,1)S(1)}, bf16[24,2176]{1,0:T(8,128)(2,1)S(1)}, u32[]{:S(2)}, u32[]{:S(2)}) collective-permute-start(bf16[24,2176]{1,0:T(8,128)(2,1)S(1)} %get-tuple-element.25), channel_id=1, source_target_pairs={{0,10},{1,11},{2,8},{3,9},{4,14},{5,15},{6,12},{7,13},{8,2},{9,3},... | collective-permute-start | bytes 313352 | tf_op jit(solution)/shard_map/ppermute | solution.py:297
  45.5 4.1 %shard_map.90 = bf16[24,2176]{1,0:T(8,128)(2,1)S(1)} custom-call(bf16[24,6272]{1,0:T(8,128)(2,1)S(1)} %collective-permute-done.10.refs_0_, bf16[3,2048,768]{2,1,0:T(8,128)(2,1)S(1)} %shard_map.87.refs_5_.refs_2_.refs_1_), custom_call_target="tpu_custom_call" | custom-call | flops 679477248 | bytes 9437184 | tf_op jit(solution)/shard_map/pallas_call | solution.py:251
  49.6 0.0 collective-permute-done.12
  49.6 0.0 collective-permute-done.13
  49.7 2.9 %collective-permute-start.14 = (bf16[24,2176]{1,0:T(8,128)(2,1)S(1)}, bf16[24,2176]{1,0:T(8,128)(2,1)S(1)}, u32[]{:S(2)}, u32[]{:S(2)}) collective-permute-start(bf16[24,2176]{1,0:T(8,128)(2,1)S(1)} %add_convert_fusion), channel_id=1, source_target_pairs={{0,12},{1,13},{2,14},{3,15},{4,0},{5,1},{6,2},{7,3},{8,4},{9,5},{1... | collective-permute-start | bytes 313352 | tf_op jit(solution)/shard_map/ppermute | solution.py:297
  52.6 0.5 collective-permute-start.11
  53.2 0.0 collective-permute-done.5.refs_1_
  53.2 0.0 collective-permute-done.8.refs_2_
  53.2 0.0 collective-permute-done.9.refs_3_
  53.2 2.1 %collective-permute-done.14.refs_5_ = bf16[24,2176]{1,0:T(8,128)(2,1)S(1)} collective-permute-done((bf16[24,2176]{1,0:T(8,128)(2,1)S(1)}, bf16[24,2176]{1,0:T(8,128)(2,1)S(1)}, u32[]{:S(2)}, u32[]{:S(2)}) %collective-permute-start.14) | collective-permute-done | bytes 104480 | tf_op jit(solution)/shard_map/ppermute | solution.py:297
  55.2 4.7 %collective-permute-done.11.refs_4_ = bf16[24,2176]{1,0:T(8,128)(2,1)S(1)} collective-permute-done((bf16[24,2176]{1,0:T(8,128)(2,1)S(1)}, bf16[24,2176]{1,0:T(8,128)(2,1)S(1)}, u32[]{:S(2)}, u32[]{:S(2)}) %collective-permute-start.11) | collective-permute-done | bytes 104480 | tf_op jit(solution)/shard_map/ppermute | solution.py:297
  60.0 0.0 copy-done
  60.0 0.0 copy-done.1
  60.0 0.0 copy-done.2
  60.0 1.0 %shard_map.91 = (f32[24,2048]{1,0:T(8,128)}, f32[1,24]{1,0:T(1,128)}) custom-call(bf16[24,2048]{1,0:T(8,128)(2,1)S(1)} %copy-done.1, f32[1,2048]{1,0:T(1,128)S(1)} %bitcast.5, s32[24,2048]{1,0:T(8,128)S(1)} %copy-done, f32[24,2176]{1,0:T(8,128)S(1)} %get-tuple-element.18.refs_0_, bf16[24,2176]{1,0:T(8,128)(2,1)S(1)} %collective-permute-done.5.refs_1_, ...), custom_call_target="tpu_custom_call" | custom-call | flops 1966080 | bytes 1277952 | tf_op jit(solution)/shard_map/pallas_call | solution.py:344
  (1 shorter events, 0.0 us)
Async XLA Ops:
  0.6 8.3 %collective-permute-start.2 = (bf16[3,2048,384]{2,1,0:T(8,128)(2,1)}, bf16[3,2048,384]{2,1,0:T(8,128)(2,1)S(1)}, u32[]{:S(2)}, u32[]{:S(2)}) collective-permute-start(bf16[3,2048,384]{2,1,0:T(8,128)(2,1)} %own.1), channel_id=1, source_target_pairs={{0,1},{1,0},{2,3},{3,2},{4,5},{5,4},{6,7},{7,6},{8,9},{9,8},{10,11... | collective-permute-start | bytes 14155784 | tf_op jit(solution)/shard_map/ppermute | solution.py:297
  2.4 10.4 %collective-permute-start.1 = (bf16[24,6272]{1,0:T(8,128)(2,1)S(1)}, bf16[24,6272]{1,0:T(8,128)(2,1)S(1)}, u32[]{:S(2)}, u32[]{:S(2)}) collective-permute-start(bf16[24,6272]{1,0:T(8,128)(2,1)S(1)} %shard_map.86.refs_0_), channel_id=1, source_target_pairs={{0,2},{1,3},{2,0},{3,1},{4,6},{5,7},{6,4},{7,5},{8,10},{9,11},{10,... | collective-permute-start | bytes 903176 | tf_op jit(solution)/shard_map/ppermute | solution.py:297
  5.0 11.1 %collective-permute-start = (bf16[24,6272]{1,0:T(8,128)(2,1)S(1)}, bf16[24,6272]{1,0:T(8,128)(2,1)S(1)}, u32[]{:S(2)}, u32[]{:S(2)}) collective-permute-start(bf16[24,6272]{1,0:T(8,128)(2,1)S(1)} %shard_map.86.refs_0_), channel_id=1, source_target_pairs={{0,4},{1,5},{2,6},{3,7},{4,8},{5,9},{6,10},{7,11},{8,12},{9,13},{1... | collective-permute-start | bytes 903176 | tf_op jit(solution)/shard_map/ppermute | solution.py:297
  16.1 10.9 %collective-permute-start.3 = (bf16[24,6272]{1,0:T(8,128)(2,1)S(1)}, bf16[24,6272]{1,0:T(8,128)(2,1)S(1)}, u32[]{:S(2)}, u32[]{:S(2)}) collective-permute-start(bf16[24,6272]{1,0:T(8,128)(2,1)S(1)} %collective-permute-done.refs_1_), channel_id=1, source_target_pairs={{0,4},{1,5},{2,6},{3,7},{4,8},{5,9},{6,10},{7,11},{8,12},{9,13},{1... | collective-permute-start | bytes 903176 | tf_op jit(solution)/shard_map/ppermute | solution.py:297
  16.1 11.5 %collective-permute-start.4 = (bf16[24,6272]{1,0:T(8,128)(2,1)S(1)}, bf16[24,6272]{1,0:T(8,128)(2,1)S(1)}, u32[]{:S(2)}, u32[]{:S(2)}) collective-permute-start(bf16[24,6272]{1,0:T(8,128)(2,1)S(1)} %collective-permute-done.refs_1_), channel_id=1, source_target_pairs={{0,2},{1,3},{2,0},{3,1},{4,6},{5,7},{6,4},{7,5},{8,10},{9,11},{10,... | collective-permute-start | bytes 903176 | tf_op jit(solution)/shard_map/ppermute | solution.py:297
  27.0 7.0 %collective-permute-start.6 = (bf16[24,6272]{1,0:T(8,128)(2,1)S(1)}, bf16[24,6272]{1,0:T(8,128)(2,1)S(1)}, u32[]{:S(2)}, u32[]{:S(2)}) collective-permute-start(bf16[24,6272]{1,0:T(8,128)(2,1)S(1)} %shard_map.86.refs_0_), channel_id=1, source_target_pairs={{0,12},{1,13},{2,14},{3,15},{4,0},{5,1},{6,2},{7,3},{8,4},{9,5},{1... | collective-permute-start | bytes 903176 | tf_op jit(solution)/shard_map/ppermute | solution.py:297
  27.0 7.3 %collective-permute-start.7 = (bf16[24,6272]{1,0:T(8,128)(2,1)S(1)}, bf16[24,6272]{1,0:T(8,128)(2,1)S(1)}, u32[]{:S(2)}, u32[]{:S(2)}) collective-permute-start(bf16[24,6272]{1,0:T(8,128)(2,1)S(1)} %collective-permute-done.3.refs_2_), channel_id=1, source_target_pairs={{0,2},{1,3},{2,0},{3,1},{4,6},{5,7},{6,4},{7,5},{8,10},{9,11},{10,... | collective-permute-start | bytes 903176 | tf_op jit(solution)/shard_map/ppermute | solution.py:297
  34.3 9.2 %collective-permute-start.10 = (bf16[24,6272]{1,0:T(8,128)(2,1)S(1)}, bf16[24,6272]{1,0:T(8,128)(2,1)S(1)}, u32[]{:S(2)}, u32[]{:S(2)}) collective-permute-start(bf16[24,6272]{1,0:T(8,128)(2,1)S(1)} %collective-permute-done.6.refs_0_), channel_id=1, source_target_pairs={{0,2},{1,3},{2,0},{3,1},{4,6},{5,7},{6,4},{7,5},{8,10},{9,11},{10,... | collective-permute-start | bytes 903176 | tf_op jit(solution)/shard_map/ppermute | solution.py:297
  35.1 18.1 %collective-permute-start.5 = (bf16[24,2176]{1,0:T(8,128)(2,1)S(1)}, bf16[24,2176]{1,0:T(8,128)(2,1)S(1)}, u32[]{:S(2)}, u32[]{:S(2)}) collective-permute-start(bf16[24,2176]{1,0:T(8,128)(2,1)S(1)} %get-tuple-element.19), channel_id=1, source_target_pairs={{0,2},{1,3},{2,0},{3,1},{4,6},{5,7},{6,4},{7,5},{8,10},{9,11},{10,... | collective-permute-start | bytes 313352 | tf_op jit(solution)/shard_map/ppermute | solution.py:297
  36.3 13.3 %collective-permute-start.12 = (bf16[24,2176]{1,0:T(8,128)(2,1)S(1)}, bf16[24,2176]{1,0:T(8,128)(2,1)S(1)}, u32[]{:S(2)}, u32[]{:S(2)}) collective-permute-start(bf16[24,2176]{1,0:T(8,128)(2,1)S(1)} %get-tuple-element.28), channel_id=1, source_target_pairs={{0,2},{1,3},{2,0},{3,1},{4,6},{5,7},{6,4},{7,5},{8,10},{9,11},{10,... | collective-permute-start | bytes 313352 | tf_op jit(solution)/shard_map/ppermute | solution.py:297
  37.1 12.5 %collective-permute-start.13 = (bf16[24,2176]{1,0:T(8,128)(2,1)S(1)}, bf16[24,2176]{1,0:T(8,128)(2,1)S(1)}, u32[]{:S(2)}, u32[]{:S(2)}) collective-permute-start(bf16[24,2176]{1,0:T(8,128)(2,1)S(1)} %get-tuple-element.29), channel_id=1, source_target_pairs={{0,12},{1,13},{2,14},{3,15},{4,0},{5,1},{6,2},{7,3},{8,4},{9,5},{1... | collective-permute-start | bytes 313352 | tf_op jit(solution)/shard_map/ppermute | solution.py:297
  43.4 9.8 %collective-permute-start.8 = (bf16[24,2176]{1,0:T(8,128)(2,1)S(1)}, bf16[24,2176]{1,0:T(8,128)(2,1)S(1)}, u32[]{:S(2)}, u32[]{:S(2)}) collective-permute-start(bf16[24,2176]{1,0:T(8,128)(2,1)S(1)} %get-tuple-element.24), channel_id=1, source_target_pairs={{0,4},{1,5},{2,6},{3,7},{4,8},{5,9},{6,10},{7,11},{8,12},{9,13},{1... | collective-permute-start | bytes 313352 | tf_op jit(solution)/shard_map/ppermute | solution.py:297
  43.5 16.5 %copy-start = (s32[24,2048]{1,0:T(8,128)S(1)}, s32[24,2048]{1,0:T(8,128)}, u32[]{:S(2)}) copy-start(s32[24,2048]{1,0:T(8,128)} %signs.1) | copy-start | bytes 589828
  43.5 16.5 %copy-start.1 = (bf16[24,2048]{1,0:T(8,128)(2,1)S(1)}, bf16[24,2048]{1,0:T(8,128)(2,1)}, u32[]{:S(2)}) copy-start(bf16[24,2048]{1,0:T(8,128)(2,1)} %tokens.1) | copy-start | bytes 294916
  43.5 16.5 %copy-start.2 = (f32[2048]{0:T(1024)S(1)}, f32[2048]{0:T(1024)}, u32[]{:S(2)}) copy-start(f32[2048]{0:T(1024)} %param.8) | copy-start | bytes 24580
  43.5 9.7 %collective-permute-start.9 = (bf16[24,2176]{1,0:T(8,128)(2,1)S(1)}, bf16[24,2176]{1,0:T(8,128)(2,1)S(1)}, u32[]{:S(2)}, u32[]{:S(2)}) collective-permute-start(bf16[24,2176]{1,0:T(8,128)(2,1)S(1)} %get-tuple-element.25), channel_id=1, source_target_pairs={{0,10},{1,11},{2,8},{3,9},{4,14},{5,15},{6,12},{7,13},{8,2},{9,3},... | collective-permute-start | bytes 313352 | tf_op jit(solution)/shard_map/ppermute | solution.py:297
  49.7 5.6 %collective-permute-start.14 = (bf16[24,2176]{1,0:T(8,128)(2,1)S(1)}, bf16[24,2176]{1,0:T(8,128)(2,1)S(1)}, u32[]{:S(2)}, u32[]{:S(2)}) collective-permute-start(bf16[24,2176]{1,0:T(8,128)(2,1)S(1)} %add_convert_fusion), channel_id=1, source_target_pairs={{0,12},{1,13},{2,14},{3,15},{4,0},{5,1},{6,2},{7,3},{8,4},{9,5},{1... | collective-permute-start | bytes 313352 | tf_op jit(solution)/shard_map/ppermute | solution.py:297
  52.6 7.4 %collective-permute-start.11 = (bf16[24,2176]{1,0:T(8,128)(2,1)S(1)}, bf16[24,2176]{1,0:T(8,128)(2,1)S(1)}, u32[]{:S(2)}, u32[]{:S(2)}) collective-permute-start(bf16[24,2176]{1,0:T(8,128)(2,1)S(1)} %shard_map.90), channel_id=1, source_target_pairs={{0,6},{1,7},{2,4},{3,5},{4,10},{5,11},{6,8},{7,9},{8,14},{9,15},{1... | collective-permute-start | bytes 313352 | tf_op jit(solution)/shard_map/ppermute | solution.py:297

commit v12 on v8

--- a/solution.py
+++ b/solution.py
@@ -168,8 +168,8 @@
 
 
 def expert_kernel(count, expert_count, *refs):
-    packs, held, outs = (refs[:count], refs[count], refs[count + 1 : 2 * count + 1])
-    both, cotan, acc = refs[2 * count + 1 :]
+    packs, held, outs = (refs[:count], refs[count], refs[count + 1 : -3])
+    both, cotan, acc = refs[-3:]
     tok_dev = packs[0].shape[0]
     _, width, hidden = held.shape
     rows = count * tok_dev
@@ -226,20 +226,21 @@
             preferred_element_type=jnp.float32,
         )
         acc[...] = total if start == 0 else acc[...] + total
-    for n in range(count):
+    homes = [out.at[:, pl.ds(at, width + 128)] for out in outs for at in range(0, out.shape[1], width + 128)]
+    for n, home in enumerate(homes):
         part = slice(n * tok_dev, (n + 1) * tok_dev)
         later = slice(rows + n * tok_dev, rows + (n + 1) * tok_dev)
         grad, tan = (acc[part] * gate_row[part], acc[later] * gate_row[part])
         scale, slope_r = (scale_row[part], slope_row[part])
         normed = packs[n][:, :width].astype(jnp.float32)
         normed_t = packs[n][:, width : 2 * width].astype(jnp.float32)
-        outs[n][:, :width] = (scale * tan + slope_r * grad).astype(outs[n].dtype)
+        home[:, :width] = (scale * tan + slope_r * grad).astype(home.dtype)
         first = jnp.mean(normed * grad, axis=1, keepdims=True)
         second = jnp.mean(normed * tan + normed_t * grad, axis=1, keepdims=True)
         second = (second - slope_r / scale * first) / scale
-        lane = lax.broadcasted_iota(jnp.int32, (tok_dev, outs[n].shape[1] - width), 1)
+        lane = lax.broadcasted_iota(jnp.int32, (tok_dev, 128), 1)
         sums = jnp.where(lane == 0, first / scale, jnp.where(lane == 1, second, 0.0))
-        outs[n][:, width:] = sums.astype(outs[n].dtype)
+        home[:, width:] = sums.astype(home.dtype)
 
 
 def experts(packs, kinds, held, expert_count):
@@ -250,9 +251,9 @@
     whole = pl.BlockSpec(memory_space=pltpu.VMEM)
     return pl.pallas_call(
         functools.partial(expert_kernel, count, expert_count),
-        out_shape=[jax.ShapeDtypeStruct((tok_dev, width + 128), kind) for kind in kinds],
+        out_shape=[jax.ShapeDtypeStruct((tok_dev, n * (width + 128)), kind) for kind, n in kinds],
         in_specs=[whole] * (count + 1),
-        out_specs=[whole] * count,
+        out_specs=[whole] * len(kinds),
         scratch_shapes=[
             pltpu.VMEM((2 * rows, width), jnp.bfloat16),
             pltpu.VMEM((rows, width), jnp.bfloat16),
@@ -274,7 +275,8 @@
     probe = (2 * signs[...] - 1).astype(jnp.float32)
     scale, along = rms_terms(xf, probe)
     slope_r = -(scale**3) * along
-    rows = sum(part[...].astype(jnp.float32) for part in arrived)
+    lanes = arrived[0].shape[1]
+    rows = sum(part[:, :lanes].astype(jnp.float32) for part in arrived)
     first = rows[:, width : width + 1]
     second = rows[:, width + 1 : width + 2]
     whole = (
@@ -307,38 +309,34 @@
     same[1] = moved(pack, 1)
     across[0] = moved(pack, 0, flip_x=True)
     same[1] = lax.optimization_barrier((same[1], across[0], held))[0]
-    same[3] = moved(pack, -1)
+    same[3] = moved(lax.optimization_barrier((pack, same[1]))[0], -1)
     same[2] = moved(same[1], 1)
     across[1] = moved(same[1], 0, flip_x=True)
     across[3] = moved(same[3], 0, flip_x=True)
-    across[2] = moved(across[1], 1)
-    wide, sent = (jnp.float32, jnp.bfloat16)
-    here, there = {}, {}
-    here[0], here[1], here[2], here[3], there[0], there[1] = experts(
+    across[2] = moved(same[2], 0, flip_x=True)
+    wide, sent, pair = ((jnp.float32, 1), (jnp.bfloat16, 1), (jnp.bfloat16, 2))
+    here = {}
+    here[0], here[1], here[2], here[3], there = experts(
         [same[0], same[1], same[2], same[3], across[0], across[1]],
-        [wide, wide, sent, sent, sent, sent],
+        [wide, wide, sent, sent, pair],
         held,
         expert_count,
     )
     late = lax.optimization_barrier((across[2], across[3], here[1]))[:2]
-    there[2], there[3] = experts(late, [sent, sent], held, expert_count)
-
-    def flipped(rows):
-        return moved(rows, 0, flip_x=True)
+    far, last = experts(late, [sent, sent], held, expert_count)
 
     def total(*parts):
         return sum(part.astype(jnp.float32) for part in parts).astype(jnp.bfloat16)
 
-    beside = flipped(there[1])
-    kept = lax.optimization_barrier((here[1], there[2]))[0]
+    beside, forward = (moved(there, 0, flip_x=True), moved(here[2], -1))
+    kept = lax.optimization_barrier((here[1], far))[0]
     arrived = [
         here[0],
-        flipped(there[0]),
-        moved(here[2], 2),
+        beside,
         moved(here[3], 1),
-        moved(there[2], 2, flip_x=True),
-        moved(there[3], 1, flip_x=True),
-        moved(total(kept, beside), -1),
+        moved(far, 2, flip_x=True),
+        moved(last, 1, flip_x=True),
+        moved(total(kept, beside[:, kept.shape[1] :], forward), -1),
     ]
     hvp, quad = pl.pallas_call(
         finish_kernel,

time: 59.4 us -> 59.7 us (level)
    ppermute x15 -> x14, starting transfers between devices: 17.2 us -> 17.7 us  [moved(): return lax.ppermute(rows, 'expert', pairs)]
    ppermute x15 -> x14, waiting for transfers between devices: 26.3 us -> 26.1 us  [moved(): return lax.ppermute(rows, 'expert', pairs)]
  transfers between devices with their start and end apart: 15 -> 14, of which waited for: 8 -> 8; matrix products, arithmetic and copies ran while one was open for 0% -> 0% of each run, Pallas kernels for 24% -> 23%
where the time goes in v12:
time: 59.7 us; the launch traced here: 59.5 us
  waiting for transfers between devices  26.1 us (44%)
  starting transfers between devices  17.7 us (30%)
  Pallas kernels  14.9 us (25%)
  between operations  0.72 us (1%)
    ppermute x14, waiting for transfers between devices, moved(): return lax.ppermute(rows, 'expert', pairs)  26.1 us
    ppermute x14, starting transfers between devices, moved(): return lax.ppermute(rows, 'expert', pairs)  17.7 us
    pallas_call x2, Pallas kernels, experts(): pl.pallas_call(functools.partial(expert_kernel, count, expert_count), out...  10.3 us
    pallas_call x1, Pallas kernels, joined(): pl.pallas_call(join_kernel, out_shape=pltpu.VMEM((parts, width, 2 * half)...  2.41 us
    pallas_call x1, Pallas kernels, packed(): pl.pallas_call(functools.partial(pack_kernel, expert_count), out_shape=ja...  1.29 us
  transfers between devices with their start and end apart: 14, of which 8 were waited for; matrix products, arithmetic and copies ran while one was open for 0% of the time, Pallas kernels for 23%

profile of v12, /device:TPU:0, one launch (start us, length us, event | category | flops | bytes accessed | tf_op | source)
XLA Modules:
  0.0 59.5 jit_solution(3219002706871888145)
XLA Ops:
  0.6 0.5 collective-permute-start.2
  1.1 1.3 %shard_map.86.refs_0_ = bf16[24,6272]{1,0:T(8,128)(2,1)S(1)} custom-call(bf16[24,2048]{1,0:T(8,128)(2,1)} %tokens.1, f32[1,2048]{1,0:T(1,128)} %bitcast.4, s32[24,2048]{1,0:T(8,128)} %signs.1, bf16[24,2048]{1,0:T(8,128)(2,1)} %refs_3_.1, s32[2,4,24]{2,1,0:T(4,128)} %bitcast.6, f32[2,4,24]{2,1,0:T(4,128)} %bitcast.7), custom_call_target="tpu_custom_call" | custom-call | flops 983040 | bytes 688128 | tf_op jit(solution)/shard_map/pallas_call | solution.py:126
  2.4 2.6 %collective-permute-start.1 = (bf16[24,6272]{1,0:T(8,128)(2,1)S(1)}, bf16[24,6272]{1,0:T(8,128)(2,1)S(1)}, u32[]{:S(2)}, u32[]{:S(2)}) collective-permute-start(bf16[24,6272]{1,0:T(8,128)(2,1)S(1)} %shard_map.86.refs_0_), channel_id=1, source_target_pairs={{0,2},{1,3},{2,0},{3,1},{4,6},{5,7},{6,4},{7,5},{8,10},{9,11},{10,... | collective-permute-start | bytes 903176 | tf_op jit(solution)/shard_map/ppermute | solution.py:299
  5.0 1.6 %collective-permute-start = (bf16[24,6272]{1,0:T(8,128)(2,1)S(1)}, bf16[24,6272]{1,0:T(8,128)(2,1)S(1)}, u32[]{:S(2)}, u32[]{:S(2)}) collective-permute-start(bf16[24,6272]{1,0:T(8,128)(2,1)S(1)} %shard_map.86.refs_0_), channel_id=1, source_target_pairs={{0,4},{1,5},{2,6},{3,7},{4,8},{5,9},{6,10},{7,11},{8,12},{9,13},{1... | collective-permute-start | bytes 903176 | tf_op jit(solution)/shard_map/ppermute | solution.py:299
  6.6 2.3 %collective-permute-done.2.other = bf16[3,2048,384]{2,1,0:T(8,128)(2,1)S(1)} collective-permute-done((bf16[3,2048,384]{2,1,0:T(8,128)(2,1)}, bf16[3,2048,384]{2,1,0:T(8,128)(2,1)S(1)}, u32[]{:S(2)}, u32[]{:S(2)}) %collective-permute-start.2) | collective-permute-done | bytes 4718624 | tf_op jit(solution)/shard_map/ppermute | solution.py:299
  8.9 2.4 %shard_map.87.refs_6_.refs_2_ = bf16[3,2048,768]{2,1,0:T(8,128)(2,1)S(1)} custom-call(bf16[3,2048,384]{2,1,0:T(8,128)(2,1)} %own.1, bf16[3,2048,384]{2,1,0:T(8,128)(2,1)S(1)} %collective-permute-done.2.other), custom_call_target="tpu_custom_call" | custom-call | bytes 18874368 | tf_op jit(solution)/shard_map/pallas_call | solution.py:157
  11.3 1.5 %collective-permute-done.1.refs_4_ = bf16[24,6272]{1,0:T(8,128)(2,1)S(1)} collective-permute-done((bf16[24,6272]{1,0:T(8,128)(2,1)S(1)}, bf16[24,6272]{1,0:T(8,128)(2,1)S(1)}, u32[]{:S(2)}, u32[]{:S(2)}) %collective-permute-start.1) | collective-permute-done | bytes 301088 | tf_op jit(solution)/shard_map/ppermute | solution.py:299
  12.8 3.3 %collective-permute-done.refs_1_ = bf16[24,6272]{1,0:T(8,128)(2,1)S(1)} collective-permute-done((bf16[24,6272]{1,0:T(8,128)(2,1)S(1)}, bf16[24,6272]{1,0:T(8,128)(2,1)S(1)}, u32[]{:S(2)}, u32[]{:S(2)}) %collective-permute-start) | collective-permute-done | bytes 301088 | tf_op jit(solution)/shard_map/ppermute | solution.py:299
  16.1 1.7 %collective-permute-start.4 = (bf16[24,6272]{1,0:T(8,128)(2,1)S(1)}, bf16[24,6272]{1,0:T(8,128)(2,1)S(1)}, u32[]{:S(2)}, u32[]{:S(2)}) collective-permute-start(bf16[24,6272]{1,0:T(8,128)(2,1)S(1)} %shard_map.86.refs_0_), channel_id=1, source_target_pairs={{0,12},{1,13},{2,14},{3,15},{4,0},{5,1},{6,2},{7,3},{8,4},{9,5},{1... | collective-permute-start | bytes 903176 | tf_op jit(solution)/shard_map/ppermute | solution.py:299
  17.9 0.3 collective-permute-start.3
  18.2 0.5 collective-permute-start.5
  18.7 7.5 %collective-permute-done.4.refs_3_ = bf16[24,6272]{1,0:T(8,128)(2,1)S(1)} collective-permute-done((bf16[24,6272]{1,0:T(8,128)(2,1)S(1)}, bf16[24,6272]{1,0:T(8,128)(2,1)S(1)}, u32[]{:S(2)}, u32[]{:S(2)}) %collective-permute-start.4) | collective-permute-done | bytes 301088 | tf_op jit(solution)/shard_map/ppermute | solution.py:299
  26.2 0.7 %collective-permute-start.9 = (bf16[24,6272]{1,0:T(8,128)(2,1)S(1)}, bf16[24,6272]{1,0:T(8,128)(2,1)S(1)}, u32[]{:S(2)}, u32[]{:S(2)}) collective-permute-start(bf16[24,6272]{1,0:T(8,128)(2,1)S(1)} %collective-permute-done.4.refs_3_), channel_id=1, source_target_pairs={{0,2},{1,3},{2,0},{3,1},{4,6},{5,7},{6,4},{7,5},{8,10},{9,11},{10,... | collective-permute-start | bytes 903176 | tf_op jit(solution)/shard_map/ppermute | solution.py:299
  26.8 4.3 %collective-permute-done.3.refs_2_ = bf16[24,6272]{1,0:T(8,128)(2,1)S(1)} collective-permute-done((bf16[24,6272]{1,0:T(8,128)(2,1)S(1)}, bf16[24,6272]{1,0:T(8,128)(2,1)S(1)}, u32[]{:S(2)}, u32[]{:S(2)}) %collective-permute-start.3) | collective-permute-done | bytes 301088 | tf_op jit(solution)/shard_map/ppermute | solution.py:299
  31.2 0.7 %collective-permute-start.8 = (bf16[24,6272]{1,0:T(8,128)(2,1)S(1)}, bf16[24,6272]{1,0:T(8,128)(2,1)S(1)}, u32[]{:S(2)}, u32[]{:S(2)}) collective-permute-start(bf16[24,6272]{1,0:T(8,128)(2,1)S(1)} %collective-permute-done.3.refs_2_), channel_id=1, source_target_pairs={{0,2},{1,3},{2,0},{3,1},{4,6},{5,7},{6,4},{7,5},{8,10},{9,11},{10,... | collective-permute-start | bytes 903176 | tf_op jit(solution)/shard_map/ppermute | solution.py:299
  31.9 0.0 collective-permute-done.5.refs_5_
  31.9 6.1 %shard_map.88 = (f32[24,2176]{1,0:T(8,128)S(1)}, f32[24,2176]{1,0:T(8,128)S(1)}, bf16[24,2176]{1,0:T(8,128)(2,1)S(1)}, bf16[24,2176]{1,0:T(8,128)(2,1)S(1)}, bf16[24,4352]{1,0:T(8,128)(2,1)S(1)}) custom-call(bf16[24,6272]{1,0:T(8,128)(2,1)S(1)} %shard_map.86.refs_0_, bf16[24,6272]{1,0:T(8,128)(2,1)S(1)} %collective-permute-done.refs_1_, ...), custom_call_target="tpu_custom_call" | custom-call | flops 4076863488 | bytes 9437184 | tf_op jit(solution)/shard_map/pallas_call | solution.py:252
  38.0 1.4 %collective-permute-start.6 = (bf16[24,4352]{1,0:T(8,128)(2,1)S(1)}, bf16[24,4352]{1,0:T(8,128)(2,1)S(1)}, u32[]{:S(2)}, u32[]{:S(2)}) collective-permute-start(bf16[24,4352]{1,0:T(8,128)(2,1)S(1)} %get-tuple-element.19), channel_id=1, source_target_pairs={{0,2},{1,3},{2,0},{3,1},{4,6},{5,7},{6,4},{7,5},{8,10},{9,11},{10,... | collective-permute-start | bytes 626696 | tf_op jit(solution)/shard_map/ppermute | solution.py:299
  39.4 1.6 %collective-permute-start.7 = (bf16[24,2176]{1,0:T(8,128)(2,1)S(1)}, bf16[24,2176]{1,0:T(8,128)(2,1)S(1)}, u32[]{:S(2)}, u32[]{:S(2)}) collective-permute-start(bf16[24,2176]{1,0:T(8,128)(2,1)S(1)} %get-tuple-element.20), channel_id=1, source_target_pairs={{0,4},{1,5},{2,6},{3,7},{4,8},{5,9},{6,10},{7,11},{8,12},{9,13},{1... | collective-permute-start | bytes 313352 | tf_op jit(solution)/shard_map/ppermute | solution.py:299
  41.0 2.2 %collective-permute-start.12 = (bf16[24,2176]{1,0:T(8,128)(2,1)S(1)}, bf16[24,2176]{1,0:T(8,128)(2,1)S(1)}, u32[]{:S(2)}, u32[]{:S(2)}) collective-permute-start(bf16[24,2176]{1,0:T(8,128)(2,1)S(1)} %get-tuple-element.27), channel_id=1, source_target_pairs={{0,12},{1,13},{2,14},{3,15},{4,0},{5,1},{6,2},{7,3},{8,4},{9,5},{1... | collective-permute-start | bytes 313352 | tf_op jit(solution)/shard_map/ppermute | solution.py:299
  43.2 0.0 collective-permute-done.9.refs_1_
  43.2 0.0 collective-permute-done.8.refs_0_
  43.2 0.0 copy-start
  43.2 0.0 copy-start.1
  43.2 0.0 copy-start.2
  43.2 4.2 %shard_map.89 = (bf16[24,2176]{1,0:T(8,128)(2,1)S(1)}, bf16[24,2176]{1,0:T(8,128)(2,1)S(1)}) custom-call(bf16[24,6272]{1,0:T(8,128)(2,1)S(1)} %collective-permute-done.8.refs_0_, bf16[24,6272]{1,0:T(8,128)(2,1)S(1)} %collective-permute-done.9.refs_1_, bf16[3,2048,768]{2,1,0:T(8,128)(2,1)S(1)} %shard_map.87.refs_6_.refs_2_), custom_call_target="tpu_custom_call" | custom-call | flops 1358954496 | bytes 9437184 | tf_op jit(solution)/shard_map/pallas_call | solution.py:252
  47.4 0.0 collective-permute-done.12
  47.4 0.0 collective-permute-done.6.refs_1_
  47.5 2.3 %collective-permute-start.13 = (bf16[24,2176]{1,0:T(8,128)(2,1)S(1)}, bf16[24,2176]{1,0:T(8,128)(2,1)S(1)}, u32[]{:S(2)}, u32[]{:S(2)}) collective-permute-start(bf16[24,2176]{1,0:T(8,128)(2,1)S(1)} %add_convert_fusion), channel_id=1, source_target_pairs={{0,12},{1,13},{2,14},{3,15},{4,0},{5,1},{6,2},{7,3},{8,4},{9,5},{1... | collective-permute-start | bytes 313352 | tf_op jit(solution)/shard_map/ppermute | solution.py:299
  49.8 0.0 collective-permute-start.11
  49.8 1.5 %collective-permute-start.10 = (bf16[24,2176]{1,0:T(8,128)(2,1)S(1)}, bf16[24,2176]{1,0:T(8,128)(2,1)S(1)}, u32[]{:S(2)}, u32[]{:S(2)}) collective-permute-start(bf16[24,2176]{1,0:T(8,128)(2,1)S(1)} %get-tuple-element.24), channel_id=1, source_target_pairs={{0,10},{1,11},{2,8},{3,9},{4,14},{5,15},{6,12},{7,13},{8,2},{9,3},... | collective-permute-start | bytes 313352 | tf_op jit(solution)/shard_map/ppermute | solution.py:299
  51.3 0.0 collective-permute-done.7.refs_2_
  51.3 2.4 %collective-permute-done.13.refs_5_ = bf16[24,2176]{1,0:T(8,128)(2,1)S(1)} collective-permute-done((bf16[24,2176]{1,0:T(8,128)(2,1)S(1)}, bf16[24,2176]{1,0:T(8,128)(2,1)S(1)}, u32[]{:S(2)}, u32[]{:S(2)}) %collective-permute-start.13) | collective-permute-done | bytes 104480 | tf_op jit(solution)/shard_map/ppermute | solution.py:299
  53.8 3.5 %collective-permute-done.11.refs_4_ = bf16[24,2176]{1,0:T(8,128)(2,1)S(1)} collective-permute-done((bf16[24,2176]{1,0:T(8,128)(2,1)S(1)}, bf16[24,2176]{1,0:T(8,128)(2,1)S(1)}, u32[]{:S(2)}, u32[]{:S(2)}) %collective-permute-start.11) | collective-permute-done | bytes 104480 | tf_op jit(solution)/shard_map/ppermute | solution.py:299
  57.3 1.2 %collective-permute-done.10.refs_3_ = bf16[24,2176]{1,0:T(8,128)(2,1)S(1)} collective-permute-done((bf16[24,2176]{1,0:T(8,128)(2,1)S(1)}, bf16[24,2176]{1,0:T(8,128)(2,1)S(1)}, u32[]{:S(2)}, u32[]{:S(2)}) %collective-permute-start.10) | collective-permute-done | bytes 104480 | tf_op jit(solution)/shard_map/ppermute | solution.py:299
  58.5 0.0 copy-done
  58.5 0.0 copy-done.1
  58.5 0.0 copy-done.2
  58.5 1.0 %shard_map.90 = (f32[24,2048]{1,0:T(8,128)}, f32[1,24]{1,0:T(1,128)}) custom-call(bf16[24,2048]{1,0:T(8,128)(2,1)S(1)} %copy-done.1, f32[1,2048]{1,0:T(1,128)S(1)} %bitcast.5, s32[24,2048]{1,0:T(8,128)S(1)} %copy-done, f32[24,2176]{1,0:T(8,128)S(1)} %get-tuple-element.18.refs_0_, bf16[24,4352]{1,0:T(8,128)(2,1)S(1)} %collective-permute-done.6.refs_1_, ...), custom_call_target="tpu_custom_call" | custom-call | flops 1966080 | bytes 1277952 | tf_op jit(solution)/shard_map/pallas_call | solution.py:341
  (1 shorter events, 0.0 us)
Async XLA Ops:
  0.6 8.3 %collective-permute-start.2 = (bf16[3,2048,384]{2,1,0:T(8,128)(2,1)}, bf16[3,2048,384]{2,1,0:T(8,128)(2,1)S(1)}, u32[]{:S(2)}, u32[]{:S(2)}) collective-permute-start(bf16[3,2048,384]{2,1,0:T(8,128)(2,1)} %own.1), channel_id=1, source_target_pairs={{0,1},{1,0},{2,3},{3,2},{4,5},{5,4},{6,7},{7,6},{8,9},{9,8},{10,11... | collective-permute-start | bytes 14155784 | tf_op jit(solution)/shard_map/ppermute | solution.py:299
  2.4 10.4 %collective-permute-start.1 = (bf16[24,6272]{1,0:T(8,128)(2,1)S(1)}, bf16[24,6272]{1,0:T(8,128)(2,1)S(1)}, u32[]{:S(2)}, u32[]{:S(2)}) collective-permute-start(bf16[24,6272]{1,0:T(8,128)(2,1)S(1)} %shard_map.86.refs_0_), channel_id=1, source_target_pairs={{0,2},{1,3},{2,0},{3,1},{4,6},{5,7},{6,4},{7,5},{8,10},{9,11},{10,... | collective-permute-start | bytes 903176 | tf_op jit(solution)/shard_map/ppermute | solution.py:299
  5.0 11.1 %collective-permute-start = (bf16[24,6272]{1,0:T(8,128)(2,1)S(1)}, bf16[24,6272]{1,0:T(8,128)(2,1)S(1)}, u32[]{:S(2)}, u32[]{:S(2)}) collective-permute-start(bf16[24,6272]{1,0:T(8,128)(2,1)S(1)} %shard_map.86.refs_0_), channel_id=1, source_target_pairs={{0,4},{1,5},{2,6},{3,7},{4,8},{5,9},{6,10},{7,11},{8,12},{9,13},{1... | collective-permute-start | bytes 903176 | tf_op jit(solution)/shard_map/ppermute | solution.py:299
  16.1 10.0 %collective-permute-start.4 = (bf16[24,6272]{1,0:T(8,128)(2,1)S(1)}, bf16[24,6272]{1,0:T(8,128)(2,1)S(1)}, u32[]{:S(2)}, u32[]{:S(2)}) collective-permute-start(bf16[24,6272]{1,0:T(8,128)(2,1)S(1)} %shard_map.86.refs_0_), channel_id=1, source_target_pairs={{0,12},{1,13},{2,14},{3,15},{4,0},{5,1},{6,2},{7,3},{8,4},{9,5},{1... | collective-permute-start | bytes 903176 | tf_op jit(solution)/shard_map/ppermute | solution.py:299
  17.9 13.3 %collective-permute-start.3 = (bf16[24,6272]{1,0:T(8,128)(2,1)S(1)}, bf16[24,6272]{1,0:T(8,128)(2,1)S(1)}, u32[]{:S(2)}, u32[]{:S(2)}) collective-permute-start(bf16[24,6272]{1,0:T(8,128)(2,1)S(1)} %collective-permute-done.refs_1_), channel_id=1, source_target_pairs={{0,4},{1,5},{2,6},{3,7},{4,8},{5,9},{6,10},{7,11},{8,12},{9,13},{1... | collective-permute-start | bytes 903176 | tf_op jit(solution)/shard_map/ppermute | solution.py:299
  18.2 13.7 %collective-permute-start.5 = (bf16[24,6272]{1,0:T(8,128)(2,1)S(1)}, bf16[24,6272]{1,0:T(8,128)(2,1)S(1)}, u32[]{:S(2)}, u32[]{:S(2)}) collective-permute-start(bf16[24,6272]{1,0:T(8,128)(2,1)S(1)} %collective-permute-done.refs_1_), channel_id=1, source_target_pairs={{0,2},{1,3},{2,0},{3,1},{4,6},{5,7},{6,4},{7,5},{8,10},{9,11},{10,... | collective-permute-start | bytes 903176 | tf_op jit(solution)/shard_map/ppermute | solution.py:299
  26.2 17.0 %collective-permute-start.9 = (bf16[24,6272]{1,0:T(8,128)(2,1)S(1)}, bf16[24,6272]{1,0:T(8,128)(2,1)S(1)}, u32[]{:S(2)}, u32[]{:S(2)}) collective-permute-start(bf16[24,6272]{1,0:T(8,128)(2,1)S(1)} %collective-permute-done.4.refs_3_), channel_id=1, source_target_pairs={{0,2},{1,3},{2,0},{3,1},{4,6},{5,7},{6,4},{7,5},{8,10},{9,11},{10,... | collective-permute-start | bytes 903176 | tf_op jit(solution)/shard_map/ppermute | solution.py:299
  31.2 12.0 %collective-permute-start.8 = (bf16[24,6272]{1,0:T(8,128)(2,1)S(1)}, bf16[24,6272]{1,0:T(8,128)(2,1)S(1)}, u32[]{:S(2)}, u32[]{:S(2)}) collective-permute-start(bf16[24,6272]{1,0:T(8,128)(2,1)S(1)} %collective-permute-done.3.refs_2_), channel_id=1, source_target_pairs={{0,2},{1,3},{2,0},{3,1},{4,6},{5,7},{6,4},{7,5},{8,10},{9,11},{10,... | collective-permute-start | bytes 903176 | tf_op jit(solution)/shard_map/ppermute | solution.py:299
  38.0 9.4 %collective-permute-start.6 = (bf16[24,4352]{1,0:T(8,128)(2,1)S(1)}, bf16[24,4352]{1,0:T(8,128)(2,1)S(1)}, u32[]{:S(2)}, u32[]{:S(2)}) collective-permute-start(bf16[24,4352]{1,0:T(8,128)(2,1)S(1)} %get-tuple-element.19), channel_id=1, source_target_pairs={{0,2},{1,3},{2,0},{3,1},{4,6},{5,7},{6,4},{7,5},{8,10},{9,11},{10,... | collective-permute-start | bytes 626696 | tf_op jit(solution)/shard_map/ppermute | solution.py:299
  39.4 12.0 %collective-permute-start.7 = (bf16[24,2176]{1,0:T(8,128)(2,1)S(1)}, bf16[24,2176]{1,0:T(8,128)(2,1)S(1)}, u32[]{:S(2)}, u32[]{:S(2)}) collective-permute-start(bf16[24,2176]{1,0:T(8,128)(2,1)S(1)} %get-tuple-element.20), channel_id=1, source_target_pairs={{0,4},{1,5},{2,6},{3,7},{4,8},{5,9},{6,10},{7,11},{8,12},{9,13},{1... | collective-permute-start | bytes 313352 | tf_op jit(solution)/shard_map/ppermute | solution.py:299
  41.0 6.4 %collective-permute-start.12 = (bf16[24,2176]{1,0:T(8,128)(2,1)S(1)}, bf16[24,2176]{1,0:T(8,128)(2,1)S(1)}, u32[]{:S(2)}, u32[]{:S(2)}) collective-permute-start(bf16[24,2176]{1,0:T(8,128)(2,1)S(1)} %get-tuple-element.27), channel_id=1, source_target_pairs={{0,12},{1,13},{2,14},{3,15},{4,0},{5,1},{6,2},{7,3},{8,4},{9,5},{1... | collective-permute-start | bytes 313352 | tf_op jit(solution)/shard_map/ppermute | solution.py:299
  43.2 15.3 %copy-start = (s32[24,2048]{1,0:T(8,128)S(1)}, s32[24,2048]{1,0:T(8,128)}, u32[]{:S(2)}) copy-start(s32[24,2048]{1,0:T(8,128)} %signs.1) | copy-start | bytes 589828
  43.2 15.3 %copy-start.1 = (bf16[24,2048]{1,0:T(8,128)(2,1)S(1)}, bf16[24,2048]{1,0:T(8,128)(2,1)}, u32[]{:S(2)}) copy-start(bf16[24,2048]{1,0:T(8,128)(2,1)} %tokens.1) | copy-start | bytes 294916
  43.2 15.3 %copy-start.2 = (f32[2048]{0:T(1024)S(1)}, f32[2048]{0:T(1024)}, u32[]{:S(2)}) copy-start(f32[2048]{0:T(1024)} %param.8) | copy-start | bytes 24580
  47.5 6.3 %collective-permute-start.13 = (bf16[24,2176]{1,0:T(8,128)(2,1)S(1)}, bf16[24,2176]{1,0:T(8,128)(2,1)S(1)}, u32[]{:S(2)}, u32[]{:S(2)}) collective-permute-start(bf16[24,2176]{1,0:T(8,128)(2,1)S(1)} %add_convert_fusion), channel_id=1, source_target_pairs={{0,12},{1,13},{2,14},{3,15},{4,0},{5,1},{6,2},{7,3},{8,4},{9,5},{1... | collective-permute-start | bytes 313352 | tf_op jit(solution)/shard_map/ppermute | solution.py:299
  49.8 7.5 %collective-permute-start.11 = (bf16[24,2176]{1,0:T(8,128)(2,1)S(1)}, bf16[24,2176]{1,0:T(8,128)(2,1)S(1)}, u32[]{:S(2)}, u32[]{:S(2)}) collective-permute-start(bf16[24,2176]{1,0:T(8,128)(2,1)S(1)} %get-tuple-element.25), channel_id=1, source_target_pairs={{0,6},{1,7},{2,4},{3,5},{4,10},{5,11},{6,8},{7,9},{8,14},{9,15},{1... | collective-permute-start | bytes 313352 | tf_op jit(solution)/shard_map/ppermute | solution.py:299
  49.8 8.7 %collective-permute-start.10 = (bf16[24,2176]{1,0:T(8,128)(2,1)S(1)}, bf16[24,2176]{1,0:T(8,128)(2,1)S(1)}, u32[]{:S(2)}, u32[]{:S(2)}) collective-permute-start(bf16[24,2176]{1,0:T(8,128)(2,1)S(1)} %get-tuple-element.24), channel_id=1, source_target_pairs={{0,10},{1,11},{2,8},{3,9},{4,14},{5,15},{6,12},{7,13},{8,2},{9,3},... | collective-permute-start | bytes 313352 | tf_op jit(solution)/shard_map/ppermute | solution.py:299

commit v13 on v12

--- a/solution.py
+++ b/solution.py
@@ -294,7 +294,8 @@
 def moved(rows, turns, flip_x=False, flip_core=False):
     count = lax.axis_size("expert")
     pairs = [
-        (i, (i + 4 * turns) % count ^ (2 * flip_x) ^ (1 * flip_core)) for i in range(count)
+        (i, (i + 4 * turns * (1 - 2 * (i % 2))) % count ^ (2 * flip_x) ^ (1 * flip_core))
+        for i in range(count)
     ]
     return lax.ppermute(rows, "expert", pairs)
 

time: 59.7 us -> 62.5 us (1.047)
  waiting for transfers between devices: 26.1 us -> 27.7 us
  starting transfers between devices: 17.7 us -> 18.9 us
    ppermute x14, waiting for transfers between devices: 26.1 us -> 27.7 us  [moved(): return lax.ppermute(rows, 'expert', pairs)]
    ppermute x14, starting transfers between devices: 17.7 us -> 18.9 us  [moved(): return lax.ppermute(rows, 'expert', pairs)]
  transfers between devices with their start and end apart: 14 -> 14, of which waited for: 8 -> 8; matrix products, arithmetic and copies ran while one was open for 0% -> 0% of each run, Pallas kernels for 23% -> 22%
where the time goes in v13:
time: 62.5 us; the launch traced here: 62.3 us
  waiting for transfers between devices  27.7 us (44%)
  starting transfers between devices  18.9 us (30%)
  Pallas kernels  14.9 us (24%)
  between operations  0.72 us (1%)
    ppermute x14, waiting for transfers between devices, moved(): return lax.ppermute(rows, 'expert', pairs)  27.7 us
    ppermute x14, starting transfers between devices, moved(): return lax.ppermute(rows, 'expert', pairs)  18.9 us
    pallas_call x2, Pallas kernels, experts(): pl.pallas_call(functools.partial(expert_kernel, count, expert_count), out...  10.3 us
    pallas_call x1, Pallas kernels, joined(): pl.pallas_call(join_kernel, out_shape=pltpu.VMEM((parts, width, 2 * half)...  2.41 us
    pallas_call x1, Pallas kernels, packed(): pl.pallas_call(functools.partial(pack_kernel, expert_count), out_shape=ja...  1.29 us
  transfers between devices with their start and end apart: 14, of which 8 were waited for; matrix products, arithmetic and copies ran while one was open for 0% of the time, Pallas kernels for 22%

profile of v13, /device:TPU:0, one launch (start us, length us, event | category | flops | bytes accessed | tf_op | source)
XLA Modules:
  0.0 62.3 jit_solution(7319976392087746678)
XLA Ops:
  0.6 0.5 collective-permute-start.2
  1.1 1.3 %shard_map.86.refs_0_ = bf16[24,6272]{1,0:T(8,128)(2,1)S(1)} custom-call(bf16[24,2048]{1,0:T(8,128)(2,1)} %tokens.1, f32[1,2048]{1,0:T(1,128)} %bitcast.4, s32[24,2048]{1,0:T(8,128)} %signs.1, bf16[24,2048]{1,0:T(8,128)(2,1)} %refs_3_.1, s32[2,4,24]{2,1,0:T(4,128)} %bitcast.6, f32[2,4,24]{2,1,0:T(4,128)} %bitcast.7), custom_call_target="tpu_custom_call" | custom-call | flops 983040 | bytes 688128 | tf_op jit(solution)/shard_map/pallas_call | solution.py:126
  2.4 2.6 %collective-permute-start.1 = (bf16[24,6272]{1,0:T(8,128)(2,1)S(1)}, bf16[24,6272]{1,0:T(8,128)(2,1)S(1)}, u32[]{:S(2)}, u32[]{:S(2)}) collective-permute-start(bf16[24,6272]{1,0:T(8,128)(2,1)S(1)} %shard_map.86.refs_0_), channel_id=1, source_target_pairs={{0,2},{1,3},{2,0},{3,1},{4,6},{5,7},{6,4},{7,5},{8,10},{9,11},{10,... | collective-permute-start | bytes 903176 | tf_op jit(solution)/shard_map/ppermute | solution.py:300
  5.0 1.6 %collective-permute-start = (bf16[24,6272]{1,0:T(8,128)(2,1)S(1)}, bf16[24,6272]{1,0:T(8,128)(2,1)S(1)}, u32[]{:S(2)}, u32[]{:S(2)}) collective-permute-start(bf16[24,6272]{1,0:T(8,128)(2,1)S(1)} %shard_map.86.refs_0_), channel_id=1, source_target_pairs={{0,4},{1,13},{2,6},{3,15},{4,8},{5,1},{6,10},{7,3},{8,12},{9,5},{1... | collective-permute-start | bytes 903176 | tf_op jit(solution)/shard_map/ppermute | solution.py:300
  6.6 2.3 %collective-permute-done.2.other = bf16[3,2048,384]{2,1,0:T(8,128)(2,1)S(1)} collective-permute-done((bf16[3,2048,384]{2,1,0:T(8,128)(2,1)}, bf16[3,2048,384]{2,1,0:T(8,128)(2,1)S(1)}, u32[]{:S(2)}, u32[]{:S(2)}) %collective-permute-start.2) | collective-permute-done | bytes 4718624 | tf_op jit(solution)/shard_map/ppermute | solution.py:300
  8.9 2.4 %shard_map.87.refs_6_.refs_2_ = bf16[3,2048,768]{2,1,0:T(8,128)(2,1)S(1)} custom-call(bf16[3,2048,384]{2,1,0:T(8,128)(2,1)} %own.1, bf16[3,2048,384]{2,1,0:T(8,128)(2,1)S(1)} %collective-permute-done.2.other), custom_call_target="tpu_custom_call" | custom-call | bytes 18874368 | tf_op jit(solution)/shard_map/pallas_call | solution.py:157
  11.3 1.5 %collective-permute-done.1.refs_4_ = bf16[24,6272]{1,0:T(8,128)(2,1)S(1)} collective-permute-done((bf16[24,6272]{1,0:T(8,128)(2,1)S(1)}, bf16[24,6272]{1,0:T(8,128)(2,1)S(1)}, u32[]{:S(2)}, u32[]{:S(2)}) %collective-permute-start.1) | collective-permute-done | bytes 301088 | tf_op jit(solution)/shard_map/ppermute | solution.py:300
  12.8 3.5 %collective-permute-done.refs_1_ = bf16[24,6272]{1,0:T(8,128)(2,1)S(1)} collective-permute-done((bf16[24,6272]{1,0:T(8,128)(2,1)S(1)}, bf16[24,6272]{1,0:T(8,128)(2,1)S(1)}, u32[]{:S(2)}, u32[]{:S(2)}) %collective-permute-start) | collective-permute-done | bytes 301088 | tf_op jit(solution)/shard_map/ppermute | solution.py:300
  16.3 2.3 %collective-permute-start.4 = (bf16[24,6272]{1,0:T(8,128)(2,1)S(1)}, bf16[24,6272]{1,0:T(8,128)(2,1)S(1)}, u32[]{:S(2)}, u32[]{:S(2)}) collective-permute-start(bf16[24,6272]{1,0:T(8,128)(2,1)S(1)} %shard_map.86.refs_0_), channel_id=1, source_target_pairs={{0,12},{1,5},{2,14},{3,7},{4,0},{5,9},{6,2},{7,11},{8,4},{9,13},{1... | collective-permute-start | bytes 903176 | tf_op jit(solution)/shard_map/ppermute | solution.py:300
  18.6 0.0 collective-permute-start.3
  18.6 0.5 collective-permute-start.5
  19.2 8.3 %collective-permute-done.4.refs_3_ = bf16[24,6272]{1,0:T(8,128)(2,1)S(1)} collective-permute-done((bf16[24,6272]{1,0:T(8,128)(2,1)S(1)}, bf16[24,6272]{1,0:T(8,128)(2,1)S(1)}, u32[]{:S(2)}, u32[]{:S(2)}) %collective-permute-start.4) | collective-permute-done | bytes 301088 | tf_op jit(solution)/shard_map/ppermute | solution.py:300
  27.5 0.8 %collective-permute-start.9 = (bf16[24,6272]{1,0:T(8,128)(2,1)S(1)}, bf16[24,6272]{1,0:T(8,128)(2,1)S(1)}, u32[]{:S(2)}, u32[]{:S(2)}) collective-permute-start(bf16[24,6272]{1,0:T(8,128)(2,1)S(1)} %collective-permute-done.4.refs_3_), channel_id=1, source_target_pairs={{0,2},{1,3},{2,0},{3,1},{4,6},{5,7},{6,4},{7,5},{8,10},{9,11},{10,... | collective-permute-start | bytes 903176 | tf_op jit(solution)/shard_map/ppermute | solution.py:300
  28.4 3.8 %collective-permute-done.3.refs_2_ = bf16[24,6272]{1,0:T(8,128)(2,1)S(1)} collective-permute-done((bf16[24,6272]{1,0:T(8,128)(2,1)S(1)}, bf16[24,6272]{1,0:T(8,128)(2,1)S(1)}, u32[]{:S(2)}, u32[]{:S(2)}) %collective-permute-start.3) | collective-permute-done | bytes 301088 | tf_op jit(solution)/shard_map/ppermute | solution.py:300
  32.2 0.5 collective-permute-start.8
  32.7 0.0 collective-permute-done.5.refs_5_
  32.7 6.1 %shard_map.88 = (f32[24,2176]{1,0:T(8,128)S(1)}, f32[24,2176]{1,0:T(8,128)S(1)}, bf16[24,2176]{1,0:T(8,128)(2,1)S(1)}, bf16[24,2176]{1,0:T(8,128)(2,1)S(1)}, bf16[24,4352]{1,0:T(8,128)(2,1)S(1)}) custom-call(bf16[24,6272]{1,0:T(8,128)(2,1)S(1)} %shard_map.86.refs_0_, bf16[24,6272]{1,0:T(8,128)(2,1)S(1)} %collective-permute-done.refs_1_, ...), custom_call_target="tpu_custom_call" | custom-call | flops 4076863488 | bytes 9437184 | tf_op jit(solution)/shard_map/pallas_call | solution.py:252
  38.8 1.6 %collective-permute-start.6 = (bf16[24,4352]{1,0:T(8,128)(2,1)S(1)}, bf16[24,4352]{1,0:T(8,128)(2,1)S(1)}, u32[]{:S(2)}, u32[]{:S(2)}) collective-permute-start(bf16[24,4352]{1,0:T(8,128)(2,1)S(1)} %get-tuple-element.19), channel_id=1, source_target_pairs={{0,2},{1,3},{2,0},{3,1},{4,6},{5,7},{6,4},{7,5},{8,10},{9,11},{10,... | collective-permute-start | bytes 626696 | tf_op jit(solution)/shard_map/ppermute | solution.py:300
  40.4 0.0 collective-permute-start.7
  40.4 3.8 %collective-permute-start.12 = (bf16[24,2176]{1,0:T(8,128)(2,1)S(1)}, bf16[24,2176]{1,0:T(8,128)(2,1)S(1)}, u32[]{:S(2)}, u32[]{:S(2)}) collective-permute-start(bf16[24,2176]{1,0:T(8,128)(2,1)S(1)} %get-tuple-element.27), channel_id=1, source_target_pairs={{0,12},{1,5},{2,14},{3,7},{4,0},{5,9},{6,2},{7,11},{8,4},{9,13},{1... | collective-permute-start | bytes 313352 | tf_op jit(solution)/shard_map/ppermute | solution.py:300
  44.2 0.0 collective-permute-done.9.refs_1_
  44.2 0.0 collective-permute-done.8.refs_0_
  44.2 0.0 copy-start
  44.2 0.0 copy-start.1
  44.2 0.0 copy-start.2
  44.2 4.2 %shard_map.89 = (bf16[24,2176]{1,0:T(8,128)(2,1)S(1)}, bf16[24,2176]{1,0:T(8,128)(2,1)S(1)}) custom-call(bf16[24,6272]{1,0:T(8,128)(2,1)S(1)} %collective-permute-done.8.refs_0_, bf16[24,6272]{1,0:T(8,128)(2,1)S(1)} %collective-permute-done.9.refs_1_, bf16[3,2048,768]{2,1,0:T(8,128)(2,1)S(1)} %shard_map.87.refs_6_.refs_2_), custom_call_target="tpu_custom_call" | custom-call | flops 1358954496 | bytes 9437184 | tf_op jit(solution)/shard_map/pallas_call | solution.py:252
  48.4 0.0 collective-permute-done.12
  48.5 0.0 collective-permute-done.6.refs_1_
  48.5 2.4 %collective-permute-start.13 = (bf16[24,2176]{1,0:T(8,128)(2,1)S(1)}, bf16[24,2176]{1,0:T(8,128)(2,1)S(1)}, u32[]{:S(2)}, u32[]{:S(2)}) collective-permute-start(bf16[24,2176]{1,0:T(8,128)(2,1)S(1)} %add_convert_fusion), channel_id=1, source_target_pairs={{0,12},{1,5},{2,14},{3,7},{4,0},{5,9},{6,2},{7,11},{8,4},{9,13},{1... | collective-permute-start | bytes 313352 | tf_op jit(solution)/shard_map/ppermute | solution.py:300
  50.9 0.0 collective-permute-start.11
  50.9 2.2 %collective-permute-start.10 = (bf16[24,2176]{1,0:T(8,128)(2,1)S(1)}, bf16[24,2176]{1,0:T(8,128)(2,1)S(1)}, u32[]{:S(2)}, u32[]{:S(2)}) collective-permute-start(bf16[24,2176]{1,0:T(8,128)(2,1)S(1)} %get-tuple-element.24), channel_id=1, source_target_pairs={{0,10},{1,11},{2,8},{3,9},{4,14},{5,15},{6,12},{7,13},{8,2},{9,3},... | collective-permute-start | bytes 313352 | tf_op jit(solution)/shard_map/ppermute | solution.py:300
  53.1 0.0 collective-permute-done.7.refs_2_
  53.1 1.7 %collective-permute-done.13.refs_5_ = bf16[24,2176]{1,0:T(8,128)(2,1)S(1)} collective-permute-done((bf16[24,2176]{1,0:T(8,128)(2,1)S(1)}, bf16[24,2176]{1,0:T(8,128)(2,1)S(1)}, u32[]{:S(2)}, u32[]{:S(2)}) %collective-permute-start.13) | collective-permute-done | bytes 104480 | tf_op jit(solution)/shard_map/ppermute | solution.py:300
  54.8 3.8 %collective-permute-done.11.refs_4_ = bf16[24,2176]{1,0:T(8,128)(2,1)S(1)} collective-permute-done((bf16[24,2176]{1,0:T(8,128)(2,1)S(1)}, bf16[24,2176]{1,0:T(8,128)(2,1)S(1)}, u32[]{:S(2)}, u32[]{:S(2)}) %collective-permute-start.11) | collective-permute-done | bytes 104480 | tf_op jit(solution)/shard_map/ppermute | solution.py:300
  58.6 2.7 %collective-permute-done.10.refs_3_ = bf16[24,2176]{1,0:T(8,128)(2,1)S(1)} collective-permute-done((bf16[24,2176]{1,0:T(8,128)(2,1)S(1)}, bf16[24,2176]{1,0:T(8,128)(2,1)S(1)}, u32[]{:S(2)}, u32[]{:S(2)}) %collective-permute-start.10) | collective-permute-done | bytes 104480 | tf_op jit(solution)/shard_map/ppermute | solution.py:300
  61.3 0.0 copy-done
  61.4 0.0 copy-done.1
  61.4 0.0 copy-done.2
  61.4 1.0 %shard_map.90 = (f32[24,2048]{1,0:T(8,128)}, f32[1,24]{1,0:T(1,128)}) custom-call(bf16[24,2048]{1,0:T(8,128)(2,1)S(1)} %copy-done.1, f32[1,2048]{1,0:T(1,128)S(1)} %bitcast.5, s32[24,2048]{1,0:T(8,128)S(1)} %copy-done, f32[24,2176]{1,0:T(8,128)S(1)} %get-tuple-element.18.refs_0_, bf16[24,4352]{1,0:T(8,128)(2,1)S(1)} %collective-permute-done.6.refs_1_, ...), custom_call_target="tpu_custom_call" | custom-call | flops 1966080 | bytes 1277952 | tf_op jit(solution)/shard_map/pallas_call | solution.py:342
  (1 shorter events, 0.0 us)
Async XLA Ops:
  0.6 8.3 %collective-permute-start.2 = (bf16[3,2048,384]{2,1,0:T(8,128)(2,1)}, bf16[3,2048,384]{2,1,0:T(8,128)(2,1)S(1)}, u32[]{:S(2)}, u32[]{:S(2)}) collective-permute-start(bf16[3,2048,384]{2,1,0:T(8,128)(2,1)} %own.1), channel_id=1, source_target_pairs={{0,1},{1,0},{2,3},{3,2},{4,5},{5,4},{6,7},{7,6},{8,9},{9,8},{10,11... | collective-permute-start | bytes 14155784 | tf_op jit(solution)/shard_map/ppermute | solution.py:300
  2.4 10.4 %collective-permute-start.1 = (bf16[24,6272]{1,0:T(8,128)(2,1)S(1)}, bf16[24,6272]{1,0:T(8,128)(2,1)S(1)}, u32[]{:S(2)}, u32[]{:S(2)}) collective-permute-start(bf16[24,6272]{1,0:T(8,128)(2,1)S(1)} %shard_map.86.refs_0_), channel_id=1, source_target_pairs={{0,2},{1,3},{2,0},{3,1},{4,6},{5,7},{6,4},{7,5},{8,10},{9,11},{10,... | collective-permute-start | bytes 903176 | tf_op jit(solution)/shard_map/ppermute | solution.py:300
  5.0 11.3 %collective-permute-start = (bf16[24,6272]{1,0:T(8,128)(2,1)S(1)}, bf16[24,6272]{1,0:T(8,128)(2,1)S(1)}, u32[]{:S(2)}, u32[]{:S(2)}) collective-permute-start(bf16[24,6272]{1,0:T(8,128)(2,1)S(1)} %shard_map.86.refs_0_), channel_id=1, source_target_pairs={{0,4},{1,13},{2,6},{3,15},{4,8},{5,1},{6,10},{7,3},{8,12},{9,5},{1... | collective-permute-start | bytes 903176 | tf_op jit(solution)/shard_map/ppermute | solution.py:300
  16.3 11.2 %collective-permute-start.4 = (bf16[24,6272]{1,0:T(8,128)(2,1)S(1)}, bf16[24,6272]{1,0:T(8,128)(2,1)S(1)}, u32[]{:S(2)}, u32[]{:S(2)}) collective-permute-start(bf16[24,6272]{1,0:T(8,128)(2,1)S(1)} %shard_map.86.refs_0_), channel_id=1, source_target_pairs={{0,12},{1,5},{2,14},{3,7},{4,0},{5,9},{6,2},{7,11},{8,4},{9,13},{1... | collective-permute-start | bytes 903176 | tf_op jit(solution)/shard_map/ppermute | solution.py:300
  18.6 13.6 %collective-permute-start.3 = (bf16[24,6272]{1,0:T(8,128)(2,1)S(1)}, bf16[24,6272]{1,0:T(8,128)(2,1)S(1)}, u32[]{:S(2)}, u32[]{:S(2)}) collective-permute-start(bf16[24,6272]{1,0:T(8,128)(2,1)S(1)} %collective-permute-done.refs_1_), channel_id=1, source_target_pairs={{0,4},{1,13},{2,6},{3,15},{4,8},{5,1},{6,10},{7,3},{8,12},{9,5},{1... | collective-permute-start | bytes 903176 | tf_op jit(solution)/shard_map/ppermute | solution.py:300
  18.6 14.1 %collective-permute-start.5 = (bf16[24,6272]{1,0:T(8,128)(2,1)S(1)}, bf16[24,6272]{1,0:T(8,128)(2,1)S(1)}, u32[]{:S(2)}, u32[]{:S(2)}) collective-permute-start(bf16[24,6272]{1,0:T(8,128)(2,1)S(1)} %collective-permute-done.refs_1_), channel_id=1, source_target_pairs={{0,2},{1,3},{2,0},{3,1},{4,6},{5,7},{6,4},{7,5},{8,10},{9,11},{10,... | collective-permute-start | bytes 903176 | tf_op jit(solution)/shard_map/ppermute | solution.py:300
  27.5 16.7 %collective-permute-start.9 = (bf16[24,6272]{1,0:T(8,128)(2,1)S(1)}, bf16[24,6272]{1,0:T(8,128)(2,1)S(1)}, u32[]{:S(2)}, u32[]{:S(2)}) collective-permute-start(bf16[24,6272]{1,0:T(8,128)(2,1)S(1)} %collective-permute-done.4.refs_3_), channel_id=1, source_target_pairs={{0,2},{1,3},{2,0},{3,1},{4,6},{5,7},{6,4},{7,5},{8,10},{9,11},{10,... | collective-permute-start | bytes 903176 | tf_op jit(solution)/shard_map/ppermute | solution.py:300
  32.2 12.0 %collective-permute-start.8 = (bf16[24,6272]{1,0:T(8,128)(2,1)S(1)}, bf16[24,6272]{1,0:T(8,128)(2,1)S(1)}, u32[]{:S(2)}, u32[]{:S(2)}) collective-permute-start(bf16[24,6272]{1,0:T(8,128)(2,1)S(1)} %collective-permute-done.3.refs_2_), channel_id=1, source_target_pairs={{0,2},{1,3},{2,0},{3,1},{4,6},{5,7},{6,4},{7,5},{8,10},{9,11},{10,... | collective-permute-start | bytes 903176 | tf_op jit(solution)/shard_map/ppermute | solution.py:300
  38.8 9.6 %collective-permute-start.6 = (bf16[24,4352]{1,0:T(8,128)(2,1)S(1)}, bf16[24,4352]{1,0:T(8,128)(2,1)S(1)}, u32[]{:S(2)}, u32[]{:S(2)}) collective-permute-start(bf16[24,4352]{1,0:T(8,128)(2,1)S(1)} %get-tuple-element.19), channel_id=1, source_target_pairs={{0,2},{1,3},{2,0},{3,1},{4,6},{5,7},{6,4},{7,5},{8,10},{9,11},{10,... | collective-permute-start | bytes 626696 | tf_op jit(solution)/shard_map/ppermute | solution.py:300
  40.4 12.7 %collective-permute-start.7 = (bf16[24,2176]{1,0:T(8,128)(2,1)S(1)}, bf16[24,2176]{1,0:T(8,128)(2,1)S(1)}, u32[]{:S(2)}, u32[]{:S(2)}) collective-permute-start(bf16[24,2176]{1,0:T(8,128)(2,1)S(1)} %get-tuple-element.20), channel_id=1, source_target_pairs={{0,4},{1,13},{2,6},{3,15},{4,8},{5,1},{6,10},{7,3},{8,12},{9,5},{1... | collective-permute-start | bytes 313352 | tf_op jit(solution)/shard_map/ppermute | solution.py:300
  40.4 8.1 %collective-permute-start.12 = (bf16[24,2176]{1,0:T(8,128)(2,1)S(1)}, bf16[24,2176]{1,0:T(8,128)(2,1)S(1)}, u32[]{:S(2)}, u32[]{:S(2)}) collective-permute-start(bf16[24,2176]{1,0:T(8,128)(2,1)S(1)} %get-tuple-element.27), channel_id=1, source_target_pairs={{0,12},{1,5},{2,14},{3,7},{4,0},{5,9},{6,2},{7,11},{8,4},{9,13},{1... | collective-permute-start | bytes 313352 | tf_op jit(solution)/shard_map/ppermute | solution.py:300
  44.2 17.1 %copy-start = (s32[24,2048]{1,0:T(8,128)S(1)}, s32[24,2048]{1,0:T(8,128)}, u32[]{:S(2)}) copy-start(s32[24,2048]{1,0:T(8,128)} %signs.1) | copy-start | bytes 589828
  44.2 17.1 %copy-start.1 = (bf16[24,2048]{1,0:T(8,128)(2,1)S(1)}, bf16[24,2048]{1,0:T(8,128)(2,1)}, u32[]{:S(2)}) copy-start(bf16[24,2048]{1,0:T(8,128)(2,1)} %tokens.1) | copy-start | bytes 294916
  44.2 17.1 %copy-start.2 = (f32[2048]{0:T(1024)S(1)}, f32[2048]{0:T(1024)}, u32[]{:S(2)}) copy-start(f32[2048]{0:T(1024)} %param.8) | copy-start | bytes 24580
  48.5 6.3 %collective-permute-start.13 = (bf16[24,2176]{1,0:T(8,128)(2,1)S(1)}, bf16[24,2176]{1,0:T(8,128)(2,1)S(1)}, u32[]{:S(2)}, u32[]{:S(2)}) collective-permute-start(bf16[24,2176]{1,0:T(8,128)(2,1)S(1)} %add_convert_fusion), channel_id=1, source_target_pairs={{0,12},{1,5},{2,14},{3,7},{4,0},{5,9},{6,2},{7,11},{8,4},{9,13},{1... | collective-permute-start | bytes 313352 | tf_op jit(solution)/shard_map/ppermute | solution.py:300
  50.9 7.7 %collective-permute-start.11 = (bf16[24,2176]{1,0:T(8,128)(2,1)S(1)}, bf16[24,2176]{1,0:T(8,128)(2,1)S(1)}, u32[]{:S(2)}, u32[]{:S(2)}) collective-permute-start(bf16[24,2176]{1,0:T(8,128)(2,1)S(1)} %get-tuple-element.25), channel_id=1, source_target_pairs={{0,6},{1,15},{2,4},{3,13},{4,10},{5,3},{6,8},{7,1},{8,14},{9,7},{1... | collective-permute-start | bytes 313352 | tf_op jit(solution)/shard_map/ppermute | solution.py:300
  50.9 10.5 %collective-permute-start.10 = (bf16[24,2176]{1,0:T(8,128)(2,1)S(1)}, bf16[24,2176]{1,0:T(8,128)(2,1)S(1)}, u32[]{:S(2)}, u32[]{:S(2)}) collective-permute-start(bf16[24,2176]{1,0:T(8,128)(2,1)S(1)} %get-tuple-element.24), channel_id=1, source_target_pairs={{0,10},{1,11},{2,8},{3,9},{4,14},{5,15},{6,12},{7,13},{8,2},{9,3},... | collective-permute-start | bytes 313352 | tf_op jit(solution)/shard_map/ppermute | solution.py:300

commit v14 on v12

--- a/solution.py
+++ b/solution.py
@@ -168,8 +168,8 @@
 
 
 def expert_kernel(count, expert_count, *refs):
-    packs, held, outs = (refs[:count], refs[count], refs[count + 1 : -3])
-    both, cotan, acc = refs[-3:]
+    packs, held, outs = (refs[:count], refs[count], refs[count + 1 : -4])
+    both, cotan, slopes, acc = refs[-4:]
     tok_dev = packs[0].shape[0]
     _, width, hidden = held.shape
     rows = count * tok_dev
@@ -213,19 +213,20 @@
         d_up = (back * act).astype(jnp.bfloat16)
         t_gate = (back * (bend * gate_t * up + slope * up_t)).astype(jnp.bfloat16)
         t_up = (back * slope * gate_t).astype(jnp.bfloat16)
-        total = lax.dot_general(
-            jnp.concatenate([d_gate, t_gate], 0),
-            weights(0, start, block),
-            contract,
-            preferred_element_type=jnp.float32,
-        )
-        total = total + lax.dot_general(
-            jnp.concatenate([d_up, t_up], 0),
-            weights(1, start, block),
-            contract,
-            preferred_element_type=jnp.float32,
-        )
-        acc[...] = total if start == 0 else acc[...] + total
+        for n, (own, along) in enumerate(((d_gate, t_gate), (d_up, t_up))):
+            slopes[n, :rows, start : start + block] = own
+            slopes[n, rows:, start : start + block] = along
+    block = 256 if width % 256 == 0 else width
+    for start in range(0, width, block):
+        acc[:, start : start + block] = sum(
+            lax.dot_general(
+                slopes[n],
+                held[n, start : start + block, :],
+                contract,
+                preferred_element_type=jnp.float32,
+            )
+            for n in range(2)
+        )
     homes = [out.at[:, pl.ds(at, width + 128)] for out in outs for at in range(0, out.shape[1], width + 128)]
     for n, home in enumerate(homes):
         part = slice(n * tok_dev, (n + 1) * tok_dev)
@@ -257,6 +258,7 @@
         scratch_shapes=[
             pltpu.VMEM((2 * rows, width), jnp.bfloat16),
             pltpu.VMEM((rows, width), jnp.bfloat16),
+            pltpu.VMEM((2, 2 * rows, hidden), jnp.bfloat16),
             pltpu.VMEM((2 * rows, width), jnp.float32),
         ],
         compiler_params=pltpu.CompilerParams(vmem_limit_bytes=VMEM),

time: 59.7 us -> 59.1 us (0.990)
  Pallas kernels: 14.9 us -> 13.4 us
  starting transfers between devices: 17.7 us -> 18.6 us
    pallas_call x2, Pallas kernels: 10.3 us -> 8.74 us  [experts(): pl.pallas_call(functools.partial(expert_kernel, count, expert_count), out...]
    ppermute x14, starting transfers between devices: 17.7 us -> 18.6 us  [moved(): return lax.ppermute(rows, 'expert', pairs)]
  transfers between devices with their start and end apart: 14 -> 14, of which waited for: 8 -> 8; matrix products, arithmetic and copies ran while one was open for 0% -> 0% of each run, Pallas kernels for 23% -> 21%
where the time goes in v14:
time: 59.1 us; the launch traced here: 58.9 us
  waiting for transfers between devices  26.1 us (44%)
  starting transfers between devices  18.6 us (31%)
  Pallas kernels  13.4 us (23%)
  between operations  0.72 us (1%)
    ppermute x14, waiting for transfers between devices, moved(): return lax.ppermute(rows, 'expert', pairs)  26.1 us
    ppermute x14, starting transfers between devices, moved(): return lax.ppermute(rows, 'expert', pairs)  18.6 us
    pallas_call x2, Pallas kernels, experts(): pl.pallas_call(functools.partial(expert_kernel, count, expert_count), out...  8.74 us
    pallas_call x1, Pallas kernels, joined(): pl.pallas_call(join_kernel, out_shape=pltpu.VMEM((parts, width, 2 * half)...  2.41 us
    pallas_call x1, Pallas kernels, packed(): pl.pallas_call(functools.partial(pack_kernel, expert_count), out_shape=ja...  1.29 us
  transfers between devices with their start and end apart: 14, of which 8 were waited for; matrix products, arithmetic and copies ran while one was open for 0% of the time, Pallas kernels for 21%

profile of v14, /device:TPU:0, one launch (start us, length us, event | category | flops | bytes accessed | tf_op | source)
XLA Modules:
  0.0 58.9 jit_solution(9361858236970794796)
XLA Ops:
  0.6 0.5 collective-permute-start.2
  1.1 1.3 %shard_map.86.refs_0_ = bf16[24,6272]{1,0:T(8,128)(2,1)S(1)} custom-call(bf16[24,2048]{1,0:T(8,128)(2,1)} %tokens.1, f32[1,2048]{1,0:T(1,128)} %bitcast.4, s32[24,2048]{1,0:T(8,128)} %signs.1, bf16[24,2048]{1,0:T(8,128)(2,1)} %refs_3_.1, s32[2,4,24]{2,1,0:T(4,128)} %bitcast.6, f32[2,4,24]{2,1,0:T(4,128)} %bitcast.7), custom_call_target="tpu_custom_call" | custom-call | flops 983040 | bytes 688128 | tf_op jit(solution)/shard_map/pallas_call | solution.py:126
  2.4 2.6 %collective-permute-start.1 = (bf16[24,6272]{1,0:T(8,128)(2,1)S(1)}, bf16[24,6272]{1,0:T(8,128)(2,1)S(1)}, u32[]{:S(2)}, u32[]{:S(2)}) collective-permute-start(bf16[24,6272]{1,0:T(8,128)(2,1)S(1)} %shard_map.86.refs_0_), channel_id=1, source_target_pairs={{0,2},{1,3},{2,0},{3,1},{4,6},{5,7},{6,4},{7,5},{8,10},{9,11},{10,... | collective-permute-start | bytes 903176 | tf_op jit(solution)/shard_map/ppermute | solution.py:301
  5.0 1.6 %collective-permute-start = (bf16[24,6272]{1,0:T(8,128)(2,1)S(1)}, bf16[24,6272]{1,0:T(8,128)(2,1)S(1)}, u32[]{:S(2)}, u32[]{:S(2)}) collective-permute-start(bf16[24,6272]{1,0:T(8,128)(2,1)S(1)} %shard_map.86.refs_0_), channel_id=1, source_target_pairs={{0,4},{1,5},{2,6},{3,7},{4,8},{5,9},{6,10},{7,11},{8,12},{9,13},{1... | collective-permute-start | bytes 903176 | tf_op jit(solution)/shard_map/ppermute | solution.py:301
  6.6 2.3 %collective-permute-done.2.other = bf16[3,2048,384]{2,1,0:T(8,128)(2,1)S(1)} collective-permute-done((bf16[3,2048,384]{2,1,0:T(8,128)(2,1)}, bf16[3,2048,384]{2,1,0:T(8,128)(2,1)S(1)}, u32[]{:S(2)}, u32[]{:S(2)}) %collective-permute-start.2) | collective-permute-done | bytes 4718624 | tf_op jit(solution)/shard_map/ppermute | solution.py:301
  8.9 2.4 %shard_map.87.refs_6_.refs_2_ = bf16[3,2048,768]{2,1,0:T(8,128)(2,1)S(1)} custom-call(bf16[3,2048,384]{2,1,0:T(8,128)(2,1)} %own.1, bf16[3,2048,384]{2,1,0:T(8,128)(2,1)S(1)} %collective-permute-done.2.other), custom_call_target="tpu_custom_call" | custom-call | bytes 18874368 | tf_op jit(solution)/shard_map/pallas_call | solution.py:157
  11.3 1.5 %collective-permute-done.1.refs_4_ = bf16[24,6272]{1,0:T(8,128)(2,1)S(1)} collective-permute-done((bf16[24,6272]{1,0:T(8,128)(2,1)S(1)}, bf16[24,6272]{1,0:T(8,128)(2,1)S(1)}, u32[]{:S(2)}, u32[]{:S(2)}) %collective-permute-start.1) | collective-permute-done | bytes 301088 | tf_op jit(solution)/shard_map/ppermute | solution.py:301
  12.8 3.3 %collective-permute-done.refs_1_ = bf16[24,6272]{1,0:T(8,128)(2,1)S(1)} collective-permute-done((bf16[24,6272]{1,0:T(8,128)(2,1)S(1)}, bf16[24,6272]{1,0:T(8,128)(2,1)S(1)}, u32[]{:S(2)}, u32[]{:S(2)}) %collective-permute-start) | collective-permute-done | bytes 301088 | tf_op jit(solution)/shard_map/ppermute | solution.py:301
  16.1 1.7 %collective-permute-start.4 = (bf16[24,6272]{1,0:T(8,128)(2,1)S(1)}, bf16[24,6272]{1,0:T(8,128)(2,1)S(1)}, u32[]{:S(2)}, u32[]{:S(2)}) collective-permute-start(bf16[24,6272]{1,0:T(8,128)(2,1)S(1)} %shard_map.86.refs_0_), channel_id=1, source_target_pairs={{0,12},{1,13},{2,14},{3,15},{4,0},{5,1},{6,2},{7,3},{8,4},{9,5},{1... | collective-permute-start | bytes 903176 | tf_op jit(solution)/shard_map/ppermute | solution.py:301
  17.9 0.3 collective-permute-start.3
  18.2 0.5 collective-permute-start.5
  18.7 7.5 %collective-permute-done.4.refs_3_ = bf16[24,6272]{1,0:T(8,128)(2,1)S(1)} collective-permute-done((bf16[24,6272]{1,0:T(8,128)(2,1)S(1)}, bf16[24,6272]{1,0:T(8,128)(2,1)S(1)}, u32[]{:S(2)}, u32[]{:S(2)}) %collective-permute-start.4) | collective-permute-done | bytes 301088 | tf_op jit(solution)/shard_map/ppermute | solution.py:301
  26.2 0.7 %collective-permute-start.9 = (bf16[24,6272]{1,0:T(8,128)(2,1)S(1)}, bf16[24,6272]{1,0:T(8,128)(2,1)S(1)}, u32[]{:S(2)}, u32[]{:S(2)}) collective-permute-start(bf16[24,6272]{1,0:T(8,128)(2,1)S(1)} %collective-permute-done.4.refs_3_), channel_id=1, source_target_pairs={{0,2},{1,3},{2,0},{3,1},{4,6},{5,7},{6,4},{7,5},{8,10},{9,11},{10,... | collective-permute-start | bytes 903176 | tf_op jit(solution)/shard_map/ppermute | solution.py:301
  26.8 4.3 %collective-permute-done.3.refs_2_ = bf16[24,6272]{1,0:T(8,128)(2,1)S(1)} collective-permute-done((bf16[24,6272]{1,0:T(8,128)(2,1)S(1)}, bf16[24,6272]{1,0:T(8,128)(2,1)S(1)}, u32[]{:S(2)}, u32[]{:S(2)}) %collective-permute-start.3) | collective-permute-done | bytes 301088 | tf_op jit(solution)/shard_map/ppermute | solution.py:301
  31.2 0.7 %collective-permute-start.8 = (bf16[24,6272]{1,0:T(8,128)(2,1)S(1)}, bf16[24,6272]{1,0:T(8,128)(2,1)S(1)}, u32[]{:S(2)}, u32[]{:S(2)}) collective-permute-start(bf16[24,6272]{1,0:T(8,128)(2,1)S(1)} %collective-permute-done.3.refs_2_), channel_id=1, source_target_pairs={{0,2},{1,3},{2,0},{3,1},{4,6},{5,7},{6,4},{7,5},{8,10},{9,11},{10,... | collective-permute-start | bytes 903176 | tf_op jit(solution)/shard_map/ppermute | solution.py:301
  31.9 0.0 collective-permute-done.5.refs_5_
  31.9 4.9 %shard_map.88 = (f32[24,2176]{1,0:T(8,128)S(1)}, f32[24,2176]{1,0:T(8,128)S(1)}, bf16[24,2176]{1,0:T(8,128)(2,1)S(1)}, bf16[24,2176]{1,0:T(8,128)(2,1)S(1)}, bf16[24,4352]{1,0:T(8,128)(2,1)S(1)}) custom-call(bf16[24,6272]{1,0:T(8,128)(2,1)S(1)} %shard_map.86.refs_0_, bf16[24,6272]{1,0:T(8,128)(2,1)S(1)} %collective-permute-done.refs_1_, ...), custom_call_target="tpu_custom_call" | custom-call | flops 4076863488 | bytes 9437184 | tf_op jit(solution)/shard_map/pallas_call | solution.py:253
  36.8 1.4 %collective-permute-start.6 = (bf16[24,4352]{1,0:T(8,128)(2,1)S(1)}, bf16[24,4352]{1,0:T(8,128)(2,1)S(1)}, u32[]{:S(2)}, u32[]{:S(2)}) collective-permute-start(bf16[24,4352]{1,0:T(8,128)(2,1)S(1)} %get-tuple-element.19), channel_id=1, source_target_pairs={{0,2},{1,3},{2,0},{3,1},{4,6},{5,7},{6,4},{7,5},{8,10},{9,11},{10,... | collective-permute-start | bytes 626696 | tf_op jit(solution)/shard_map/ppermute | solution.py:301
  38.2 1.6 %collective-permute-start.7 = (bf16[24,2176]{1,0:T(8,128)(2,1)S(1)}, bf16[24,2176]{1,0:T(8,128)(2,1)S(1)}, u32[]{:S(2)}, u32[]{:S(2)}) collective-permute-start(bf16[24,2176]{1,0:T(8,128)(2,1)S(1)} %get-tuple-element.20), channel_id=1, source_target_pairs={{0,4},{1,5},{2,6},{3,7},{4,8},{5,9},{6,10},{7,11},{8,12},{9,13},{1... | collective-permute-start | bytes 313352 | tf_op jit(solution)/shard_map/ppermute | solution.py:301
  39.8 2.2 %collective-permute-start.12 = (bf16[24,2176]{1,0:T(8,128)(2,1)S(1)}, bf16[24,2176]{1,0:T(8,128)(2,1)S(1)}, u32[]{:S(2)}, u32[]{:S(2)}) collective-permute-start(bf16[24,2176]{1,0:T(8,128)(2,1)S(1)} %get-tuple-element.27), channel_id=1, source_target_pairs={{0,12},{1,13},{2,14},{3,15},{4,0},{5,1},{6,2},{7,3},{8,4},{9,5},{1... | collective-permute-start | bytes 313352 | tf_op jit(solution)/shard_map/ppermute | solution.py:301
  42.0 0.0 collective-permute-done.9.refs_1_
  42.0 0.0 collective-permute-done.8.refs_0_
  42.0 0.0 copy-start
  42.0 0.0 copy-start.1
  42.0 0.0 copy-start.2
  42.1 3.8 %shard_map.89 = (bf16[24,2176]{1,0:T(8,128)(2,1)S(1)}, bf16[24,2176]{1,0:T(8,128)(2,1)S(1)}) custom-call(bf16[24,6272]{1,0:T(8,128)(2,1)S(1)} %collective-permute-done.8.refs_0_, bf16[24,6272]{1,0:T(8,128)(2,1)S(1)} %collective-permute-done.9.refs_1_, bf16[3,2048,768]{2,1,0:T(8,128)(2,1)S(1)} %shard_map.87.refs_6_.refs_2_), custom_call_target="tpu_custom_call" | custom-call | flops 1358954496 | bytes 9437184 | tf_op jit(solution)/shard_map/pallas_call | solution.py:253
  45.9 0.0 collective-permute-done.12
  45.9 0.0 collective-permute-done.6.refs_1_
  46.0 3.2 %collective-permute-start.13 = (bf16[24,2176]{1,0:T(8,128)(2,1)S(1)}, bf16[24,2176]{1,0:T(8,128)(2,1)S(1)}, u32[]{:S(2)}, u32[]{:S(2)}) collective-permute-start(bf16[24,2176]{1,0:T(8,128)(2,1)S(1)} %add_convert_fusion), channel_id=1, source_target_pairs={{0,12},{1,13},{2,14},{3,15},{4,0},{5,1},{6,2},{7,3},{8,4},{9,5},{1... | collective-permute-start | bytes 313352 | tf_op jit(solution)/shard_map/ppermute | solution.py:301
  49.2 0.0 collective-permute-start.11
  49.2 1.5 %collective-permute-start.10 = (bf16[24,2176]{1,0:T(8,128)(2,1)S(1)}, bf16[24,2176]{1,0:T(8,128)(2,1)S(1)}, u32[]{:S(2)}, u32[]{:S(2)}) collective-permute-start(bf16[24,2176]{1,0:T(8,128)(2,1)S(1)} %get-tuple-element.24), channel_id=1, source_target_pairs={{0,10},{1,11},{2,8},{3,9},{4,14},{5,15},{6,12},{7,13},{8,2},{9,3},... | collective-permute-start | bytes 313352 | tf_op jit(solution)/shard_map/ppermute | solution.py:301
  50.7 0.0 collective-permute-done.7.refs_2_
  50.7 1.6 %collective-permute-done.13.refs_5_ = bf16[24,2176]{1,0:T(8,128)(2,1)S(1)} collective-permute-done((bf16[24,2176]{1,0:T(8,128)(2,1)S(1)}, bf16[24,2176]{1,0:T(8,128)(2,1)S(1)}, u32[]{:S(2)}, u32[]{:S(2)}) %collective-permute-start.13) | collective-permute-done | bytes 104480 | tf_op jit(solution)/shard_map/ppermute | solution.py:301
  52.3 4.4 %collective-permute-done.11.refs_4_ = bf16[24,2176]{1,0:T(8,128)(2,1)S(1)} collective-permute-done((bf16[24,2176]{1,0:T(8,128)(2,1)S(1)}, bf16[24,2176]{1,0:T(8,128)(2,1)S(1)}, u32[]{:S(2)}, u32[]{:S(2)}) %collective-permute-start.11) | collective-permute-done | bytes 104480 | tf_op jit(solution)/shard_map/ppermute | solution.py:301
  56.7 1.2 %collective-permute-done.10.refs_3_ = bf16[24,2176]{1,0:T(8,128)(2,1)S(1)} collective-permute-done((bf16[24,2176]{1,0:T(8,128)(2,1)S(1)}, bf16[24,2176]{1,0:T(8,128)(2,1)S(1)}, u32[]{:S(2)}, u32[]{:S(2)}) %collective-permute-start.10) | collective-permute-done | bytes 104480 | tf_op jit(solution)/shard_map/ppermute | solution.py:301
  57.9 0.0 copy-done
  57.9 0.0 copy-done.1
  57.9 0.0 copy-done.2
  57.9 1.0 %shard_map.90 = (f32[24,2048]{1,0:T(8,128)}, f32[1,24]{1,0:T(1,128)}) custom-call(bf16[24,2048]{1,0:T(8,128)(2,1)S(1)} %copy-done.1, f32[1,2048]{1,0:T(1,128)S(1)} %bitcast.5, s32[24,2048]{1,0:T(8,128)S(1)} %copy-done, f32[24,2176]{1,0:T(8,128)S(1)} %get-tuple-element.18.refs_0_, bf16[24,4352]{1,0:T(8,128)(2,1)S(1)} %collective-permute-done.6.refs_1_, ...), custom_call_target="tpu_custom_call" | custom-call | flops 1966080 | bytes 1277952 | tf_op jit(solution)/shard_map/pallas_call | solution.py:343
  (1 shorter events, 0.0 us)
Async XLA Ops:
  0.6 8.3 %collective-permute-start.2 = (bf16[3,2048,384]{2,1,0:T(8,128)(2,1)}, bf16[3,2048,384]{2,1,0:T(8,128)(2,1)S(1)}, u32[]{:S(2)}, u32[]{:S(2)}) collective-permute-start(bf16[3,2048,384]{2,1,0:T(8,128)(2,1)} %own.1), channel_id=1, source_target_pairs={{0,1},{1,0},{2,3},{3,2},{4,5},{5,4},{6,7},{7,6},{8,9},{9,8},{10,11... | collective-permute-start | bytes 14155784 | tf_op jit(solution)/shard_map/ppermute | solution.py:301
  2.4 10.4 %collective-permute-start.1 = (bf16[24,6272]{1,0:T(8,128)(2,1)S(1)}, bf16[24,6272]{1,0:T(8,128)(2,1)S(1)}, u32[]{:S(2)}, u32[]{:S(2)}) collective-permute-start(bf16[24,6272]{1,0:T(8,128)(2,1)S(1)} %shard_map.86.refs_0_), channel_id=1, source_target_pairs={{0,2},{1,3},{2,0},{3,1},{4,6},{5,7},{6,4},{7,5},{8,10},{9,11},{10,... | collective-permute-start | bytes 903176 | tf_op jit(solution)/shard_map/ppermute | solution.py:301
  5.0 11.1 %collective-permute-start = (bf16[24,6272]{1,0:T(8,128)(2,1)S(1)}, bf16[24,6272]{1,0:T(8,128)(2,1)S(1)}, u32[]{:S(2)}, u32[]{:S(2)}) collective-permute-start(bf16[24,6272]{1,0:T(8,128)(2,1)S(1)} %shard_map.86.refs_0_), channel_id=1, source_target_pairs={{0,4},{1,5},{2,6},{3,7},{4,8},{5,9},{6,10},{7,11},{8,12},{9,13},{1... | collective-permute-start | bytes 903176 | tf_op jit(solution)/shard_map/ppermute | solution.py:301
  16.1 10.0 %collective-permute-start.4 = (bf16[24,6272]{1,0:T(8,128)(2,1)S(1)}, bf16[24,6272]{1,0:T(8,128)(2,1)S(1)}, u32[]{:S(2)}, u32[]{:S(2)}) collective-permute-start(bf16[24,6272]{1,0:T(8,128)(2,1)S(1)} %shard_map.86.refs_0_), channel_id=1, source_target_pairs={{0,12},{1,13},{2,14},{3,15},{4,0},{5,1},{6,2},{7,3},{8,4},{9,5},{1... | collective-permute-start | bytes 903176 | tf_op jit(solution)/shard_map/ppermute | solution.py:301
  17.9 13.3 %collective-permute-start.3 = (bf16[24,6272]{1,0:T(8,128)(2,1)S(1)}, bf16[24,6272]{1,0:T(8,128)(2,1)S(1)}, u32[]{:S(2)}, u32[]{:S(2)}) collective-permute-start(bf16[24,6272]{1,0:T(8,128)(2,1)S(1)} %collective-permute-done.refs_1_), channel_id=1, source_target_pairs={{0,4},{1,5},{2,6},{3,7},{4,8},{5,9},{6,10},{7,11},{8,12},{9,13},{1... | collective-permute-start | bytes 903176 | tf_op jit(solution)/shard_map/ppermute | solution.py:301
  18.2 13.7 %collective-permute-start.5 = (bf16[24,6272]{1,0:T(8,128)(2,1)S(1)}, bf16[24,6272]{1,0:T(8,128)(2,1)S(1)}, u32[]{:S(2)}, u32[]{:S(2)}) collective-permute-start(bf16[24,6272]{1,0:T(8,128)(2,1)S(1)} %collective-permute-done.refs_1_), channel_id=1, source_target_pairs={{0,2},{1,3},{2,0},{3,1},{4,6},{5,7},{6,4},{7,5},{8,10},{9,11},{10,... | collective-permute-start | bytes 903176 | tf_op jit(solution)/shard_map/ppermute | solution.py:301
  26.2 15.8 %collective-permute-start.9 = (bf16[24,6272]{1,0:T(8,128)(2,1)S(1)}, bf16[24,6272]{1,0:T(8,128)(2,1)S(1)}, u32[]{:S(2)}, u32[]{:S(2)}) collective-permute-start(bf16[24,6272]{1,0:T(8,128)(2,1)S(1)} %collective-permute-done.4.refs_3_), channel_id=1, source_target_pairs={{0,2},{1,3},{2,0},{3,1},{4,6},{5,7},{6,4},{7,5},{8,10},{9,11},{10,... | collective-permute-start | bytes 903176 | tf_op jit(solution)/shard_map/ppermute | solution.py:301
  31.2 10.8 %collective-permute-start.8 = (bf16[24,6272]{1,0:T(8,128)(2,1)S(1)}, bf16[24,6272]{1,0:T(8,128)(2,1)S(1)}, u32[]{:S(2)}, u32[]{:S(2)}) collective-permute-start(bf16[24,6272]{1,0:T(8,128)(2,1)S(1)} %collective-permute-done.3.refs_2_), channel_id=1, source_target_pairs={{0,2},{1,3},{2,0},{3,1},{4,6},{5,7},{6,4},{7,5},{8,10},{9,11},{10,... | collective-permute-start | bytes 903176 | tf_op jit(solution)/shard_map/ppermute | solution.py:301
  36.8 9.1 %collective-permute-start.6 = (bf16[24,4352]{1,0:T(8,128)(2,1)S(1)}, bf16[24,4352]{1,0:T(8,128)(2,1)S(1)}, u32[]{:S(2)}, u32[]{:S(2)}) collective-permute-start(bf16[24,4352]{1,0:T(8,128)(2,1)S(1)} %get-tuple-element.19), channel_id=1, source_target_pairs={{0,2},{1,3},{2,0},{3,1},{4,6},{5,7},{6,4},{7,5},{8,10},{9,11},{10,... | collective-permute-start | bytes 626696 | tf_op jit(solution)/shard_map/ppermute | solution.py:301
  38.2 12.6 %collective-permute-start.7 = (bf16[24,2176]{1,0:T(8,128)(2,1)S(1)}, bf16[24,2176]{1,0:T(8,128)(2,1)S(1)}, u32[]{:S(2)}, u32[]{:S(2)}) collective-permute-start(bf16[24,2176]{1,0:T(8,128)(2,1)S(1)} %get-tuple-element.20), channel_id=1, source_target_pairs={{0,4},{1,5},{2,6},{3,7},{4,8},{5,9},{6,10},{7,11},{8,12},{9,13},{1... | collective-permute-start | bytes 313352 | tf_op jit(solution)/shard_map/ppermute | solution.py:301
  39.8 6.1 %collective-permute-start.12 = (bf16[24,2176]{1,0:T(8,128)(2,1)S(1)}, bf16[24,2176]{1,0:T(8,128)(2,1)S(1)}, u32[]{:S(2)}, u32[]{:S(2)}) collective-permute-start(bf16[24,2176]{1,0:T(8,128)(2,1)S(1)} %get-tuple-element.27), channel_id=1, source_target_pairs={{0,12},{1,13},{2,14},{3,15},{4,0},{5,1},{6,2},{7,3},{8,4},{9,5},{1... | collective-permute-start | bytes 313352 | tf_op jit(solution)/shard_map/ppermute | solution.py:301
  42.0 15.9 %copy-start = (s32[24,2048]{1,0:T(8,128)S(1)}, s32[24,2048]{1,0:T(8,128)}, u32[]{:S(2)}) copy-start(s32[24,2048]{1,0:T(8,128)} %signs.1) | copy-start | bytes 589828
  42.0 15.9 %copy-start.1 = (bf16[24,2048]{1,0:T(8,128)(2,1)S(1)}, bf16[24,2048]{1,0:T(8,128)(2,1)}, u32[]{:S(2)}) copy-start(bf16[24,2048]{1,0:T(8,128)(2,1)} %tokens.1) | copy-start | bytes 294916
  42.0 15.9 %copy-start.2 = (f32[2048]{0:T(1024)S(1)}, f32[2048]{0:T(1024)}, u32[]{:S(2)}) copy-start(f32[2048]{0:T(1024)} %param.8) | copy-start | bytes 24580
  46.0 6.3 %collective-permute-start.13 = (bf16[24,2176]{1,0:T(8,128)(2,1)S(1)}, bf16[24,2176]{1,0:T(8,128)(2,1)S(1)}, u32[]{:S(2)}, u32[]{:S(2)}) collective-permute-start(bf16[24,2176]{1,0:T(8,128)(2,1)S(1)} %add_convert_fusion), channel_id=1, source_target_pairs={{0,12},{1,13},{2,14},{3,15},{4,0},{5,1},{6,2},{7,3},{8,4},{9,5},{1... | collective-permute-start | bytes 313352 | tf_op jit(solution)/shard_map/ppermute | solution.py:301
  49.2 7.5 %collective-permute-start.11 = (bf16[24,2176]{1,0:T(8,128)(2,1)S(1)}, bf16[24,2176]{1,0:T(8,128)(2,1)S(1)}, u32[]{:S(2)}, u32[]{:S(2)}) collective-permute-start(bf16[24,2176]{1,0:T(8,128)(2,1)S(1)} %get-tuple-element.25), channel_id=1, source_target_pairs={{0,6},{1,7},{2,4},{3,5},{4,10},{5,11},{6,8},{7,9},{8,14},{9,15},{1... | collective-permute-start | bytes 313352 | tf_op jit(solution)/shard_map/ppermute | solution.py:301
  49.2 8.7 %collective-permute-start.10 = (bf16[24,2176]{1,0:T(8,128)(2,1)S(1)}, bf16[24,2176]{1,0:T(8,128)(2,1)S(1)}, u32[]{:S(2)}, u32[]{:S(2)}) collective-permute-start(bf16[24,2176]{1,0:T(8,128)(2,1)S(1)} %get-tuple-element.24), channel_id=1, source_target_pairs={{0,10},{1,11},{2,8},{3,9},{4,14},{5,15},{6,12},{7,13},{8,2},{9,3},... | collective-permute-start | bytes 313352 | tf_op jit(solution)/shard_map/ppermute | solution.py:301

commit v15 on v14

--- a/solution.py
+++ b/solution.py
@@ -310,8 +310,8 @@
     same, across = {0: pack}, {}
     same[1] = moved(pack, 1)
     across[0] = moved(pack, 0, flip_x=True)
-    same[1] = lax.optimization_barrier((same[1], across[0], held))[0]
-    same[3] = moved(lax.optimization_barrier((pack, same[1]))[0], -1)
+    same[1] = lax.optimization_barrier((same[1], across[0]))[0]
+    same[3] = moved(lax.optimization_barrier((pack, same[1], held))[0], -1)
     same[2] = moved(same[1], 1)
     across[1] = moved(same[1], 0, flip_x=True)
     across[3] = moved(same[3], 0, flip_x=True)

time: 59.1 us -> 58.9 us (level)
  starting transfers between devices: 18.6 us -> 16.2 us
  waiting for transfers between devices: 26.1 us -> 28.4 us
    ppermute x14, starting transfers between devices: 18.6 us -> 16.2 us  [moved(): return lax.ppermute(rows, 'expert', pairs)]
    ppermute x14, waiting for transfers between devices: 26.1 us -> 28.4 us  [moved(): return lax.ppermute(rows, 'expert', pairs)]
where the time goes in v15:
time: 58.9 us; the launch traced here: 58.7 us
  waiting for transfers between devices  28.4 us (48%)
  starting transfers between devices  16.2 us (28%)
  Pallas kernels  13.4 us (23%)
  between operations  0.71 us (1%)
    ppermute x14, waiting for transfers between devices, moved(): return lax.ppermute(rows, 'expert', pairs)  28.4 us
    ppermute x14, starting transfers between devices, moved(): return lax.ppermute(rows, 'expert', pairs)  16.2 us
    pallas_call x2, Pallas kernels, experts(): pl.pallas_call(functools.partial(expert_kernel, count, expert_count), out...  8.73 us
    pallas_call x1, Pallas kernels, joined(): pl.pallas_call(join_kernel, out_shape=pltpu.VMEM((parts, width, 2 * half)...  2.41 us
    pallas_call x1, Pallas kernels, packed(): pl.pallas_call(functools.partial(pack_kernel, expert_count), out_shape=ja...  1.29 us
  transfers between devices with their start and end apart: 14, of which 8 were waited for; matrix products, arithmetic and copies ran while one was open for 0% of the time, Pallas kernels for 21%

profile of v15, /device:TPU:0, one launch (start us, length us, event | category | flops | bytes accessed | tf_op | source)
XLA Modules:
  0.0 58.7 jit_solution(9715523267867389579)
XLA Ops:
  0.6 0.5 collective-permute-start.3
  1.1 1.3 %shard_map.86.refs_0_ = bf16[24,6272]{1,0:T(8,128)(2,1)S(1)} custom-call(bf16[24,2048]{1,0:T(8,128)(2,1)} %tokens.1, f32[1,2048]{1,0:T(1,128)} %bitcast.4, s32[24,2048]{1,0:T(8,128)} %signs.1, bf16[24,2048]{1,0:T(8,128)(2,1)} %refs_3_.1, s32[2,4,24]{2,1,0:T(4,128)} %bitcast.6, f32[2,4,24]{2,1,0:T(4,128)} %bitcast.7), custom_call_target="tpu_custom_call" | custom-call | flops 983040 | bytes 688128 | tf_op jit(solution)/shard_map/pallas_call | solution.py:126
  2.4 2.6 %collective-permute-start.1 = (bf16[24,6272]{1,0:T(8,128)(2,1)S(1)}, bf16[24,6272]{1,0:T(8,128)(2,1)S(1)}, u32[]{:S(2)}, u32[]{:S(2)}) collective-permute-start(bf16[24,6272]{1,0:T(8,128)(2,1)S(1)} %shard_map.86.refs_0_), channel_id=1, source_target_pairs={{0,2},{1,3},{2,0},{3,1},{4,6},{5,7},{6,4},{7,5},{8,10},{9,11},{10,... | collective-permute-start | bytes 903176 | tf_op jit(solution)/shard_map/ppermute | solution.py:301
  5.0 1.6 %collective-permute-start = (bf16[24,6272]{1,0:T(8,128)(2,1)S(1)}, bf16[24,6272]{1,0:T(8,128)(2,1)S(1)}, u32[]{:S(2)}, u32[]{:S(2)}) collective-permute-start(bf16[24,6272]{1,0:T(8,128)(2,1)S(1)} %shard_map.86.refs_0_), channel_id=1, source_target_pairs={{0,4},{1,5},{2,6},{3,7},{4,8},{5,9},{6,10},{7,11},{8,12},{9,13},{1... | collective-permute-start | bytes 903176 | tf_op jit(solution)/shard_map/ppermute | solution.py:301
  6.6 6.2 %collective-permute-done.1.refs_4_ = bf16[24,6272]{1,0:T(8,128)(2,1)S(1)} collective-permute-done((bf16[24,6272]{1,0:T(8,128)(2,1)S(1)}, bf16[24,6272]{1,0:T(8,128)(2,1)S(1)}, u32[]{:S(2)}, u32[]{:S(2)}) %collective-permute-start.1) | collective-permute-done | bytes 301088 | tf_op jit(solution)/shard_map/ppermute | solution.py:301
  12.8 3.3 %collective-permute-done.refs_1_ = bf16[24,6272]{1,0:T(8,128)(2,1)S(1)} collective-permute-done((bf16[24,6272]{1,0:T(8,128)(2,1)S(1)}, bf16[24,6272]{1,0:T(8,128)(2,1)S(1)}, u32[]{:S(2)}, u32[]{:S(2)}) %collective-permute-start) | collective-permute-done | bytes 301088 | tf_op jit(solution)/shard_map/ppermute | solution.py:301
  16.1 0.0 collective-permute-start.2
  16.1 0.0 collective-permute-done.3.other
  16.1 2.4 %shard_map.87.refs_6_.refs_2_ = bf16[3,2048,768]{2,1,0:T(8,128)(2,1)S(1)} custom-call(bf16[3,2048,384]{2,1,0:T(8,128)(2,1)} %own.1, bf16[3,2048,384]{2,1,0:T(8,128)(2,1)S(1)} %collective-permute-done.3.other), custom_call_target="tpu_custom_call" | custom-call | bytes 18874368 | tf_op jit(solution)/shard_map/pallas_call | solution.py:157
  18.6 3.9 %collective-permute-start.4 = (bf16[24,6272]{1,0:T(8,128)(2,1)S(1)}, bf16[24,6272]{1,0:T(8,128)(2,1)S(1)}, u32[]{:S(2)}, u32[]{:S(2)}) collective-permute-start(bf16[24,6272]{1,0:T(8,128)(2,1)S(1)} %shard_map.86.refs_0_), channel_id=1, source_target_pairs={{0,12},{1,13},{2,14},{3,15},{4,0},{5,1},{6,2},{7,3},{8,4},{9,5},{1... | collective-permute-start | bytes 903176 | tf_op jit(solution)/shard_map/ppermute | solution.py:301
  22.4 0.5 collective-permute-start.5
  23.0 5.1 %collective-permute-done.2.refs_2_ = bf16[24,6272]{1,0:T(8,128)(2,1)S(1)} collective-permute-done((bf16[24,6272]{1,0:T(8,128)(2,1)S(1)}, bf16[24,6272]{1,0:T(8,128)(2,1)S(1)}, u32[]{:S(2)}, u32[]{:S(2)}) %collective-permute-start.2) | collective-permute-done | bytes 301088 | tf_op jit(solution)/shard_map/ppermute | solution.py:301
  28.1 0.5 collective-permute-start.8
  28.6 4.3 %collective-permute-done.4.refs_3_ = bf16[24,6272]{1,0:T(8,128)(2,1)S(1)} collective-permute-done((bf16[24,6272]{1,0:T(8,128)(2,1)S(1)}, bf16[24,6272]{1,0:T(8,128)(2,1)S(1)}, u32[]{:S(2)}, u32[]{:S(2)}) %collective-permute-start.4) | collective-permute-done | bytes 301088 | tf_op jit(solution)/shard_map/ppermute | solution.py:301
  32.9 0.8 %collective-permute-start.9 = (bf16[24,6272]{1,0:T(8,128)(2,1)S(1)}, bf16[24,6272]{1,0:T(8,128)(2,1)S(1)}, u32[]{:S(2)}, u32[]{:S(2)}) collective-permute-start(bf16[24,6272]{1,0:T(8,128)(2,1)S(1)} %collective-permute-done.4.refs_3_), channel_id=1, source_target_pairs={{0,2},{1,3},{2,0},{3,1},{4,6},{5,7},{6,4},{7,5},{8,10},{9,11},{10,... | collective-permute-start | bytes 903176 | tf_op jit(solution)/shard_map/ppermute | solution.py:301
  33.7 0.0 collective-permute-done.5.refs_5_
  33.7 4.9 %shard_map.88 = (f32[24,2176]{1,0:T(8,128)S(1)}, f32[24,2176]{1,0:T(8,128)S(1)}, bf16[24,2176]{1,0:T(8,128)(2,1)S(1)}, bf16[24,2176]{1,0:T(8,128)(2,1)S(1)}, bf16[24,4352]{1,0:T(8,128)(2,1)S(1)}) custom-call(bf16[24,6272]{1,0:T(8,128)(2,1)S(1)} %shard_map.86.refs_0_, bf16[24,6272]{1,0:T(8,128)(2,1)S(1)} %collective-permute-done.refs_1_, ...), custom_call_target="tpu_custom_call" | custom-call | flops 4076863488 | bytes 9437184 | tf_op jit(solution)/shard_map/pallas_call | solution.py:253
  38.6 1.3 %collective-permute-start.6 = (bf16[24,4352]{1,0:T(8,128)(2,1)S(1)}, bf16[24,4352]{1,0:T(8,128)(2,1)S(1)}, u32[]{:S(2)}, u32[]{:S(2)}) collective-permute-start(bf16[24,4352]{1,0:T(8,128)(2,1)S(1)} %get-tuple-element.19), channel_id=1, source_target_pairs={{0,2},{1,3},{2,0},{3,1},{4,6},{5,7},{6,4},{7,5},{8,10},{9,11},{10,... | collective-permute-start | bytes 626696 | tf_op jit(solution)/shard_map/ppermute | solution.py:301
  39.9 0.3 collective-permute-start.12
  40.2 1.7 %collective-permute-start.7 = (bf16[24,2176]{1,0:T(8,128)(2,1)S(1)}, bf16[24,2176]{1,0:T(8,128)(2,1)S(1)}, u32[]{:S(2)}, u32[]{:S(2)}) collective-permute-start(bf16[24,2176]{1,0:T(8,128)(2,1)S(1)} %get-tuple-element.20), channel_id=1, source_target_pairs={{0,4},{1,5},{2,6},{3,7},{4,8},{5,9},{6,10},{7,11},{8,12},{9,13},{1... | collective-permute-start | bytes 313352 | tf_op jit(solution)/shard_map/ppermute | solution.py:301
  41.9 0.0 collective-permute-done.8.refs_0_
  41.9 2.7 %collective-permute-done.9.refs_1_ = bf16[24,6272]{1,0:T(8,128)(2,1)S(1)} collective-permute-done((bf16[24,6272]{1,0:T(8,128)(2,1)S(1)}, bf16[24,6272]{1,0:T(8,128)(2,1)S(1)}, u32[]{:S(2)}, u32[]{:S(2)}) %collective-permute-start.9) | collective-permute-done | bytes 301088 | tf_op jit(solution)/shard_map/ppermute | solution.py:301
  44.6 0.0 copy-start
  44.6 0.0 copy-start.1
  44.6 0.0 copy-start.2
  44.6 3.8 %shard_map.89 = (bf16[24,2176]{1,0:T(8,128)(2,1)S(1)}, bf16[24,2176]{1,0:T(8,128)(2,1)S(1)}) custom-call(bf16[24,6272]{1,0:T(8,128)(2,1)S(1)} %collective-permute-done.8.refs_0_, bf16[24,6272]{1,0:T(8,128)(2,1)S(1)} %collective-permute-done.9.refs_1_, bf16[3,2048,768]{2,1,0:T(8,128)(2,1)S(1)} %shard_map.87.refs_6_.refs_2_), custom_call_target="tpu_custom_call" | custom-call | flops 1358954496 | bytes 9437184 | tf_op jit(solution)/shard_map/pallas_call | solution.py:253
  48.4 0.1 collective-permute-start.10
  48.5 0.0 collective-permute-done.12
  48.5 0.0 collective-permute-done.6.refs_1_
  48.6 1.0 %collective-permute-start.13 = (bf16[24,2176]{1,0:T(8,128)(2,1)S(1)}, bf16[24,2176]{1,0:T(8,128)(2,1)S(1)}, u32[]{:S(2)}, u32[]{:S(2)}) collective-permute-start(bf16[24,2176]{1,0:T(8,128)(2,1)S(1)} %add_convert_fusion), channel_id=1, source_target_pairs={{0,12},{1,13},{2,14},{3,15},{4,0},{5,1},{6,2},{7,3},{8,4},{9,5},{1... | collective-permute-start | bytes 313352 | tf_op jit(solution)/shard_map/ppermute | solution.py:301
  49.6 1.5 %collective-permute-start.11 = (bf16[24,2176]{1,0:T(8,128)(2,1)S(1)}, bf16[24,2176]{1,0:T(8,128)(2,1)S(1)}, u32[]{:S(2)}, u32[]{:S(2)}) collective-permute-start(bf16[24,2176]{1,0:T(8,128)(2,1)S(1)} %get-tuple-element.25), channel_id=1, source_target_pairs={{0,6},{1,7},{2,4},{3,5},{4,10},{5,11},{6,8},{7,9},{8,14},{9,15},{1... | collective-permute-start | bytes 313352 | tf_op jit(solution)/shard_map/ppermute | solution.py:301
  51.0 0.0 collective-permute-done.7.refs_2_
  51.0 2.3 %collective-permute-done.13.refs_5_ = bf16[24,2176]{1,0:T(8,128)(2,1)S(1)} collective-permute-done((bf16[24,2176]{1,0:T(8,128)(2,1)S(1)}, bf16[24,2176]{1,0:T(8,128)(2,1)S(1)}, u32[]{:S(2)}, u32[]{:S(2)}) %collective-permute-start.13) | collective-permute-done | bytes 104480 | tf_op jit(solution)/shard_map/ppermute | solution.py:301
  53.3 2.8 %collective-permute-done.10.refs_3_ = bf16[24,2176]{1,0:T(8,128)(2,1)S(1)} collective-permute-done((bf16[24,2176]{1,0:T(8,128)(2,1)S(1)}, bf16[24,2176]{1,0:T(8,128)(2,1)S(1)}, u32[]{:S(2)}, u32[]{:S(2)}) %collective-permute-start.10) | collective-permute-done | bytes 104480 | tf_op jit(solution)/shard_map/ppermute | solution.py:301
  56.2 1.6 %collective-permute-done.11.refs_4_ = bf16[24,2176]{1,0:T(8,128)(2,1)S(1)} collective-permute-done((bf16[24,2176]{1,0:T(8,128)(2,1)S(1)}, bf16[24,2176]{1,0:T(8,128)(2,1)S(1)}, u32[]{:S(2)}, u32[]{:S(2)}) %collective-permute-start.11) | collective-permute-done | bytes 104480 | tf_op jit(solution)/shard_map/ppermute | solution.py:301
  57.8 0.0 copy-done
  57.8 0.0 copy-done.1
  57.8 0.0 copy-done.2
  57.8 1.0 %shard_map.90 = (f32[24,2048]{1,0:T(8,128)}, f32[1,24]{1,0:T(1,128)}) custom-call(bf16[24,2048]{1,0:T(8,128)(2,1)S(1)} %copy-done.1, f32[1,2048]{1,0:T(1,128)S(1)} %bitcast.5, s32[24,2048]{1,0:T(8,128)S(1)} %copy-done, f32[24,2176]{1,0:T(8,128)S(1)} %get-tuple-element.18.refs_0_, bf16[24,4352]{1,0:T(8,128)(2,1)S(1)} %collective-permute-done.6.refs_1_, ...), custom_call_target="tpu_custom_call" | custom-call | flops 1966080 | bytes 1277952 | tf_op jit(solution)/shard_map/pallas_call | solution.py:343
  (1 shorter events, 0.0 us)
Async XLA Ops:
  0.6 15.5 %collective-permute-start.3 = (bf16[3,2048,384]{2,1,0:T(8,128)(2,1)}, bf16[3,2048,384]{2,1,0:T(8,128)(2,1)S(1)}, u32[]{:S(2)}, u32[]{:S(2)}) collective-permute-start(bf16[3,2048,384]{2,1,0:T(8,128)(2,1)} %own.1), channel_id=1, source_target_pairs={{0,1},{1,0},{2,3},{3,2},{4,5},{5,4},{6,7},{7,6},{8,9},{9,8},{10,11... | collective-permute-start | bytes 14155784 | tf_op jit(solution)/shard_map/ppermute | solution.py:301
  2.4 10.4 %collective-permute-start.1 = (bf16[24,6272]{1,0:T(8,128)(2,1)S(1)}, bf16[24,6272]{1,0:T(8,128)(2,1)S(1)}, u32[]{:S(2)}, u32[]{:S(2)}) collective-permute-start(bf16[24,6272]{1,0:T(8,128)(2,1)S(1)} %shard_map.86.refs_0_), channel_id=1, source_target_pairs={{0,2},{1,3},{2,0},{3,1},{4,6},{5,7},{6,4},{7,5},{8,10},{9,11},{10,... | collective-permute-start | bytes 903176 | tf_op jit(solution)/shard_map/ppermute | solution.py:301
  5.0 11.1 %collective-permute-start = (bf16[24,6272]{1,0:T(8,128)(2,1)S(1)}, bf16[24,6272]{1,0:T(8,128)(2,1)S(1)}, u32[]{:S(2)}, u32[]{:S(2)}) collective-permute-start(bf16[24,6272]{1,0:T(8,128)(2,1)S(1)} %shard_map.86.refs_0_), channel_id=1, source_target_pairs={{0,4},{1,5},{2,6},{3,7},{4,8},{5,9},{6,10},{7,11},{8,12},{9,13},{1... | collective-permute-start | bytes 903176 | tf_op jit(solution)/shard_map/ppermute | solution.py:301
  16.1 11.9 %collective-permute-start.2 = (bf16[24,6272]{1,0:T(8,128)(2,1)S(1)}, bf16[24,6272]{1,0:T(8,128)(2,1)S(1)}, u32[]{:S(2)}, u32[]{:S(2)}) collective-permute-start(bf16[24,6272]{1,0:T(8,128)(2,1)S(1)} %collective-permute-done.refs_1_), channel_id=1, source_target_pairs={{0,4},{1,5},{2,6},{3,7},{4,8},{5,9},{6,10},{7,11},{8,12},{9,13},{1... | collective-permute-start | bytes 903176 | tf_op jit(solution)/shard_map/ppermute | solution.py:301
  18.6 14.3 %collective-permute-start.4 = (bf16[24,6272]{1,0:T(8,128)(2,1)S(1)}, bf16[24,6272]{1,0:T(8,128)(2,1)S(1)}, u32[]{:S(2)}, u32[]{:S(2)}) collective-permute-start(bf16[24,6272]{1,0:T(8,128)(2,1)S(1)} %shard_map.86.refs_0_), channel_id=1, source_target_pairs={{0,12},{1,13},{2,14},{3,15},{4,0},{5,1},{6,2},{7,3},{8,4},{9,5},{1... | collective-permute-start | bytes 903176 | tf_op jit(solution)/shard_map/ppermute | solution.py:301
  22.4 11.2 %collective-permute-start.5 = (bf16[24,6272]{1,0:T(8,128)(2,1)S(1)}, bf16[24,6272]{1,0:T(8,128)(2,1)S(1)}, u32[]{:S(2)}, u32[]{:S(2)}) collective-permute-start(bf16[24,6272]{1,0:T(8,128)(2,1)S(1)} %collective-permute-done.refs_1_), channel_id=1, source_target_pairs={{0,2},{1,3},{2,0},{3,1},{4,6},{5,7},{6,4},{7,5},{8,10},{9,11},{10,... | collective-permute-start | bytes 903176 | tf_op jit(solution)/shard_map/ppermute | solution.py:301
  28.1 13.9 %collective-permute-start.8 = (bf16[24,6272]{1,0:T(8,128)(2,1)S(1)}, bf16[24,6272]{1,0:T(8,128)(2,1)S(1)}, u32[]{:S(2)}, u32[]{:S(2)}) collective-permute-start(bf16[24,6272]{1,0:T(8,128)(2,1)S(1)} %collective-permute-done.2.refs_2_), channel_id=1, source_target_pairs={{0,2},{1,3},{2,0},{3,1},{4,6},{5,7},{6,4},{7,5},{8,10},{9,11},{10,... | collective-permute-start | bytes 903176 | tf_op jit(solution)/shard_map/ppermute | solution.py:301
  32.9 11.7 %collective-permute-start.9 = (bf16[24,6272]{1,0:T(8,128)(2,1)S(1)}, bf16[24,6272]{1,0:T(8,128)(2,1)S(1)}, u32[]{:S(2)}, u32[]{:S(2)}) collective-permute-start(bf16[24,6272]{1,0:T(8,128)(2,1)S(1)} %collective-permute-done.4.refs_3_), channel_id=1, source_target_pairs={{0,2},{1,3},{2,0},{3,1},{4,6},{5,7},{6,4},{7,5},{8,10},{9,11},{10,... | collective-permute-start | bytes 903176 | tf_op jit(solution)/shard_map/ppermute | solution.py:301
  38.6 10.0 %collective-permute-start.6 = (bf16[24,4352]{1,0:T(8,128)(2,1)S(1)}, bf16[24,4352]{1,0:T(8,128)(2,1)S(1)}, u32[]{:S(2)}, u32[]{:S(2)}) collective-permute-start(bf16[24,4352]{1,0:T(8,128)(2,1)S(1)} %get-tuple-element.19), channel_id=1, source_target_pairs={{0,2},{1,3},{2,0},{3,1},{4,6},{5,7},{6,4},{7,5},{8,10},{9,11},{10,... | collective-permute-start | bytes 626696 | tf_op jit(solution)/shard_map/ppermute | solution.py:301
  39.9 8.6 %collective-permute-start.12 = (bf16[24,2176]{1,0:T(8,128)(2,1)S(1)}, bf16[24,2176]{1,0:T(8,128)(2,1)S(1)}, u32[]{:S(2)}, u32[]{:S(2)}) collective-permute-start(bf16[24,2176]{1,0:T(8,128)(2,1)S(1)} %get-tuple-element.27), channel_id=1, source_target_pairs={{0,12},{1,13},{2,14},{3,15},{4,0},{5,1},{6,2},{7,3},{8,4},{9,5},{1... | collective-permute-start | bytes 313352 | tf_op jit(solution)/shard_map/ppermute | solution.py:301
  40.2 10.9 %collective-permute-start.7 = (bf16[24,2176]{1,0:T(8,128)(2,1)S(1)}, bf16[24,2176]{1,0:T(8,128)(2,1)S(1)}, u32[]{:S(2)}, u32[]{:S(2)}) collective-permute-start(bf16[24,2176]{1,0:T(8,128)(2,1)S(1)} %get-tuple-element.20), channel_id=1, source_target_pairs={{0,4},{1,5},{2,6},{3,7},{4,8},{5,9},{6,10},{7,11},{8,12},{9,13},{1... | collective-permute-start | bytes 313352 | tf_op jit(solution)/shard_map/ppermute | solution.py:301
  44.6 13.2 %copy-start = (s32[24,2048]{1,0:T(8,128)S(1)}, s32[24,2048]{1,0:T(8,128)}, u32[]{:S(2)}) copy-start(s32[24,2048]{1,0:T(8,128)} %signs.1) | copy-start | bytes 589828
  44.6 13.2 %copy-start.1 = (bf16[24,2048]{1,0:T(8,128)(2,1)S(1)}, bf16[24,2048]{1,0:T(8,128)(2,1)}, u32[]{:S(2)}) copy-start(bf16[24,2048]{1,0:T(8,128)(2,1)} %tokens.1) | copy-start | bytes 294916
  44.6 13.2 %copy-start.2 = (f32[2048]{0:T(1024)S(1)}, f32[2048]{0:T(1024)}, u32[]{:S(2)}) copy-start(f32[2048]{0:T(1024)} %param.8) | copy-start | bytes 24580
  48.4 7.7 %collective-permute-start.10 = (bf16[24,2176]{1,0:T(8,128)(2,1)S(1)}, bf16[24,2176]{1,0:T(8,128)(2,1)S(1)}, u32[]{:S(2)}, u32[]{:S(2)}) collective-permute-start(bf16[24,2176]{1,0:T(8,128)(2,1)S(1)} %get-tuple-element.24), channel_id=1, source_target_pairs={{0,10},{1,11},{2,8},{3,9},{4,14},{5,15},{6,12},{7,13},{8,2},{9,3},... | collective-permute-start | bytes 313352 | tf_op jit(solution)/shard_map/ppermute | solution.py:301
  48.6 4.7 %collective-permute-start.13 = (bf16[24,2176]{1,0:T(8,128)(2,1)S(1)}, bf16[24,2176]{1,0:T(8,128)(2,1)S(1)}, u32[]{:S(2)}, u32[]{:S(2)}) collective-permute-start(bf16[24,2176]{1,0:T(8,128)(2,1)S(1)} %add_convert_fusion), channel_id=1, source_target_pairs={{0,12},{1,13},{2,14},{3,15},{4,0},{5,1},{6,2},{7,3},{8,4},{9,5},{1... | collective-permute-start | bytes 313352 | tf_op jit(solution)/shard_map/ppermute | solution.py:301
  49.6 8.2 %collective-permute-start.11 = (bf16[24,2176]{1,0:T(8,128)(2,1)S(1)}, bf16[24,2176]{1,0:T(8,128)(2,1)S(1)}, u32[]{:S(2)}, u32[]{:S(2)}) collective-permute-start(bf16[24,2176]{1,0:T(8,128)(2,1)S(1)} %get-tuple-element.25), channel_id=1, source_target_pairs={{0,6},{1,7},{2,4},{3,5},{4,10},{5,11},{6,8},{7,9},{8,14},{9,15},{1... | collective-permute-start | bytes 313352 | tf_op jit(solution)/shard_map/ppermute | solution.py:301

commit v16 on v15

--- a/solution.py
+++ b/solution.py
@@ -311,8 +311,9 @@
     same[1] = moved(pack, 1)
     across[0] = moved(pack, 0, flip_x=True)
     same[1] = lax.optimization_barrier((same[1], across[0]))[0]
-    same[3] = moved(lax.optimization_barrier((pack, same[1], held))[0], -1)
+    same[3] = moved(lax.optimization_barrier((pack, same[1]))[0], -1)
     same[2] = moved(same[1], 1)
+    same[2] = lax.optimization_barrier((same[2], held))[0]
     across[1] = moved(same[1], 0, flip_x=True)
     across[3] = moved(same[3], 0, flip_x=True)
     across[2] = moved(same[2], 0, flip_x=True)

time: 58.9 us -> 56.4 us (0.958)
  waiting for transfers between devices: 28.4 us -> 21.8 us
  starting transfers between devices: 16.2 us -> 20.2 us
    ppermute x14, waiting for transfers between devices: 28.4 us -> 21.8 us  [moved(): return lax.ppermute(rows, 'expert', pairs)]
    ppermute x14, starting transfers between devices: 16.2 us -> 20.2 us  [moved(): return lax.ppermute(rows, 'expert', pairs)]
  transfers between devices with their start and end apart: 14 -> 14, of which waited for: 8 -> 5; matrix products, arithmetic and copies ran while one was open for 0% -> 0% of each run, Pallas kernels for 21% -> 22%
where the time goes in v16:
time: 56.4 us; the launch traced here: 56.3 us
  waiting for transfers between devices  21.8 us (39%)
  starting transfers between devices  20.2 us (36%)
  Pallas kernels  13.4 us (24%)
  between operations  0.7 us (1%)
    ppermute x14, waiting for transfers between devices, moved(): return lax.ppermute(rows, 'expert', pairs)  21.8 us
    ppermute x14, starting transfers between devices, moved(): return lax.ppermute(rows, 'expert', pairs)  20.2 us
    pallas_call x2, Pallas kernels, experts(): pl.pallas_call(functools.partial(expert_kernel, count, expert_count), out...  8.76 us
    pallas_call x1, Pallas kernels, joined(): pl.pallas_call(join_kernel, out_shape=pltpu.VMEM((parts, width, 2 * half)...  2.41 us
    pallas_call x1, Pallas kernels, packed(): pl.pallas_call(functools.partial(pack_kernel, expert_count), out_shape=ja...  1.29 us
  transfers between devices with their start and end apart: 14, of which 5 were waited for; matrix products, arithmetic and copies ran while one was open for 0% of the time, Pallas kernels for 22%

profile of v16, /device:TPU:0, one launch (start us, length us, event | category | flops | bytes accessed | tf_op | source)
XLA Modules:
  0.0 56.3 jit_solution(8609795164818120661)
XLA Ops:
  0.6 0.5 collective-permute-start.3
  1.1 1.3 %shard_map.86.refs_0_ = bf16[24,6272]{1,0:T(8,128)(2,1)S(1)} custom-call(bf16[24,2048]{1,0:T(8,128)(2,1)} %tokens.1, f32[1,2048]{1,0:T(1,128)} %bitcast.4, s32[24,2048]{1,0:T(8,128)} %signs.1, bf16[24,2048]{1,0:T(8,128)(2,1)} %refs_3_.1, s32[2,4,24]{2,1,0:T(4,128)} %bitcast.6, f32[2,4,24]{2,1,0:T(4,128)} %bitcast.7), custom_call_target="tpu_custom_call" | custom-call | flops 983040 | bytes 688128 | tf_op jit(solution)/shard_map/pallas_call | solution.py:126
  2.4 2.6 %collective-permute-start = (bf16[24,6272]{1,0:T(8,128)(2,1)S(1)}, bf16[24,6272]{1,0:T(8,128)(2,1)S(1)}, u32[]{:S(2)}, u32[]{:S(2)}) collective-permute-start(bf16[24,6272]{1,0:T(8,128)(2,1)S(1)} %shard_map.86.refs_0_), channel_id=1, source_target_pairs={{0,4},{1,5},{2,6},{3,7},{4,8},{5,9},{6,10},{7,11},{8,12},{9,13},{1... | collective-permute-start | bytes 903176 | tf_op jit(solution)/shard_map/ppermute | solution.py:301
  5.1 1.5 %collective-permute-start.1 = (bf16[24,6272]{1,0:T(8,128)(2,1)S(1)}, bf16[24,6272]{1,0:T(8,128)(2,1)S(1)}, u32[]{:S(2)}, u32[]{:S(2)}) collective-permute-start(bf16[24,6272]{1,0:T(8,128)(2,1)S(1)} %shard_map.86.refs_0_), channel_id=1, source_target_pairs={{0,2},{1,3},{2,0},{3,1},{4,6},{5,7},{6,4},{7,5},{8,10},{9,11},{10,... | collective-permute-start | bytes 903176 | tf_op jit(solution)/shard_map/ppermute | solution.py:301
  6.6 8.3 %collective-permute-done.refs_1_ = bf16[24,6272]{1,0:T(8,128)(2,1)S(1)} collective-permute-done((bf16[24,6272]{1,0:T(8,128)(2,1)S(1)}, bf16[24,6272]{1,0:T(8,128)(2,1)S(1)}, u32[]{:S(2)}, u32[]{:S(2)}) %collective-permute-start) | collective-permute-done | bytes 301088 | tf_op jit(solution)/shard_map/ppermute | solution.py:301
  14.9 0.0 collective-permute-done.1.refs_4_
  14.9 1.8 %collective-permute-start.4 = (bf16[24,6272]{1,0:T(8,128)(2,1)S(1)}, bf16[24,6272]{1,0:T(8,128)(2,1)S(1)}, u32[]{:S(2)}, u32[]{:S(2)}) collective-permute-start(bf16[24,6272]{1,0:T(8,128)(2,1)S(1)} %shard_map.86.refs_0_), channel_id=1, source_target_pairs={{0,12},{1,13},{2,14},{3,15},{4,0},{5,1},{6,2},{7,3},{8,4},{9,5},{1... | collective-permute-start | bytes 903176 | tf_op jit(solution)/shard_map/ppermute | solution.py:301
  16.7 0.2 collective-permute-start.2
  16.9 1.5 %collective-permute-start.5 = (bf16[24,6272]{1,0:T(8,128)(2,1)S(1)}, bf16[24,6272]{1,0:T(8,128)(2,1)S(1)}, u32[]{:S(2)}, u32[]{:S(2)}) collective-permute-start(bf16[24,6272]{1,0:T(8,128)(2,1)S(1)} %collective-permute-done.refs_1_), channel_id=1, source_target_pairs={{0,2},{1,3},{2,0},{3,1},{4,6},{5,7},{6,4},{7,5},{8,10},{9,11},{10,... | collective-permute-start | bytes 903176 | tf_op jit(solution)/shard_map/ppermute | solution.py:301
  18.4 6.1 %collective-permute-done.4.refs_3_ = bf16[24,6272]{1,0:T(8,128)(2,1)S(1)} collective-permute-done((bf16[24,6272]{1,0:T(8,128)(2,1)S(1)}, bf16[24,6272]{1,0:T(8,128)(2,1)S(1)}, u32[]{:S(2)}, u32[]{:S(2)}) %collective-permute-start.4) | collective-permute-done | bytes 301088 | tf_op jit(solution)/shard_map/ppermute | solution.py:301
  24.6 1.2 %collective-permute-start.9 = (bf16[24,6272]{1,0:T(8,128)(2,1)S(1)}, bf16[24,6272]{1,0:T(8,128)(2,1)S(1)}, u32[]{:S(2)}, u32[]{:S(2)}) collective-permute-start(bf16[24,6272]{1,0:T(8,128)(2,1)S(1)} %collective-permute-done.4.refs_3_), channel_id=1, source_target_pairs={{0,2},{1,3},{2,0},{3,1},{4,6},{5,7},{6,4},{7,5},{8,10},{9,11},{10,... | collective-permute-start | bytes 903176 | tf_op jit(solution)/shard_map/ppermute | solution.py:301
  25.8 0.0 collective-permute-done.3.other
  25.8 2.4 %shard_map.87.refs_6_.refs_2_ = bf16[3,2048,768]{2,1,0:T(8,128)(2,1)S(1)} custom-call(bf16[3,2048,384]{2,1,0:T(8,128)(2,1)} %own.1, bf16[3,2048,384]{2,1,0:T(8,128)(2,1)S(1)} %collective-permute-done.3.other), custom_call_target="tpu_custom_call" | custom-call | bytes 18874368 | tf_op jit(solution)/shard_map/pallas_call | solution.py:157
  28.2 3.0 %collective-permute-done.2.refs_2_ = bf16[24,6272]{1,0:T(8,128)(2,1)S(1)} collective-permute-done((bf16[24,6272]{1,0:T(8,128)(2,1)S(1)}, bf16[24,6272]{1,0:T(8,128)(2,1)S(1)}, u32[]{:S(2)}, u32[]{:S(2)}) %collective-permute-start.2) | collective-permute-done | bytes 301088 | tf_op jit(solution)/shard_map/ppermute | solution.py:301
  31.3 1.5 %collective-permute-start.8 = (bf16[24,6272]{1,0:T(8,128)(2,1)S(1)}, bf16[24,6272]{1,0:T(8,128)(2,1)S(1)}, u32[]{:S(2)}, u32[]{:S(2)}) collective-permute-start(bf16[24,6272]{1,0:T(8,128)(2,1)S(1)} %collective-permute-done.2.refs_2_), channel_id=1, source_target_pairs={{0,2},{1,3},{2,0},{3,1},{4,6},{5,7},{6,4},{7,5},{8,10},{9,11},{10,... | collective-permute-start | bytes 903176 | tf_op jit(solution)/shard_map/ppermute | solution.py:301
  32.8 0.0 collective-permute-done.5.refs_5_
  32.8 4.9 %shard_map.88 = (f32[24,2176]{1,0:T(8,128)S(1)}, f32[24,2176]{1,0:T(8,128)S(1)}, bf16[24,2176]{1,0:T(8,128)(2,1)S(1)}, bf16[24,2176]{1,0:T(8,128)(2,1)S(1)}, bf16[24,4352]{1,0:T(8,128)(2,1)S(1)}) custom-call(bf16[24,6272]{1,0:T(8,128)(2,1)S(1)} %shard_map.86.refs_0_, bf16[24,6272]{1,0:T(8,128)(2,1)S(1)} %collective-permute-done.refs_1_, ...), custom_call_target="tpu_custom_call" | custom-call | flops 4076863488 | bytes 9437184 | tf_op jit(solution)/shard_map/pallas_call | solution.py:253
  37.7 0.6 %collective-permute-start.6 = (bf16[24,4352]{1,0:T(8,128)(2,1)S(1)}, bf16[24,4352]{1,0:T(8,128)(2,1)S(1)}, u32[]{:S(2)}, u32[]{:S(2)}) collective-permute-start(bf16[24,4352]{1,0:T(8,128)(2,1)S(1)} %get-tuple-element.21), channel_id=1, source_target_pairs={{0,2},{1,3},{2,0},{3,1},{4,6},{5,7},{6,4},{7,5},{8,10},{9,11},{10,... | collective-permute-start | bytes 626696 | tf_op jit(solution)/shard_map/ppermute | solution.py:301
  38.3 0.7 %collective-permute-start.7 = (bf16[24,2176]{1,0:T(8,128)(2,1)S(1)}, bf16[24,2176]{1,0:T(8,128)(2,1)S(1)}, u32[]{:S(2)}, u32[]{:S(2)}) collective-permute-start(bf16[24,2176]{1,0:T(8,128)(2,1)S(1)} %get-tuple-element.22), channel_id=1, source_target_pairs={{0,4},{1,5},{2,6},{3,7},{4,8},{5,9},{6,10},{7,11},{8,12},{9,13},{1... | collective-permute-start | bytes 313352 | tf_op jit(solution)/shard_map/ppermute | solution.py:301
  39.0 3.1 %collective-permute-start.12 = (bf16[24,2176]{1,0:T(8,128)(2,1)S(1)}, bf16[24,2176]{1,0:T(8,128)(2,1)S(1)}, u32[]{:S(2)}, u32[]{:S(2)}) collective-permute-start(bf16[24,2176]{1,0:T(8,128)(2,1)S(1)} %get-tuple-element.29), channel_id=1, source_target_pairs={{0,12},{1,13},{2,14},{3,15},{4,0},{5,1},{6,2},{7,3},{8,4},{9,5},{1... | collective-permute-start | bytes 313352 | tf_op jit(solution)/shard_map/ppermute | solution.py:301
  42.1 0.0 collective-permute-done.9.refs_1_
  42.1 0.0 collective-permute-done.8.refs_0_
  42.1 0.0 copy-start
  42.1 0.0 copy-start.1
  42.1 0.0 copy-start.2
  42.1 3.8 %shard_map.89 = (bf16[24,2176]{1,0:T(8,128)(2,1)S(1)}, bf16[24,2176]{1,0:T(8,128)(2,1)S(1)}) custom-call(bf16[24,6272]{1,0:T(8,128)(2,1)S(1)} %collective-permute-done.8.refs_0_, bf16[24,6272]{1,0:T(8,128)(2,1)S(1)} %collective-permute-done.9.refs_1_, bf16[3,2048,768]{2,1,0:T(8,128)(2,1)S(1)} %shard_map.87.refs_6_.refs_2_), custom_call_target="tpu_custom_call" | custom-call | flops 1358954496 | bytes 9437184 | tf_op jit(solution)/shard_map/pallas_call | solution.py:253
  46.0 0.3 collective-permute-start.10
  46.3 1.6 %collective-permute-start.11 = (bf16[24,2176]{1,0:T(8,128)(2,1)S(1)}, bf16[24,2176]{1,0:T(8,128)(2,1)S(1)}, u32[]{:S(2)}, u32[]{:S(2)}) collective-permute-start(bf16[24,2176]{1,0:T(8,128)(2,1)S(1)} %get-tuple-element.27), channel_id=1, source_target_pairs={{0,6},{1,7},{2,4},{3,5},{4,10},{5,11},{6,8},{7,9},{8,14},{9,15},{1... | collective-permute-start | bytes 313352 | tf_op jit(solution)/shard_map/ppermute | solution.py:301
  47.9 0.0 collective-permute-done.12
  47.9 0.0 collective-permute-done.6.refs_1_
  48.0 3.0 %collective-permute-start.13 = (bf16[24,2176]{1,0:T(8,128)(2,1)S(1)}, bf16[24,2176]{1,0:T(8,128)(2,1)S(1)}, u32[]{:S(2)}, u32[]{:S(2)}) collective-permute-start(bf16[24,2176]{1,0:T(8,128)(2,1)S(1)} %add_convert_fusion), channel_id=1, source_target_pairs={{0,12},{1,13},{2,14},{3,15},{4,0},{5,1},{6,2},{7,3},{8,4},{9,5},{1... | collective-permute-start | bytes 313352 | tf_op jit(solution)/shard_map/ppermute | solution.py:301
  51.0 0.0 collective-permute-done.7.refs_2_
  51.0 3.7 %collective-permute-done.10.refs_3_ = bf16[24,2176]{1,0:T(8,128)(2,1)S(1)} collective-permute-done((bf16[24,2176]{1,0:T(8,128)(2,1)S(1)}, bf16[24,2176]{1,0:T(8,128)(2,1)S(1)}, u32[]{:S(2)}, u32[]{:S(2)}) %collective-permute-start.10) | collective-permute-done | bytes 104480 | tf_op jit(solution)/shard_map/ppermute | solution.py:301
  54.7 0.0 collective-permute-done.11.refs_4_
  54.7 0.6 %collective-permute-done.13.refs_5_ = bf16[24,2176]{1,0:T(8,128)(2,1)S(1)} collective-permute-done((bf16[24,2176]{1,0:T(8,128)(2,1)S(1)}, bf16[24,2176]{1,0:T(8,128)(2,1)S(1)}, u32[]{:S(2)}, u32[]{:S(2)}) %collective-permute-start.13) | collective-permute-done | bytes 104480 | tf_op jit(solution)/shard_map/ppermute | solution.py:301
  55.3 0.0 copy-done
  55.3 0.0 copy-done.1
  55.3 0.0 copy-done.2
  55.3 1.0 %shard_map.90 = (f32[24,2048]{1,0:T(8,128)}, f32[1,24]{1,0:T(1,128)}) custom-call(bf16[24,2048]{1,0:T(8,128)(2,1)S(1)} %copy-done.1, f32[1,2048]{1,0:T(1,128)S(1)} %bitcast.5, s32[24,2048]{1,0:T(8,128)S(1)} %copy-done, f32[24,2176]{1,0:T(8,128)S(1)} %get-tuple-element.20.refs_0_, bf16[24,4352]{1,0:T(8,128)(2,1)S(1)} %collective-permute-done.6.refs_1_, ...), custom_call_target="tpu_custom_call" | custom-call | flops 1966080 | bytes 1277952 | tf_op jit(solution)/shard_map/pallas_call | solution.py:344
  (1 shorter events, 0.0 us)
Async XLA Ops:
  0.6 25.2 %collective-permute-start.3 = (bf16[3,2048,384]{2,1,0:T(8,128)(2,1)}, bf16[3,2048,384]{2,1,0:T(8,128)(2,1)S(1)}, u32[]{:S(2)}, u32[]{:S(2)}) collective-permute-start(bf16[3,2048,384]{2,1,0:T(8,128)(2,1)} %own.1), channel_id=1, source_target_pairs={{0,1},{1,0},{2,3},{3,2},{4,5},{5,4},{6,7},{7,6},{8,9},{9,8},{10,11... | collective-permute-start | bytes 14155784 | tf_op jit(solution)/shard_map/ppermute | solution.py:301
  2.4 12.5 %collective-permute-start = (bf16[24,6272]{1,0:T(8,128)(2,1)S(1)}, bf16[24,6272]{1,0:T(8,128)(2,1)S(1)}, u32[]{:S(2)}, u32[]{:S(2)}) collective-permute-start(bf16[24,6272]{1,0:T(8,128)(2,1)S(1)} %shard_map.86.refs_0_), channel_id=1, source_target_pairs={{0,4},{1,5},{2,6},{3,7},{4,8},{5,9},{6,10},{7,11},{8,12},{9,13},{1... | collective-permute-start | bytes 903176 | tf_op jit(solution)/shard_map/ppermute | solution.py:301
  5.1 9.8 %collective-permute-start.1 = (bf16[24,6272]{1,0:T(8,128)(2,1)S(1)}, bf16[24,6272]{1,0:T(8,128)(2,1)S(1)}, u32[]{:S(2)}, u32[]{:S(2)}) collective-permute-start(bf16[24,6272]{1,0:T(8,128)(2,1)S(1)} %shard_map.86.refs_0_), channel_id=1, source_target_pairs={{0,2},{1,3},{2,0},{3,1},{4,6},{5,7},{6,4},{7,5},{8,10},{9,11},{10,... | collective-permute-start | bytes 903176 | tf_op jit(solution)/shard_map/ppermute | solution.py:301
  14.9 9.7 %collective-permute-start.4 = (bf16[24,6272]{1,0:T(8,128)(2,1)S(1)}, bf16[24,6272]{1,0:T(8,128)(2,1)S(1)}, u32[]{:S(2)}, u32[]{:S(2)}) collective-permute-start(bf16[24,6272]{1,0:T(8,128)(2,1)S(1)} %shard_map.86.refs_0_), channel_id=1, source_target_pairs={{0,12},{1,13},{2,14},{3,15},{4,0},{5,1},{6,2},{7,3},{8,4},{9,5},{1... | collective-permute-start | bytes 903176 | tf_op jit(solution)/shard_map/ppermute | solution.py:301
  16.7 14.5 %collective-permute-start.2 = (bf16[24,6272]{1,0:T(8,128)(2,1)S(1)}, bf16[24,6272]{1,0:T(8,128)(2,1)S(1)}, u32[]{:S(2)}, u32[]{:S(2)}) collective-permute-start(bf16[24,6272]{1,0:T(8,128)(2,1)S(1)} %collective-permute-done.refs_1_), channel_id=1, source_target_pairs={{0,4},{1,5},{2,6},{3,7},{4,8},{5,9},{6,10},{7,11},{8,12},{9,13},{1... | collective-permute-start | bytes 903176 | tf_op jit(solution)/shard_map/ppermute | solution.py:301
  16.9 15.8 %collective-permute-start.5 = (bf16[24,6272]{1,0:T(8,128)(2,1)S(1)}, bf16[24,6272]{1,0:T(8,128)(2,1)S(1)}, u32[]{:S(2)}, u32[]{:S(2)}) collective-permute-start(bf16[24,6272]{1,0:T(8,128)(2,1)S(1)} %collective-permute-done.refs_1_), channel_id=1, source_target_pairs={{0,2},{1,3},{2,0},{3,1},{4,6},{5,7},{6,4},{7,5},{8,10},{9,11},{10,... | collective-permute-start | bytes 903176 | tf_op jit(solution)/shard_map/ppermute | solution.py:301
  24.6 17.5 %collective-permute-start.9 = (bf16[24,6272]{1,0:T(8,128)(2,1)S(1)}, bf16[24,6272]{1,0:T(8,128)(2,1)S(1)}, u32[]{:S(2)}, u32[]{:S(2)}) collective-permute-start(bf16[24,6272]{1,0:T(8,128)(2,1)S(1)} %collective-permute-done.4.refs_3_), channel_id=1, source_target_pairs={{0,2},{1,3},{2,0},{3,1},{4,6},{5,7},{6,4},{7,5},{8,10},{9,11},{10,... | collective-permute-start | bytes 903176 | tf_op jit(solution)/shard_map/ppermute | solution.py:301
  31.3 10.9 %collective-permute-start.8 = (bf16[24,6272]{1,0:T(8,128)(2,1)S(1)}, bf16[24,6272]{1,0:T(8,128)(2,1)S(1)}, u32[]{:S(2)}, u32[]{:S(2)}) collective-permute-start(bf16[24,6272]{1,0:T(8,128)(2,1)S(1)} %collective-permute-done.2.refs_2_), channel_id=1, source_target_pairs={{0,2},{1,3},{2,0},{3,1},{4,6},{5,7},{6,4},{7,5},{8,10},{9,11},{10,... | collective-permute-start | bytes 903176 | tf_op jit(solution)/shard_map/ppermute | solution.py:301
  37.7 10.2 %collective-permute-start.6 = (bf16[24,4352]{1,0:T(8,128)(2,1)S(1)}, bf16[24,4352]{1,0:T(8,128)(2,1)S(1)}, u32[]{:S(2)}, u32[]{:S(2)}) collective-permute-start(bf16[24,4352]{1,0:T(8,128)(2,1)S(1)} %get-tuple-element.21), channel_id=1, source_target_pairs={{0,2},{1,3},{2,0},{3,1},{4,6},{5,7},{6,4},{7,5},{8,10},{9,11},{10,... | collective-permute-start | bytes 626696 | tf_op jit(solution)/shard_map/ppermute | solution.py:301
  38.3 12.7 %collective-permute-start.7 = (bf16[24,2176]{1,0:T(8,128)(2,1)S(1)}, bf16[24,2176]{1,0:T(8,128)(2,1)S(1)}, u32[]{:S(2)}, u32[]{:S(2)}) collective-permute-start(bf16[24,2176]{1,0:T(8,128)(2,1)S(1)} %get-tuple-element.22), channel_id=1, source_target_pairs={{0,4},{1,5},{2,6},{3,7},{4,8},{5,9},{6,10},{7,11},{8,12},{9,13},{1... | collective-permute-start | bytes 313352 | tf_op jit(solution)/shard_map/ppermute | solution.py:301
  39.0 8.9 %collective-permute-start.12 = (bf16[24,2176]{1,0:T(8,128)(2,1)S(1)}, bf16[24,2176]{1,0:T(8,128)(2,1)S(1)}, u32[]{:S(2)}, u32[]{:S(2)}) collective-permute-start(bf16[24,2176]{1,0:T(8,128)(2,1)S(1)} %get-tuple-element.29), channel_id=1, source_target_pairs={{0,12},{1,13},{2,14},{3,15},{4,0},{5,1},{6,2},{7,3},{8,4},{9,5},{1... | collective-permute-start | bytes 313352 | tf_op jit(solution)/shard_map/ppermute | solution.py:301
  42.1 13.2 %copy-start = (s32[24,2048]{1,0:T(8,128)S(1)}, s32[24,2048]{1,0:T(8,128)}, u32[]{:S(2)}) copy-start(s32[24,2048]{1,0:T(8,128)} %signs.1) | copy-start | bytes 589828
  42.1 13.2 %copy-start.1 = (bf16[24,2048]{1,0:T(8,128)(2,1)S(1)}, bf16[24,2048]{1,0:T(8,128)(2,1)}, u32[]{:S(2)}) copy-start(bf16[24,2048]{1,0:T(8,128)(2,1)} %tokens.1) | copy-start | bytes 294916
  42.1 13.2 %copy-start.2 = (f32[2048]{0:T(1024)S(1)}, f32[2048]{0:T(1024)}, u32[]{:S(2)}) copy-start(f32[2048]{0:T(1024)} %param.8) | copy-start | bytes 24580
  46.0 8.7 %collective-permute-start.10 = (bf16[24,2176]{1,0:T(8,128)(2,1)S(1)}, bf16[24,2176]{1,0:T(8,128)(2,1)S(1)}, u32[]{:S(2)}, u32[]{:S(2)}) collective-permute-start(bf16[24,2176]{1,0:T(8,128)(2,1)S(1)} %get-tuple-element.26), channel_id=1, source_target_pairs={{0,10},{1,11},{2,8},{3,9},{4,14},{5,15},{6,12},{7,13},{8,2},{9,3},... | collective-permute-start | bytes 313352 | tf_op jit(solution)/shard_map/ppermute | solution.py:301
  46.3 8.4 %collective-permute-start.11 = (bf16[24,2176]{1,0:T(8,128)(2,1)S(1)}, bf16[24,2176]{1,0:T(8,128)(2,1)S(1)}, u32[]{:S(2)}, u32[]{:S(2)}) collective-permute-start(bf16[24,2176]{1,0:T(8,128)(2,1)S(1)} %get-tuple-element.27), channel_id=1, source_target_pairs={{0,6},{1,7},{2,4},{3,5},{4,10},{5,11},{6,8},{7,9},{8,14},{9,15},{1... | collective-permute-start | bytes 313352 | tf_op jit(solution)/shard_map/ppermute | solution.py:301
  48.0 7.3 %collective-permute-start.13 = (bf16[24,2176]{1,0:T(8,128)(2,1)S(1)}, bf16[24,2176]{1,0:T(8,128)(2,1)S(1)}, u32[]{:S(2)}, u32[]{:S(2)}) collective-permute-start(bf16[24,2176]{1,0:T(8,128)(2,1)S(1)} %add_convert_fusion), channel_id=1, source_target_pairs={{0,12},{1,13},{2,14},{3,15},{4,0},{5,1},{6,2},{7,3},{8,4},{9,5},{1... | collective-permute-start | bytes 313352 | tf_op jit(solution)/shard_map/ppermute | solution.py:301

commit v17 on v16

--- a/solution.py
+++ b/solution.py
@@ -310,11 +310,10 @@
     same, across = {0: pack}, {}
     same[1] = moved(pack, 1)
     across[0] = moved(pack, 0, flip_x=True)
-    same[1] = lax.optimization_barrier((same[1], across[0]))[0]
     same[3] = moved(lax.optimization_barrier((pack, same[1]))[0], -1)
     same[2] = moved(same[1], 1)
     same[2] = lax.optimization_barrier((same[2], held))[0]
-    across[1] = moved(same[1], 0, flip_x=True)
+    across[1] = moved(lax.optimization_barrier((same[1], across[0]))[0], 0, flip_x=True)
     across[3] = moved(same[3], 0, flip_x=True)
     across[2] = moved(same[2], 0, flip_x=True)
     wide, sent, pair = ((jnp.float32, 1), (jnp.bfloat16, 1), (jnp.bfloat16, 2))

time: 56.4 us -> 56 us (level)
  no operation moved by 1% of the time
where the time goes in v17:
time: 56 us; the launch traced here: 55.9 us
  waiting for transfers between devices  21.8 us (39%)
  starting transfers between devices  19.9 us (36%)
  Pallas kernels  13.4 us (24%)
  between operations  0.7 us (1%)
    ppermute x14, waiting for transfers between devices, moved(): return lax.ppermute(rows, 'expert', pairs)  21.8 us
    ppermute x14, starting transfers between devices, moved(): return lax.ppermute(rows, 'expert', pairs)  19.9 us
    pallas_call x2, Pallas kernels, experts(): pl.pallas_call(functools.partial(expert_kernel, count, expert_count), out...  8.77 us
    pallas_call x1, Pallas kernels, joined(): pl.pallas_call(join_kernel, out_shape=pltpu.VMEM((parts, width, 2 * half)...  2.41 us
    pallas_call x1, Pallas kernels, packed(): pl.pallas_call(functools.partial(pack_kernel, expert_count), out_shape=ja...  1.29 us
  transfers between devices with their start and end apart: 14, of which 5 were waited for; matrix products, arithmetic and copies ran while one was open for 0% of the time, Pallas kernels for 22%

profile of v17, /device:TPU:0, one launch (start us, length us, event | category | flops | bytes accessed | tf_op | source)
XLA Modules:
  0.0 55.9 jit_solution(3236460897617626308)
XLA Ops:
  0.6 0.5 collective-permute-start.2
  1.1 1.3 %shard_map.86.refs_0_ = bf16[24,6272]{1,0:T(8,128)(2,1)S(1)} custom-call(bf16[24,2048]{1,0:T(8,128)(2,1)} %tokens.1, f32[1,2048]{1,0:T(1,128)} %bitcast.4, s32[24,2048]{1,0:T(8,128)} %signs.1, bf16[24,2048]{1,0:T(8,128)(2,1)} %refs_3_.1, s32[2,4,24]{2,1,0:T(4,128)} %bitcast.6, f32[2,4,24]{2,1,0:T(4,128)} %bitcast.7), custom_call_target="tpu_custom_call" | custom-call | flops 983040 | bytes 688128 | tf_op jit(solution)/shard_map/pallas_call | solution.py:126
  2.4 2.6 %collective-permute-start = (bf16[24,6272]{1,0:T(8,128)(2,1)S(1)}, bf16[24,6272]{1,0:T(8,128)(2,1)S(1)}, u32[]{:S(2)}, u32[]{:S(2)}) collective-permute-start(bf16[24,6272]{1,0:T(8,128)(2,1)S(1)} %shard_map.86.refs_0_), channel_id=1, source_target_pairs={{0,4},{1,5},{2,6},{3,7},{4,8},{5,9},{6,10},{7,11},{8,12},{9,13},{1... | collective-permute-start | bytes 903176 | tf_op jit(solution)/shard_map/ppermute | solution.py:301
  5.1 1.5 %collective-permute-start.4 = (bf16[24,6272]{1,0:T(8,128)(2,1)S(1)}, bf16[24,6272]{1,0:T(8,128)(2,1)S(1)}, u32[]{:S(2)}, u32[]{:S(2)}) collective-permute-start(bf16[24,6272]{1,0:T(8,128)(2,1)S(1)} %shard_map.86.refs_0_), channel_id=1, source_target_pairs={{0,2},{1,3},{2,0},{3,1},{4,6},{5,7},{6,4},{7,5},{8,10},{9,11},{10,... | collective-permute-start | bytes 903176 | tf_op jit(solution)/shard_map/ppermute | solution.py:301
  6.6 8.3 %collective-permute-done.refs_1_ = bf16[24,6272]{1,0:T(8,128)(2,1)S(1)} collective-permute-done((bf16[24,6272]{1,0:T(8,128)(2,1)S(1)}, bf16[24,6272]{1,0:T(8,128)(2,1)S(1)}, u32[]{:S(2)}, u32[]{:S(2)}) %collective-permute-start) | collective-permute-done | bytes 301088 | tf_op jit(solution)/shard_map/ppermute | solution.py:301
  14.9 1.7 %collective-permute-start.3 = (bf16[24,6272]{1,0:T(8,128)(2,1)S(1)}, bf16[24,6272]{1,0:T(8,128)(2,1)S(1)}, u32[]{:S(2)}, u32[]{:S(2)}) collective-permute-start(bf16[24,6272]{1,0:T(8,128)(2,1)S(1)} %shard_map.86.refs_0_), channel_id=1, source_target_pairs={{0,12},{1,13},{2,14},{3,15},{4,0},{5,1},{6,2},{7,3},{8,4},{9,5},{1... | collective-permute-start | bytes 903176 | tf_op jit(solution)/shard_map/ppermute | solution.py:301
  16.7 0.3 collective-permute-start.1
  16.9 0.0 collective-permute-done.4.refs_4_
  16.9 1.5 %collective-permute-start.5 = (bf16[24,6272]{1,0:T(8,128)(2,1)S(1)}, bf16[24,6272]{1,0:T(8,128)(2,1)S(1)}, u32[]{:S(2)}, u32[]{:S(2)}) collective-permute-start(bf16[24,6272]{1,0:T(8,128)(2,1)S(1)} %collective-permute-done.refs_1_), channel_id=1, source_target_pairs={{0,2},{1,3},{2,0},{3,1},{4,6},{5,7},{6,4},{7,5},{8,10},{9,11},{10,... | collective-permute-start | bytes 903176 | tf_op jit(solution)/shard_map/ppermute | solution.py:301
  18.4 7.1 %collective-permute-done.3.refs_3_ = bf16[24,6272]{1,0:T(8,128)(2,1)S(1)} collective-permute-done((bf16[24,6272]{1,0:T(8,128)(2,1)S(1)}, bf16[24,6272]{1,0:T(8,128)(2,1)S(1)}, u32[]{:S(2)}, u32[]{:S(2)}) %collective-permute-start.3) | collective-permute-done | bytes 301088 | tf_op jit(solution)/shard_map/ppermute | solution.py:301
  25.5 0.9 %collective-permute-start.9 = (bf16[24,6272]{1,0:T(8,128)(2,1)S(1)}, bf16[24,6272]{1,0:T(8,128)(2,1)S(1)}, u32[]{:S(2)}, u32[]{:S(2)}) collective-permute-start(bf16[24,6272]{1,0:T(8,128)(2,1)S(1)} %collective-permute-done.3.refs_3_), channel_id=1, source_target_pairs={{0,2},{1,3},{2,0},{3,1},{4,6},{5,7},{6,4},{7,5},{8,10},{9,11},{10,... | collective-permute-start | bytes 903176 | tf_op jit(solution)/shard_map/ppermute | solution.py:301
  26.4 0.0 collective-permute-done.2.other
  26.4 2.4 %shard_map.87.refs_6_.refs_2_ = bf16[3,2048,768]{2,1,0:T(8,128)(2,1)S(1)} custom-call(bf16[3,2048,384]{2,1,0:T(8,128)(2,1)} %own.1, bf16[3,2048,384]{2,1,0:T(8,128)(2,1)S(1)} %collective-permute-done.2.other), custom_call_target="tpu_custom_call" | custom-call | bytes 18874368 | tf_op jit(solution)/shard_map/pallas_call | solution.py:157
  28.9 1.5 %collective-permute-done.1.refs_2_ = bf16[24,6272]{1,0:T(8,128)(2,1)S(1)} collective-permute-done((bf16[24,6272]{1,0:T(8,128)(2,1)S(1)}, bf16[24,6272]{1,0:T(8,128)(2,1)S(1)}, u32[]{:S(2)}, u32[]{:S(2)}) %collective-permute-start.1) | collective-permute-done | bytes 301088 | tf_op jit(solution)/shard_map/ppermute | solution.py:301
  30.3 1.5 %collective-permute-start.8 = (bf16[24,6272]{1,0:T(8,128)(2,1)S(1)}, bf16[24,6272]{1,0:T(8,128)(2,1)S(1)}, u32[]{:S(2)}, u32[]{:S(2)}) collective-permute-start(bf16[24,6272]{1,0:T(8,128)(2,1)S(1)} %collective-permute-done.1.refs_2_), channel_id=1, source_target_pairs={{0,2},{1,3},{2,0},{3,1},{4,6},{5,7},{6,4},{7,5},{8,10},{9,11},{10,... | collective-permute-start | bytes 903176 | tf_op jit(solution)/shard_map/ppermute | solution.py:301
  31.8 0.0 collective-permute-done.5.refs_5_
  31.8 4.9 %shard_map.88 = (f32[24,2176]{1,0:T(8,128)S(1)}, f32[24,2176]{1,0:T(8,128)S(1)}, bf16[24,2176]{1,0:T(8,128)(2,1)S(1)}, bf16[24,2176]{1,0:T(8,128)(2,1)S(1)}, bf16[24,4352]{1,0:T(8,128)(2,1)S(1)}) custom-call(bf16[24,6272]{1,0:T(8,128)(2,1)S(1)} %shard_map.86.refs_0_, bf16[24,6272]{1,0:T(8,128)(2,1)S(1)} %collective-permute-done.refs_1_, ...), custom_call_target="tpu_custom_call" | custom-call | flops 4076863488 | bytes 9437184 | tf_op jit(solution)/shard_map/pallas_call | solution.py:253
  36.7 0.6 %collective-permute-start.6 = (bf16[24,4352]{1,0:T(8,128)(2,1)S(1)}, bf16[24,4352]{1,0:T(8,128)(2,1)S(1)}, u32[]{:S(2)}, u32[]{:S(2)}) collective-permute-start(bf16[24,4352]{1,0:T(8,128)(2,1)S(1)} %get-tuple-element.21), channel_id=1, source_target_pairs={{0,2},{1,3},{2,0},{3,1},{4,6},{5,7},{6,4},{7,5},{8,10},{9,11},{10,... | collective-permute-start | bytes 626696 | tf_op jit(solution)/shard_map/ppermute | solution.py:301
  37.3 1.6 %collective-permute-start.7 = (bf16[24,2176]{1,0:T(8,128)(2,1)S(1)}, bf16[24,2176]{1,0:T(8,128)(2,1)S(1)}, u32[]{:S(2)}, u32[]{:S(2)}) collective-permute-start(bf16[24,2176]{1,0:T(8,128)(2,1)S(1)} %get-tuple-element.22), channel_id=1, source_target_pairs={{0,4},{1,5},{2,6},{3,7},{4,8},{5,9},{6,10},{7,11},{8,12},{9,13},{1... | collective-permute-start | bytes 313352 | tf_op jit(solution)/shard_map/ppermute | solution.py:301
  38.9 2.2 %collective-permute-start.12 = (bf16[24,2176]{1,0:T(8,128)(2,1)S(1)}, bf16[24,2176]{1,0:T(8,128)(2,1)S(1)}, u32[]{:S(2)}, u32[]{:S(2)}) collective-permute-start(bf16[24,2176]{1,0:T(8,128)(2,1)S(1)} %get-tuple-element.29), channel_id=1, source_target_pairs={{0,12},{1,13},{2,14},{3,15},{4,0},{5,1},{6,2},{7,3},{8,4},{9,5},{1... | collective-permute-start | bytes 313352 | tf_op jit(solution)/shard_map/ppermute | solution.py:301
  41.2 0.0 collective-permute-done.9.refs_1_
  41.2 0.0 collective-permute-done.8.refs_0_
  41.2 0.0 copy-start
  41.2 0.0 copy-start.1
  41.2 0.0 copy-start.2
  41.2 3.8 %shard_map.89 = (bf16[24,2176]{1,0:T(8,128)(2,1)S(1)}, bf16[24,2176]{1,0:T(8,128)(2,1)S(1)}) custom-call(bf16[24,6272]{1,0:T(8,128)(2,1)S(1)} %collective-permute-done.8.refs_0_, bf16[24,6272]{1,0:T(8,128)(2,1)S(1)} %collective-permute-done.9.refs_1_, bf16[3,2048,768]{2,1,0:T(8,128)(2,1)S(1)} %shard_map.87.refs_6_.refs_2_), custom_call_target="tpu_custom_call" | custom-call | flops 1358954496 | bytes 9437184 | tf_op jit(solution)/shard_map/pallas_call | solution.py:253
  45.1 0.5 collective-permute-start.10
  45.6 3.7 %collective-permute-start.11 = (bf16[24,2176]{1,0:T(8,128)(2,1)S(1)}, bf16[24,2176]{1,0:T(8,128)(2,1)S(1)}, u32[]{:S(2)}, u32[]{:S(2)}) collective-permute-start(bf16[24,2176]{1,0:T(8,128)(2,1)S(1)} %get-tuple-element.27), channel_id=1, source_target_pairs={{0,6},{1,7},{2,4},{3,5},{4,10},{5,11},{6,8},{7,9},{8,14},{9,15},{1... | collective-permute-start | bytes 313352 | tf_op jit(solution)/shard_map/ppermute | solution.py:301
  49.3 0.0 collective-permute-done.12
  49.3 0.0 collective-permute-done.6.refs_1_
  49.3 0.7 %collective-permute-start.13 = (bf16[24,2176]{1,0:T(8,128)(2,1)S(1)}, bf16[24,2176]{1,0:T(8,128)(2,1)S(1)}, u32[]{:S(2)}, u32[]{:S(2)}) collective-permute-start(bf16[24,2176]{1,0:T(8,128)(2,1)S(1)} %add_convert_fusion), channel_id=1, source_target_pairs={{0,12},{1,13},{2,14},{3,15},{4,0},{5,1},{6,2},{7,3},{8,4},{9,5},{1... | collective-permute-start | bytes 313352 | tf_op jit(solution)/shard_map/ppermute | solution.py:301
  50.0 0.0 collective-permute-done.7.refs_2_
  50.0 4.3 %collective-permute-done.10.refs_3_ = bf16[24,2176]{1,0:T(8,128)(2,1)S(1)} collective-permute-done((bf16[24,2176]{1,0:T(8,128)(2,1)S(1)}, bf16[24,2176]{1,0:T(8,128)(2,1)S(1)}, u32[]{:S(2)}, u32[]{:S(2)}) %collective-permute-start.10) | collective-permute-done | bytes 104480 | tf_op jit(solution)/shard_map/ppermute | solution.py:301
  54.4 0.0 collective-permute-done.11.refs_4_
  54.4 0.6 %collective-permute-done.13.refs_5_ = bf16[24,2176]{1,0:T(8,128)(2,1)S(1)} collective-permute-done((bf16[24,2176]{1,0:T(8,128)(2,1)S(1)}, bf16[24,2176]{1,0:T(8,128)(2,1)S(1)}, u32[]{:S(2)}, u32[]{:S(2)}) %collective-permute-start.13) | collective-permute-done | bytes 104480 | tf_op jit(solution)/shard_map/ppermute | solution.py:301
  54.9 0.0 copy-done
  54.9 0.0 copy-done.1
  54.9 0.0 copy-done.2
  54.9 1.0 %shard_map.90 = (f32[24,2048]{1,0:T(8,128)}, f32[1,24]{1,0:T(1,128)}) custom-call(bf16[24,2048]{1,0:T(8,128)(2,1)S(1)} %copy-done.1, f32[1,2048]{1,0:T(1,128)S(1)} %bitcast.5, s32[24,2048]{1,0:T(8,128)S(1)} %copy-done, f32[24,2176]{1,0:T(8,128)S(1)} %get-tuple-element.20.refs_0_, bf16[24,4352]{1,0:T(8,128)(2,1)S(1)} %collective-permute-done.6.refs_1_, ...), custom_call_target="tpu_custom_call" | custom-call | flops 1966080 | bytes 1277952 | tf_op jit(solution)/shard_map/pallas_call | solution.py:343
  (1 shorter events, 0.0 us)
Async XLA Ops:
  0.6 25.8 %collective-permute-start.2 = (bf16[3,2048,384]{2,1,0:T(8,128)(2,1)}, bf16[3,2048,384]{2,1,0:T(8,128)(2,1)S(1)}, u32[]{:S(2)}, u32[]{:S(2)}) collective-permute-start(bf16[3,2048,384]{2,1,0:T(8,128)(2,1)} %own.1), channel_id=1, source_target_pairs={{0,1},{1,0},{2,3},{3,2},{4,5},{5,4},{6,7},{7,6},{8,9},{9,8},{10,11... | collective-permute-start | bytes 14155784 | tf_op jit(solution)/shard_map/ppermute | solution.py:301
  2.4 12.5 %collective-permute-start = (bf16[24,6272]{1,0:T(8,128)(2,1)S(1)}, bf16[24,6272]{1,0:T(8,128)(2,1)S(1)}, u32[]{:S(2)}, u32[]{:S(2)}) collective-permute-start(bf16[24,6272]{1,0:T(8,128)(2,1)S(1)} %shard_map.86.refs_0_), channel_id=1, source_target_pairs={{0,4},{1,5},{2,6},{3,7},{4,8},{5,9},{6,10},{7,11},{8,12},{9,13},{1... | collective-permute-start | bytes 903176 | tf_op jit(solution)/shard_map/ppermute | solution.py:301
  5.1 11.8 %collective-permute-start.4 = (bf16[24,6272]{1,0:T(8,128)(2,1)S(1)}, bf16[24,6272]{1,0:T(8,128)(2,1)S(1)}, u32[]{:S(2)}, u32[]{:S(2)}) collective-permute-start(bf16[24,6272]{1,0:T(8,128)(2,1)S(1)} %shard_map.86.refs_0_), channel_id=1, source_target_pairs={{0,2},{1,3},{2,0},{3,1},{4,6},{5,7},{6,4},{7,5},{8,10},{9,11},{10,... | collective-permute-start | bytes 903176 | tf_op jit(solution)/shard_map/ppermute | solution.py:301
  14.9 10.6 %collective-permute-start.3 = (bf16[24,6272]{1,0:T(8,128)(2,1)S(1)}, bf16[24,6272]{1,0:T(8,128)(2,1)S(1)}, u32[]{:S(2)}, u32[]{:S(2)}) collective-permute-start(bf16[24,6272]{1,0:T(8,128)(2,1)S(1)} %shard_map.86.refs_0_), channel_id=1, source_target_pairs={{0,12},{1,13},{2,14},{3,15},{4,0},{5,1},{6,2},{7,3},{8,4},{9,5},{1... | collective-permute-start | bytes 903176 | tf_op jit(solution)/shard_map/ppermute | solution.py:301
  16.7 13.7 %collective-permute-start.1 = (bf16[24,6272]{1,0:T(8,128)(2,1)S(1)}, bf16[24,6272]{1,0:T(8,128)(2,1)S(1)}, u32[]{:S(2)}, u32[]{:S(2)}) collective-permute-start(bf16[24,6272]{1,0:T(8,128)(2,1)S(1)} %collective-permute-done.refs_1_), channel_id=1, source_target_pairs={{0,4},{1,5},{2,6},{3,7},{4,8},{5,9},{6,10},{7,11},{8,12},{9,13},{1... | collective-permute-start | bytes 903176 | tf_op jit(solution)/shard_map/ppermute | solution.py:301
  16.9 14.8 %collective-permute-start.5 = (bf16[24,6272]{1,0:T(8,128)(2,1)S(1)}, bf16[24,6272]{1,0:T(8,128)(2,1)S(1)}, u32[]{:S(2)}, u32[]{:S(2)}) collective-permute-start(bf16[24,6272]{1,0:T(8,128)(2,1)S(1)} %collective-permute-done.refs_1_), channel_id=1, source_target_pairs={{0,2},{1,3},{2,0},{3,1},{4,6},{5,7},{6,4},{7,5},{8,10},{9,11},{10,... | collective-permute-start | bytes 903176 | tf_op jit(solution)/shard_map/ppermute | solution.py:301
  25.5 15.7 %collective-permute-start.9 = (bf16[24,6272]{1,0:T(8,128)(2,1)S(1)}, bf16[24,6272]{1,0:T(8,128)(2,1)S(1)}, u32[]{:S(2)}, u32[]{:S(2)}) collective-permute-start(bf16[24,6272]{1,0:T(8,128)(2,1)S(1)} %collective-permute-done.3.refs_3_), channel_id=1, source_target_pairs={{0,2},{1,3},{2,0},{3,1},{4,6},{5,7},{6,4},{7,5},{8,10},{9,11},{10,... | collective-permute-start | bytes 903176 | tf_op jit(solution)/shard_map/ppermute | solution.py:301
  30.3 10.8 %collective-permute-start.8 = (bf16[24,6272]{1,0:T(8,128)(2,1)S(1)}, bf16[24,6272]{1,0:T(8,128)(2,1)S(1)}, u32[]{:S(2)}, u32[]{:S(2)}) collective-permute-start(bf16[24,6272]{1,0:T(8,128)(2,1)S(1)} %collective-permute-done.1.refs_2_), channel_id=1, source_target_pairs={{0,2},{1,3},{2,0},{3,1},{4,6},{5,7},{6,4},{7,5},{8,10},{9,11},{10,... | collective-permute-start | bytes 903176 | tf_op jit(solution)/shard_map/ppermute | solution.py:301
  36.7 12.6 %collective-permute-start.6 = (bf16[24,4352]{1,0:T(8,128)(2,1)S(1)}, bf16[24,4352]{1,0:T(8,128)(2,1)S(1)}, u32[]{:S(2)}, u32[]{:S(2)}) collective-permute-start(bf16[24,4352]{1,0:T(8,128)(2,1)S(1)} %get-tuple-element.21), channel_id=1, source_target_pairs={{0,2},{1,3},{2,0},{3,1},{4,6},{5,7},{6,4},{7,5},{8,10},{9,11},{10,... | collective-permute-start | bytes 626696 | tf_op jit(solution)/shard_map/ppermute | solution.py:301
  37.3 12.7 %collective-permute-start.7 = (bf16[24,2176]{1,0:T(8,128)(2,1)S(1)}, bf16[24,2176]{1,0:T(8,128)(2,1)S(1)}, u32[]{:S(2)}, u32[]{:S(2)}) collective-permute-start(bf16[24,2176]{1,0:T(8,128)(2,1)S(1)} %get-tuple-element.22), channel_id=1, source_target_pairs={{0,4},{1,5},{2,6},{3,7},{4,8},{5,9},{6,10},{7,11},{8,12},{9,13},{1... | collective-permute-start | bytes 313352 | tf_op jit(solution)/shard_map/ppermute | solution.py:301
  38.9 10.3 %collective-permute-start.12 = (bf16[24,2176]{1,0:T(8,128)(2,1)S(1)}, bf16[24,2176]{1,0:T(8,128)(2,1)S(1)}, u32[]{:S(2)}, u32[]{:S(2)}) collective-permute-start(bf16[24,2176]{1,0:T(8,128)(2,1)S(1)} %get-tuple-element.29), channel_id=1, source_target_pairs={{0,12},{1,13},{2,14},{3,15},{4,0},{5,1},{6,2},{7,3},{8,4},{9,5},{1... | collective-permute-start | bytes 313352 | tf_op jit(solution)/shard_map/ppermute | solution.py:301
  41.2 13.8 %copy-start = (s32[24,2048]{1,0:T(8,128)S(1)}, s32[24,2048]{1,0:T(8,128)}, u32[]{:S(2)}) copy-start(s32[24,2048]{1,0:T(8,128)} %signs.1) | copy-start | bytes 589828
  41.2 13.8 %copy-start.1 = (bf16[24,2048]{1,0:T(8,128)(2,1)S(1)}, bf16[24,2048]{1,0:T(8,128)(2,1)}, u32[]{:S(2)}) copy-start(bf16[24,2048]{1,0:T(8,128)(2,1)} %tokens.1) | copy-start | bytes 294916
  41.2 13.7 %copy-start.2 = (f32[2048]{0:T(1024)S(1)}, f32[2048]{0:T(1024)}, u32[]{:S(2)}) copy-start(f32[2048]{0:T(1024)} %param.8) | copy-start | bytes 24580
  45.1 9.3 %collective-permute-start.10 = (bf16[24,2176]{1,0:T(8,128)(2,1)S(1)}, bf16[24,2176]{1,0:T(8,128)(2,1)S(1)}, u32[]{:S(2)}, u32[]{:S(2)}) collective-permute-start(bf16[24,2176]{1,0:T(8,128)(2,1)S(1)} %get-tuple-element.26), channel_id=1, source_target_pairs={{0,10},{1,11},{2,8},{3,9},{4,14},{5,15},{6,12},{7,13},{8,2},{9,3},... | collective-permute-start | bytes 313352 | tf_op jit(solution)/shard_map/ppermute | solution.py:301
  45.6 8.8 %collective-permute-start.11 = (bf16[24,2176]{1,0:T(8,128)(2,1)S(1)}, bf16[24,2176]{1,0:T(8,128)(2,1)S(1)}, u32[]{:S(2)}, u32[]{:S(2)}) collective-permute-start(bf16[24,2176]{1,0:T(8,128)(2,1)S(1)} %get-tuple-element.27), channel_id=1, source_target_pairs={{0,6},{1,7},{2,4},{3,5},{4,10},{5,11},{6,8},{7,9},{8,14},{9,15},{1... | collective-permute-start | bytes 313352 | tf_op jit(solution)/shard_map/ppermute | solution.py:301
  49.3 5.6 %collective-permute-start.13 = (bf16[24,2176]{1,0:T(8,128)(2,1)S(1)}, bf16[24,2176]{1,0:T(8,128)(2,1)S(1)}, u32[]{:S(2)}, u32[]{:S(2)}) collective-permute-start(bf16[24,2176]{1,0:T(8,128)(2,1)S(1)} %add_convert_fusion), channel_id=1, source_target_pairs={{0,12},{1,13},{2,14},{3,15},{4,0},{5,1},{6,2},{7,3},{8,4},{9,5},{1... | collective-permute-start | bytes 313352 | tf_op jit(solution)/shard_map/ppermute | solution.py:301
